TPU v7x, 32 devices: a whole 2x2x4 slice. The times are simulated.
32 devices in a mesh: batch: 8 (over z, core), row: 4 (over y, x).
Axes of the slice: x: 2, y: 2, z: 4, core: 2. Of those that a mesh axis runs over, the one named last changes fastest.
Arguments:
- context_map: bfloat16 [32, 64, 64, 256], P('batch', 'row'), may hold values from -6 to 6
- future_feats: bfloat16 [32, 480, 256], P(('batch', 'row')), may hold values from -6 to 6
- horizon: int32 [32], P(('batch', 'row')), may hold values from 4 to 30, as said below
- cotangent: bfloat16 [32, 736, 768], P(('batch', 'row')), may hold values from -6 to 6
- tile_owner: int32 [124], replicated, may hold values from 0 to 31, as said below
- master_tiles: float32 [256, 256, 256], P(('batch', 'row')), as said below
- moment_first: float32 [256, 256, 256], P(('batch', 'row')), may hold values from -0.00061035156 to 0.00061035156
- moment_second: float32 [256, 256, 256], P(('batch', 'row')), may hold values from 1.2305475e-10 to 4.92219e-10
- norm_gains: float32 [2, 768], replicated, may hold values from 0.5 to 1.5
- gain_first: float32 [2, 768], replicated, may hold values from -0.0024414062 to 0.0024414062
- gain_second: float32 [2, 768], replicated, may hold values from 1.968876e-09 to 7.875504e-09
Outputs:
- block_out: float32 [32, 736, 768], P(('batch', 'row'))
- context_grad: float32 [32, 64, 64, 256], P('batch', 'row')
- future_grad: float32 [32, 480, 256], P(('batch', 'row'))
- new_first: float32 [256, 256, 256], P(('batch', 'row'))
- new_second: float32 [256, 256, 256], P(('batch', 'row'))
- new_master: float32 [256, 256, 256], P(('batch', 'row'))
- new_gain_first: float32 [2, 768], replicated
- new_gain_second: float32 [2, 768], replicated
- new_gains: float32 [2, 768], replicated
- grad_norm: float32 [], replicated
Inputs may be any that keep to these rules, and one draw needn't show every extreme that they name: `horizon`: some clip has 30 future frames and some clip has 4. `tile_owner`: owner index counts devices over batch, then row. No device owns more than 8 tiles, and some device owns exactly 8. `master_tiles`: slots that hold no tile carry values that no output reads.
All inputs are finite; a program needn't handle non-finite values.
Results may differ from a plain program's by a relative error of at most 0.017.
The roundings to bfloat16 on the way count: a program that leaves them out, or rounds other values in their place, can miss the bound.
Values may be sent and summed in bfloat16 or wider, within the bound.
No kernel may reach another device: no remote copies, remote signals or barrier semaphores. Data moves between devices by JAX's collectives and lax.ppermute only.
A program may use at most 448 MiB of HBM per device.

v0:
```python
import jax
import jax.numpy as jnp
from jax import lax
from jax.sharding import PartitionSpec as P

CH = 256
HD = 64
HEADS = 12
D = 768
FF = 3072
TH = 4
IMG = 64
PATCH = 4
FT = 16
CTX = 256
SEQ = 736
STEP = 10


eps_norm = 1e-05
beta_one = 0.9
beta_two = 0.999
learn_rate = 0.02
gain_rate = 0.6
decay_rate = 0.1
adam_eps = 1e-08
clip_level = 1.0
neg_large = -1e30


def padded_2(cells, sides, width):
    for axis, dim in sides:
        count = lax.axis_size(axis)
        ends = count - 1
        head = lax.slice_in_dim(cells, 0, width, axis=dim)
        tail = lax.slice_in_dim(cells, cells.shape[dim] - width, cells.shape[dim], axis=dim)
        cells = jnp.concatenate(
            [
                lax.ppermute(tail, axis, [(i, (i + 1) % count) for i in range(ends)]),
                cells,
                lax.ppermute(head, axis, [((i + 1) % count, i) for i in range(ends)]),
            ],
            axis=dim,
        )
    return cells


def slot_index(tile_owner, slot_count):
    ordinal = jnp.arange(tile_owner.shape[0])
    earlier = (tile_owner[None, :] == tile_owner[:, None]) & (ordinal[None, :] < ordinal[:, None])
    return tile_owner * slot_count + jnp.sum(earlier.astype(jnp.int32), 1)


def unpack(tile_stack):
    per_model = D // CH
    per_hidden = FF // CH
    conv_tiles = tile_stack[0:9]
    att_tiles = tile_stack[9:13]
    offset = 13
    matrices = []
    for tile_rows, tile_cols in (
        (1, per_model),
        (per_model, 3 * per_model),
        (per_model, per_model),
        (per_model, per_hidden),
        (per_hidden, per_model),
    ):
        amount = tile_rows * tile_cols
        tile_block = tile_stack[offset : offset + amount].reshape(tile_rows, tile_cols, CH, CH)
        matrices.append(tile_block.transpose(0, 2, 1, 3).reshape(tile_rows * CH, tile_cols * CH))
        offset = offset + amount
    return (conv_tiles, att_tiles, matrices)


def pack(conv_grad, att_grad, matrices):
    pieces = [conv_grad, att_grad]
    for matrix in matrices:
        tile_rows = matrix.shape[0] // CH
        tile_cols = matrix.shape[1] // CH
        pieces.append(
            matrix.reshape(tile_rows, CH, tile_cols, CH)
            .transpose(0, 2, 1, 3)
            .reshape(tile_rows * tile_cols, CH, CH)
        )
    return jnp.concatenate(pieces, 0)


def rms_norm(values, gain):
    return values * lax.rsqrt(jnp.mean(values * values, -1, keepdims=True) + eps_norm) * gain


def gelu_tanh(values):
    return jax.nn.gelu(values, approximate=True)


def adam_step(weight, grad_now, first, second, rate, decay):
    first_new = beta_one * first + (1.0 - beta_one) * grad_now
    second_new = beta_two * second + (1.0 - beta_two) * grad_now * grad_now
    corr_first = first_new / (1.0 - beta_one**STEP)
    corr_second = second_new / (1.0 - beta_two**STEP)
    weight_new = weight - rate * (corr_first / (jnp.sqrt(corr_second) + adam_eps) + decay * weight)
    return (first_new, second_new, weight_new)


def pad_columns(values):
    return jnp.pad(values, ((0, 0), (0, 0), (1, 1), (0, 0)))


def conv_forward(padded, conv_tiles, height):
    conv_sum = jnp.zeros((padded.shape[0], height, IMG, CH), jnp.float32)
    for offset_y in range(3):
        for offset_x in range(3):
            window = padded[:, offset_y : offset_y + height, offset_x : offset_x + IMG]
            conv_sum = conv_sum + jnp.einsum(
                "nabc,cd->nabd",
                window,
                conv_tiles[3 * offset_y + offset_x],
                preferred_element_type=jnp.float32,
            )
    return conv_sum


def conv_weight_grad(padded, d_conv, height):
    tap_grads = []
    for offset_y in range(3):
        for offset_x in range(3):
            window = padded[:, offset_y : offset_y + height, offset_x : offset_x + IMG]
            tap_grads.append(
                jnp.einsum("nabc,nabd->cd", window, d_conv, preferred_element_type=jnp.float32)
            )
    return jnp.stack(tap_grads)


def conv_input_grad(d_padded, conv_tiles, height):
    input_sum = jnp.zeros((d_padded.shape[0], height, IMG, CH), jnp.float32)
    for offset_y in range(3):
        for offset_x in range(3):
            window = d_padded[
                :, 2 - offset_y : 2 - offset_y + height, 2 - offset_x : 2 - offset_x + IMG
            ]
            input_sum = input_sum + jnp.einsum(
                "nabd,cd->nabc",
                window,
                conv_tiles[3 * offset_y + offset_x],
                preferred_element_type=jnp.float32,
            )
    return input_sum


def cross_forward(feats_b, kv_clip, to_query, to_out):
    score_scale = HD ** (-0.5)
    query_b = jnp.dot(feats_b, to_query, preferred_element_type=jnp.float32).astype(jnp.bfloat16)
    key_heads = kv_clip[:, :CH].reshape(-1, TH, HD)
    value_heads = kv_clip[:, CH:].reshape(-1, TH, HD)
    scores = (
        jnp.einsum(
            "qhd,khd->hqk",
            query_b.reshape(-1, TH, HD),
            key_heads,
            preferred_element_type=jnp.float32,
        )
        * score_scale
    )
    row_peak = jnp.max(scores, -1, keepdims=True)
    shifted = jnp.exp(scores - row_peak)
    row_total = jnp.sum(shifted, -1, keepdims=True)
    probs_b = (shifted / row_total).astype(jnp.bfloat16)
    mixed_b = (
        jnp.einsum("hqk,khd->qhd", probs_b, value_heads, preferred_element_type=jnp.float32)
        .reshape(-1, CH)
        .astype(jnp.bfloat16)
    )
    updated = feats_b.astype(jnp.float32) + jnp.dot(
        mixed_b, to_out, preferred_element_type=jnp.float32
    )
    return (query_b, mixed_b, row_peak + jnp.log(row_total), updated)


def cross_backward(feats_b, kv_clip, query_b, mixed_b, log_total, d_updated, to_query, to_out):
    score_scale = HD ** (-0.5)
    d_branch = d_updated.astype(jnp.bfloat16)
    grad_out = jnp.dot(mixed_b.T, d_branch, preferred_element_type=jnp.float32)
    d_mixed = (
        jnp.dot(d_branch, to_out.T, preferred_element_type=jnp.float32)
        .astype(jnp.bfloat16)
        .reshape(-1, TH, HD)
    )
    key_heads = kv_clip[:, :CH].reshape(-1, TH, HD)
    value_heads = kv_clip[:, CH:].reshape(-1, TH, HD)
    query_heads = query_b.reshape(-1, TH, HD)
    scores = (
        jnp.einsum("qhd,khd->hqk", query_heads, key_heads, preferred_element_type=jnp.float32)
        * score_scale
    )
    probs = jnp.exp(scores - log_total)
    d_probs = jnp.einsum("qhd,khd->hqk", d_mixed, value_heads, preferred_element_type=jnp.float32)
    d_values = jnp.einsum(
        "hqk,qhd->khd", probs.astype(jnp.bfloat16), d_mixed, preferred_element_type=jnp.float32
    )
    d_scores = (probs * (d_probs - jnp.sum(probs * d_probs, -1, keepdims=True))).astype(
        jnp.bfloat16
    )
    d_query = (
        (
            jnp.einsum("hqk,khd->qhd", d_scores, key_heads, preferred_element_type=jnp.float32)
            * score_scale
        )
        .reshape(-1, CH)
        .astype(jnp.bfloat16)
    )
    d_keys = (
        jnp.einsum("hqk,qhd->khd", d_scores, query_heads, preferred_element_type=jnp.float32)
        * score_scale
    )
    d_kv = jnp.concatenate([d_keys.reshape(-1, CH), d_values.reshape(-1, CH)], 1).astype(
        jnp.bfloat16
    )
    grad_query = jnp.dot(feats_b.T, d_query, preferred_element_type=jnp.float32)
    d_feats = d_updated + jnp.dot(d_query, to_query.T, preferred_element_type=jnp.float32)
    return (d_kv, d_feats, grad_query, grad_out)


def causal_scores(qkv_b, length):
    position = jnp.arange(qkv_b.shape[0])
    allowed = (position[None, :] <= position[:, None]) & (position[None, :] < length)
    query_heads = qkv_b[:, :D].reshape(-1, HEADS, HD)
    key_heads = qkv_b[:, D : 2 * D].reshape(-1, HEADS, HD)
    raw_scores = jnp.einsum(
        "qhd,khd->hqk", query_heads, key_heads, preferred_element_type=jnp.float32
    ) * HD ** (-0.5)
    return jnp.where(allowed[None], raw_scores, neg_large)


def gpt_forward(seq_in, length, norm_gains, matrices):
    w_emb, w_qkv, w_att, w_up, w_down = matrices
    embed = jnp.dot(seq_in, w_emb, preferred_element_type=jnp.float32)
    normed_b = rms_norm(embed, norm_gains[0]).astype(jnp.bfloat16)
    qkv_b = jnp.dot(normed_b, w_qkv, preferred_element_type=jnp.float32).astype(jnp.bfloat16)
    scores = causal_scores(qkv_b, length)
    row_peak = jnp.max(scores, -1, keepdims=True)
    shifted = jnp.exp(scores - row_peak)
    row_total = jnp.sum(shifted, -1, keepdims=True)
    probs_b = (shifted / row_total).astype(jnp.bfloat16)
    value_heads = qkv_b[:, 2 * D :].reshape(-1, HEADS, HD)
    mixed_b = (
        jnp.einsum("hqk,khd->qhd", probs_b, value_heads, preferred_element_type=jnp.float32)
        .reshape(-1, D)
        .astype(jnp.bfloat16)
    )
    stream = embed + jnp.dot(mixed_b, w_att, preferred_element_type=jnp.float32)
    normed_two = rms_norm(stream, norm_gains[1]).astype(jnp.bfloat16)
    pre_act = jnp.dot(normed_two, w_up, preferred_element_type=jnp.float32)
    act_b = gelu_tanh(pre_act).astype(jnp.bfloat16)
    result = stream + jnp.dot(act_b, w_down, preferred_element_type=jnp.float32)
    return (result, (embed, qkv_b, row_peak + jnp.log(row_total), mixed_b, stream, pre_act))


def gpt_backward(seq_in, length, norm_gains, matrices, kept, d_result):
    w_emb, w_qkv, w_att, w_up, w_down = matrices
    embed, qkv_b, log_total, mixed_b, stream, pre_act = kept
    d_down = d_result.astype(jnp.bfloat16)
    act_b = gelu_tanh(pre_act).astype(jnp.bfloat16)
    grad_down = jnp.dot(act_b.T, d_down, preferred_element_type=jnp.float32)
    d_act = jnp.dot(d_down, w_down.T, preferred_element_type=jnp.float32)
    d_pre = jax.vjp(gelu_tanh, pre_act)[1](d_act)[0].astype(jnp.bfloat16)
    normed_two, norm_back_two = jax.vjp(rms_norm, stream, norm_gains[1])
    grad_up = jnp.dot(normed_two.astype(jnp.bfloat16).T, d_pre, preferred_element_type=jnp.float32)
    d_stream_norm, d_gain_two = norm_back_two(
        jnp.dot(d_pre, w_up.T, preferred_element_type=jnp.float32)
    )
    d_stream = d_result + d_stream_norm
    d_att = d_stream.astype(jnp.bfloat16)
    grad_att = jnp.dot(mixed_b.T, d_att, preferred_element_type=jnp.float32)
    d_mixed = (
        jnp.dot(d_att, w_att.T, preferred_element_type=jnp.float32)
        .astype(jnp.bfloat16)
        .reshape(-1, HEADS, HD)
    )
    probs = jnp.exp(causal_scores(qkv_b, length) - log_total)
    query_heads = qkv_b[:, :D].reshape(-1, HEADS, HD)
    key_heads = qkv_b[:, D : 2 * D].reshape(-1, HEADS, HD)
    value_heads = qkv_b[:, 2 * D :].reshape(-1, HEADS, HD)
    d_probs = jnp.einsum("qhd,khd->hqk", d_mixed, value_heads, preferred_element_type=jnp.float32)
    d_values = jnp.einsum(
        "hqk,qhd->khd", probs.astype(jnp.bfloat16), d_mixed, preferred_element_type=jnp.float32
    )
    d_scores = (probs * (d_probs - jnp.sum(probs * d_probs, -1, keepdims=True))).astype(
        jnp.bfloat16
    )
    d_query = jnp.einsum(
        "hqk,khd->qhd", d_scores, key_heads, preferred_element_type=jnp.float32
    ) * HD ** (-0.5)
    d_keys = jnp.einsum(
        "hqk,qhd->khd", d_scores, query_heads, preferred_element_type=jnp.float32
    ) * HD ** (-0.5)
    d_qkv = jnp.concatenate(
        [d_query.reshape(-1, D), d_keys.reshape(-1, D), d_values.reshape(-1, D)], 1
    ).astype(jnp.bfloat16)
    normed_one, norm_back_one = jax.vjp(rms_norm, embed, norm_gains[0])
    grad_qkv = jnp.dot(normed_one.astype(jnp.bfloat16).T, d_qkv, preferred_element_type=jnp.float32)
    d_embed_norm, d_gain_one = norm_back_one(
        jnp.dot(d_qkv, w_qkv.T, preferred_element_type=jnp.float32)
    )
    d_embed = (d_stream + d_embed_norm).astype(jnp.bfloat16)
    grad_emb = jnp.dot(seq_in.T, d_embed, preferred_element_type=jnp.float32)
    d_seq = jnp.dot(d_embed, w_emb.T, preferred_element_type=jnp.float32)
    return (
        d_seq,
        (grad_emb, grad_qkv, grad_att, grad_up, grad_down),
        jnp.stack([d_gain_one, d_gain_two]),
    )


def local(
    context_map,
    future_feats,
    horizon,
    cotangent,
    tile_owner,
    master_tiles,
    moment_first,
    moment_second,
    norm_gains,
    gain_first,
    gain_second,
):
    slot_count = master_tiles.shape[0]
    slot_of = slot_index(tile_owner, slot_count)
    gathered = lax.all_gather(
        master_tiles.astype(jnp.bfloat16), ("batch", "row"), axis=0, tiled=True
    )
    tile_stack = jnp.take(gathered, slot_of, axis=0)
    conv_tiles, att_tiles, matrices = unpack(tile_stack)
    kv_weight = jnp.concatenate([att_tiles[1], att_tiles[2]], 1)
    height = context_map.shape[1]
    padded = pad_columns(padded_2(context_map, (("row", 1),), 1))
    conv_out = conv_forward(padded, conv_tiles, height)
    hidden = padded[:, 1 : height + 1, 1 : IMG + 1].astype(jnp.float32) + jax.nn.silu(conv_out)
    hidden_b = hidden.astype(jnp.bfloat16)
    groups = hidden.shape[0]
    kv_local = (
        jnp.einsum("nabc,ce->nabe", hidden_b, kv_weight, preferred_element_type=jnp.float32)
        .astype(jnp.bfloat16)
        .reshape(groups, height * IMG, 2 * CH)
    )
    pooled = (
        jnp.mean(
            hidden.reshape(groups, height // PATCH, PATCH, IMG // PATCH, PATCH, CH), axis=(2, 4)
        )
        .reshape(groups, -1, CH)
        .astype(jnp.bfloat16)
    )
    whole_kv, whole_pool = (
        lax.all_to_all(kv_local, "row", split_axis=0, concat_axis=1, tiled=True),
        lax.all_to_all(pooled, "row", split_axis=0, concat_axis=1, tiled=True),
    )
    valid_len = CTX + FT * horizon
    totals_init = (
        jnp.zeros((CH, CH), jnp.float32),
        jnp.zeros((CH, CH), jnp.float32),
        jnp.zeros((CH, D), jnp.float32),
        jnp.zeros((D, 3 * D), jnp.float32),
        jnp.zeros((D, D), jnp.float32),
        jnp.zeros((D, FF), jnp.float32),
        jnp.zeros((FF, D), jnp.float32),
        jnp.zeros((2, D), jnp.float32),
    )

    def clip_step(totals, clip_item):
        kv_clip, pool_clip, feats_b, length, back_rows = clip_item
        query_b, mixed_b, cross_total, updated = cross_forward(
            feats_b, kv_clip, att_tiles[0], att_tiles[3]
        )
        seq_in = jnp.concatenate([pool_clip, updated.astype(jnp.bfloat16)], 0)
        result, kept = gpt_forward(seq_in, length, norm_gains, matrices)
        position = jnp.arange(SEQ)
        d_result = back_rows.astype(jnp.float32) * (position < length).astype(jnp.float32)[:, None]
        d_seq, mat_grads, gain_grad = gpt_backward(
            seq_in, length, norm_gains, matrices, kept, d_result
        )
        d_pool = d_seq[:CTX].astype(jnp.bfloat16)
        d_kv, d_feats, grad_query, grad_out = cross_backward(
            feats_b, kv_clip, query_b, mixed_b, cross_total, d_seq[CTX:], att_tiles[0], att_tiles[3]
        )
        new_totals = jax.tree.map(
            jnp.add, totals, (grad_query, grad_out) + tuple(mat_grads) + (gain_grad,)
        )
        return (new_totals, (result, d_kv, d_pool, d_feats))

    totals, outputs = lax.scan(
        clip_step, totals_init, (whole_kv, whole_pool, future_feats, valid_len, cotangent)
    )
    grad_query, grad_out, grad_emb, grad_qkv, grad_att, grad_up, grad_down, gain_grads = totals
    block_out, d_kv_all, d_pool_all, future_grad = outputs
    d_kv_local, d_pool_local = (
        lax.all_to_all(d_kv_all, "row", split_axis=1, concat_axis=0, tiled=True),
        lax.all_to_all(d_pool_all, "row", split_axis=1, concat_axis=0, tiled=True),
    )
    grad_kv = jnp.einsum(
        "npc,npe->ce",
        hidden_b.reshape(groups, height * IMG, CH),
        d_kv_local,
        preferred_element_type=jnp.float32,
    )
    d_hidden = jnp.einsum(
        "npe,ce->npc", d_kv_local, kv_weight, preferred_element_type=jnp.float32
    ).reshape(groups, height, IMG, CH)
    pool_spread = d_pool_local.astype(jnp.float32).reshape(
        groups, height // PATCH, 1, IMG // PATCH, 1, CH
    ) * (1.0 / (PATCH * PATCH))
    d_hidden = d_hidden + jnp.broadcast_to(
        pool_spread, (groups, height // PATCH, PATCH, IMG // PATCH, PATCH, CH)
    ).reshape(groups, height, IMG, CH)
    d_conv = jax.vjp(jax.nn.silu, conv_out)[1](d_hidden)[0].astype(jnp.bfloat16)
    grad_conv = conv_weight_grad(padded, d_conv, height)
    d_conv_pad = pad_columns(padded_2(d_conv, (("row", 1),), 1))
    context_grad = d_hidden + conv_input_grad(d_conv_pad, conv_tiles, height)
    att_grads = jnp.stack([grad_query, grad_kv[:, :CH], grad_kv[:, CH:], grad_out])
    tile_grads = pack(grad_conv, att_grads, (grad_emb, grad_qkv, grad_att, grad_up, grad_down))
    mine_index = lax.axis_index(("batch", "row")) * slot_count + jnp.arange(slot_count)
    select = (slot_of[None, :] == mine_index[:, None]).astype(jnp.float32)
    used = jnp.sum(select, 1)[:, None, None]
    spread = (
        jnp.zeros((lax.axis_size(("batch", "row")) * slot_count, CH, CH), jnp.float32)
        .at[slot_of]
        .set(tile_grads)
    )
    mine = lax.psum_scatter(spread, ("batch", "row"), scatter_dimension=0, tiled=True)
    square_part, gain_total = lax.psum((jnp.sum(mine * mine), gain_grads), ("batch", "row"))
    grad_norm = jnp.sqrt(square_part + jnp.sum(gain_total * gain_total))
    factor = jnp.minimum(1.0, clip_level / (grad_norm + 1e-06))
    new_first, new_second, new_master = adam_step(
        master_tiles, mine * factor, moment_first, moment_second, learn_rate, decay_rate
    )
    new_gain_first, new_gain_second, new_gains = adam_step(
        norm_gains, gain_total * factor, gain_first, gain_second, gain_rate, 0.0
    )
    return (
        block_out,
        context_grad,
        future_grad,
        new_first * used,
        new_second * used,
        new_master * used,
        new_gain_first,
        new_gain_second,
        new_gains,
        grad_norm,
    )


def solution(mesh):
    in_specs = (
        P("batch", "row", None, None),
        P(("batch", "row"), None, None),
        P(("batch", "row")),
        P(("batch", "row"), None, None),
        P(),
        P(("batch", "row"), None, None),
        P(("batch", "row"), None, None),
        P(("batch", "row"), None, None),
        P(),
        P(),
        P(),
    )
    out_specs = (
        P(("batch", "row"), None, None),
        P("batch", "row", None, None),
        P(("batch", "row"), None, None),
        P(("batch", "row"), None, None),
        P(("batch", "row"), None, None),
        P(("batch", "row"), None, None),
        P(),
        P(),
        P(),
        P(),
    )
    return jax.shard_map(local, mesh=mesh, in_specs=in_specs, out_specs=out_specs, check_vma=False)
```

profile of v0, /device:TPU:0, one launch (start us, length us, event | category | flops | bytes accessed | tf_op | source)
XLA Modules:
  0.0 2464.3 jit_solution(64059964451197120)
XLA Ops:
  24.7 184.3 %all-gather.2.cloned.1.call-done = bf16[256,256,256]{2,1,0:T(8,128)(2,1)} async-done(((bf16[8,256,256]{2,1,0:T(8,128)(2,1)}), bf16[256,256,256]{2,1,0:T(8,128)(2,1)}) %all-gather.2.cloned.1.call-update) | async-done | bytes 33554448 | tf_op jit(solution)/shard_map/all_gather | solution.py:329
  209.0 12.0 gather_fusion
  254.3 15.9 fusion.216
  371.3 12.4 multiply_reduce_fusion.2
  383.6 13.6 fusion
  397.3 13.9 fusion.98
  426.0 11.6 fusion.223
  437.6 11.7 fusion.1
  500.9 12.2 fusion.90
  513.1 22.3 multiply_reduce_fusion.1
  535.4 22.9 multiply_convert_fusion.1
  584.8 14.6 fusion.30
  599.5 21.1 multiply_reduce_fusion
  640.7 26.4 %multiply_convert_fusion = bf16[4,480,4096]{2,1,0:T(8,128)(2,1)} fusion(f32[4,480,4096]{2,1,0:T(8,128)} %get-tuple-element.141, f32[4,480,4096]{2,1,0:T(8,128)} %get-tuple-element.129, f32[4,480]{1,0:T(4,128)S(1)} %get-tuple-element.140, f32[4,480]{1,0:T(4,128)S(1)} %copy-done.59), kind=kLoop, calls=%fused_computation.2 | loop fusion | flops 39321600 | bytes 78658560 | tf_op jit(solution)/shard_map/while/body/eval_jaxpr/convert_element_type | solution.py:200
  715.9 12.4 reshape.389
  728.4 13.8 copy.321
  742.1 28.5 %reduce.5 = bf16[4096,512]{1,0:T(8,128)(2,1)} reduce(bf16[4096,1,512]{2,1,0:T(2,128)(2,1)} %fusion.224, bf16[]{:T(256)} %broadcast.309), dimensions={1}, to_apply=%fusion.224.reduce_sub_computation | reduce | bytes 8388610
  783.7 11.6 reshape.386
  899.7 21.2 broadcast_in_dim.125
  920.8 59.6 %scatter_fusion = f32[256,256,256]{2,1,0:T(8,128)} fusion(f32[256,256,256]{2,1,0:T(8,128)} %broadcast_in_dim.125, s32[124]{0:T(128)S(1)} %copy-done.80, f32[124,256,256]{2,1,0:T(8,128)} %constant_dynamic-update-slice_fusion.4), kind=kCustom, calls=%fused_computation.1 | custom fusion | bytes 97518064 | tf_op jit(solution)/shard_map/scatter | solution.py:426
  983.3 13.3 add_bitcast_fusion
  1034.3 1354.0 %reduce-scatter.2.cloned.1.call-done = f32[8,256,256]{2,1,0:T(8,128)} async-done(((f32[256,256,256]{2,1,0:T(8,128)}), f32[8,256,256]{2,1,0:T(8,128)}) %reduce-scatter.2.cloned.1.call-update) | async-done | bytes 2097168 | tf_op jit(solution)/shard_map/reduce_scatter | solution.py:428
  2391.1 15.1 add_add_fusion
  2406.2 39.9 %all-reduce.2 = (f32[]{:T(128)}, f32[2,768]{1,0:T(2,128)S(1)}) all-reduce(f32[]{:T(128)} %multiply_reduce_fusion.9, f32[2,768]{1,0:T(2,128)S(1)} %pad_maximum_fusion.7), channel_id=1, replica_groups=mesh['batch'=8,'row'=4] {'batch','row'}, use_global_device_ids=true, to_apply=%region_15.16 | all-reduce | flops 1537 | bytes 12296 | tf_op jit(solution)/shard_map/psum | solution.py:429
  (391 shorter events, 481.1 us)
Async XLA Ops:
  7.2 201.8 %all-gather.2.cloned.1.call-start = ((), (), s32[]{:S(2)}) async-start(), calls=%async_computation.5 | async-start | bytes 34603008 | tf_op jit(solution)/shard_map/all_gather | solution.py:329
  10.1 7.7 collective-permute-start
  15.1 7.5 collective-permute-start.1
  229.5 40.7 %copy-start.60 = (bf16[256,256]{1,0:T(8,128)(2,1)}, bf16[256,256]{1,0:T(8,128)(2,1)S(1)}, u32[]{:S(2)}) copy-start(bf16[256,256]{1,0:T(8,128)(2,1)S(1)} %get-tuple-element.104) | copy-start | bytes 393220
  229.5 40.7 %copy-start.62 = (bf16[256,256]{1,0:T(8,128)(2,1)}, bf16[256,256]{1,0:T(8,128)(2,1)S(1)}, u32[]{:S(2)}) copy-start(bf16[256,256]{1,0:T(8,128)(2,1)S(1)} %get-tuple-element.105) | copy-start | bytes 393220
  275.0 80.0 %all-to-all-start.1 = ((bf16[4,1024,512]{2,1,0:T(8,128)(2,1)}), bf16[4,1024,512]{2,1,0:T(8,128)(2,1)}, u32[]{:S(2)}, u32[]{:S(2)}) async-start(bf16[4,1024,512]{2,1,0:T(8,128)(2,1)} %bitcast.416), calls=%async_computation.1 | async-start | bytes 8388608 | tf_op jit(solution)/shard_map/all_to_all | solution.py:354
  282.1 131.7 %copy-start.71 = (f32[768]{0:T(1024)}, f32[768]{0:T(1024)S(1)}, u32[]{:S(2)}) copy-start(f32[768]{0:T(1024)S(1)} %get-tuple-element.65) | copy-start | bytes 9220
  294.8 76.5 %copy-start.33 = (bf16[480,256]{0,1:T(8,128)(2,1)}, bf16[480,256]{0,1:T(8,128)(2,1)S(1)}, u32[]{:S(2)}) copy-start(bf16[480,256]{0,1:T(8,128)(2,1)S(1)} %copy.277) | copy-start | bytes 737284
  296.1 117.1 %copy-start.30 = (bf16[1,256,3,256]{1,3,2,0:T(8,128)(2,1)}, bf16[1,256,3,256]{1,3,2,0:T(8,128)(2,1)S(1)}, u32[]{:S(2)}) copy-start(bf16[1,256,3,256]{1,3,2,0:T(8,128)(2,1)S(1)} %copy.279) | copy-start | bytes 1179652
  355.0 58.1 %all-to-all-start = ((bf16[4,64,256]{2,1,0:T(8,128)(2,1)}), bf16[4,64,256]{2,1,0:T(8,128)(2,1)S(1)}, u32[]{:S(2)}, u32[]{:S(2)}) async-start(bf16[4,64,256]{2,1,0:T(8,128)(2,1)} %bitcast.28), calls=%async_computation | async-start | bytes 262144 | tf_op jit(solution)/shard_map/all_to_all | solution.py:355
  462.8 30.9 %copy-start.11 = (f32[736,768]{1,0:T(8,128)}, f32[736,768]{1,0:T(8,128)S(1)}, u32[]{:S(2)}) copy-start(f32[736,768]{1,0:T(8,128)S(1)} %get-tuple-element.135) | copy-start | bytes 6782980
  626.6 150.3 %all-to-all-start.3 = ((bf16[4,2,8192]{2,1,0:T(2,128)(2,1)}), bf16[4,2,8192]{2,1,0:T(2,128)(2,1)}, u32[]{:S(2)}, u32[]{:S(2)}) async-start(bf16[4,2,8192]{2,1,0:T(2,128)(2,1)} %reshape.439), calls=%async_computation.3 | async-start | bytes 262144 | tf_op jit(solution)/shard_map/all_to_all | solution.py:397
  640.7 26.4 %copy-start.34 = (bf16[480,256]{0,1:T(8,128)(2,1)S(1)}, bf16[480,256]{0,1:T(8,128)(2,1)}, u32[]{:S(2)}) copy-start(bf16[480,256]{0,1:T(8,128)(2,1)} %copy-done.33) | copy-start | bytes 737284
  776.9 62.3 %all-to-all-start.2 = ((bf16[4,2,262144]{2,1,0:T(2,128)(2,1)}), bf16[4,2,262144]{2,1,0:T(2,128)(2,1)}, u32[]{:S(2)}, u32[]{:S(2)}) async-start(bf16[4,2,262144]{2,1,0:T(2,128)(2,1)} %reshape.441), calls=%async_computation.2 | async-start | bytes 8388608 | tf_op jit(solution)/shard_map/all_to_all | solution.py:396
  781.9 1606.5 %reduce-scatter.2.cloned.1.call-start = ((), (), s32[]{:S(2)}) async-start(), calls=%async_computation.6 | async-start | bytes 69206016 | tf_op jit(solution)/shard_map/reduce_scatter | solution.py:428
  856.3 158.7 %copy-start.1 = (bf16[4,16,64,256]{3,2,1,0:T(8,128)(2,1)}, bf16[4,16,64,256]{3,2,1,0:T(8,128)(2,1)S(1)}, u32[]{:S(2)}) copy-start(bf16[4,16,64,256]{3,2,1,0:T(8,128)(2,1)S(1)} %get-tuple-element.142) | copy-start | bytes 6291460
  983.3 31.7 %slice-start.8 = ((s8[16252928]{0:T(1024)(128)(4,1)}), s8[3670016]{0:T(1024)(128)(4,1)S(1)}, s32[]{:S(2)}) async-start(s8[16252928]{0:T(1024)(128)(4,1)} %bitcast.404), calls=%async_computation.15 | async-start | bytes 7340032
  983.3 31.7 %slice-start.9 = ((s8[16252928]{0:T(1024)(128)(4,1)}), s8[4194304]{0:T(1024)(128)(4,1)S(1)}, s32[]{:S(2)}) async-start(s8[16252928]{0:T(1024)(128)(4,1)} %bitcast.404), calls=%async_computation.16 | async-start | bytes 8388608
  983.3 31.7 %slice-start.10 = ((s8[16252928]{0:T(1024)(128)(4,1)}), s8[4194304]{0:T(1024)(128)(4,1)S(1)}, s32[]{:S(2)}) async-start(s8[16252928]{0:T(1024)(128)(4,1)} %bitcast.404), calls=%async_computation.17 | async-start | bytes 8388608
  996.6 11.6 collective-permute-start.2
  1004.5 10.4 collective-permute-start.3
  2391.1 57.0 %copy-start.69 = (f32[2,768]{1,0:T(2,128)S(1)}, f32[2,768]{1,0:T(2,128)}, u32[]{:S(2)}) copy-start(f32[2,768]{1,0:T(2,128)} %param.19) | copy-start | bytes 18436
  2391.1 57.0 %copy-start.75 = (f32[2,768]{1,0:T(2,128)S(1)}, f32[2,768]{1,0:T(2,128)}, u32[]{:S(2)}) copy-start(f32[2,768]{1,0:T(2,128)} %param.21) | copy-start | bytes 18436
  2391.1 57.0 %copy-start.76 = (f32[2,768]{1,0:T(2,128)S(1)}, f32[2,768]{1,0:T(2,128)}, u32[]{:S(2)}) copy-start(f32[2,768]{1,0:T(2,128)} %param.20) | copy-start | bytes 18436
  (95 other events, 708.9 us)
Sparse Core Ops, SparseCore 0:
  11.5 197.4 all-gather.1
  980.6 1407.7 reduce-scatter.1
where the time goes:
time: 2480 us; the launch traced here: 2460 us
  waiting for transfers between devices  1550 us (62%)
  matrix products  347 us (14%)
  local copies, waits for them, and re-layouts  327 us (13%)
  other arithmetic  154 us (6%)
  blocking collectives  39.9 us (2%)
  starting transfers between devices  30.6 us (1%)
    reduce_scatter x1, waiting for transfers between devices, local(): lax.psum_scatter(spread, ('batch', 'row'), scatter_dimension=0, tiled=True)  1350 us
    all_gather x1, waiting for transfers between devices, local(): lax.all_gather(master_tiles.astype(jnp.bfloat16), ('batch', 'row'), axis=...  184 us
    unnamed x238, local copies, waits for them, and re-layouts  70.9 us
    scatter x1, local copies, waits for them, and re-layouts, local(): spread = jnp.zeros((lax.axis_size(('batch', 'row')) * slot_count, CH, CH)...  59.6 us
  transfers between devices with their start and end apart: 10, of which 6 were waited for; matrix products, arithmetic and copies ran while one was open for 15% of the time, Pallas kernels for 0%

commit v1 on v0

--- a/solution.py
+++ b/solution.py
@@ -26,23 +26,7 @@
 adam_eps = 1e-08
 clip_level = 1.0
 neg_large = -1e30
-
-
-def padded_2(cells, sides, width):
-    for axis, dim in sides:
-        count = lax.axis_size(axis)
-        ends = count - 1
-        head = lax.slice_in_dim(cells, 0, width, axis=dim)
-        tail = lax.slice_in_dim(cells, cells.shape[dim] - width, cells.shape[dim], axis=dim)
-        cells = jnp.concatenate(
-            [
-                lax.ppermute(tail, axis, [(i, (i + 1) % count) for i in range(ends)]),
-                cells,
-                lax.ppermute(head, axis, [((i + 1) % count, i) for i in range(ends)]),
-            ],
-            axis=dim,
-        )
-    return cells
+AXES = ("z", "c", "y", "x")
 
 
 def slot_index(tile_owner, slot_count):
@@ -102,49 +86,62 @@
     return (first_new, second_new, weight_new)
 
 
-def pad_columns(values):
-    return jnp.pad(values, ((0, 0), (0, 0), (1, 1), (0, 0)))
-
-
-def conv_forward(padded, conv_tiles, height):
-    conv_sum = jnp.zeros((padded.shape[0], height, IMG, CH), jnp.float32)
-    for offset_y in range(3):
-        for offset_x in range(3):
-            window = padded[:, offset_y : offset_y + height, offset_x : offset_x + IMG]
-            conv_sum = conv_sum + jnp.einsum(
-                "nabc,cd->nabd",
-                window,
-                conv_tiles[3 * offset_y + offset_x],
-                preferred_element_type=jnp.float32,
-            )
-    return conv_sum
-
-
-def conv_weight_grad(padded, d_conv, height):
-    tap_grads = []
-    for offset_y in range(3):
-        for offset_x in range(3):
-            window = padded[:, offset_y : offset_y + height, offset_x : offset_x + IMG]
-            tap_grads.append(
-                jnp.einsum("nabc,nabd->cd", window, d_conv, preferred_element_type=jnp.float32)
-            )
-    return jnp.stack(tap_grads)
-
-
-def conv_input_grad(d_padded, conv_tiles, height):
-    input_sum = jnp.zeros((d_padded.shape[0], height, IMG, CH), jnp.float32)
-    for offset_y in range(3):
-        for offset_x in range(3):
-            window = d_padded[
-                :, 2 - offset_y : 2 - offset_y + height, 2 - offset_x : 2 - offset_x + IMG
-            ]
-            input_sum = input_sum + jnp.einsum(
-                "nabd,cd->nabc",
-                window,
-                conv_tiles[3 * offset_y + offset_x],
-                preferred_element_type=jnp.float32,
-            )
-    return input_sum
+def conv_forward(image, conv_tiles):
+    return lax.conv_general_dilated(
+        image[None],
+        conv_tiles.reshape(3, 3, CH, CH),
+        (1, 1),
+        [(1, 1), (1, 1)],
+        dimension_numbers=("NHWC", "HWIO", "NHWC"),
+        preferred_element_type=jnp.float32,
+    )[0]
+
+
+def conv_weight_grad(image, d_conv):
+    return lax.conv_general_dilated(
+        image[None],
+        d_conv[None],
+        (1, 1),
+        [(1, 1), (1, 1)],
+        dimension_numbers=("CHWN", "IHWO", "HWNC"),
+        preferred_element_type=jnp.float32,
+    ).reshape(9, CH, CH)
+
+
+def conv_input_grad(d_conv, conv_tiles):
+    flipped = conv_tiles[::-1].transpose(0, 2, 1)
+    return conv_forward(d_conv, flipped)
+
+
+def swap_bit(values, axis, bit):
+    count = lax.axis_size(axis)
+    return lax.ppermute(values, axis, [(i, i ^ bit) for i in range(count)])
+
+
+def halve(values, axis, dim):
+    count = lax.axis_size(axis)
+    index = lax.axis_index(axis)
+    bit = 1
+    while bit < count:
+        high = (index // bit) % 2
+        shape = values.shape
+        parts = values.reshape(
+            shape[:dim] + (shape[dim] // 2, 2) + shape[dim + 1 :]
+        )
+        keep = lax.dynamic_index_in_dim(parts, high, dim + 1, keepdims=False)
+        give = lax.dynamic_index_in_dim(parts, 1 - high, dim + 1, keepdims=False)
+        got = swap_bit(give, axis, bit)
+        values = (keep.astype(jnp.float32) + got.astype(jnp.float32)).astype(values.dtype)
+        bit = bit * 2
+    return values
+
+
+def scatter_sum(matrix, order):
+    sizes = [lax.axis_size(axis) for axis in AXES]
+    values = matrix.astype(jnp.bfloat16).reshape(sizes + [-1, matrix.shape[-1]])
+    for axis in order:
+        values = halve(values, axis, AXES.index(axis))
+    return values.reshape(-1, matrix.shape[-1])
 
 
 def cross_forward(feats_b, kv_clip, to_query, to_out):
@@ -326,108 +323,89 @@
 ):
     slot_count = master_tiles.shape[0]
     slot_of = slot_index(tile_owner, slot_count)
-    gathered = lax.all_gather(
-        master_tiles.astype(jnp.bfloat16), ("batch", "row"), axis=0, tiled=True
-    )
-    tile_stack = jnp.take(gathered, slot_of, axis=0)
+    gathered = lax.all_gather(master_tiles.astype(jnp.bfloat16), AXES, axis=0, tiled=True)
+    image = lax.all_to_all(context_map, ("y", "x"), split_axis=0, concat_axis=1, tiled=True)[0]
+    tile_stack = gathered.at[slot_of].get(mode="promise_in_bounds")
     conv_tiles, att_tiles, matrices = unpack(tile_stack)
     kv_weight = jnp.concatenate([att_tiles[1], att_tiles[2]], 1)
-    height = context_map.shape[1]
-    padded = pad_columns(padded_2(context_map, (("row", 1),), 1))
-    conv_out = conv_forward(padded, conv_tiles, height)
-    hidden = padded[:, 1 : height + 1, 1 : IMG + 1].astype(jnp.float32) + jax.nn.silu(conv_out)
-    hidden_b = hidden.astype(jnp.bfloat16)
-    groups = hidden.shape[0]
-    kv_local = (
-        jnp.einsum("nabc,ce->nabe", hidden_b, kv_weight, preferred_element_type=jnp.float32)
-        .astype(jnp.bfloat16)
-        .reshape(groups, height * IMG, 2 * CH)
-    )
-    pooled = (
-        jnp.mean(
-            hidden.reshape(groups, height // PATCH, PATCH, IMG // PATCH, PATCH, CH), axis=(2, 4)
-        )
-        .reshape(groups, -1, CH)
-        .astype(jnp.bfloat16)
-    )
-    whole_kv, whole_pool = (
-        lax.all_to_all(kv_local, "row", split_axis=0, concat_axis=1, tiled=True),
-        lax.all_to_all(pooled, "row", split_axis=0, concat_axis=1, tiled=True),
-    )
-    valid_len = CTX + FT * horizon
-    totals_init = (
-        jnp.zeros((CH, CH), jnp.float32),
-        jnp.zeros((CH, CH), jnp.float32),
-        jnp.zeros((CH, D), jnp.float32),
-        jnp.zeros((D, 3 * D), jnp.float32),
-        jnp.zeros((D, D), jnp.float32),
-        jnp.zeros((D, FF), jnp.float32),
-        jnp.zeros((FF, D), jnp.float32),
-        jnp.zeros((2, D), jnp.float32),
-    )
-
-    def clip_step(totals, clip_item):
-        kv_clip, pool_clip, feats_b, length, back_rows = clip_item
-        query_b, mixed_b, cross_total, updated = cross_forward(
-            feats_b, kv_clip, att_tiles[0], att_tiles[3]
-        )
-        seq_in = jnp.concatenate([pool_clip, updated.astype(jnp.bfloat16)], 0)
-        result, kept = gpt_forward(seq_in, length, norm_gains, matrices)
-        position = jnp.arange(SEQ)
-        d_result = back_rows.astype(jnp.float32) * (position < length).astype(jnp.float32)[:, None]
-        d_seq, mat_grads, gain_grad = gpt_backward(
-            seq_in, length, norm_gains, matrices, kept, d_result
-        )
-        d_pool = d_seq[:CTX].astype(jnp.bfloat16)
-        d_kv, d_feats, grad_query, grad_out = cross_backward(
-            feats_b, kv_clip, query_b, mixed_b, cross_total, d_seq[CTX:], att_tiles[0], att_tiles[3]
-        )
-        new_totals = jax.tree.map(
-            jnp.add, totals, (grad_query, grad_out) + tuple(mat_grads) + (gain_grad,)
-        )
-        return (new_totals, (result, d_kv, d_pool, d_feats))
-
-    totals, outputs = lax.scan(
-        clip_step, totals_init, (whole_kv, whole_pool, future_feats, valid_len, cotangent)
-    )
-    grad_query, grad_out, grad_emb, grad_qkv, grad_att, grad_up, grad_down, gain_grads = totals
-    block_out, d_kv_all, d_pool_all, future_grad = outputs
-    d_kv_local, d_pool_local = (
-        lax.all_to_all(d_kv_all, "row", split_axis=1, concat_axis=0, tiled=True),
-        lax.all_to_all(d_pool_all, "row", split_axis=1, concat_axis=0, tiled=True),
-    )
-    grad_kv = jnp.einsum(
-        "npc,npe->ce",
-        hidden_b.reshape(groups, height * IMG, CH),
-        d_kv_local,
-        preferred_element_type=jnp.float32,
-    )
-    d_hidden = jnp.einsum(
-        "npe,ce->npc", d_kv_local, kv_weight, preferred_element_type=jnp.float32
-    ).reshape(groups, height, IMG, CH)
-    pool_spread = d_pool_local.astype(jnp.float32).reshape(
-        groups, height // PATCH, 1, IMG // PATCH, 1, CH
-    ) * (1.0 / (PATCH * PATCH))
-    d_hidden = d_hidden + jnp.broadcast_to(
-        pool_spread, (groups, height // PATCH, PATCH, IMG // PATCH, PATCH, CH)
-    ).reshape(groups, height, IMG, CH)
+    conv_out = conv_forward(image, conv_tiles)
+    hidden = image.astype(jnp.float32) + jax.nn.silu(conv_out)
+    hidden_b = hidden.astype(jnp.bfloat16).reshape(IMG * IMG, CH)
+    kv_clip = jnp.dot(hidden_b, kv_weight, preferred_element_type=jnp.float32).astype(jnp.bfloat16)
+    side = IMG // PATCH
+    pool_clip = (
+        jnp.mean(hidden.reshape(side, PATCH, side, PATCH, CH), axis=(1, 3))
+        .reshape(CTX, CH)
+        .astype(jnp.bfloat16)
+    )
+    feats_b = future_feats[0]
+    length = CTX + FT * horizon[0]
+    query_b, mixed_b, cross_total, updated = cross_forward(
+        feats_b, kv_clip, att_tiles[0], att_tiles[3]
+    )
+    seq_in = jnp.concatenate([pool_clip, updated.astype(jnp.bfloat16)], 0)
+    block_out, kept = gpt_forward(seq_in, length, norm_gains, matrices)
+    position = jnp.arange(SEQ)
+    d_result = cotangent[0].astype(jnp.float32) * (position < length).astype(jnp.float32)[:, None]
+    d_seq, mat_grads, gain_grad = gpt_backward(
+        seq_in, length, norm_gains, matrices, kept, d_result
+    )
+    grad_emb, grad_qkv, grad_att, grad_up, grad_down = mat_grads
+    gain_total = lax.psum(gain_grad, AXES)
+    sums = [
+        scatter_sum(grad_down, ("c", "x", "y", "z")),
+        scatter_sum(grad_up, ("c", "y", "x", "z")),
+        scatter_sum(grad_att, ("c", "x", "y", "z")),
+        scatter_sum(grad_qkv, ("c", "y", "x", "z")),
+        scatter_sum(grad_emb, ("c", "x", "y", "z")),
+    ]
+    d_pool = d_seq[:CTX].astype(jnp.bfloat16)
+    d_kv, d_feats, grad_query, grad_out = cross_backward(
+        feats_b, kv_clip, query_b, mixed_b, cross_total, d_seq[CTX:], att_tiles[0], att_tiles[3]
+    )
+    grad_kv = jnp.dot(hidden_b.T, d_kv, preferred_element_type=jnp.float32)
+    d_hidden = jnp.dot(d_kv, kv_weight.T, preferred_element_type=jnp.float32).reshape(IMG, IMG, CH)
+    pool_spread = d_pool.astype(jnp.float32).reshape(side, 1, side, 1, CH) * (
+        1.0 / (PATCH * PATCH)
+    )
+    d_hidden = d_hidden + jnp.broadcast_to(pool_spread, (side, PATCH, side, PATCH, CH)).reshape(
+        IMG, IMG, CH
+    )
     d_conv = jax.vjp(jax.nn.silu, conv_out)[1](d_hidden)[0].astype(jnp.bfloat16)
-    grad_conv = conv_weight_grad(padded, d_conv, height)
-    d_conv_pad = pad_columns(padded_2(d_conv, (("row", 1),), 1))
-    context_grad = d_hidden + conv_input_grad(d_conv_pad, conv_tiles, height)
-    att_grads = jnp.stack([grad_query, grad_kv[:, :CH], grad_kv[:, CH:], grad_out])
-    tile_grads = pack(grad_conv, att_grads, (grad_emb, grad_qkv, grad_att, grad_up, grad_down))
-    mine_index = lax.axis_index(("batch", "row")) * slot_count + jnp.arange(slot_count)
-    select = (slot_of[None, :] == mine_index[:, None]).astype(jnp.float32)
-    used = jnp.sum(select, 1)[:, None, None]
-    spread = (
-        jnp.zeros((lax.axis_size(("batch", "row")) * slot_count, CH, CH), jnp.float32)
-        .at[slot_of]
-        .set(tile_grads)
-    )
-    mine = lax.psum_scatter(spread, ("batch", "row"), scatter_dimension=0, tiled=True)
-    square_part, gain_total = lax.psum((jnp.sum(mine * mine), gain_grads), ("batch", "row"))
-    grad_norm = jnp.sqrt(square_part + jnp.sum(gain_total * gain_total))
+    grad_conv = conv_weight_grad(image, d_conv)
+    context_grad = d_hidden + conv_input_grad(d_conv, conv_tiles)
+    rows = lax.all_to_all(
+        context_grad.astype(jnp.bfloat16)[None],
+        ("y", "x"),
+        split_axis=1,
+        concat_axis=0,
+        tiled=True,
+    ).astype(jnp.float32)
+    early = jnp.concatenate(
+        [
+            grad_conv.reshape(9 * CH, CH),
+            grad_query,
+            grad_kv[:, :CH],
+            grad_kv[:, CH:],
+            grad_out,
+        ],
+        0,
+    )
+    sums.append(scatter_sum(early, ("c", "x", "y", "z")))
+    whole = [lax.all_gather(part, AXES, axis=0, tiled=True) for part in sums]
+    down_all, up_all, att_all, qkv_all, emb_all, early_all = whole
+    tile_grads = pack(
+        early_all.reshape(13, CH, CH)[:9],
+        early_all.reshape(13, CH, CH)[9:],
+        (emb_all, qkv_all, att_all, up_all, down_all),
+    )
+    square_total = jnp.sum(tile_grads.astype(jnp.float32) ** 2)
+    my_slots = lax.axis_index(AXES) * slot_count + jnp.arange(slot_count)
+    found = slot_of[None, :] == my_slots[:, None]
+    used = jnp.any(found, 1).astype(jnp.float32)[:, None, None]
+    my_tiles = jnp.sum(jnp.where(found, jnp.arange(found.shape[1])[None], 0), 1)
+    mine = tile_grads.at[my_tiles].get(mode="promise_in_bounds").astype(jnp.float32)
+    grad_norm = jnp.sqrt(square_total + jnp.sum(gain_total * gain_total))
     factor = jnp.minimum(1.0, clip_level / (grad_norm + 1e-06))
     new_first, new_second, new_master = adam_step(
         master_tiles, mine * factor, moment_first, moment_second, learn_rate, decay_rate
@@ -436,9 +414,9 @@
         norm_gains, gain_total * factor, gain_first, gain_second, gain_rate, 0.0
     )
     return (
-        block_out,
-        context_grad,
-        future_grad,
+        block_out[None],
+        rows,
+        d_feats[None],
         new_first * used,
         new_second * used,
         new_master * used,
@@ -450,29 +428,10 @@
 
 
 def solution(mesh):
-    in_specs = (
-        P("batch", "row", None, None),
-        P(("batch", "row"), None, None),
-        P(("batch", "row")),
-        P(("batch", "row"), None, None),
-        P(),
-        P(("batch", "row"), None, None),
-        P(("batch", "row"), None, None),
-        P(("batch", "row"), None, None),
-        P(),
-        P(),
-        P(),
-    )
-    out_specs = (
-        P(("batch", "row"), None, None),
-        P("batch", "row", None, None),
-        P(("batch", "row"), None, None),
-        P(("batch", "row"), None, None),
-        P(("batch", "row"), None, None),
-        P(("batch", "row"), None, None),
-        P(),
-        P(),
-        P(),
-        P(),
-    )
-    return jax.shard_map(local, mesh=mesh, in_specs=in_specs, out_specs=out_specs, check_vma=False)
+    groups, rows = mesh.devices.shape
+    fine = jax.sharding.Mesh(mesh.devices.reshape(groups // 2, 2, rows // 2, 2), AXES)
+    whole = P(AXES, None, None)
+    image = P(("z", "c"), ("y", "x"), None, None)
+    in_specs = (image, whole, P(AXES), whole, P(), whole, whole, whole, P(), P(), P())
+    out_specs = (whole, image, whole, whole, whole, whole, P(), P(), P(), P())
+    return jax.shard_map(local, mesh=fine, in_specs=in_specs, out_specs=out_specs, check_vma=False)

time: 2480 us -> 1220 us (0.49)
  waiting for transfers between devices: 1550 us -> 374 us
  local copies, waits for them, and re-layouts: 327 us -> 225 us
  blocking collectives: 39.9 us -> 108 us
  matrix products: 347 us -> 292 us
    reduce_scatter x1 -> x0, waiting for transfers between devices: 1350 us -> none  [local(): lax.psum_scatter(spread, ('batch', 'row'), scatter_dimension=0, tiled=True)]
    ppermute x4 -> x30, waiting for transfers between devices: 9.47 us -> 181 us  [swap_bit(): return lax.ppermute(values, axis, [(i, i ^ bit) for i in range(count)])]
    dot_general x31 -> x4, matrix products: 118 us -> 19 us  [the longest x1 12.4 us: cross_forward(): jnp.einsum('qhd,khd->hqk', query_b.reshape(-1, TH, HD), key_heads, prefer...]
    all_gather x0 -> x1, blocking collectives: none -> 68.5 us  [local(): whole = [lax.all_gather(part, AXES, axis=0, tiled=True) for part in sums]]
    scatter x1 -> x0, local copies, waits for them, and re-layouts: 59.6 us -> none  [local(): spread = jnp.zeros((lax.axis_size(('batch', 'row')) * slot_count, CH, CH)...]
    conv_general_dilated x0 -> x3, matrix products: none -> 59.2 us  [the longest x1 43.9 us: conv_weight_grad(): lax.conv_general_dilated(image[None], d_conv[None], (1, 1), [(1, 1), (1,...]
    convert_element_type x1 -> x36, other arithmetic: 0.68 us -> 44.5 us  [the longest x30 19.5 us: halve(): (keep.astype(jnp.float32) + got.astype(jnp.float32)).astype(values.dtype)]
    unnamed x11 -> x8, other arithmetic: 42.9 us -> 0.01 us
  transfers between devices with their start and end apart: 10 -> 38, of which waited for: 6 -> 21; matrix products, arithmetic and copies ran while one was open for 15% -> 17% of each run, Pallas kernels for 0% -> 0%
where the time goes in v1:
time: 1220 us; the launch traced here: 1210 us
  waiting for transfers between devices  374 us (31%)
  matrix products  292 us (24%)
  local copies, waits for them, and re-layouts  225 us (18%)
  other arithmetic  149 us (12%)
  blocking collectives  108 us (9%)
  starting transfers between devices  39.6 us (3%)
  between operations  20 us (2%)
    ppermute x30, waiting for transfers between devices, swap_bit(): return lax.ppermute(values, axis, [(i, i ^ bit) for i in range(count)])  181 us
    all_gather x1, waiting for transfers between devices, local(): lax.all_gather(master_tiles.astype(jnp.bfloat16), AXES, axis=0, tiled=True)  164 us
    all_gather x1, blocking collectives, local(): whole = [lax.all_gather(part, AXES, axis=0, tiled=True) for part in sums]  68.5 us
    conv_general_dilated x1, matrix products, conv_weight_grad(): lax.conv_general_dilated(image[None], d_conv[None], (1, 1), [(1, 1), (1,...  43.9 us
    unnamed x250, local copies, waits for them, and re-layouts  42.5 us
    psum x1, blocking collectives, local(): gain_total = lax.psum(gain_grad, AXES)  39.5 us
    ppermute x30, starting transfers between devices, swap_bit(): return lax.ppermute(values, axis, [(i, i ^ bit) for i in range(count)])  29.6 us
    all_to_all x1, waiting for transfers between devices, local(): lax.all_to_all(context_map, ('y', 'x'), split_axis=0, concat_axis=1, tile...  28.7 us
  transfers between devices with their start and end apart: 38, of which 21 were waited for; matrix products, arithmetic and copies ran while one was open for 17% of the time, Pallas kernels for 0%

profile of v1, /device:TPU:0, one launch (start us, length us, event | category | flops | bytes accessed | tf_op | source)
XLA Modules:
  0.0 1208.1 jit_solution(14170749442528807533)
XLA Ops:
  18.7 28.7 %all-to-all-done = bf16[4,16,64,256]{3,2,1,0:T(8,128)(2,1)S(1)} async-done(((bf16[4,16,64,256]{3,2,1,0:T(8,128)(2,1)}), bf16[4,16,64,256]{3,2,1,0:T(8,128)(2,1)S(1)}, u32[]{:S(2)}, u32[]{:S(2)}) %all-to-all-start) | async-done | bytes 2097184 | tf_op jit(solution)/shard_map/all_to_all | solution.py:327
  54.8 164.4 %all-gather.13.cloned.1.call-done = bf16[256,256,256]{2,1,0:T(8,128)(2,1)} async-done(((bf16[8,256,256]{2,1,0:T(8,128)(2,1)}), bf16[256,256,256]{2,1,0:T(8,128)(2,1)}) %all-gather.13.cloned.1.call-update) | async-done | bytes 33554448 | tf_op jit(solution)/shard_map/all_gather | solution.py:326
  219.2 11.9 gather_fusion
  331.8 12.4 %multiply_reduce_fusion.3 = (f32[4,480]{1,0:T(4,128)S(1)}, f32[4,480,4096]{2,1,0:T(8,128)}) fusion(bf16[480,4,64]{0,2,1:T(8,128)(2,1)S(1)} %bitcast.429, bf16[4096,4,64]{0,2,1:T(8,128)(2,1)S(1)} %bitcast.360), kind=kOutput, calls=%fused_computation.15 | convolution fusion | flops 1022359680 | bytes 33807872 | tf_op jit(solution)/shard_map/qhd,khd->hqk/dot_general | solution.py:153
  344.1 13.5 %fusion = f32[4,480]{1,0:T(4,128)S(1)} fusion(f32[4,480,4096]{2,1,0:T(8,128)} %get-tuple-element.78, f32[4,480]{1,0:T(4,128)S(1)} %get-tuple-element.77), kind=kLoop, calls=%fused_computation.8 | loop fusion | flops 23591040 | bytes 31472640 | tf_op jit(solution)/shard_map/reduce_sum | solution.py:163
  358.2 13.3 %fusion.89 = bf16[4,64,480]{2,1,0:T(8,128)(2,1)S(1)} fusion(bf16[4096,4,64]{0,2,1:T(8,128)(2,1)S(1)} %bitcast.391, f32[4,480,4096]{2,1,0:T(8,128)} %get-tuple-element.78, f32[4,480]{1,0:T(4,128)S(1)} %fusion, f32[4,480]{1,0:T(4,128)S(1)} %get-tuple-element.77), kind=kOutput, calls=%fused_computation.153 | convolution fusion | flops 1038213120 | bytes 33815552 | tf_op jit(solution)/shard_map/hqk,khd->qhd/dot_general | solution.py:166
  383.5 11.5 fusion.146
  395.0 11.7 fusion.1
  407.4 11.5 fusion.77
  448.6 12.1 %fusion.74 = bf16[12,64,736]{2,1,0:T(8,128)(2,1)} fusion(bf16[736,12,64]{0,2,1:T(8,128)(2,1)S(1)} %bitcast.386, f32[12,736,736]{1,2,0:T(8,128)} %get-tuple-element.82, f32[12,736]{1,0:T(8,128)} %log_add_fusion), kind=kOutput, calls=%fused_computation.138 | convolution fusion | flops 845611008 | bytes 28297728 | tf_op jit(solution)/shard_map/hqk,qhd->khd/dot_general | solution.py:281
  460.7 22.1 %multiply_reduce_fusion.2 = (f32[12,736]{1,0:T(8,128)}, f32[12,736,736]{1,2,0:T(8,128)}) fusion(f32[12,736,736]{1,2,0:T(8,128)} %get-tuple-element.82, f32[12,736]{1,0:T(8,128)} %log_add_fusion, bf16[736,12,64]{0,2,1:T(8,128)(2,1)S(1)} %bitcast.387, bf16[736,12,64]{0,2,1:T(8,128)(2,1)} %bitcast.420), kind=kOutput, calls=%fused_computation.10 | convolution fusion | flops 851537280 | bytes 54334464 | tf_op jit(solution)/shard_map/qhd,khd->hqk/dot_general | solution.py:280
  482.8 23.0 %multiply_convert_fusion.1 = bf16[12,736,736]{1,2,0:T(8,128)(2,1)} fusion(f32[12,736,736]{1,2,0:T(8,128)} %get-tuple-element.88, f32[12,736,736]{1,2,0:T(8,128)} %get-tuple-element.82, f32[12,736]{1,0:T(8,128)} %get-tuple-element.87, f32[12,736]{1,0:T(8,128)} %log_add_fusion), kind=kLoop, calls=%fused_computation.9 | loop fusion | flops 26001408 | bytes 65074176 | tf_op jit(solution)/shard_map/convert_element_type | solution.py:284
  531.2 14.3 %fusion.23 = bf16[4,64,4096]{2,1,0:T(8,128)(2,1)} fusion(bf16[480,4,64]{0,2,1:T(8,128)(2,1)S(1)} %bitcast.431, f32[4,480,4096]{2,1,0:T(8,128)} %get-tuple-element.78, f32[4,480]{1,0:T(4,128)S(1)} %copy-done.66), kind=kOutput, calls=%fused_computation.43 | convolution fusion | flops 1031274496 | bytes 33807872 | tf_op jit(solution)/shard_map/hqk,qhd->khd/dot_general | solution.py:194
  545.5 21.1 %multiply_reduce_fusion.1 = (f32[4,480]{1,0:T(4,128)S(1)}, f32[4,480,4096]{2,1,0:T(8,128)}) fusion(f32[4,480,4096]{2,1,0:T(8,128)} %get-tuple-element.78, f32[4,480]{1,0:T(4,128)S(1)} %copy-done.66, bf16[480,4,64]{0,2,1:T(8,128)(2,1)S(1)} %bitcast.432, bf16[4096,4,64]{0,2,1:T(8,128)(2,1)S(1)} %bitcast.392), kind=kOutput, calls=%fused_computation.4 | convolution fusion | flops 1038088320 | bytes 65272832 | tf_op jit(solution)/shard_map/qhd,khd->hqk/dot_general | solution.py:193
  566.7 27.0 %multiply_convert_fusion = bf16[4,480,4096]{2,1,0:T(8,128)(2,1)} fusion(f32[4,480,4096]{2,1,0:T(8,128)} %get-tuple-element.91, f32[4,480,4096]{2,1,0:T(8,128)} %get-tuple-element.78, f32[4,480]{1,0:T(4,128)S(1)} %get-tuple-element.90, f32[4,480]{1,0:T(4,128)S(1)} %copy-done.66), kind=kLoop, calls=%fused_computation.3 | loop fusion | flops 39321600 | bytes 78658560 | tf_op jit(solution)/shard_map/convert_element_type | solution.py:197
  645.1 43.9 %fusion.78 = bf16[3,3,256,256]{3,2,1,0:T(8,128)(2,1)S(1)} fusion(bf16[1,64,64,256]{3,1,2,0:T(8,128)(2,1)S(1)} %fusion.33, bf16[1,64,64,256]{3,2,1,0:T(8,128)(2,1)S(1)} %bitcast.359), kind=kOutput, calls=%fused_computation.141 | convolution fusion | flops 4732289024 | bytes 5373952 | tf_op jit(solution)/shard_map/conv_general_dilated | solution.py:101
  732.5 17.3 %collective-permute-done.2 = bf16[4,1,1,1,104,256]{5,4,3,2,0,1:T(8,128)(2,1)S(1)} collective-permute-done((bf16[4,1,1,1,104,256]{5,4,3,2,0,1:T(8,128)(2,1)S(1)}, bf16[4,1,1,1,104,256]{5,4,3,2,0,1:T(8,128)(2,1)S(1)}, u32[]{:S(2)}, u32[]{:S(2)}) %collective-permute-start.2) | collective-permute-done | bytes 213024 | tf_op jit(solution)/shard_map/ppermute | solution.py:118
  783.8 28.1 %collective-permute-done.26 = bf16[4,1,2,1,96,768]{5,4,0,3,2,1:T(8,128)(2,1)S(1)} collective-permute-done((bf16[4,1,2,1,96,768]{5,4,0,3,2,1:T(8,128)(2,1)S(1)}, bf16[4,1,2,1,96,768]{5,4,0,3,2,1:T(8,128)(2,1)S(1)}, u32[]{:S(2)}, u32[]{:S(2)}) %collective-permute-start.26) | collective-permute-done | bytes 1179680 | tf_op jit(solution)/shard_map/ppermute | solution.py:118
  852.1 24.6 %collective-permute-done.21 = bf16[4,1,1,2,24,3072]{5,4,0,3,2,1:T(8,128)(2,1)S(1)} collective-permute-done((bf16[4,1,1,2,24,3072]{5,4,0,3,2,1:T(8,128)(2,1)S(1)}, bf16[4,1,1,2,24,3072]{5,4,0,3,2,1:T(8,128)(2,1)S(1)}, u32[]{:S(2)}, u32[]{:S(2)}) %collective-permute-start.21) | collective-permute-done | bytes 1179680 | tf_op jit(solution)/shard_map/ppermute | solution.py:118
  877.8 14.3 %collective-permute-done.22 = bf16[4,1,1,1,24,3072]{5,4,0,3,2,1:T(8,128)(2,1)S(1)} collective-permute-done((bf16[4,1,1,1,24,3072]{5,4,0,3,2,1:T(8,128)(2,1)S(1)}, bf16[4,1,1,1,24,3072]{5,4,0,3,2,1:T(8,128)(2,1)S(1)}, u32[]{:S(2)}, u32[]{:S(2)}) %collective-permute-start.22) | collective-permute-done | bytes 589856 | tf_op jit(solution)/shard_map/ppermute | solution.py:118
  892.4 12.0 collective-permute-done.23
  957.8 27.0 %collective-permute-done.7 = bf16[4,1,1,1,8,768]{5,4,0,3,2,1:T(8,128)(2,1)S(1)} collective-permute-done((bf16[4,1,1,1,8,768]{5,4,0,3,2,1:T(8,128)(2,1)S(1)}, bf16[4,1,1,1,8,768]{5,4,0,3,2,1:T(8,128)(2,1)S(1)}, u32[]{:S(2)}, u32[]{:S(2)}) %collective-permute-start.7) | collective-permute-done | bytes 49184 | tf_op jit(solution)/shard_map/ppermute | solution.py:118
  986.4 39.5 %psum.7 = f32[2,768]{1,0:T(2,128)S(1)} all-reduce(f32[2,768]{1,0:T(2,128)S(1)} %pad_maximum_fusion.14), channel_id=1, replica_groups=mesh['z'=4,'c'=2,'y'=2,'x'=2] {'z','c','y','x'}, use_global_device_ids=true, to_apply=%region_16.17 | all-reduce | flops 1536 | bytes 12288 | tf_op jit(solution)/shard_map/psum | solution.py:354
  1030.7 68.5 %all-gather.1 = bf16[1,1,1,1,256,768]{5,4,0,3,2,1:T(8,128)(2,1)S(1)} all-gather(bf16[1,1,1,1,8,768]{5,4,0,3,2,1:T(8,128)(2,1)S(1)} %add_convert_fusion.17), channel_id=3, replica_groups=mesh['z'=4,'c'=2,'y'=2,'x'=2] {'z','c','y','x'}, dimensions={4}, use_global_device_ids=true | all-gather | bytes 405504 | tf_op jit(solution)/shard_map/all_gather | solution.py:395
  (521 shorter events, 514.3 us)
Async XLA Ops:
  7.2 212.0 %all-gather.13.cloned.1.call-start = ((), (), s32[]{:S(2)}) async-start(), calls=%async_computation.2 | async-start | bytes 34603008 | tf_op jit(solution)/shard_map/all_gather | solution.py:326
  9.9 37.5 %all-to-all-start = ((bf16[4,16,64,256]{3,2,1,0:T(8,128)(2,1)}), bf16[4,16,64,256]{3,2,1,0:T(8,128)(2,1)S(1)}, u32[]{:S(2)}, u32[]{:S(2)}) async-start(bf16[4,16,64,256]{3,2,1,0:T(8,128)(2,1)} %param.11), calls=%async_computation | async-start | bytes 4194304 | tf_op jit(solution)/shard_map/all_to_all | solution.py:327
  15.1 1087.0 %all-gather.19.cloned.1.call-start = ((), (), s32[]{:S(2)}) async-start(), calls=%async_computation.5 | async-start | bytes 1216512 | tf_op jit(solution)/shard_map/all_gather | solution.py:395
  627.4 70.0 %collective-permute-start.15 = (bf16[4,1,2,2,24,768]{5,4,0,3,2,1:T(8,128)(2,1)}, bf16[4,1,2,2,24,768]{5,4,0,3,2,1:T(8,128)(2,1)}, u32[]{:S(2)}, u32[]{:S(2)}) collective-permute-start(bf16[4,1,2,2,24,768]{5,4,0,3,2,1:T(8,128)(2,1)} %bitcast.352), channel_id=1, source_target_pairs={{0,4},{4,0},{1,5},{5,1},{2,6},{6,2},{3,7},{7,3},{8,12},{12,8},{9,1... | collective-permute-start | bytes 1769480 | tf_op jit(solution)/shard_map/ppermute | solution.py:118
  692.7 22.4 %collective-permute-start = (bf16[4,1,2,2,104,256]{5,4,3,2,0,1:T(8,128)(2,1)}, bf16[4,1,2,2,104,256]{5,4,3,2,0,1:T(8,128)(2,1)}, u32[]{:S(2)}, u32[]{:S(2)}) collective-permute-start(bf16[4,1,2,2,104,256]{5,4,3,2,0,1:T(8,128)(2,1)} %dynamic-slice_bitcast_fusion), channel_id=1, source_target_pairs={{0,4},{4,0},{1,5},{5,1},{2,6},{6,2},{3,7},{7,3},{8,12},{12,8},{9,1... | collective-permute-start | bytes 2555912 | tf_op jit(solution)/shard_map/ppermute | solution.py:118
  701.8 23.3 %collective-permute-start.10 = (bf16[4,1,2,2,24,2304]{5,4,0,3,2,1:T(8,128)(2,1)}, bf16[4,1,2,2,24,2304]{5,4,0,3,2,1:T(8,128)(2,1)}, u32[]{:S(2)}, u32[]{:S(2)}) collective-permute-start(bf16[4,1,2,2,24,2304]{5,4,0,3,2,1:T(8,128)(2,1)} %bitcast.351), channel_id=1, source_target_pairs={{0,4},{4,0},{1,5},{5,1},{2,6},{6,2},{3,7},{7,3},{8,12},{12,8},{9,1... | collective-permute-start | bytes 5308424 | tf_op jit(solution)/shard_map/ppermute | solution.py:118
  725.1 380.6 %all-gather.15.cloned.1.call-start = ((), (), s32[]{:S(2)}) async-start(), calls=%async_computation.3 | async-start | bytes 1757184 | tf_op jit(solution)/shard_map/all_gather | solution.py:395
  727.2 23.2 %collective-permute-start.11 = (bf16[4,1,1,2,24,2304]{5,4,0,3,2,1:T(8,128)(2,1)S(1)}, bf16[4,1,1,2,24,2304]{5,4,0,3,2,1:T(8,128)(2,1)S(1)}, u32[]{:S(2)}, u32[]{:S(2)}) collective-permute-start(bf16[4,1,1,2,24,2304]{5,4,0,3,2,1:T(8,128)(2,1)S(1)} %constant_dynamic-slice_fusion.17), channel_id=1, source_target_pairs={{0,2},{2,0},{1,3},{3,1},{4,6},{6,4},{5,7},{7,5},{8,10},{10,8},{9,1... | collective-permute-start | bytes 2654216 | tf_op jit(solution)/shard_map/ppermute | solution.py:118
  730.9 18.9 %collective-permute-start.2 = (bf16[4,1,1,1,104,256]{5,4,3,2,0,1:T(8,128)(2,1)S(1)}, bf16[4,1,1,1,104,256]{5,4,3,2,0,1:T(8,128)(2,1)S(1)}, u32[]{:S(2)}, u32[]{:S(2)}) collective-permute-start(bf16[4,1,1,1,104,256]{5,4,3,2,0,1:T(8,128)(2,1)S(1)} %constant_dynamic-slice_fusion.27), channel_id=1, source_target_pairs={{0,2},{2,0},{1,3},{3,1},{4,6},{6,4},{5,7},{7,5},{8,10},{10,8},{9,1... | collective-permute-start | bytes 638984 | tf_op jit(solution)/shard_map/ppermute | solution.py:118
  750.7 11.2 collective-permute-start.12
  761.5 348.2 %all-gather.17.cloned.1.call-start = ((), (), s32[]{:S(2)}) async-start(), calls=%async_computation.4 | async-start | bytes 3649536 | tf_op jit(solution)/shard_map/all_gather | solution.py:395
  779.7 349.7 %all-gather.23.cloned.1.call-start = ((), (), s32[]{:S(2)}) async-start(), calls=%async_computation.7 | async-start | bytes 4866048 | tf_op jit(solution)/shard_map/all_gather | solution.py:395
  782.2 29.6 %collective-permute-start.26 = (bf16[4,1,2,1,96,768]{5,4,0,3,2,1:T(8,128)(2,1)S(1)}, bf16[4,1,2,1,96,768]{5,4,0,3,2,1:T(8,128)(2,1)S(1)}, u32[]{:S(2)}, u32[]{:S(2)}) collective-permute-start(bf16[4,1,2,1,96,768]{5,4,0,3,2,1:T(8,128)(2,1)S(1)} %constant_dynamic-slice_fusion.2), channel_id=1, source_target_pairs={{0,1},{1,0},{2,3},{3,2},{4,5},{5,4},{6,7},{7,6},{8,9},{9,8},{10,11... | collective-permute-start | bytes 3538952 | tf_op jit(solution)/shard_map/ppermute | solution.py:118
  812.2 17.9 %collective-permute-start.27 = (bf16[4,1,1,1,96,768]{5,4,0,3,2,1:T(8,128)(2,1)S(1)}, bf16[4,1,1,1,96,768]{5,4,0,3,2,1:T(8,128)(2,1)S(1)}, u32[]{:S(2)}, u32[]{:S(2)}) collective-permute-start(bf16[4,1,1,1,96,768]{5,4,0,3,2,1:T(8,128)(2,1)S(1)} %constant_dynamic-slice_fusion.1), channel_id=1, source_target_pairs={{0,2},{2,0},{1,3},{3,1},{4,6},{6,4},{5,7},{7,5},{8,10},{10,8},{9,1... | collective-permute-start | bytes 1769480 | tf_op jit(solution)/shard_map/ppermute | solution.py:118
  832.4 14.7 %collective-permute-start.20 = (bf16[4,1,2,2,24,3072]{5,4,0,3,2,1:T(8,128)(2,1)}, bf16[4,1,2,2,24,3072]{5,4,0,3,2,1:T(8,128)(2,1)}, u32[]{:S(2)}, u32[]{:S(2)}) collective-permute-start(bf16[4,1,2,2,24,3072]{5,4,0,3,2,1:T(8,128)(2,1)} %bitcast.349), channel_id=1, source_target_pairs={{0,4},{4,0},{1,5},{5,1},{2,6},{6,2},{3,7},{7,3},{8,12},{12,8},{9,1... | collective-permute-start | bytes 7077896 | tf_op jit(solution)/shard_map/ppermute | solution.py:118
  846.8 307.3 %all-gather.21.cloned.1.call-start = ((), (), s32[]{:S(2)}) async-start(), calls=%async_computation.6 | async-start | bytes 4866048 | tf_op jit(solution)/shard_map/all_gather | solution.py:395
  849.7 27.0 %collective-permute-start.21 = (bf16[4,1,1,2,24,3072]{5,4,0,3,2,1:T(8,128)(2,1)S(1)}, bf16[4,1,1,2,24,3072]{5,4,0,3,2,1:T(8,128)(2,1)S(1)}, u32[]{:S(2)}, u32[]{:S(2)}) collective-permute-start(bf16[4,1,1,2,24,3072]{5,4,0,3,2,1:T(8,128)(2,1)S(1)} %constant_dynamic-slice_fusion.7), channel_id=1, source_target_pairs={{0,2},{2,0},{1,3},{3,1},{4,6},{6,4},{5,7},{7,5},{8,10},{10,8},{9,1... | collective-permute-start | bytes 3538952 | tf_op jit(solution)/shard_map/ppermute | solution.py:118
  877.2 14.9 %collective-permute-start.22 = (bf16[4,1,1,1,24,3072]{5,4,0,3,2,1:T(8,128)(2,1)S(1)}, bf16[4,1,1,1,24,3072]{5,4,0,3,2,1:T(8,128)(2,1)S(1)}, u32[]{:S(2)}, u32[]{:S(2)}) collective-permute-start(bf16[4,1,1,1,24,3072]{5,4,0,3,2,1:T(8,128)(2,1)S(1)} %constant_dynamic-slice_fusion.6), channel_id=1, source_target_pairs={{0,1},{1,0},{2,3},{3,2},{4,5},{5,4},{6,7},{7,6},{8,9},{9,8},{10,11... | collective-permute-start | bytes 1769480 | tf_op jit(solution)/shard_map/ppermute | solution.py:118
  892.3 12.1 collective-permute-start.23
  918.1 22.1 %collective-permute-start.5 = (bf16[4,1,2,2,8,768]{5,4,0,3,2,1:T(8,128)(2,1)}, bf16[4,1,2,2,8,768]{5,4,0,3,2,1:T(8,128)(2,1)}, u32[]{:S(2)}, u32[]{:S(2)}) collective-permute-start(bf16[4,1,2,2,8,768]{5,4,0,3,2,1:T(8,128)(2,1)} %bitcast.353), channel_id=1, source_target_pairs={{0,4},{4,0},{1,5},{5,1},{2,6},{6,2},{3,7},{7,3},{8,12},{12,8},{9,1... | collective-permute-start | bytes 589832 | tf_op jit(solution)/shard_map/ppermute | solution.py:118
  942.0 10.8 collective-permute-start.6
  948.8 150.8 %all-to-all-start.1 = ((bf16[1,64,64,256]{3,2,0,1:T(8,128)(2,1)}), bf16[1,64,64,256]{3,2,0,1:T(8,128)(2,1)S(1)}, u32[]{:S(2)}, u32[]{:S(2)}) async-start(bf16[1,64,64,256]{3,2,0,1:T(8,128)(2,1)} %copy.261), calls=%async_computation.1 | async-start | bytes 4194304 | tf_op jit(solution)/shard_map/all_to_all | solution.py:377
  953.7 31.0 %collective-permute-start.7 = (bf16[4,1,1,1,8,768]{5,4,0,3,2,1:T(8,128)(2,1)S(1)}, bf16[4,1,1,1,8,768]{5,4,0,3,2,1:T(8,128)(2,1)S(1)}, u32[]{:S(2)}, u32[]{:S(2)}) collective-permute-start(bf16[4,1,1,1,8,768]{5,4,0,3,2,1:T(8,128)(2,1)S(1)} %constant_dynamic-slice_fusion.22), channel_id=1, source_target_pairs={{0,2},{2,0},{1,3},{3,1},{4,6},{6,4},{5,7},{7,5},{8,10},{10,8},{9,1... | collective-permute-start | bytes 147464 | tf_op jit(solution)/shard_map/ppermute | solution.py:118
  984.8 41.1 %collective-permute-start.8 = (bf16[2,1,1,1,8,768]{5,4,0,3,2,1:T(8,128)(2,1)S(1)}, bf16[2,1,1,1,8,768]{5,4,0,3,2,1:T(8,128)(2,1)S(1)}, u32[]{:S(2)}, u32[]{:S(2)}) collective-permute-start(bf16[2,1,1,1,8,768]{5,4,0,3,2,1:T(8,128)(2,1)S(1)} %dynamic-slice_bitcast_fusion.6), channel_id=1, source_target_pairs={{0,8},{8,0},{16,24},{24,16},{1,9},{9,1},{17,25},{25,17},{2,10},{10... | collective-permute-start | bytes 73736 | tf_op jit(solution)/shard_map/ppermute | solution.py:118
  (135 other events, 1193.3 us)
Sparse Core Ops, SparseCore 0:
  11.5 207.7 all-gather.12
  725.2 54.0 all-gather.18
  782.2 56.5 all-gather.14
  841.5 62.2 all-gather.16
  906.5 82.7 all-gather.22
  992.7 64.1 all-gather.20

commit v2 on v1

v2 whole, which is shorter than its diff:
```python
import jax
import jax.numpy as jnp
from jax import lax
from jax.experimental import pallas as pl
from jax.experimental.pallas import tpu as pltpu
from jax.sharding import PartitionSpec as P

CH = 256
HD = 64
HEADS = 12
D = 768
FF = 3072
TH = 4
IMG = 64
PATCH = 4
FT = 16
CTX = 256
SEQ = 736
STEP = 10


eps_norm = 1e-05
beta_one = 0.9
beta_two = 0.999
learn_rate = 0.02
gain_rate = 0.6
decay_rate = 0.1
adam_eps = 1e-08
clip_level = 1.0
neg_large = -1e30
AXES = ("z", "c", "y", "x")
CELLS = IMG * IMG
BLOCK = 512
GROUP = 4
EARLY = 13
VMEM_BYTES = 56 * 1024 * 1024
ROW_BLOCKS = ((0, 256), (256, 256), (512, 224))
bf16 = jnp.bfloat16
f32 = jnp.float32


def slot_index(tile_owner, slot_count):
    ordinal = jnp.arange(tile_owner.shape[0])
    earlier = (tile_owner[None, :] == tile_owner[:, None]) & (ordinal[None, :] < ordinal[:, None])
    return tile_owner * slot_count + jnp.sum(earlier.astype(jnp.int32), 1)


def adam_step(weight, grad_now, first, second, rate, decay):
    first_new = beta_one * first + (1.0 - beta_one) * grad_now
    second_new = beta_two * second + (1.0 - beta_two) * grad_now * grad_now
    corr_first = first_new / (1.0 - beta_one**STEP)
    corr_second = second_new / (1.0 - beta_two**STEP)
    weight_new = weight - rate * (corr_first / (jnp.sqrt(corr_second) + adam_eps) + decay * weight)
    return (first_new, second_new, weight_new)


def xor_permute(values, axes, mask):
    count = lax.axis_size(axes)
    return lax.ppermute(values, axes, [(i, i ^ mask) for i in range(count)])


def scatter_axes(values, axes, dim, keep_wide=False):
    count = lax.axis_size(axes)
    mine = lax.axis_index(axes)
    total = lax.dynamic_index_in_dim(values, mine, dim, keepdims=False).astype(f32)
    for mask in range(1, count):
        give = lax.dynamic_index_in_dim(values, mine ^ mask, dim, keepdims=False)
        total = total + xor_permute(give, axes, mask).astype(f32)
    return total if keep_wide else total.astype(values.dtype)


def gather_axes(values, axes):
    pieces = [values]
    for mask in range(1, lax.axis_size(axes)):
        pieces.append(xor_permute(values, axes, mask))
    return jnp.stack(pieces)


def gather_all(values):
    shape = values.shape
    values = gather_axes(values, "z")
    values = gather_axes(values, ("y", "x"))
    values = gather_axes(values, "c")
    cores, rows, depth = values.shape[:3]
    order = jnp.arange(depth * cores * rows)
    z, c, row = order // (cores * rows), (order // rows) % cores, order % rows
    own = lax.axis_index("z"), lax.axis_index("c"), lax.axis_index(("y", "x"))
    at = ((c ^ own[1]) * rows + (row ^ own[2])) * depth + (z ^ own[0])
    return values.reshape((-1,) + shape).at[at].get(mode="promise_in_bounds")


def sum_all(values):
    for axis in ("c", "x", "y", "z"):
        bit = 1
        while bit < lax.axis_size(axis):
            values = values + xor_permute(values, axis, bit)
            bit = bit * 2
    return values


def cut(matrix):
    sizes = [lax.axis_size(axis) for axis in AXES]
    return matrix.astype(bf16).reshape([-1] + sizes + [CH // lax.axis_size(AXES), matrix.shape[-1]])


def sum_core(slices):
    return scatter_axes(slices, "c", 2)


def sum_x(slices):
    return scatter_axes(slices, "x", slices.ndim - 3)


def sum_y(slices):
    return scatter_axes(slices, "y", 2)


def sum_z(slices):
    return scatter_axes(slices, "z", 1, keep_wide=True)


def to_tiles(slices):
    blocks, rows, columns = slices.shape
    return (
        slices.reshape(blocks, rows, columns // CH, CH)
        .transpose(0, 2, 1, 3)
        .reshape(-1, rows, CH)
    )


def dot_nt(a, b):
    return lax.dot_general(a, b, (((1,), (1,)), ((), ())), preferred_element_type=f32)


def dot_nn(a, b):
    return lax.dot_general(a, b, (((1,), (0,)), ((), ())), preferred_element_type=f32)


def dot_tn(a, b):
    return lax.dot_general(a, b, (((0,), (0,)), ((), ())), preferred_element_type=f32)


def head_mask(shape, head):
    return (lax.broadcasted_iota(jnp.int32, shape, len(shape) - 1) // HD) == head


def cost(flops, moved, transcendentals=0):
    return pl.CostEstimate(
        flops=int(flops), bytes_accessed=int(moved), transcendentals=int(transcendentals)
    )


def params():
    return pltpu.CompilerParams(vmem_limit_bytes=VMEM_BYTES)


def cross_forward_kernel(q_ref, k_ref, v_ref, o_ref, l_ref):
    rows = q_ref.shape[0]
    lane = lax.broadcasted_iota(jnp.int32, (rows, 128), 1)
    q = q_ref[...]
    mixed = jnp.zeros((rows, CH), f32)
    stat = jnp.zeros((rows, 128), f32)
    for head in range(TH):
        mask = head_mask((rows, CH), head)
        q_head = jnp.where(mask, q.astype(f32) * 0.125, 0.0).astype(bf16)
        scores = dot_nt(q_head, k_ref[...])
        peak = jnp.max(scores, -1, keepdims=True)
        shifted = jnp.exp(scores - peak)
        total = jnp.sum(shifted, -1, keepdims=True)
        part = dot_nn(shifted.astype(bf16), v_ref[...])
        mixed = jnp.where(mask, part / total, mixed)
        stat = jnp.where(lane == head, peak + jnp.log(total), stat)
    o_ref[...] = mixed.astype(bf16)
    l_ref[...] = stat


def cross_forward(query, kv):
    rows = query.shape[0] // 2
    cells = kv.shape[0]
    return pl.pallas_call(
        cross_forward_kernel,
        grid=(2,),
        in_specs=[
            pl.BlockSpec((rows, CH), lambda i: (i, 0)),
            pl.BlockSpec((cells, CH), lambda i: (0, 0)),
            pl.BlockSpec((cells, CH), lambda i: (0, 1)),
        ],
        out_specs=[
            pl.BlockSpec((rows, CH), lambda i: (i, 0)),
            pl.BlockSpec((rows, 128), lambda i: (i, 0)),
        ],
        out_shape=[
            jax.ShapeDtypeStruct((2 * rows, CH), bf16),
            jax.ShapeDtypeStruct((2 * rows, 128), f32),
        ],
        compiler_params=params(),
        cost_estimate=cost(16 * TH * rows * cells * CH // 2, 8 * cells * CH, 2 * TH * rows * cells),
    )(query, kv, kv)


def delta_rows(d_out, out):
    product = d_out.astype(f32) * out.astype(f32)
    head = lax.broadcasted_iota(jnp.int32, (8, CH), 0)
    lane = lax.broadcasted_iota(jnp.int32, (8, CH), 1)
    pick = ((lane // HD) == head).astype(f32)
    return lax.dot_general(
        pick,
        product,
        (((1,), (1,)), ((), ())),
        precision=lax.Precision.HIGHEST,
        preferred_element_type=f32,
    )


def cross_backward_kernel(
    q_ref, k_ref, v_ref, do_ref, o_ref, l_ref, dq_ref, dkv_ref, q_s, do_s, delta_s, dq_s
):
    step = pl.program_id(0)
    rows = q_ref.shape[0]

    @pl.when(step == 0)
    def _():
        for head in range(TH):
            mask = head_mask((rows, CH), head)
            q_s[head] = jnp.where(mask, q_ref[...].astype(f32) * 0.125, 0.0).astype(bf16)
            do_s[head] = jnp.where(mask, do_ref[...].astype(f32), 0.0).astype(bf16)
        delta_s[...] = delta_rows(do_ref[...], o_ref[...])
        dq_s[...] = jnp.zeros_like(dq_s)

    cells = k_ref.shape[0]
    dk = jnp.zeros((cells, CH), f32)
    dv = jnp.zeros((cells, CH), f32)
    dq = dq_s[...]
    k = k_ref[...]
    for head in range(TH):
        probs = jnp.exp(dot_nt(k, q_s[head]) - l_ref[head : head + 1, :])
        d_probs = dot_nt(v_ref[...], do_s[head])
        d_scores = (probs * (d_probs - delta_s[head : head + 1, :])).astype(bf16)
        dv = dv + dot_nn(probs.astype(bf16), do_s[head])
        dk = dk + dot_nn(d_scores, q_s[head])
        dq = dq + jnp.where(head_mask((rows, CH), head), dot_tn(d_scores, k), 0.0)
    dq_s[...] = dq
    dkv_ref[:, :CH] = dk.astype(bf16)
    dkv_ref[:, CH:] = dv.astype(bf16)

    @pl.when(step == pl.num_programs(0) - 1)
    def _():
        dq_ref[...] = (dq_s[...] * 0.125).astype(bf16)


def cross_backward(query, kv, d_out, out, log_rows):
    rows = query.shape[0]
    cells = kv.shape[0]
    block = 1024
    whole = lambda i: (0, 0)
    return pl.pallas_call(
        cross_backward_kernel,
        grid=(cells // block,),
        in_specs=[
            pl.BlockSpec((rows, CH), whole),
            pl.BlockSpec((block, CH), lambda i: (i, 0)),
            pl.BlockSpec((block, CH), lambda i: (i, 1)),
            pl.BlockSpec((rows, CH), whole),
            pl.BlockSpec((rows, CH), whole),
            pl.BlockSpec((TH, rows), whole),
        ],
        out_specs=[
            pl.BlockSpec((rows, CH), whole),
            pl.BlockSpec((block, 2 * CH), lambda i: (i, 0)),
        ],
        out_shape=[
            jax.ShapeDtypeStruct((rows, CH), bf16),
            jax.ShapeDtypeStruct((cells, 2 * CH), bf16),
        ],
        scratch_shapes=[
            pltpu.VMEM((TH, rows, CH), bf16),
            pltpu.VMEM((TH, rows, CH), bf16),
            pltpu.VMEM((8, rows), f32),
            pltpu.VMEM((rows, CH), f32),
        ],
        compiler_params=params(),
        cost_estimate=cost(10 * TH * rows * cells * CH, 8 * cells * CH, TH * rows * cells),
    )(query, kv, kv, d_out, out, log_rows)


def self_forward_kernel(len_ref, q_ref, k_ref, v_ref, o_ref, l_ref):
    group = pl.program_id(0)
    length = len_ref[0]
    for start, count in ROW_BLOCKS:
        stop = start + count
        q = q_ref[start:stop, :].astype(f32) * 0.125
        row = lax.broadcasted_iota(jnp.int32, (count, 1), 0) + start
        bound = jnp.minimum(row, length - 1)
        allowed = lax.broadcasted_iota(jnp.int32, (count, stop), 1) <= bound
        mixed = jnp.zeros((count, CH), f32)
        stat = l_ref[start:stop, :]
        lane = lax.broadcasted_iota(jnp.int32, (count, 128), 1)
        for head in range(GROUP):
            mask = head_mask((count, CH), head)
            q_head = jnp.where(mask, q, 0.0).astype(bf16)
            scores = jnp.where(allowed, dot_nt(q_head, k_ref[:stop, :]), neg_large)
            peak = jnp.max(scores, -1, keepdims=True)
            shifted = jnp.exp(scores - peak)
            total = jnp.sum(shifted, -1, keepdims=True)
            part = dot_nn(shifted.astype(bf16), v_ref[:stop, :])
            mixed = jnp.where(mask, part / total, mixed)
            stat = jnp.where(lane == group * GROUP + head, peak + jnp.log(total), stat)
        o_ref[start:stop, :] = mixed.astype(bf16)
        l_ref[start:stop, :] = stat


def self_forward(qkv, length):
    groups = D // CH
    return pl.pallas_call(
        self_forward_kernel,
        grid_spec=pltpu.PrefetchScalarGridSpec(
            num_scalar_prefetch=1,
            grid=(groups,),
            in_specs=[
                pl.BlockSpec((SEQ, CH), lambda i, n: (0, i)),
                pl.BlockSpec((SEQ, CH), lambda i, n: (0, groups + i)),
                pl.BlockSpec((SEQ, CH), lambda i, n: (0, 2 * groups + i)),
            ],
            out_specs=[
                pl.BlockSpec((SEQ, CH), lambda i, n: (0, i)),
                pl.BlockSpec((SEQ, 128), lambda i, n: (0, 0)),
            ],
        ),
        out_shape=[
            jax.ShapeDtypeStruct((SEQ, D), bf16),
            jax.ShapeDtypeStruct((SEQ, 128), f32),
        ],
        compiler_params=params(),
        cost_estimate=cost(4 * HEADS * SEQ * SEQ * CH, 8 * SEQ * D, HEADS * SEQ * SEQ),
    )(length, qkv, qkv, qkv)


def self_backward_kernel(
    len_ref, q_ref, k_ref, v_ref, do_ref, o_ref, l_ref, out_ref, dk_s, dv_s
):
    length = len_ref[0]
    dk_s[...] = jnp.zeros_like(dk_s)
    dv_s[...] = jnp.zeros_like(dv_s)
    delta = delta_rows(do_ref[...], o_ref[...])
    for start, count in ROW_BLOCKS:
        stop = start + count
        q = q_ref[start:stop, :].astype(f32) * 0.125
        d_out = do_ref[start:stop, :].astype(f32)
        row = lax.broadcasted_iota(jnp.int32, (1, count), 1) + start
        bound = jnp.minimum(row, length - 1)
        allowed = lax.broadcasted_iota(jnp.int32, (stop, count), 0) <= bound
        dq = jnp.zeros((count, CH), f32)
        k = k_ref[:stop, :]
        v = v_ref[:stop, :]
        dk = dk_s[:stop, :]
        dv = dv_s[:stop, :]
        for head in range(GROUP):
            mask = head_mask((count, CH), head)
            q_head = jnp.where(mask, q, 0.0).astype(bf16)
            d_head = jnp.where(mask, d_out, 0.0).astype(bf16)
            scores = dot_nt(k, q_head)
            logs = l_ref[0, head : head + 1, start:stop]
            probs = jnp.where(allowed, jnp.exp(scores - logs), 0.0)
            d_probs = dot_nt(v, d_head)
            d_scores = (probs * (d_probs - delta[head : head + 1, start:stop])).astype(bf16)
            dv = dv + dot_nn(probs.astype(bf16), d_head)
            dk = dk + dot_nn(d_scores, q_head)
            dq = dq + jnp.where(mask, dot_tn(d_scores, k), 0.0)
        dk_s[:stop, :] = dk
        dv_s[:stop, :] = dv
        out_ref[0, start:stop, :] = (dq * 0.125).astype(bf16)
    out_ref[1] = dk_s[...].astype(bf16)
    out_ref[2] = dv_s[...].astype(bf16)


def self_backward(qkv, d_out, out, log_rows, length):
    groups = D // CH
    at = lambda j: (lambda i, n: (0, j * groups + i))
    return pl.pallas_call(
        self_backward_kernel,
        grid_spec=pltpu.PrefetchScalarGridSpec(
            num_scalar_prefetch=1,
            grid=(groups,),
            in_specs=[
                pl.BlockSpec((SEQ, CH), at(0)),
                pl.BlockSpec((SEQ, CH), at(1)),
                pl.BlockSpec((SEQ, CH), at(2)),
                pl.BlockSpec((SEQ, CH), at(0)),
                pl.BlockSpec((SEQ, CH), at(0)),
                pl.BlockSpec((1, GROUP, SEQ), lambda i, n: (i, 0, 0)),
            ],
            out_specs=pl.BlockSpec((3, SEQ, CH), lambda i, n: (0, 0, i)),
            scratch_shapes=[pltpu.VMEM((SEQ, CH), f32), pltpu.VMEM((SEQ, CH), f32)],
        ),
        out_shape=jax.ShapeDtypeStruct((3, SEQ, D), bf16),
        compiler_params=params(),
        cost_estimate=cost(8 * HEADS * SEQ * SEQ * CH, 16 * SEQ * D, HEADS * SEQ * SEQ),
    )(length, qkv, qkv, qkv, d_out, out, log_rows)


def patch_pick(rows, columns, patch_dim):
    patch = lax.broadcasted_iota(jnp.int32, (rows, columns), patch_dim)
    cell = lax.broadcasted_iota(jnp.int32, (rows, columns), 1 - patch_dim)
    inside = (cell // (PATCH * IMG)) * (IMG // PATCH) + (cell % IMG) // PATCH
    return jnp.where(patch == inside, 1.0 / (PATCH * PATCH), 0.0).astype(bf16)


def image_rows(step, row):
    return pl.ds(pl.multiple_of(step * BLOCK + row * IMG, IMG), BLOCK)


def token_forward_kernel(x_ref, conv_ref, kv_w_ref, slope_ref, hidden_ref, kv_ref, pool_ref):
    step = pl.program_id(0)
    z = jnp.zeros((BLOCK, CH), f32)
    for row in range(3):
        z = z + dot_nn(x_ref[image_rows(step, row), :], conv_ref[row])
    center = x_ref[image_rows(step, 1), CH : 2 * CH].astype(f32)
    gate = 1.0 / (1.0 + jnp.exp(-z))
    hidden = center + z * gate
    slope_ref[...] = (gate * (1.0 + z * (1.0 - gate))).astype(bf16)
    hidden_b = hidden.astype(bf16)
    hidden_ref[...] = hidden_b
    kv_ref[...] = dot_nn(hidden_b, kv_w_ref[...]).astype(bf16)
    rest = (hidden - hidden_b.astype(f32)).astype(bf16)
    pick = patch_pick(pool_ref.shape[0], BLOCK, 0)
    pool_ref[...] = (dot_nn(pick, hidden_b) + dot_nn(pick, rest)).astype(bf16)


def token_forward(wide, conv_rows, kv_weight):
    steps = CELLS // BLOCK
    whole = lambda i: (0, 0)
    block = lambda i: (i, 0)
    return pl.pallas_call(
        token_forward_kernel,
        grid=(steps,),
        in_specs=[
            pl.BlockSpec(wide.shape, whole),
            pl.BlockSpec((3, 3 * CH, CH), lambda i: (0, 0, 0)),
            pl.BlockSpec((CH, 2 * CH), whole),
        ],
        out_specs=[
            pl.BlockSpec((BLOCK, CH), block),
            pl.BlockSpec((BLOCK, CH), block),
            pl.BlockSpec((BLOCK, 2 * CH), block),
            pl.BlockSpec((CTX // steps, CH), block),
        ],
        out_shape=[
            jax.ShapeDtypeStruct((CELLS, CH), bf16),
            jax.ShapeDtypeStruct((CELLS, CH), bf16),
            jax.ShapeDtypeStruct((CELLS, 2 * CH), bf16),
            jax.ShapeDtypeStruct((CTX, CH), bf16),
        ],
        compiler_params=params(),
        cost_estimate=cost(22 * CELLS * CH * CH, 14 * CELLS * CH, CELLS * CH),
    )(wide, conv_rows, kv_weight)


def token_backward_kernel(
    dkv_ref, slope_ref, pool_ref, hidden_ref, x_ref, kv_w_ref,
    d_hidden_ref, gz_ref, conv_ref, kv_g_ref, conv_s, kv_s,
):
    step = pl.program_id(0)

    @pl.when(step == 0)
    def _():
        conv_s[...] = jnp.zeros_like(conv_s)
        kv_s[...] = jnp.zeros_like(kv_s)

    dkv = dkv_ref[...]
    d_hidden = dot_nt(dkv, kv_w_ref[...])
    d_hidden = d_hidden + dot_nn(patch_pick(BLOCK, pool_ref.shape[0], 1), pool_ref[...])
    gz = (d_hidden * slope_ref[...].astype(f32)).astype(bf16)
    d_hidden_ref[...] = d_hidden
    gz_ref[...] = gz
    kv_s[...] += dot_tn(hidden_ref[...], dkv)
    gz_t = gz.T
    for row in range(3):
        conv_s[row] += dot_nn(gz_t, x_ref[image_rows(step, row), :])

    @pl.when(step == pl.num_programs(0) - 1)
    def _():
        for row in range(3):
            for col in range(3):
                conv_ref[3 * row + col] = conv_s[row, :, col * CH : (col + 1) * CH].T.astype(bf16)
        kv_g_ref[0] = kv_s[:, :CH].astype(bf16)
        kv_g_ref[1] = kv_s[:, CH:].astype(bf16)


def token_backward(dkv, slope, d_pool, hidden_b, wide, kv_weight):
    steps = CELLS // BLOCK
    whole = lambda i: (0, 0)
    whole_3 = lambda i: (0, 0, 0)
    block = lambda i: (i, 0)
    return pl.pallas_call(
        token_backward_kernel,
        grid=(steps,),
        in_specs=[
            pl.BlockSpec((BLOCK, 2 * CH), block),
            pl.BlockSpec((BLOCK, CH), block),
            pl.BlockSpec((CTX // steps, CH), block),
            pl.BlockSpec((BLOCK, CH), block),
            pl.BlockSpec(wide.shape, whole),
            pl.BlockSpec((CH, 2 * CH), whole),
        ],
        out_specs=[
            pl.BlockSpec((BLOCK, CH), block),
            pl.BlockSpec((BLOCK, CH), block),
            pl.BlockSpec((9, CH, CH), whole_3),
            pl.BlockSpec((2, CH, CH), whole_3),
        ],
        out_shape=[
            jax.ShapeDtypeStruct((CELLS, CH), f32),
            jax.ShapeDtypeStruct((CELLS, CH), bf16),
            jax.ShapeDtypeStruct((9, CH, CH), bf16),
            jax.ShapeDtypeStruct((2, CH, CH), bf16),
        ],
        scratch_shapes=[pltpu.VMEM((3, CH, 3 * CH), f32), pltpu.VMEM((CH, 2 * CH), f32)],
        compiler_params=params(),
        cost_estimate=cost(26 * CELLS * CH * CH, 20 * CELLS * CH),
    )(dkv, slope, d_pool, hidden_b, wide, kv_weight)


def context_backward_kernel(gz_ref, d_hidden_ref, conv_ref, out_ref, wide_s):
    step = pl.program_id(0)
    steps = pl.num_programs(0)

    def widen(at):
        values = gz_ref[image_rows(at, 0), :].astype(f32)
        col = lax.broadcasted_iota(jnp.int32, (BLOCK, CH), 0) % IMG
        left = jnp.where(col == 0, 0.0, pltpu.roll(values, 1, 0))
        right = jnp.where(col == IMG - 1, 0.0, pltpu.roll(values, BLOCK - 1, 0))
        wide_s[image_rows(at, 1), 0:CH] = left.astype(bf16)
        wide_s[image_rows(at, 1), CH : 2 * CH] = values.astype(bf16)
        wide_s[image_rows(at, 1), 2 * CH :] = right.astype(bf16)

    @pl.when(step == 0)
    def _():
        wide_s[0:IMG, :] = jnp.zeros((IMG, 3 * CH), bf16)
        wide_s[CELLS + IMG :, :] = jnp.zeros((IMG, 3 * CH), bf16)
        widen(0)

    @pl.when(step < steps - 1)
    def _():
        widen(step + 1)

    total = d_hidden_ref[...]
    for row in range(3):
        values = wide_s[image_rows(step, row), :]
        for col in range(3):
            tap = conv_ref[3 * (2 - row) + (2 - col)]
            total = total + dot_nt(values[:, col * CH : (col + 1) * CH], tap)
    out_ref[...] = total.astype(bf16)


def context_backward(gz, d_hidden, conv_tiles):
    block = lambda i: (i, 0)
    return pl.pallas_call(
        context_backward_kernel,
        grid=(CELLS // BLOCK,),
        in_specs=[
            pl.BlockSpec((CELLS, CH), lambda i: (0, 0)),
            pl.BlockSpec((BLOCK, CH), block),
            pl.BlockSpec((9, CH, CH), lambda i: (0, 0, 0)),
        ],
        out_specs=pl.BlockSpec((BLOCK, CH), block),
        out_shape=jax.ShapeDtypeStruct((CELLS, CH), bf16),
        scratch_shapes=[pltpu.VMEM((CELLS + 2 * IMG, 3 * CH), bf16)],
        compiler_params=params(),
        cost_estimate=cost(18 * CELLS * CH * CH, 8 * CELLS * CH),
    )(gz, d_hidden, conv_tiles)


def dot(a, b):
    return jnp.dot(a, b, preferred_element_type=f32)


def gelu_slope(v):
    inner = jnp.sqrt(2.0 / jnp.pi) * (v + 0.044715 * v * v * v)
    bend = jnp.tanh(inner)
    d_inner = jnp.sqrt(2.0 / jnp.pi) * (1.0 + 3.0 * 0.044715 * v * v)
    return 0.5 * (1.0 + bend) + 0.5 * v * (1.0 - bend * bend) * d_inner


def inverse_rms(values):
    return lax.rsqrt(jnp.mean(values * values, -1, keepdims=True) + eps_norm)


def norm_backward(d_normed, values, scale, gain):
    d_gain = jnp.sum(d_normed * values * scale, 0)
    scaled = d_normed * gain
    inner = jnp.mean(scaled * values, -1, keepdims=True)
    return d_gain, scale * scaled - (scale * scale * scale) * values * inner


def local(
    context_map,
    future_feats,
    horizon,
    cotangent,
    tile_owner,
    master_tiles,
    moment_first,
    moment_second,
    norm_gains,
    gain_first,
    gain_second,
):
    slot_count = master_tiles.shape[0]
    devices = lax.axis_size(AXES)
    rows = CH // devices
    slot_of = slot_index(tile_owner, slot_count)

    slices = (
        master_tiles.astype(bf16)
        .reshape(slot_count, devices, rows, CH)
        .transpose(1, 0, 2, 3)
    )
    slices = lax.all_to_all(slices, AXES, split_axis=0, concat_axis=0, tiled=True)
    slices = slices.reshape(devices * slot_count, rows, CH)
    slices = slices.at[slot_of].get(mode="promise_in_bounds")
    early = gather_all(slices[:EARLY]).transpose(1, 0, 2, 3).reshape(EARLY, CH, CH)
    later = slices[EARLY:].reshape(-1, D // CH, rows, CH).transpose(0, 2, 1, 3)
    later = lax.all_gather(later.reshape(-1, D), AXES, axis=0, tiled=True)
    later = later.reshape(devices, -1, rows, D)

    def matrix(start, row_blocks, parts):
        part = later[:, start : start + row_blocks * parts]
        part = part.reshape(devices, row_blocks, parts, rows, D)
        return part.transpose(1, 0, 3, 2, 4).reshape(row_blocks * CH, parts * D)

    image = lax.all_to_all(context_map, ("y", "x"), split_axis=0, concat_axis=1, tiled=True)[0]
    padded = jnp.pad(image, ((1, 1), (1, 1), (0, 0)))
    wide = jnp.concatenate([padded[:, col : col + IMG] for col in range(3)], -1)
    wide = wide.reshape((IMG + 2) * IMG, 3 * CH)

    conv_tiles = early[:9]
    to_query, to_out = early[9], early[12]
    kv_weight = jnp.concatenate([early[10], early[11]], 1)
    w_emb = matrix(0, 1, 1)
    w_qkv = matrix(1, 3, 3)
    w_att = matrix(10, 3, 1)
    w_up = matrix(13, 3, 4)
    w_down = matrix(25, 12, 1)

    slope, hidden_b, kv, pooled = token_forward(wide, conv_tiles.reshape(3, 3 * CH, CH), kv_weight)
    feats_b = future_feats[0]
    length = CTX + FT * horizon
    query = dot(feats_b, to_query).astype(bf16)
    cross_mixed, cross_logs = cross_forward(query, kv)
    updated = feats_b.astype(f32) + dot(cross_mixed, to_out)
    seq = jnp.concatenate([pooled, updated.astype(bf16)], 0)

    gain_one, gain_two = norm_gains[0], norm_gains[1]
    embed = dot(seq, w_emb)
    scale_one = inverse_rms(embed)
    normed_one = (embed * scale_one * gain_one).astype(bf16)
    qkv = dot(normed_one, w_qkv).astype(bf16)
    mixed, logs = self_forward(qkv, length)
    stream = embed + dot(mixed, w_att)
    scale_two = inverse_rms(stream)
    normed_two = (stream * scale_two * gain_two).astype(bf16)
    pre = dot(normed_two, w_up)
    act = jax.nn.gelu(pre, approximate=True).astype(bf16)
    block_out = stream + dot(act, w_down)

    valid = jnp.arange(SEQ) < length[0]
    gd = jnp.where(valid[:, None], cotangent[0], jnp.zeros((), bf16))
    sum_down = cut(dot(act.T, gd))
    gd, sum_down = lax.optimization_barrier((gd, sum_down))
    gpre = (dot(gd, w_down.T) * gelu_slope(pre)).astype(bf16)
    sum_down = sum_core(sum_down)
    sum_up = cut(dot(normed_two.T, gpre))
    gpre, sum_up, sum_down = lax.optimization_barrier((gpre, sum_up, sum_down))
    d_gain_two, d_stream = norm_backward(dot(gpre, w_up.T), stream, scale_two, gain_two)
    d_stream = gd.astype(f32) + d_stream
    ga = d_stream.astype(bf16)
    sum_up = sum_core(sum_up)
    ga, sum_up = lax.optimization_barrier((ga, sum_up))
    sum_down = sum_x(sum_down)
    sum_up = sum_y(sum_up)
    sum_att = cut(dot(mixed.T, ga))
    gog = dot(ga, w_att.T).astype(bf16)
    gog, sum_att = lax.optimization_barrier((gog, sum_att))
    sum_att = sum_core(sum_att)
    log_rows = logs[:, :HEADS].T.reshape(D // CH, GROUP, SEQ)
    gqkv = self_backward(qkv, gog, mixed, log_rows, length)
    gqkv, sum_down, sum_up, sum_att = lax.optimization_barrier((gqkv, sum_down, sum_up, sum_att))
    sum_down = sum_y(sum_down)
    sum_up = sum_x(sum_up)
    sum_att = sum_x(sum_att)
    gqkv = jnp.concatenate([gqkv[0], gqkv[1], gqkv[2]], 1)
    sum_qkv = cut(dot(normed_one.T, gqkv))
    gqkv, sum_qkv = lax.optimization_barrier((gqkv, sum_qkv))
    d_gain_one, d_embed = norm_backward(dot(gqkv, w_qkv.T), embed, scale_one, gain_one)
    gembed = (d_stream + d_embed).astype(bf16)
    sum_qkv = sum_core(sum_qkv)
    sum_emb = cut(dot(seq.T, gembed))
    gseq = dot(gembed, w_emb.T)
    gseq, sum_emb, sum_qkv, sum_down, sum_up, sum_att = lax.optimization_barrier(
        (gseq, sum_emb, sum_qkv, sum_down, sum_up, sum_att)
    )
    sum_down = sum_z(sum_down)
    sum_up = sum_z(sum_up)
    sum_att = sum_y(sum_att)
    sum_emb = sum_core(sum_emb)
    sum_qkv = sum_y(sum_qkv)
    gains = sum_all(jnp.stack([d_gain_one, d_gain_two]))

    gupd = gseq[CTX:]
    gb = gupd.astype(bf16)
    grad_out = dot(cross_mixed.T, gb)
    gox = dot(gb, to_out.T).astype(bf16)
    gq, gkv = cross_backward(query, kv, gox, cross_mixed, cross_logs[:, :TH].T)
    gkv, sum_qkv, sum_emb, sum_down, sum_up, sum_att, gains = lax.optimization_barrier(
        (gkv, sum_qkv, sum_emb, sum_down, sum_up, sum_att, gains)
    )
    grad_query = dot(feats_b.T, gq)
    future_grad = gupd + dot(gq, to_query.T)
    sum_qkv = sum_x(sum_qkv)
    sum_emb = sum_y(sum_emb)
    sum_att = sum_z(sum_att)

    d_hidden, gz, grad_conv, grad_kv = token_backward(
        gkv, slope, gseq[:CTX].astype(bf16), hidden_b, wide, kv_weight
    )
    sum_early = jnp.concatenate(
        [
            grad_conv,
            grad_query.astype(bf16)[None],
            grad_kv,
            grad_out.astype(bf16)[None],
        ],
        0,
    )
    sum_early = cut(sum_early.reshape(EARLY * CH, CH))
    d_hidden, gz, sum_early, sum_qkv, sum_emb = lax.optimization_barrier(
        (d_hidden, gz, sum_early, sum_qkv, sum_emb)
    )
    sum_early = sum_core(sum_early)
    sum_emb = sum_x(sum_emb)
    context_grad = context_backward(gz, d_hidden, conv_tiles)
    sum_qkv = sum_z(sum_qkv)
    sum_emb = sum_z(sum_emb)
    sum_early = scatter_axes(
        sum_early.reshape(sum_early.shape[:2] + (-1,) + sum_early.shape[-2:]), ("y", "x"), 2
    )
    sum_early = sum_z(sum_early)

    sums = [sum_early, sum_emb, sum_qkv, sum_att, sum_up, sum_down]
    sums = jnp.concatenate([to_tiles(part) for part in sums], 0)
    square_total = sum_all(jnp.sum(sums * sums))
    slots = jnp.arange(devices * slot_count)
    found = slot_of[None, :] == slots[:, None]
    tile_of = jnp.sum(jnp.where(found, jnp.arange(found.shape[1])[None], 0), 1)
    mine = sums.astype(bf16).at[tile_of].get(mode="promise_in_bounds")
    mine = mine.reshape(devices, slot_count, rows, CH)
    mine = lax.all_to_all(mine, AXES, split_axis=0, concat_axis=0, tiled=True)
    mine = mine.transpose(1, 0, 2, 3).reshape(slot_count, CH, CH).astype(f32)
    context_rows = lax.all_to_all(
        context_grad.reshape(1, IMG, IMG, CH),
        ("y", "x"),
        split_axis=1,
        concat_axis=0,
        tiled=True,
    ).astype(f32)

    used = jnp.any(found, 1).astype(f32).reshape(devices, slot_count)
    used = lax.dynamic_index_in_dim(used, lax.axis_index(AXES), 0, keepdims=False)[:, None, None]
    grad_norm = jnp.sqrt(square_total + jnp.sum(gains * gains))
    factor = jnp.minimum(1.0, clip_level / (grad_norm + 1e-06))
    new_first, new_second, new_master = adam_step(
        master_tiles, mine * factor, moment_first, moment_second, learn_rate, decay_rate
    )
    new_gain_first, new_gain_second, new_gains = adam_step(
        norm_gains, gains * factor, gain_first, gain_second, gain_rate, 0.0
    )
    return (
        block_out[None],
        context_rows,
        future_grad[None],
        jnp.where(used > 0, new_first, 0.0),
        jnp.where(used > 0, new_second, 0.0),
        jnp.where(used > 0, new_master, 0.0),
        new_gain_first,
        new_gain_second,
        new_gains,
        grad_norm,
    )


def solution(mesh):
    groups, rows = mesh.devices.shape
    fine = jax.sharding.Mesh(mesh.devices.reshape(groups // 2, 2, rows // 2, 2), AXES)
    whole = P(AXES, None, None)
    image = P(("z", "c"), ("y", "x"), None, None)
    in_specs = (image, whole, P(AXES), whole, P(), whole, whole, whole, P(), P(), P())
    out_specs = (whole, image, whole, whole, whole, whole, P(), P(), P(), P())
    return jax.shard_map(local, mesh=fine, in_specs=in_specs, out_specs=out_specs, check_vma=False)
```

time: 1220 us -> 573 us (0.47)
  matrix products: 292 us -> 77.4 us
  waiting for transfers between devices: 374 us -> 170 us
  local copies, waits for them, and re-layouts: 225 us -> 45.2 us
  Pallas kernels: 0 us -> 121 us
  other arithmetic: 149 us -> 39.6 us
  blocking collectives: 108 us -> 0 us
  starting transfers between devices: 39.6 us -> 86.9 us
    dot_general x36 -> x21, matrix products: 233 us -> 77.4 us  [dot(): return jnp.dot(a, b, preferred_element_type=f32)]
    all_gather x6 -> x1, waiting for transfers between devices: 164 us -> 19.5 us  [local(): later = lax.all_gather(later.reshape(-1, D), AXES, axis=0, tiled=True)]
    pallas_call x0 -> x7, Pallas kernels: none -> 121 us  [the longest x1 27.7 us: cross_backward(): pl.pallas_call(cross_backward_kernel, grid=(cells // block,), in_specs=[p...]
    convert_element_type x40 -> x21, other arithmetic: 97.7 us -> 13.4 us  [the longest x17 8.82 us: scatter_axes(): return total if keep_wide else total.astype(values.dtype)]
    all_gather x1 -> x0, blocking collectives: 68.5 us -> none  [local(): whole = [lax.all_gather(part, AXES, axis=0, tiled=True) for part in sums]]
    conv_general_dilated x3 -> x0, matrix products: 59.2 us -> none  [the longest x1 43.9 us: conv_weight_grad(): lax.conv_general_dilated(image[None], d_conv[None], (1, 1), [(1, 1), (1,...]
    ppermute x30 -> x54, waiting for transfers between devices: 181 us -> 124 us  [xor_permute(): return lax.ppermute(values, axes, [(i, i ^ mask) for i in range(count)])]
    reshape x12 -> x3, local copies, waits for them, and re-layouts: 50.9 us -> 6 us  [the longest x2 5.36 us: matrix(): part = part.reshape(devices, row_blocks, parts, rows, D)]
  transfers between devices with their start and end apart: 38 -> 59, of which waited for: 21 -> 32; matrix products, arithmetic and copies ran while one was open for 17% -> 15% of each run, Pallas kernels for 0% -> 17%
where the time goes in v2:
time: 573 us; the launch traced here: 563 us
  waiting for transfers between devices  170 us (30%)
  Pallas kernels  121 us (21%)
  starting transfers between devices  86.9 us (15%)
  matrix products  77.4 us (14%)
  local copies, waits for them, and re-layouts  45.2 us (8%)
  other arithmetic  39.6 us (7%)
  between operations  22.3 us (4%)
    ppermute x54, waiting for transfers between devices, xor_permute(): return lax.ppermute(values, axes, [(i, i ^ mask) for i in range(count)])  124 us
    dot_general x21, matrix products, dot(): return jnp.dot(a, b, preferred_element_type=f32)  77.4 us
    ppermute x54, starting transfers between devices, xor_permute(): return lax.ppermute(values, axes, [(i, i ^ mask) for i in range(count)])  68.7 us
    pallas_call x1, Pallas kernels, cross_backward(): pl.pallas_call(cross_backward_kernel, grid=(cells // block,), in_specs=[p...  27.7 us
    all_to_all x1, waiting for transfers between devices, local(): lax.all_to_all(slices, AXES, split_axis=0, concat_axis=0, tiled=True)  26.2 us
    all_gather x1, waiting for transfers between devices, local(): later = lax.all_gather(later.reshape(-1, D), AXES, axis=0, tiled=True)  19.5 us
    pallas_call x1, Pallas kernels, self_backward(): pl.pallas_call(self_backward_kernel, grid_spec=pltpu.PrefetchScalarGridSp...  19.4 us
    pallas_call x1, Pallas kernels, cross_forward(): pl.pallas_call(cross_forward_kernel, grid=(2,), in_specs=[pl.BlockSpec((r...  16.9 us
  transfers between devices with their start and end apart: 59, of which 32 were waited for; matrix products, arithmetic and copies ran while one was open for 15% of the time, Pallas kernels for 17%

profile of v2, /device:TPU:0, one launch (start us, length us, event | category | flops | bytes accessed | tf_op | source)
XLA Modules:
  0.0 562.5 jit_solution(9311082530900054568)
XLA Ops:
  10.0 7.3 %all-to-all-start.1 = ((bf16[32,8,8,256]{3,2,1,0:T(8,128)(2,1)}), bf16[32,8,8,256]{3,2,1,0:T(8,128)(2,1)S(1)}, u32[]{:S(2)}, u32[]{:S(2)}) async-start(bf16[32,8,8,256]{3,2,1,0:T(8,128)(2,1)} %copy.50), calls=%async_computation.1 | async-start | bytes 2097152 | tf_op jit(solution)/shard_map/all_to_all | solution.py:618
  17.6 26.2 %all-to-all-done.1 = bf16[32,8,8,256]{3,2,1,0:T(8,128)(2,1)S(1)} async-done(((bf16[32,8,8,256]{3,2,1,0:T(8,128)(2,1)}), bf16[32,8,8,256]{3,2,1,0:T(8,128)(2,1)S(1)}, u32[]{:S(2)}, u32[]{:S(2)}) %all-to-all-start.1) | async-done | bytes 1048608 | tf_op jit(solution)/shard_map/all_to_all | solution.py:618
  65.5 16.5 %collective-permute-done.4 = bf16[4,13,8,256]{3,2,1,0:T(8,128)(2,1)S(1)} collective-permute-done((bf16[4,13,8,256]{3,2,1,0:T(8,128)(2,1)S(1)}, bf16[4,13,8,256]{3,2,1,0:T(8,128)(2,1)S(1)}, u32[]{:S(2)}, u32[]{:S(2)}) %collective-permute-start.4) | collective-permute-done | bytes 213024 | tf_op jit(solution)/shard_map/ppermute | solution.py:59
  82.9 8.6 %collective-permute-done.5 = bf16[4,13,8,256]{3,2,1,0:T(8,128)(2,1)S(1)} collective-permute-done((bf16[4,13,8,256]{3,2,1,0:T(8,128)(2,1)S(1)}, bf16[4,13,8,256]{3,2,1,0:T(8,128)(2,1)S(1)}, u32[]{:S(2)}, u32[]{:S(2)}) %collective-permute-start.5) | collective-permute-done | bytes 213024 | tf_op jit(solution)/shard_map/ppermute | solution.py:59
  104.7 15.8 %shard_map.186 = (bf16[4096,256]{1,0:T(8,128)(2,1)}, bf16[4096,256]{1,0:T(8,128)(2,1)}, bf16[4096,512]{1,0:T(8,128)(2,1)}, bf16[256,256]{1,0:T(8,128)(2,1)}) custom-call(bf16[4224,768]{1,0:T(8,128)(2,1)} %bitcast.338, bf16[3,768,256]{2,1,0:T(8,128)(2,1)} %bitcast.360, bf16[256,512]{1,0:T(8,128)(2,1)} %pad_maximum_fusion.7.kv_w_ref), custom_call_target="tpu_custom_call" | custom-call | flops 5905580032 | bytes 14680064 | tf_op jit(solution)/shard_map/pallas_call | solution.py:433
  120.5 16.9 %shard_map.187 = (bf16[480,256]{1,0:T(8,128)(2,1)}, f32[480,128]{1,0:T(8,128)}) custom-call(bf16[480,256]{1,0:T(8,128)(2,1)} %fusion.30.q_ref, bf16[4096,512]{1,0:T(8,128)(2,1)} %get-tuple-element.58.k_ref.v_ref, bf16[4096,512]{1,0:T(8,128)(2,1)} %get-tuple-element.58.k_ref.v_ref), custom_call_target="tpu_custom_call" | custom-call | flops 8053063680 | bytes 8388608 | tf_op jit(solution)/shard_map/pallas_call | solution.py:180
  141.0 19.5 %all-gather.2.cloned.1.call-done = bf16[9472,768]{1,0:T(8,128)(2,1)} async-done(((bf16[296,768]{1,0:T(8,128)(2,1)}), bf16[9472,768]{1,0:T(8,128)(2,1)}) %all-gather.2.cloned.1.call-update) | async-done | bytes 14549008 | tf_op jit(solution)/shard_map/all_gather | solution.py:623
  164.1 6.5 %fusion.84 = (bf16[32,12,8,768]{3,2,1,0:T(8,128)(2,1)}, bf16[12,32,8,1,768]{4,2,0,1,3:T(8,128)(2,1)S(1)}) fusion(bf16[32,37,8,768]{3,2,1,0:T(8,128)(2,1)} %bitcast.325), kind=kLoop, calls=%fused_computation.254 | loop fusion | bytes 18874368 | tf_op jit(solution)/shard_map/slice | solution.py:627
  182.3 13.6 %shard_map.188 = (bf16[736,768]{1,0:T(8,128)(2,1)}, f32[736,128]{1,0:T(8,128)}) custom-call(s32[1]{0:T(128)} %add.472.len_ref, bf16[736,2304]{1,0:T(8,128)(2,1)} %convolution_convert_fusion.3.q_ref.k_ref.v_ref, bf16[736,2304]{1,0:T(8,128)(2,1)} %convolution_convert_fusion.3.q_ref.k_ref.v_ref, bf16[736,2304]{1,0:T(8,128)(2,1)} %convolution_convert_fusion.3.q_ref.k_ref.v_ref), custom_call_target="tpu_custom_call" | custom-call | flops 6656360448 | bytes 4521984 | tf_op jit(solution)/shard_map/pallas_call | solution.py:314
  211.3 5.4 convolution_convert_fusion.1
  217.3 10.1 %fusion.15 = bf16[736,3072]{1,0:T(8,128)(2,1)S(1)} fusion(f32[736,3072]{1,0:T(8,128)} %copy-done.41, bf16[736,768]{1,0:T(8,128)(2,1)S(1)} %copy-done.7, bf16[3072,768]{1,0:T(8,128)(2,1)S(1)} %bitcast.346), kind=kOutput, calls=%fused_computation.21 | convolution fusion | flops 3515842560 | bytes 19415040 | tf_op jit(solution)/shard_map/dot_general | solution.py:574
  239.8 8.8 %multiply_reduce_fusion = (f32[768]{0:T(1024)S(1)}, f32[736]{0:T(1024)S(1)}, f32[736,768]{1,0:T(8,128)S(1)}) fusion(f32[736,768]{1,0:T(8,128)} %get-tuple-element.177, f32[736]{0:T(1024)S(1)} %get-tuple-element.173, f32[768]{0:T(1024)S(1)} %get-tuple-element.108, bf16[736,3072]{1,0:T(8,128)(2,1)} %copy-done.40, bf16[768,3072]{1,0:T(8,128)(2,1)} %bitcast.349), kind=kOutput, calls=%fused_computation.42 | convolution fusion | flops 3476273664 | bytes 13774592 | tf_op jit(solution)/shard_map/dot_general | solution.py:574
  250.0 16.5 %collective-permute-done.9 = bf16[12,4,2,8,768]{4,3,2,1,0:T(8,128)(2,1)S(1)} collective-permute-done((bf16[12,4,2,8,768]{4,3,2,1,0:T(8,128)(2,1)S(1)}, bf16[12,4,2,8,768]{4,3,2,1,0:T(8,128)(2,1)S(1)}, u32[]{:S(2)}, u32[]{:S(2)}) %collective-permute-start.9) | collective-permute-done | bytes 1179680 | tf_op jit(solution)/shard_map/ppermute | solution.py:59
  275.4 19.4 %shard_map.189 = bf16[3,736,768]{2,1,0:T(8,128)(2,1)} custom-call(s32[1]{0:T(128)} %add.472.len_ref, bf16[736,2304]{1,0:T(8,128)(2,1)} %convolution_convert_fusion.3.q_ref.k_ref.v_ref, bf16[736,2304]{1,0:T(8,128)(2,1)} %convolution_convert_fusion.3.q_ref.k_ref.v_ref, bf16[736,2304]{1,0:T(8,128)(2,1)} %convolution_convert_fusion.3.q_ref.k_ref.v_ref, ...), custom_call_target="tpu_custom_call" | custom-call | flops 13312720896 | bytes 9043968 | tf_op jit(solution)/shard_map/pallas_call | solution.py:379
  296.2 6.2 %collective-permute-done.10 = bf16[3,4,2,8,3072]{4,3,2,1,0:T(8,128)(2,1)} collective-permute-done((bf16[3,4,2,8,3072]{4,3,2,1,0:T(8,128)(2,1)S(1)}, bf16[3,4,2,8,3072]{4,3,2,1,0:T(8,128)(2,1)}, u32[]{:S(2)}, u32[]{:S(2)}) %collective-permute-start.10) | collective-permute-done | bytes 1179680 | tf_op jit(solution)/shard_map/ppermute | solution.py:59
  319.2 12.7 %collective-permute-done.26 = f32[2,768]{1,0:T(2,128)S(1)} collective-permute-done((f32[2,768]{1,0:T(2,128)S(1)}, f32[2,768]{1,0:T(2,128)S(1)}, u32[]{:S(2)}, u32[]{:S(2)}) %collective-permute-start.26) | collective-permute-done | bytes 6176 | tf_op jit(solution)/shard_map/ppermute | solution.py:59
  349.6 27.7 %shard_map.190 = (bf16[480,256]{1,0:T(8,128)(2,1)}, bf16[4096,512]{1,0:T(8,128)(2,1)}) custom-call(bf16[480,256]{1,0:T(8,128)(2,1)} %fusion.30.q_ref, bf16[4096,512]{1,0:T(8,128)(2,1)} %get-tuple-element.58.k_ref.v_ref, bf16[4096,512]{1,0:T(8,128)(2,1)} %get-tuple-element.58.k_ref.v_ref, bf16[480,256]{1,0:T(8,128)(2,1)} %convolution_convert_fusion.8.do_ref, ...), custom_call_target="tpu_custom_call" | custom-call | flops 20132659200 | bytes 8388608 | tf_op jit(solution)/shard_map/pallas_call | solution.py:256
  393.8 5.8 %collective-permute-done.22 = bf16[3,8,3072]{2,1,0:T(8,128)(2,1)S(1)} collective-permute-done((bf16[3,8,3072]{2,1,0:T(8,128)(2,1)S(1)}, bf16[3,8,3072]{2,1,0:T(8,128)(2,1)S(1)}, u32[]{:S(2)}, u32[]{:S(2)}) %collective-permute-start.22) | collective-permute-done | bytes 147488 | tf_op jit(solution)/shard_map/ppermute | solution.py:59
  403.1 10.6 %collective-permute-done.16 = bf16[3,4,2,8,2304]{4,3,2,1,0:T(8,128)(2,1)S(1)} collective-permute-done((bf16[3,4,2,8,2304]{4,3,2,1,0:T(8,128)(2,1)S(1)}, bf16[3,4,2,8,2304]{4,3,2,1,0:T(8,128)(2,1)S(1)}, u32[]{:S(2)}, u32[]{:S(2)}) %collective-permute-start.16) | collective-permute-done | bytes 884768 | tf_op jit(solution)/shard_map/ppermute | solution.py:59
  419.7 16.4 %shard_map.191 = (f32[4096,256]{1,0:T(8,128)}, bf16[4096,256]{1,0:T(8,128)(2,1)}, bf16[9,256,256]{2,1,0:T(8,128)(2,1)}, bf16[2,256,256]{2,1,0:T(8,128)(2,1)}) custom-call(bf16[4096,512]{1,0:T(8,128)(2,1)} %get-tuple-element.85.dkv_ref, bf16[4096,256]{1,0:T(8,128)(2,1)} %get-tuple-element.86.slope_ref, bf16[256,256]{1,0:T(8,128)(2,1)} %slice.196.pool_ref, ...), custom_call_target="tpu_custom_call" | custom-call | flops 6979321856 | bytes 20971520 | tf_op jit(solution)/shard_map/pallas_call | solution.py:494
  439.9 11.1 %shard_map.192 = bf16[4096,256]{1,0:T(8,128)(2,1)} custom-call(bf16[4096,256]{1,0:T(8,128)(2,1)} %get-tuple-element.95.gz_ref, f32[4096,256]{1,0:T(8,128)} %get-tuple-element.96.d_hidden_ref, bf16[9,256,256]{2,1,0:T(8,128)(2,1)} %get-tuple-element.130.conv_ref), custom_call_target="tpu_custom_call" | custom-call | flops 4831838208 | bytes 8388608 | tf_op jit(solution)/shard_map/pallas_call | solution.py:557
  458.1 14.9 %collective-permute-done.39 = bf16[1,4,8,768]{3,2,1,0:T(8,128)(2,1)S(1)} collective-permute-done((bf16[1,4,8,768]{3,2,1,0:T(8,128)(2,1)S(1)}, bf16[1,4,8,768]{3,2,1,0:T(8,128)(2,1)S(1)}, u32[]{:S(2)}, u32[]{:S(2)}) %collective-permute-start.39) | collective-permute-done | bytes 49184 | tf_op jit(solution)/shard_map/ppermute | solution.py:59
  507.8 12.4 %add_bitcast_fusion = f32[1,736,768]{2,1,0:T(8,128)} fusion(f32[736,768]{1,0:T(8,128)} %get-tuple-element.177, bf16[3072,768]{1,0:T(8,128)(2,1)} %bitcast.347, f32[736,3072]{1,0:T(8,128)} %copy-done.41), kind=kOutput, calls=%fused_computation.48 | convolution fusion | flops 3493797888 | bytes 18284544 | tf_op jit(solution)/shard_map/dot_general | solution.py:574
  547.2 7.1 %subtract_select_fusion = (f32[8,256,256]{2,1,0:T(8,128)}, f32[8,256,256]{2,1,0:T(8,128)}, f32[8,256,256]{2,1,0:T(8,128)}) fusion(f32[8,256,256]{2,1,0:T(8,128)} %param.16, pred[8]{0:T(512)(128)(4,1)S(1)} %compare_bitcast_fusion, f32[8,256,256]{2,1,0:T(8,128)} %param.17, f32[8,256,256]{2,1,0:T(8,128)} %param.18, bf16[32,8,8,256]{3,2,1,0:T(8,128)(2,1)} %all-to-all-done.3, ...), kind=kLoop, calls=%fused_computation.59 | loop fusion | flops 10485760 | bytes 13631500 | tf_op jit(solution)/shard_map/jit(_where)/select_n | solution.py:783
  (339 shorter events, 224.4 us)
Async XLA Ops:
  10.0 33.7 %all-to-all-start.1 = ((bf16[32,8,8,256]{3,2,1,0:T(8,128)(2,1)}), bf16[32,8,8,256]{3,2,1,0:T(8,128)(2,1)S(1)}, u32[]{:S(2)}, u32[]{:S(2)}) async-start(bf16[32,8,8,256]{3,2,1,0:T(8,128)(2,1)} %copy.50), calls=%async_computation.1 | async-start | bytes 2097152 | tf_op jit(solution)/shard_map/all_to_all | solution.py:618
  17.3 143.2 %all-gather.2.cloned.1.call-start = ((), (), s32[]{:S(2)}) async-start(), calls=%async_computation.4 | async-start | bytes 15003648 | tf_op jit(solution)/shard_map/all_gather | solution.py:623
  45.2 47.3 %all-to-all-start = ((bf16[4,16,64,256]{3,2,1,0:T(8,128)(2,1)}), bf16[4,16,64,256]{3,2,1,0:T(8,128)(2,1)S(1)}, u32[]{:S(2)}, u32[]{:S(2)}) async-start(bf16[4,16,64,256]{3,2,1,0:T(8,128)(2,1)} %param.11), calls=%async_computation | async-start | bytes 4194304 | tf_op jit(solution)/shard_map/all_to_all | solution.py:631
  59.6 22.5 %collective-permute-start.4 = (bf16[4,13,8,256]{3,2,1,0:T(8,128)(2,1)S(1)}, bf16[4,13,8,256]{3,2,1,0:T(8,128)(2,1)S(1)}, u32[]{:S(2)}, u32[]{:S(2)}) collective-permute-start(bf16[4,13,8,256]{3,2,1,0:T(8,128)(2,1)S(1)} %get-tuple-element.157), channel_id=1, source_target_pairs={{0,2},{1,3},{2,0},{3,1},{4,6},{5,7},{6,4},{7,5},{8,10},{9,11},{10,... | collective-permute-start | bytes 638984 | tf_op jit(solution)/shard_map/ppermute | solution.py:59
  61.5 21.4 %collective-permute-start.3 = (bf16[4,13,8,256]{3,2,1,0:T(8,128)(2,1)S(1)}, bf16[4,13,8,256]{3,2,1,0:T(8,128)(2,1)S(1)}, u32[]{:S(2)}, u32[]{:S(2)}) collective-permute-start(bf16[4,13,8,256]{3,2,1,0:T(8,128)(2,1)S(1)} %get-tuple-element.157), channel_id=1, source_target_pairs={{0,1},{1,0},{2,3},{3,2},{4,5},{5,4},{6,7},{7,6},{8,9},{9,8},{10,11... | collective-permute-start | bytes 638984 | tf_op jit(solution)/shard_map/ppermute | solution.py:59
  62.9 28.5 %collective-permute-start.5 = (bf16[4,13,8,256]{3,2,1,0:T(8,128)(2,1)S(1)}, bf16[4,13,8,256]{3,2,1,0:T(8,128)(2,1)S(1)}, u32[]{:S(2)}, u32[]{:S(2)}) collective-permute-start(bf16[4,13,8,256]{3,2,1,0:T(8,128)(2,1)S(1)} %get-tuple-element.157), channel_id=1, source_target_pairs={{0,3},{1,2},{2,1},{3,0},{4,7},{5,6},{6,5},{7,4},{8,11},{9,10},{10,... | collective-permute-start | bytes 638984 | tf_op jit(solution)/shard_map/ppermute | solution.py:59
  235.4 31.5 %collective-permute-start.8 = (bf16[3,4,2,2,8,3072]{5,4,3,2,1,0:T(8,128)(2,1)}, bf16[3,4,2,2,8,3072]{5,4,3,2,1,0:T(8,128)(2,1)}, u32[]{:S(2)}, u32[]{:S(2)}) collective-permute-start(bf16[3,4,2,2,8,3072]{5,4,3,2,1,0:T(8,128)(2,1)} %dynamic-slice_bitcast_fusion), channel_id=1, source_target_pairs={{0,4},{4,0},{1,5},{5,1},{2,6},{6,2},{3,7},{7,3},{8,12},{12,8},{9,1... | collective-permute-start | bytes 7077896 | tf_op jit(solution)/shard_map/ppermute | solution.py:59
  238.3 28.2 %collective-permute-start.9 = (bf16[12,4,2,8,768]{4,3,2,1,0:T(8,128)(2,1)S(1)}, bf16[12,4,2,8,768]{4,3,2,1,0:T(8,128)(2,1)S(1)}, u32[]{:S(2)}, u32[]{:S(2)}) collective-permute-start(bf16[12,4,2,8,768]{4,3,2,1,0:T(8,128)(2,1)S(1)} %dynamic-slice_bitcast_fusion.4), channel_id=1, source_target_pairs={{0,1},{1,0},{2,3},{3,2},{4,5},{5,4},{6,7},{7,6},{8,9},{9,8},{10,11... | collective-permute-start | bytes 3538952 | tf_op jit(solution)/shard_map/ppermute | solution.py:59
  273.7 21.1 %collective-permute-start.11 = (bf16[3,4,2,2,8,768]{5,4,3,2,1,0:T(8,128)(2,1)}, bf16[3,4,2,2,8,768]{5,4,3,2,1,0:T(8,128)(2,1)}, u32[]{:S(2)}, u32[]{:S(2)}) collective-permute-start(bf16[3,4,2,2,8,768]{5,4,3,2,1,0:T(8,128)(2,1)} %dynamic-slice_bitcast_fusion.9), channel_id=1, source_target_pairs={{0,4},{4,0},{1,5},{5,1},{2,6},{6,2},{3,7},{7,3},{8,12},{12,8},{9,1... | collective-permute-start | bytes 1769480 | tf_op jit(solution)/shard_map/ppermute | solution.py:59
  273.8 28.6 %collective-permute-start.10 = (bf16[3,4,2,8,3072]{4,3,2,1,0:T(8,128)(2,1)S(1)}, bf16[3,4,2,8,3072]{4,3,2,1,0:T(8,128)(2,1)}, u32[]{:S(2)}, u32[]{:S(2)}) collective-permute-start(bf16[3,4,2,8,3072]{4,3,2,1,0:T(8,128)(2,1)S(1)} %dynamic-slice_bitcast_fusion.3), channel_id=1, source_target_pairs={{0,2},{2,0},{1,3},{3,1},{4,6},{6,4},{5,7},{7,5},{8,10},{10,8},{9,1... | collective-permute-start | bytes 3538952 | tf_op jit(solution)/shard_map/ppermute | solution.py:59
  310.4 33.4 %collective-permute-start.15 = (bf16[3,4,2,8,768]{4,3,2,1,0:T(8,128)(2,1)S(1)}, bf16[3,4,2,8,768]{4,3,2,1,0:T(8,128)(2,1)S(1)}, u32[]{:S(2)}, u32[]{:S(2)}) collective-permute-start(bf16[3,4,2,8,768]{4,3,2,1,0:T(8,128)(2,1)S(1)} %dynamic-slice_bitcast_fusion.11), channel_id=1, source_target_pairs={{0,1},{1,0},{2,3},{3,2},{4,5},{5,4},{6,7},{7,6},{8,9},{9,8},{10,11... | collective-permute-start | bytes 884744 | tf_op jit(solution)/shard_map/ppermute | solution.py:59
  312.1 32.0 %collective-permute-start.14 = (bf16[3,4,8,3072]{3,2,1,0:T(8,128)(2,1)S(1)}, bf16[3,4,8,3072]{3,2,1,0:T(8,128)(2,1)S(1)}, u32[]{:S(2)}, u32[]{:S(2)}) collective-permute-start(bf16[3,4,8,3072]{3,2,1,0:T(8,128)(2,1)S(1)} %dynamic-slice_bitcast_fusion.7), channel_id=1, source_target_pairs={{0,1},{1,0},{2,3},{3,2},{4,5},{5,4},{6,7},{7,6},{8,9},{9,8},{10,11... | collective-permute-start | bytes 1769480 | tf_op jit(solution)/shard_map/ppermute | solution.py:59
  312.7 31.2 %collective-permute-start.13 = (bf16[12,4,8,768]{3,2,1,0:T(8,128)(2,1)S(1)}, bf16[12,4,8,768]{3,2,1,0:T(8,128)(2,1)S(1)}, u32[]{:S(2)}, u32[]{:S(2)}) collective-permute-start(bf16[12,4,8,768]{3,2,1,0:T(8,128)(2,1)S(1)} %dynamic-slice_bitcast_fusion.8), channel_id=1, source_target_pairs={{0,2},{2,0},{1,3},{3,1},{4,6},{6,4},{5,7},{7,5},{8,10},{10,8},{9,1... | collective-permute-start | bytes 1769480 | tf_op jit(solution)/shard_map/ppermute | solution.py:59
  319.2 25.1 %collective-permute-start.12 = (bf16[3,4,2,2,8,2304]{5,4,3,2,1,0:T(8,128)(2,1)S(1)}, bf16[3,4,2,2,8,2304]{5,4,3,2,1,0:T(8,128)(2,1)S(1)}, u32[]{:S(2)}, u32[]{:S(2)}) collective-permute-start(bf16[3,4,2,2,8,2304]{5,4,3,2,1,0:T(8,128)(2,1)S(1)} %dynamic-slice_bitcast_fusion.2), channel_id=1, source_target_pairs={{0,4},{4,0},{1,5},{5,1},{2,6},{6,2},{3,7},{7,3},{8,12},{12,8},{9,1... | collective-permute-start | bytes 5308424 | tf_op jit(solution)/shard_map/ppermute | solution.py:59
  348.0 55.0 %collective-permute-start.24 = (bf16[3,4,8,768]{3,2,1,0:T(8,128)(2,1)S(1)}, bf16[3,4,8,768]{3,2,1,0:T(8,128)(2,1)S(1)}, u32[]{:S(2)}, u32[]{:S(2)}) collective-permute-start(bf16[3,4,8,768]{3,2,1,0:T(8,128)(2,1)S(1)} %dynamic-slice_bitcast_fusion.16), channel_id=1, source_target_pairs={{0,2},{2,0},{1,3},{3,1},{4,6},{6,4},{5,7},{7,5},{8,10},{10,8},{9,1... | collective-permute-start | bytes 442376 | tf_op jit(solution)/shard_map/ppermute | solution.py:59
  413.9 25.8 %collective-permute-start.31 = (bf16[1,4,2,8,768]{4,3,2,1,0:T(8,128)(2,1)S(1)}, bf16[1,4,2,8,768]{4,3,2,1,0:T(8,128)(2,1)S(1)}, u32[]{:S(2)}, u32[]{:S(2)}) collective-permute-start(bf16[1,4,2,8,768]{4,3,2,1,0:T(8,128)(2,1)S(1)} %dynamic-slice_bitcast_fusion.26), channel_id=1, source_target_pairs={{0,2},{2,0},{1,3},{3,1},{4,6},{6,4},{5,7},{7,5},{8,10},{10,8},{9,1... | collective-permute-start | bytes 294920 | tf_op jit(solution)/shard_map/ppermute | solution.py:59
  414.6 25.1 %collective-permute-start.46 = (bf16[3,8,768]{2,1,0:T(8,128)(2,1)S(1)}, bf16[3,8,768]{2,1,0:T(8,128)(2,1)S(1)}, u32[]{:S(2)}, u32[]{:S(2)}) collective-permute-start(bf16[3,8,768]{2,1,0:T(8,128)(2,1)S(1)} %get-tuple-element.158), channel_id=1, source_target_pairs={{0,8},{8,0},{16,24},{24,16},{1,9},{9,1},{17,25},{25,17},{2,10},{10... | collective-permute-start | bytes 110600 | tf_op jit(solution)/shard_map/ppermute | solution.py:59
  414.6 25.0 %collective-permute-start.48 = (bf16[3,8,768]{2,1,0:T(8,128)(2,1)S(1)}, bf16[3,8,768]{2,1,0:T(8,128)(2,1)S(1)}, u32[]{:S(2)}, u32[]{:S(2)}) collective-permute-start(bf16[3,8,768]{2,1,0:T(8,128)(2,1)S(1)} %get-tuple-element.159), channel_id=1, source_target_pairs={{0,24},{8,16},{16,8},{24,0},{1,25},{9,17},{17,9},{25,1},{2,26},{10... | collective-permute-start | bytes 110600 | tf_op jit(solution)/shard_map/ppermute | solution.py:59
  416.1 23.5 %collective-permute-start.47 = (bf16[3,8,768]{2,1,0:T(8,128)(2,1)S(1)}, bf16[3,8,768]{2,1,0:T(8,128)(2,1)S(1)}, u32[]{:S(2)}, u32[]{:S(2)}) collective-permute-start(bf16[3,8,768]{2,1,0:T(8,128)(2,1)S(1)} %get-tuple-element.160), channel_id=1, source_target_pairs={{0,16},{8,24},{16,0},{24,8},{1,17},{9,25},{17,1},{25,9},{2,18},{10... | collective-permute-start | bytes 110600 | tf_op jit(solution)/shard_map/ppermute | solution.py:59
  418.2 21.6 %collective-permute-start.30 = (bf16[3,4,8,2304]{3,2,1,0:T(8,128)(2,1)S(1)}, bf16[3,4,8,2304]{3,2,1,0:T(8,128)(2,1)S(1)}, u32[]{:S(2)}, u32[]{:S(2)}) collective-permute-start(bf16[3,4,8,2304]{3,2,1,0:T(8,128)(2,1)S(1)} %dynamic-slice_bitcast_fusion.10), channel_id=1, source_target_pairs={{0,1},{1,0},{2,3},{3,2},{4,5},{5,4},{6,7},{7,6},{8,9},{9,8},{10,11... | collective-permute-start | bytes 1327112 | tf_op jit(solution)/shard_map/ppermute | solution.py:59
  451.1 52.8 %all-to-all-start.2 = ((bf16[1,64,64,256]{3,2,0,1:T(8,128)(2,1)}), bf16[1,64,64,256]{3,2,0,1:T(8,128)(2,1)S(1)}, u32[]{:S(2)}, u32[]{:S(2)}) async-start(bf16[1,64,64,256]{3,2,0,1:T(8,128)(2,1)} %bitcast.358), calls=%async_computation.2 | async-start | bytes 4194304 | tf_op jit(solution)/shard_map/all_to_all | solution.py:759
  458.0 22.2 %collective-permute-start.32 = (bf16[13,4,2,2,8,256]{5,4,3,2,1,0:T(8,128)(2,1)S(1)}, bf16[13,4,2,2,8,256]{5,4,3,2,1,0:T(8,128)(2,1)S(1)}, u32[]{:S(2)}, u32[]{:S(2)}) collective-permute-start(bf16[13,4,2,2,8,256]{5,4,3,2,1,0:T(8,128)(2,1)S(1)} %dynamic-slice_bitcast_fusion.6), channel_id=1, source_target_pairs={{0,4},{4,0},{1,5},{5,1},{2,6},{6,2},{3,7},{7,3},{8,12},{12,8},{9,1... | collective-permute-start | bytes 2555912 | tf_op jit(solution)/shard_map/ppermute | solution.py:59
  476.5 18.6 %collective-permute-start.43 = (bf16[3,8,2304]{2,1,0:T(8,128)(2,1)S(1)}, bf16[3,8,2304]{2,1,0:T(8,128)(2,1)S(1)}, u32[]{:S(2)}, u32[]{:S(2)}) collective-permute-start(bf16[3,8,2304]{2,1,0:T(8,128)(2,1)S(1)} %get-tuple-element.147), channel_id=1, source_target_pairs={{0,8},{8,0},{16,24},{24,16},{1,9},{9,1},{17,25},{25,17},{2,10},{10... | collective-permute-start | bytes 331784 | tf_op jit(solution)/shard_map/ppermute | solution.py:59
  503.9 43.3 %all-to-all-start.3 = ((bf16[32,8,8,256]{3,2,1,0:T(8,128)(2,1)}), bf16[32,8,8,256]{3,2,1,0:T(8,128)(2,1)}, u32[]{:S(2)}, u32[]{:S(2)}) async-start(bf16[32,8,8,256]{3,2,1,0:T(8,128)(2,1)} %bitcast.350), calls=%async_computation.3 | async-start | bytes 2097152 | tf_op jit(solution)/shard_map/all_to_all | solution.py:757
  (81 other events, 858.1 us)
Sparse Core Ops, SparseCore 0:
  45.4 115.0 all-gather.1

commit v3 on v2

--- a/solution.py
+++ b/solution.py
@@ -89,13 +89,15 @@
     return values.reshape((-1,) + shape).at[at].get(mode="promise_in_bounds")
 
 
-def sum_all(values):
-    for axis in ("c", "x", "y", "z"):
-        bit = 1
-        while bit < lax.axis_size(axis):
-            values = values + xor_permute(values, axis, bit)
-            bit = bit * 2
-    return values
+def trade_rows(values):
+    count = lax.axis_size(("y", "x"))
+    mine = lax.axis_index(("y", "x"))
+    pieces = [lax.dynamic_index_in_dim(values, mine, 0, keepdims=False)]
+    for mask in range(1, count):
+        give = lax.dynamic_index_in_dim(values, mine ^ mask, 0, keepdims=False)
+        pieces.append(xor_permute(give, ("y", "x"), mask))
+    order = jnp.arange(count) ^ mine
+    return jnp.stack(pieces).at[order].get(mode="promise_in_bounds")
 
 
 def cut(matrix):
@@ -117,6 +119,23 @@
 
 def sum_z(slices):
     return scatter_axes(slices, "z", 1, keep_wide=True)
+
+
+def sum_rows(slices):
+    merged = slices.reshape(slices.shape[:2] + (-1,) + slices.shape[-2:])
+    return scatter_axes(merged, ("y", "x"), 2)
+
+
+def split_wide(slices):
+    parts = slices.shape[-1] // D
+    if parts == 1:
+        return slices
+    cutted = slices.reshape(slices.shape[:-1] + (parts, D))
+    cutted = jnp.moveaxis(cutted, -2, 1)
+    return cutted.reshape((-1,) + slices.shape[1:-1] + (D,))
+
+
+tie = lax.optimization_barrier
 
 
 def to_tiles(slices):
@@ -610,6 +629,8 @@
     rows = CH // devices
     slot_of = slot_index(tile_owner, slot_count)
 
+    image = trade_rows(context_map).reshape(IMG, IMG, CH)
+
     slices = (
         master_tiles.astype(bf16)
         .reshape(slot_count, devices, rows, CH)
@@ -628,7 +649,6 @@
         part = part.reshape(devices, row_blocks, parts, rows, D)
         return part.transpose(1, 0, 3, 2, 4).reshape(row_blocks * CH, parts * D)
 
-    image = lax.all_to_all(context_map, ("y", "x"), split_axis=0, concat_axis=1, tiled=True)[0]
     padded = jnp.pad(image, ((1, 1), (1, 1), (0, 0)))
     wide = jnp.concatenate([padded[:, col : col + IMG] for col in range(3)], -1)
     wide = wide.reshape((IMG + 2) * IMG, 3 * CH)
@@ -666,63 +686,64 @@
     valid = jnp.arange(SEQ) < length[0]
     gd = jnp.where(valid[:, None], cotangent[0], jnp.zeros((), bf16))
     sum_down = cut(dot(act.T, gd))
-    gd, sum_down = lax.optimization_barrier((gd, sum_down))
+    gd, sum_down = tie((gd, sum_down))
     gpre = (dot(gd, w_down.T) * gelu_slope(pre)).astype(bf16)
     sum_down = sum_core(sum_down)
     sum_up = cut(dot(normed_two.T, gpre))
-    gpre, sum_up, sum_down = lax.optimization_barrier((gpre, sum_up, sum_down))
+    gpre, sum_up, sum_down = tie((gpre, sum_up, sum_down))
     d_gain_two, d_stream = norm_backward(dot(gpre, w_up.T), stream, scale_two, gain_two)
     d_stream = gd.astype(f32) + d_stream
     ga = d_stream.astype(bf16)
-    sum_up = sum_core(sum_up)
-    ga, sum_up = lax.optimization_barrier((ga, sum_up))
+    sum_up = split_wide(sum_core(sum_up))
     sum_down = sum_x(sum_down)
+    ga, sum_up = tie((ga, sum_up))
     sum_up = sum_y(sum_up)
     sum_att = cut(dot(mixed.T, ga))
     gog = dot(ga, w_att.T).astype(bf16)
-    gog, sum_att = lax.optimization_barrier((gog, sum_att))
-    sum_att = sum_core(sum_att)
     log_rows = logs[:, :HEADS].T.reshape(D // CH, GROUP, SEQ)
     gqkv = self_backward(qkv, gog, mixed, log_rows, length)
-    gqkv, sum_down, sum_up, sum_att = lax.optimization_barrier((gqkv, sum_down, sum_up, sum_att))
+    gqkv, sum_down, sum_up, sum_att = tie((gqkv, sum_down, sum_up, sum_att))
     sum_down = sum_y(sum_down)
     sum_up = sum_x(sum_up)
-    sum_att = sum_x(sum_att)
+    sum_att = sum_core(sum_att)
     gqkv = jnp.concatenate([gqkv[0], gqkv[1], gqkv[2]], 1)
     sum_qkv = cut(dot(normed_one.T, gqkv))
-    gqkv, sum_qkv = lax.optimization_barrier((gqkv, sum_qkv))
+    gqkv, sum_qkv = tie((gqkv, sum_qkv))
+    sum_qkv = split_wide(sum_core(sum_qkv))
     d_gain_one, d_embed = norm_backward(dot(gqkv, w_qkv.T), embed, scale_one, gain_one)
     gembed = (d_stream + d_embed).astype(bf16)
-    sum_qkv = sum_core(sum_qkv)
     sum_emb = cut(dot(seq.T, gembed))
+    gains = jnp.stack([d_gain_one, d_gain_two]).reshape(devices, 1, -1)
+    gain_count = gains.shape[-1]
+    gains = jnp.pad(gains, ((0, 0), (0, rows - 1), (0, D - gain_count))).astype(bf16)
+    sum_emb = jnp.concatenate([sum_emb, gains.reshape((1,) + sum_emb.shape[1:])], 0)
     gseq = dot(gembed, w_emb.T)
-    gseq, sum_emb, sum_qkv, sum_down, sum_up, sum_att = lax.optimization_barrier(
+    gseq, sum_emb, sum_qkv, sum_down, sum_up, sum_att = tie(
         (gseq, sum_emb, sum_qkv, sum_down, sum_up, sum_att)
     )
-    sum_down = sum_z(sum_down)
-    sum_up = sum_z(sum_up)
-    sum_att = sum_y(sum_att)
-    sum_emb = sum_core(sum_emb)
-    sum_qkv = sum_y(sum_qkv)
-    gains = sum_all(jnp.stack([d_gain_one, d_gain_two]))
+    sum_mlp = jnp.concatenate([sum_up, sum_down], 0)
+    half = sum_qkv.shape[0] * 2 // 3
+    first = sum_qkv[:half]
+    second = jnp.concatenate([sum_qkv[half:], sum_att], 0)
 
     gupd = gseq[CTX:]
     gb = gupd.astype(bf16)
     grad_out = dot(cross_mixed.T, gb)
     gox = dot(gb, to_out.T).astype(bf16)
     gq, gkv = cross_backward(query, kv, gox, cross_mixed, cross_logs[:, :TH].T)
-    gkv, sum_qkv, sum_emb, sum_down, sum_up, sum_att, gains = lax.optimization_barrier(
-        (gkv, sum_qkv, sum_emb, sum_down, sum_up, sum_att, gains)
-    )
+    first = sum_x(first)
+    second = sum_y(second)
+    sum_mlp = sum_z(sum_mlp)
+    sum_emb = sum_core(sum_emb)
+    gkv, first, second, sum_mlp, sum_emb = tie((gkv, first, second, sum_mlp, sum_emb))
     grad_query = dot(feats_b.T, gq)
-    future_grad = gupd + dot(gq, to_query.T)
-    sum_qkv = sum_x(sum_qkv)
-    sum_emb = sum_y(sum_emb)
-    sum_att = sum_z(sum_att)
 
     d_hidden, gz, grad_conv, grad_kv = token_backward(
         gkv, slope, gseq[:CTX].astype(bf16), hidden_b, wide, kv_weight
     )
+    first = sum_y(first)
+    second = sum_x(second)
+    sum_emb = sum_rows(sum_emb)
     sum_early = jnp.concatenate(
         [
             grad_conv,
@@ -733,40 +754,48 @@
         0,
     )
     sum_early = cut(sum_early.reshape(EARLY * CH, CH))
-    d_hidden, gz, sum_early, sum_qkv, sum_emb = lax.optimization_barrier(
-        (d_hidden, gz, sum_early, sum_qkv, sum_emb)
-    )
-    sum_early = sum_core(sum_early)
-    sum_emb = sum_x(sum_emb)
+    own_core = lax.axis_index("c")
+    keep = lax.dynamic_index_in_dim(sum_early, own_core, 2, keepdims=False)
+    give = lax.dynamic_index_in_dim(sum_early, own_core ^ 1, 2, keepdims=False)
+    d_hidden, gz, keep, give, first, second, sum_emb = tie(
+        (d_hidden, gz, keep, give, first, second, sum_emb)
+    )
+    sum_early = (keep.astype(f32) + xor_permute(give, "c", 1).astype(f32)).astype(bf16)
     context_grad = context_backward(gz, d_hidden, conv_tiles)
-    sum_qkv = sum_z(sum_qkv)
+    context_grad, sum_early = tie((context_grad, sum_early))
+    sum_att = sum_z(jnp.concatenate([first, second], 0))
     sum_emb = sum_z(sum_emb)
-    sum_early = scatter_axes(
-        sum_early.reshape(sum_early.shape[:2] + (-1,) + sum_early.shape[-2:]), ("y", "x"), 2
-    )
+    sum_early = sum_rows(sum_early)
     sum_early = sum_z(sum_early)
-
-    sums = [sum_early, sum_emb, sum_qkv, sum_att, sum_up, sum_down]
+    context_rows = trade_rows(context_grad.reshape(context_map.shape))
+    future_grad = gupd + dot(gq, to_query.T)
+
+    sums = [sum_early, sum_emb[:1], sum_att, sum_mlp]
     sums = jnp.concatenate([to_tiles(part) for part in sums], 0)
-    square_total = sum_all(jnp.sum(sums * sums))
+    gains = sum_emb[1, 0, :gain_count]
+    square = jnp.sum(sums * sums) + jnp.sum(gains * gains)
+    share = jnp.concatenate([square[None], gains])
+    share_high = share.astype(bf16)
+    share_low = (share - share_high.astype(f32)).astype(bf16)
+    share = jnp.pad(
+        jnp.stack([share_high, share_low]), ((0, rows - 2), (0, CH - 1 - gain_count))
+    )
     slots = jnp.arange(devices * slot_count)
     found = slot_of[None, :] == slots[:, None]
     tile_of = jnp.sum(jnp.where(found, jnp.arange(found.shape[1])[None], 0), 1)
     mine = sums.astype(bf16).at[tile_of].get(mode="promise_in_bounds")
     mine = mine.reshape(devices, slot_count, rows, CH)
+    share = jnp.broadcast_to(share[None, None], (devices, 1, rows, CH))
+    mine = jnp.concatenate([mine, share], 1)
     mine = lax.all_to_all(mine, AXES, split_axis=0, concat_axis=0, tiled=True)
-    mine = mine.transpose(1, 0, 2, 3).reshape(slot_count, CH, CH).astype(f32)
-    context_rows = lax.all_to_all(
-        context_grad.reshape(1, IMG, IMG, CH),
-        ("y", "x"),
-        split_axis=1,
-        concat_axis=0,
-        tiled=True,
-    ).astype(f32)
+    shares = mine[:, slot_count, :2].astype(f32)
+    shares = shares[:, 0] + shares[:, 1]
+    gains = shares[:, 1 : 1 + gain_count].reshape(2, D)
+    mine = mine[:, :slot_count].transpose(1, 0, 2, 3).reshape(slot_count, CH, CH).astype(f32)
 
     used = jnp.any(found, 1).astype(f32).reshape(devices, slot_count)
     used = lax.dynamic_index_in_dim(used, lax.axis_index(AXES), 0, keepdims=False)[:, None, None]
-    grad_norm = jnp.sqrt(square_total + jnp.sum(gains * gains))
+    grad_norm = jnp.sqrt(jnp.sum(shares[:, 0]))
     factor = jnp.minimum(1.0, clip_level / (grad_norm + 1e-06))
     new_first, new_second, new_master = adam_step(
         master_tiles, mine * factor, moment_first, moment_second, learn_rate, decay_rate
@@ -776,7 +805,7 @@
     )
     return (
         block_out[None],
-        context_rows,
+        context_rows.reshape(context_map.shape).astype(f32),
         future_grad[None],
         jnp.where(used > 0, new_first, 0.0),
         jnp.where(used > 0, new_second, 0.0),

time: 573 us -> 546 us (0.953)
  starting transfers between devices: 86.9 us -> 57.4 us
  waiting for transfers between devices: 170 us -> 150 us
  local copies, waits for them, and re-layouts: 45.2 us -> 60.5 us
  other arithmetic: 39.6 us -> 47.3 us
    ppermute x54 -> x45, starting transfers between devices: 68.7 us -> 47.1 us  [xor_permute(): return lax.ppermute(values, axes, [(i, i ^ mask) for i in range(count)])]
    ppermute x54 -> x45, waiting for transfers between devices: 124 us -> 104 us  [xor_permute(): return lax.ppermute(values, axes, [(i, i ^ mask) for i in range(count)])]
    all_to_all x2 -> x0, starting transfers between devices: 7.23 us -> none  [the longest x1 3.62 us: local(): lax.all_to_all(context_map, ('y', 'x'), split_axis=0, concat_axis=1, tile...]
    unnamed x97 -> x116, local copies, waits for them, and re-layouts: 8.7 us -> 11.5 us
  transfers between devices with their start and end apart: 59 -> 48, of which waited for: 32 -> 22; matrix products, arithmetic and copies ran while one was open for 15% -> 18% of each run, Pallas kernels for 17% -> 15%
where the time goes in v3:
time: 546 us; the launch traced here: 536 us
  waiting for transfers between devices  150 us (27%)
  Pallas kernels  121 us (22%)
  matrix products  79.2 us (15%)
  local copies, waits for them, and re-layouts  60.5 us (11%)
  starting transfers between devices  57.4 us (11%)
  other arithmetic  47.3 us (9%)
  between operations  19.5 us (4%)
    ppermute x45, waiting for transfers between devices, xor_permute(): return lax.ppermute(values, axes, [(i, i ^ mask) for i in range(count)])  104 us
    dot_general x21, matrix products, dot(): return jnp.dot(a, b, preferred_element_type=f32)  79.2 us
    ppermute x45, starting transfers between devices, xor_permute(): return lax.ppermute(values, axes, [(i, i ^ mask) for i in range(count)])  47.1 us
    pallas_call x1, Pallas kernels, cross_backward(): pl.pallas_call(cross_backward_kernel, grid=(cells // block,), in_specs=[p...  27.9 us
    all_to_all x1, waiting for transfers between devices, local(): lax.all_to_all(slices, AXES, split_axis=0, concat_axis=0, tiled=True)  26.2 us
    all_gather x1, waiting for transfers between devices, local(): later = lax.all_gather(later.reshape(-1, D), AXES, axis=0, tiled=True)  19.9 us
    pallas_call x1, Pallas kernels, self_backward(): pl.pallas_call(self_backward_kernel, grid_spec=pltpu.PrefetchScalarGridSp...  19.4 us
    pallas_call x1, Pallas kernels, cross_forward(): pl.pallas_call(cross_forward_kernel, grid=(2,), in_specs=[pl.BlockSpec((r...  17.2 us
  transfers between devices with their start and end apart: 48, of which 22 were waited for; matrix products, arithmetic and copies ran while one was open for 18% of the time, Pallas kernels for 15%

profile of v3, /device:TPU:0, one launch (start us, length us, event | category | flops | bytes accessed | tf_op | source)
XLA Modules:
  0.0 535.5 jit_solution(13444812809097147011)
XLA Ops:
  10.0 7.3 %all-to-all-start = ((bf16[32,8,8,256]{3,2,1,0:T(8,128)(2,1)}), bf16[32,8,8,256]{3,2,1,0:T(8,128)(2,1)S(1)}, u32[]{:S(2)}, u32[]{:S(2)}) async-start(bf16[32,8,8,256]{3,2,1,0:T(8,128)(2,1)} %copy.69), calls=%async_computation | async-start | bytes 2097152 | tf_op jit(solution)/shard_map/all_to_all | solution.py:639
  17.6 26.2 %all-to-all-done = bf16[32,8,8,256]{3,2,1,0:T(8,128)(2,1)S(1)} async-done(((bf16[32,8,8,256]{3,2,1,0:T(8,128)(2,1)}), bf16[32,8,8,256]{3,2,1,0:T(8,128)(2,1)S(1)}, u32[]{:S(2)}, u32[]{:S(2)}) %all-to-all-start) | async-done | bytes 1048608 | tf_op jit(solution)/shard_map/all_to_all | solution.py:639
  58.2 6.2 %collective-permute-done.4 = bf16[13,8,256]{2,1,0:T(8,128)(2,1)S(1)} collective-permute-done((bf16[13,8,256]{2,1,0:T(8,128)(2,1)S(1)}, bf16[13,8,256]{2,1,0:T(8,128)(2,1)S(1)}, u32[]{:S(2)}, u32[]{:S(2)}) %collective-permute-start.4) | collective-permute-done | bytes 53280 | tf_op jit(solution)/shard_map/ppermute | solution.py:59
  84.6 6.0 %collective-permute-done.7 = bf16[4,13,8,256]{3,2,1,0:T(8,128)(2,1)} collective-permute-done((bf16[4,13,8,256]{3,2,1,0:T(8,128)(2,1)}, bf16[4,13,8,256]{3,2,1,0:T(8,128)(2,1)}, u32[]{:S(2)}, u32[]{:S(2)}) %collective-permute-start.7) | collective-permute-done | bytes 213024 | tf_op jit(solution)/shard_map/ppermute | solution.py:59
  103.0 15.8 %shard_map.186 = (bf16[4096,256]{1,0:T(8,128)(2,1)}, bf16[4096,256]{1,0:T(8,128)(2,1)}, bf16[4096,512]{1,0:T(8,128)(2,1)}, bf16[256,256]{1,0:T(8,128)(2,1)}) custom-call(bf16[4224,768]{1,0:T(8,128)(2,1)} %bitcast.338, bf16[3,768,256]{2,1,0:T(8,128)(2,1)} %bitcast.367, bf16[256,512]{1,0:T(8,128)(2,1)} %pad_maximum_fusion.15.kv_w_ref), custom_call_target="tpu_custom_call" | custom-call | flops 5905580032 | bytes 14680064 | tf_op jit(solution)/shard_map/pallas_call | solution.py:452
  118.8 17.2 %shard_map.187 = (bf16[480,256]{1,0:T(8,128)(2,1)}, f32[480,128]{1,0:T(8,128)}) custom-call(bf16[480,256]{1,0:T(8,128)(2,1)} %fusion.30.q_ref, bf16[4096,512]{1,0:T(8,128)(2,1)} %get-tuple-element.58.k_ref.v_ref, bf16[4096,512]{1,0:T(8,128)(2,1)} %get-tuple-element.58.k_ref.v_ref), custom_call_target="tpu_custom_call" | custom-call | flops 8053063680 | bytes 8388608 | tf_op jit(solution)/shard_map/pallas_call | solution.py:199
  139.6 19.9 %all-gather.2.cloned.1.call-done = bf16[9472,768]{1,0:T(8,128)(2,1)} async-done(((bf16[296,768]{1,0:T(8,128)(2,1)}), bf16[9472,768]{1,0:T(8,128)(2,1)}) %all-gather.2.cloned.1.call-update) | async-done | bytes 14549008 | tf_op jit(solution)/shard_map/all_gather | solution.py:644
  163.1 6.5 %fusion.83 = (bf16[32,12,8,768]{3,2,1,0:T(8,128)(2,1)}, bf16[12,32,8,1,768]{4,2,0,1,3:T(8,128)(2,1)S(1)}) fusion(bf16[32,37,8,768]{3,2,1,0:T(8,128)(2,1)} %bitcast.322), kind=kLoop, calls=%fused_computation.276 | loop fusion | bytes 18874368 | tf_op jit(solution)/shard_map/slice | solution.py:648
  180.7 13.4 %shard_map.188 = (bf16[736,768]{1,0:T(8,128)(2,1)}, f32[736,128]{1,0:T(8,128)}) custom-call(s32[1]{0:T(128)} %add.452.len_ref, bf16[736,2304]{1,0:T(8,128)(2,1)} %convolution_convert_fusion.3.q_ref.k_ref.v_ref, bf16[736,2304]{1,0:T(8,128)(2,1)} %convolution_convert_fusion.3.q_ref.k_ref.v_ref, bf16[736,2304]{1,0:T(8,128)(2,1)} %convolution_convert_fusion.3.q_ref.k_ref.v_ref), custom_call_target="tpu_custom_call" | custom-call | flops 6656360448 | bytes 4521984 | tf_op jit(solution)/shard_map/pallas_call | solution.py:333
  215.5 10.3 %fusion.15 = bf16[736,3072]{1,0:T(8,128)(2,1)S(1)} fusion(f32[736,3072]{1,0:T(8,128)} %copy-done.50, bf16[736,768]{1,0:T(8,128)(2,1)S(1)} %copy-done.10, bf16[3072,768]{1,0:T(8,128)(2,1)S(1)} %bitcast.348), kind=kOutput, calls=%fused_computation.23 | convolution fusion | flops 3515842560 | bytes 19415040 | tf_op jit(solution)/shard_map/dot_general | solution.py:593
  238.4 8.7 %multiply_reduce_fusion = (bf16[768]{0:T(1024)(128)(2,1)S(1)}, f32[736]{0:T(1024)S(1)}, f32[736,768]{1,0:T(8,128)S(1)}) fusion(f32[736,768]{1,0:T(8,128)} %get-tuple-element.191, f32[736]{0:T(1024)} %copy-done.40, f32[768]{0:T(1024)S(1)} %get-tuple-element.108, bf16[736,3072]{1,0:T(8,128)(2,1)} %copy-done.49, bf16[768,3072]{1,0:T(8,128)(2,1)} %bitcast.351), kind=kOutput, calls=%fused_computation.45 | convolution fusion | flops 3476273664 | bytes 13773056 | tf_op jit(solution)/shard_map/dot_general | solution.py:593
  249.3 15.8 %collective-permute-done.12 = bf16[12,4,2,8,768]{4,3,2,1,0:T(8,128)(2,1)S(1)} collective-permute-done((bf16[12,4,2,8,768]{4,3,2,1,0:T(8,128)(2,1)S(1)}, bf16[12,4,2,8,768]{4,3,2,1,0:T(8,128)(2,1)S(1)}, u32[]{:S(2)}, u32[]{:S(2)}) %collective-permute-start.12) | collective-permute-done | bytes 1179680 | tf_op jit(solution)/shard_map/ppermute | solution.py:59
  275.9 19.4 %shard_map.189 = bf16[3,736,768]{2,1,0:T(8,128)(2,1)} custom-call(s32[1]{0:T(128)} %add.452.len_ref, bf16[736,2304]{1,0:T(8,128)(2,1)} %convolution_convert_fusion.3.q_ref.k_ref.v_ref, bf16[736,2304]{1,0:T(8,128)(2,1)} %convolution_convert_fusion.3.q_ref.k_ref.v_ref, bf16[736,2304]{1,0:T(8,128)(2,1)} %convolution_convert_fusion.3.q_ref.k_ref.v_ref, ...), custom_call_target="tpu_custom_call" | custom-call | flops 13312720896 | bytes 9043968 | tf_op jit(solution)/shard_map/pallas_call | solution.py:398
  295.3 6.3 %collective-permute-done.13 = bf16[12,4,2,8,768]{4,3,1,0,2:T(8,128)(2,1)S(1)} collective-permute-done((bf16[12,4,2,8,768]{4,3,1,0,2:T(8,128)(2,1)S(1)}, bf16[12,4,2,8,768]{4,3,1,0,2:T(8,128)(2,1)S(1)}, u32[]{:S(2)}, u32[]{:S(2)}) %collective-permute-start.13) | collective-permute-done | bytes 1179680 | tf_op jit(solution)/shard_map/ppermute | solution.py:59
  336.4 27.9 %shard_map.190 = (bf16[480,256]{1,0:T(8,128)(2,1)}, bf16[4096,512]{1,0:T(8,128)(2,1)}) custom-call(bf16[480,256]{1,0:T(8,128)(2,1)} %fusion.30.q_ref, bf16[4096,512]{1,0:T(8,128)(2,1)} %get-tuple-element.58.k_ref.v_ref, bf16[4096,512]{1,0:T(8,128)(2,1)} %get-tuple-element.58.k_ref.v_ref, bf16[480,256]{1,0:T(8,128)(2,1)} %convolution_convert_fusion.8.do_ref, ...), custom_call_target="tpu_custom_call" | custom-call | flops 20132659200 | bytes 8388608 | tf_op jit(solution)/shard_map/pallas_call | solution.py:275
  376.8 6.5 %collective-permute-done.22 = bf16[24,8,768]{2,1,0:T(8,128)(2,1)S(1)} collective-permute-done((bf16[24,8,768]{2,1,0:T(8,128)(2,1)S(1)}, bf16[24,8,768]{2,1,0:T(8,128)(2,1)S(1)}, u32[]{:S(2)}, u32[]{:S(2)}) %collective-permute-start.22) | collective-permute-done | bytes 294944 | tf_op jit(solution)/shard_map/ppermute | solution.py:59
  383.3 12.2 %collective-permute-done.21 = bf16[24,8,768]{2,1,0:T(8,128)(2,1)S(1)} collective-permute-done((bf16[24,8,768]{2,1,0:T(8,128)(2,1)S(1)}, bf16[24,8,768]{2,1,0:T(8,128)(2,1)S(1)}, u32[]{:S(2)}, u32[]{:S(2)}) %collective-permute-start.21) | collective-permute-done | bytes 294944 | tf_op jit(solution)/shard_map/ppermute | solution.py:59
  401.9 16.4 %shard_map.191 = (f32[4096,256]{1,0:T(8,128)}, bf16[4096,256]{1,0:T(8,128)(2,1)}, bf16[9,256,256]{2,1,0:T(8,128)(2,1)}, bf16[2,256,256]{2,1,0:T(8,128)(2,1)}) custom-call(bf16[4096,512]{1,0:T(8,128)(2,1)} %get-tuple-element.83.dkv_ref, bf16[4096,256]{1,0:T(8,128)(2,1)} %get-tuple-element.84.slope_ref, bf16[256,256]{1,0:T(8,128)(2,1)} %slice.292.pool_ref, ...), custom_call_target="tpu_custom_call" | custom-call | flops 6979321856 | bytes 20971520 | tf_op jit(solution)/shard_map/pallas_call | solution.py:513
  426.6 11.3 %shard_map.192 = bf16[4096,256]{1,0:T(8,128)(2,1)} custom-call(bf16[4096,256]{1,0:T(8,128)(2,1)} %get-tuple-element.94.gz_ref, f32[4096,256]{1,0:T(8,128)} %get-tuple-element.95.d_hidden_ref, bf16[9,256,256]{2,1,0:T(8,128)(2,1)} %get-tuple-element.147.conv_ref), custom_call_target="tpu_custom_call" | custom-call | flops 4831838208 | bytes 8388608 | tf_op jit(solution)/shard_map/pallas_call | solution.py:576
  439.6 5.5 %collective-permute-done.43 = bf16[12,8,768]{2,1,0:T(8,128)(2,1)S(1)} collective-permute-done((bf16[12,8,768]{2,1,0:T(8,128)(2,1)S(1)}, bf16[12,8,768]{2,1,0:T(8,128)(2,1)S(1)}, u32[]{:S(2)}, u32[]{:S(2)}) %collective-permute-start.43) | collective-permute-done | bytes 147488 | tf_op jit(solution)/shard_map/ppermute | solution.py:59
  478.6 11.6 %add_bitcast_fusion = f32[1,736,768]{2,1,0:T(8,128)} fusion(f32[736,768]{1,0:T(8,128)S(1)} %copy-done.19, bf16[3072,768]{1,0:T(8,128)(2,1)} %bitcast.349, f32[736,3072]{1,0:T(8,128)} %copy-done.50), kind=kOutput, calls=%fused_computation.51 | convolution fusion | flops 3493797888 | bytes 18284544 | tf_op jit(solution)/shard_map/dot_general | solution.py:593
  492.2 8.8 %collective-permute-done.32 = bf16[16,64,256]{2,1,0:T(8,128)(2,1)S(1)} collective-permute-done((bf16[16,64,256]{2,1,0:T(8,128)(2,1)S(1)}, bf16[16,64,256]{2,1,0:T(8,128)(2,1)S(1)}, u32[]{:S(2)}, u32[]{:S(2)}) %collective-permute-start.32) | collective-permute-done | bytes 524320 | tf_op jit(solution)/shard_map/ppermute | solution.py:59
  501.0 10.5 %collective-permute-done.31 = bf16[16,64,256]{2,1,0:T(8,128)(2,1)S(1)} collective-permute-done((bf16[16,64,256]{2,1,0:T(8,128)(2,1)S(1)}, bf16[16,64,256]{2,1,0:T(8,128)(2,1)S(1)}, u32[]{:S(2)}, u32[]{:S(2)}) %collective-permute-start.31) | collective-permute-done | bytes 524320 | tf_op jit(solution)/shard_map/ppermute | solution.py:59
  520.5 6.8 %subtract_select_fusion = (f32[8,256,256]{2,1,0:T(8,128)}, f32[8,256,256]{2,1,0:T(8,128)}, f32[8,256,256]{2,1,0:T(8,128)}) fusion(f32[8,256,256]{2,1,0:T(8,128)} %param.16, pred[8]{0:T(512)(128)(4,1)S(1)} %compare_bitcast_fusion, f32[8,256,256]{2,1,0:T(8,128)} %param.17, f32[8,256,256]{2,1,0:T(8,128)} %param.18, ...), kind=kLoop, calls=%fused_computation.64 | loop fusion | flops 10485760 | bytes 13632004 | tf_op jit(solution)/shard_map/jit(_where)/select_n | solution.py:812
  (357 shorter events, 219.6 us)
Async XLA Ops:
  10.0 33.7 %all-to-all-start = ((bf16[32,8,8,256]{3,2,1,0:T(8,128)(2,1)}), bf16[32,8,8,256]{3,2,1,0:T(8,128)(2,1)S(1)}, u32[]{:S(2)}, u32[]{:S(2)}) async-start(bf16[32,8,8,256]{3,2,1,0:T(8,128)(2,1)} %copy.69), calls=%async_computation | async-start | bytes 2097152 | tf_op jit(solution)/shard_map/all_to_all | solution.py:639
  17.3 142.2 %all-gather.2.cloned.1.call-start = ((), (), s32[]{:S(2)}) async-start(), calls=%async_computation.2 | async-start | bytes 15003648 | tf_op jit(solution)/shard_map/all_gather | solution.py:644
  48.3 25.4 %collective-permute-start = (bf16[16,64,256]{2,1,0:T(8,128)(2,1)}, bf16[16,64,256]{2,1,0:T(8,128)(2,1)S(1)}, u32[]{:S(2)}, u32[]{:S(2)}) collective-permute-start(bf16[16,64,256]{2,1,0:T(8,128)(2,1)} %get-tuple-element.137), channel_id=1, source_target_pairs={{0,1},{1,0},{2,3},{3,2},{4,5},{5,4},{6,7},{7,6},{8,9},{9,8},{10,11... | collective-permute-start | bytes 1572872 | tf_op jit(solution)/shard_map/ppermute | solution.py:59
  49.6 28.9 %collective-permute-start.2 = (bf16[16,64,256]{2,1,0:T(8,128)(2,1)}, bf16[16,64,256]{2,1,0:T(8,128)(2,1)S(1)}, u32[]{:S(2)}, u32[]{:S(2)}) collective-permute-start(bf16[16,64,256]{2,1,0:T(8,128)(2,1)} %get-tuple-element.138), channel_id=1, source_target_pairs={{0,3},{1,2},{2,1},{3,0},{4,7},{5,6},{6,5},{7,4},{8,11},{9,10},{10,... | collective-permute-start | bytes 1572872 | tf_op jit(solution)/shard_map/ppermute | solution.py:59
  51.0 29.3 %collective-permute-start.1 = (bf16[16,64,256]{2,1,0:T(8,128)(2,1)S(1)}, bf16[16,64,256]{2,1,0:T(8,128)(2,1)S(1)}, u32[]{:S(2)}, u32[]{:S(2)}) collective-permute-start(bf16[16,64,256]{2,1,0:T(8,128)(2,1)S(1)} %get-tuple-element.139), channel_id=1, source_target_pairs={{0,2},{1,3},{2,0},{3,1},{4,6},{5,7},{6,4},{7,5},{8,10},{9,11},{10,... | collective-permute-start | bytes 1572872 | tf_op jit(solution)/shard_map/ppermute | solution.py:59
  71.9 18.6 %collective-permute-start.7 = (bf16[4,13,8,256]{3,2,1,0:T(8,128)(2,1)}, bf16[4,13,8,256]{3,2,1,0:T(8,128)(2,1)}, u32[]{:S(2)}, u32[]{:S(2)}) collective-permute-start(bf16[4,13,8,256]{3,2,1,0:T(8,128)(2,1)} %get-tuple-element.175), channel_id=1, source_target_pairs={{0,2},{1,3},{2,0},{3,1},{4,6},{5,7},{6,4},{7,5},{8,10},{9,11},{10,... | collective-permute-start | bytes 638984 | tf_op jit(solution)/shard_map/ppermute | solution.py:59
  72.7 17.8 %collective-permute-start.6 = (bf16[4,13,8,256]{3,2,1,0:T(8,128)(2,1)}, bf16[4,13,8,256]{3,2,1,0:T(8,128)(2,1)}, u32[]{:S(2)}, u32[]{:S(2)}) collective-permute-start(bf16[4,13,8,256]{3,2,1,0:T(8,128)(2,1)} %get-tuple-element.175), channel_id=1, source_target_pairs={{0,1},{1,0},{2,3},{3,2},{4,5},{5,4},{6,7},{7,6},{8,9},{9,8},{10,11... | collective-permute-start | bytes 638984 | tf_op jit(solution)/shard_map/ppermute | solution.py:59
  233.9 31.5 %collective-permute-start.11 = (bf16[3,4,2,2,8,3072]{5,4,3,2,1,0:T(8,128)(2,1)}, bf16[3,4,2,2,8,3072]{5,4,3,2,1,0:T(8,128)(2,1)}, u32[]{:S(2)}, u32[]{:S(2)}) collective-permute-start(bf16[3,4,2,2,8,3072]{5,4,3,2,1,0:T(8,128)(2,1)} %dynamic-slice_bitcast_fusion), channel_id=1, source_target_pairs={{0,4},{4,0},{1,5},{5,1},{2,6},{6,2},{3,7},{7,3},{8,12},{12,8},{9,1... | collective-permute-start | bytes 7077896 | tf_op jit(solution)/shard_map/ppermute | solution.py:59
  236.8 28.2 %collective-permute-start.12 = (bf16[12,4,2,8,768]{4,3,2,1,0:T(8,128)(2,1)S(1)}, bf16[12,4,2,8,768]{4,3,2,1,0:T(8,128)(2,1)S(1)}, u32[]{:S(2)}, u32[]{:S(2)}) collective-permute-start(bf16[12,4,2,8,768]{4,3,2,1,0:T(8,128)(2,1)S(1)} %dynamic-slice_bitcast_fusion.4), channel_id=1, source_target_pairs={{0,1},{1,0},{2,3},{3,2},{4,5},{5,4},{6,7},{7,6},{8,9},{9,8},{10,11... | collective-permute-start | bytes 3538952 | tf_op jit(solution)/shard_map/ppermute | solution.py:59
  274.2 27.4 %collective-permute-start.13 = (bf16[12,4,2,8,768]{4,3,1,0,2:T(8,128)(2,1)S(1)}, bf16[12,4,2,8,768]{4,3,1,0,2:T(8,128)(2,1)S(1)}, u32[]{:S(2)}, u32[]{:S(2)}) collective-permute-start(bf16[12,4,2,8,768]{4,3,1,0,2:T(8,128)(2,1)S(1)} %dynamic-slice_bitcast_fusion.3), channel_id=1, source_target_pairs={{0,2},{2,0},{1,3},{3,1},{4,6},{6,4},{5,7},{7,5},{8,10},{10,8},{9,1... | collective-permute-start | bytes 3538952 | tf_op jit(solution)/shard_map/ppermute | solution.py:59
  365.6 30.0 %collective-permute-start.23 = (bf16[2,4,2,2,8,768]{5,4,3,2,1,0:T(8,128)(2,1)S(1)}, bf16[2,4,2,2,8,768]{5,4,3,2,1,0:T(8,128)(2,1)S(1)}, u32[]{:S(2)}, u32[]{:S(2)}) collective-permute-start(bf16[2,4,2,2,8,768]{5,4,3,2,1,0:T(8,128)(2,1)S(1)} %dynamic-slice_bitcast_fusion.18), channel_id=1, source_target_pairs={{0,4},{4,0},{1,5},{5,1},{2,6},{6,2},{3,7},{7,3},{8,12},{12,8},{9,1... | collective-permute-start | bytes 1179656 | tf_op jit(solution)/shard_map/ppermute | solution.py:59
  369.1 26.4 %collective-permute-start.21 = (bf16[24,8,768]{2,1,0:T(8,128)(2,1)S(1)}, bf16[24,8,768]{2,1,0:T(8,128)(2,1)S(1)}, u32[]{:S(2)}, u32[]{:S(2)}) collective-permute-start(bf16[24,8,768]{2,1,0:T(8,128)(2,1)S(1)} %get-tuple-element.151), channel_id=1, source_target_pairs={{0,16},{8,24},{16,0},{24,8},{1,17},{9,25},{17,1},{25,9},{2,18},{10... | collective-permute-start | bytes 884744 | tf_op jit(solution)/shard_map/ppermute | solution.py:59
  369.7 26.1 %collective-permute-start.18 = (bf16[6,4,2,8,768]{4,3,1,0,2:T(8,128)(2,1)S(1)}, bf16[6,4,2,8,768]{4,3,1,0,2:T(8,128)(2,1)S(1)}, u32[]{:S(2)}, u32[]{:S(2)}) collective-permute-start(bf16[6,4,2,8,768]{4,3,1,0,2:T(8,128)(2,1)S(1)} %dynamic-slice_bitcast_fusion.8), channel_id=1, source_target_pairs={{0,1},{1,0},{2,3},{3,2},{4,5},{5,4},{6,7},{7,6},{8,9},{9,8},{10,11... | collective-permute-start | bytes 1769480 | tf_op jit(solution)/shard_map/ppermute | solution.py:59
  375.3 20.6 %collective-permute-start.19 = (bf16[6,4,2,8,768]{4,3,2,1,0:T(8,128)(2,1)S(1)}, bf16[6,4,2,8,768]{4,3,2,1,0:T(8,128)(2,1)S(1)}, u32[]{:S(2)}, u32[]{:S(2)}) collective-permute-start(bf16[6,4,2,8,768]{4,3,2,1,0:T(8,128)(2,1)S(1)} %dynamic-slice_bitcast_fusion.7), channel_id=1, source_target_pairs={{0,2},{2,0},{1,3},{3,1},{4,6},{6,4},{5,7},{7,5},{8,10},{10,8},{9,1... | collective-permute-start | bytes 1769480 | tf_op jit(solution)/shard_map/ppermute | solution.py:59
  396.2 24.1 %collective-permute-start.25 = (bf16[6,4,8,768]{3,2,1,0:T(8,128)(2,1)S(1)}, bf16[6,4,8,768]{3,2,1,0:T(8,128)(2,1)S(1)}, u32[]{:S(2)}, u32[]{:S(2)}) collective-permute-start(bf16[6,4,8,768]{3,2,1,0:T(8,128)(2,1)S(1)} %dynamic-slice_bitcast_fusion.19), channel_id=1, source_target_pairs={{0,1},{1,0},{2,3},{3,2},{4,5},{5,4},{6,7},{7,6},{8,9},{9,8},{10,11... | collective-permute-start | bytes 884744 | tf_op jit(solution)/shard_map/ppermute | solution.py:59
  397.8 22.5 %collective-permute-start.24 = (bf16[6,4,8,768]{3,2,1,0:T(8,128)(2,1)S(1)}, bf16[6,4,8,768]{3,2,1,0:T(8,128)(2,1)S(1)}, u32[]{:S(2)}, u32[]{:S(2)}) collective-permute-start(bf16[6,4,8,768]{3,2,1,0:T(8,128)(2,1)S(1)} %dynamic-slice_bitcast_fusion.20), channel_id=1, source_target_pairs={{0,2},{2,0},{1,3},{3,1},{4,6},{6,4},{5,7},{7,5},{8,10},{10,8},{9,1... | collective-permute-start | bytes 884744 | tf_op jit(solution)/shard_map/ppermute | solution.py:59
  398.3 21.8 %collective-permute-start.26 = (bf16[2,4,8,768]{3,2,0,1:T(8,128)(2,1)S(1)}, bf16[2,4,8,768]{3,2,0,1:T(8,128)(2,1)S(1)}, u32[]{:S(2)}, u32[]{:S(2)}) collective-permute-start(bf16[2,4,8,768]{3,2,0,1:T(8,128)(2,1)S(1)} %get-tuple-element.165), channel_id=1, source_target_pairs={{0,1},{1,0},{2,3},{3,2},{4,5},{5,4},{6,7},{7,6},{8,9},{9,8},{10,11... | collective-permute-start | bytes 294920 | tf_op jit(solution)/shard_map/ppermute | solution.py:59
  399.9 20.2 %collective-permute-start.28 = (bf16[2,4,8,768]{3,2,0,1:T(8,128)(2,1)S(1)}, bf16[2,4,8,768]{3,2,0,1:T(8,128)(2,1)S(1)}, u32[]{:S(2)}, u32[]{:S(2)}) collective-permute-start(bf16[2,4,8,768]{3,2,0,1:T(8,128)(2,1)S(1)} %get-tuple-element.166), channel_id=1, source_target_pairs={{0,3},{1,2},{2,1},{3,0},{4,7},{5,6},{6,5},{7,4},{8,11},{9,10},{10,... | collective-permute-start | bytes 294920 | tf_op jit(solution)/shard_map/ppermute | solution.py:59
  401.4 18.7 %collective-permute-start.27 = (bf16[2,4,8,768]{3,2,0,1:T(8,128)(2,1)S(1)}, bf16[2,4,8,768]{3,2,0,1:T(8,128)(2,1)S(1)}, u32[]{:S(2)}, u32[]{:S(2)}) collective-permute-start(bf16[2,4,8,768]{3,2,0,1:T(8,128)(2,1)S(1)} %get-tuple-element.167), channel_id=1, source_target_pairs={{0,2},{1,3},{2,0},{3,1},{4,6},{5,7},{6,4},{7,5},{8,10},{9,11},{10,... | collective-permute-start | bytes 294920 | tf_op jit(solution)/shard_map/ppermute | solution.py:59
  420.5 18.4 %collective-permute-start.41 = (bf16[2,8,768]{2,1,0:T(8,128)(2,1)S(1)}, bf16[2,8,768]{2,1,0:T(8,128)(2,1)S(1)}, u32[]{:S(2)}, u32[]{:S(2)}) collective-permute-start(bf16[2,8,768]{2,1,0:T(8,128)(2,1)S(1)} %get-tuple-element.177), channel_id=1, source_target_pairs={{0,24},{8,16},{16,8},{24,0},{1,25},{9,17},{17,9},{25,1},{2,26},{10... | collective-permute-start | bytes 73736 | tf_op jit(solution)/shard_map/ppermute | solution.py:59
  470.0 48.3 %all-to-all-start.1 = ((bf16[32,9,8,256]{3,2,1,0:T(8,128)(2,1)}), bf16[32,9,8,256]{3,2,1,0:T(8,128)(2,1)S(1)}, u32[]{:S(2)}, u32[]{:S(2)}) async-start(bf16[32,9,8,256]{3,2,1,0:T(8,128)(2,1)} %pad_maximum_fusion.8), calls=%async_computation.1 | async-start | bytes 2359296 | tf_op jit(solution)/shard_map/all_to_all | solution.py:790
  475.1 25.9 %collective-permute-start.32 = (bf16[16,64,256]{2,1,0:T(8,128)(2,1)S(1)}, bf16[16,64,256]{2,1,0:T(8,128)(2,1)S(1)}, u32[]{:S(2)}, u32[]{:S(2)}) collective-permute-start(bf16[16,64,256]{2,1,0:T(8,128)(2,1)S(1)} %get-tuple-element.130), channel_id=1, source_target_pairs={{0,3},{1,2},{2,1},{3,0},{4,7},{5,6},{6,5},{7,4},{8,11},{9,10},{10,... | collective-permute-start | bytes 1572872 | tf_op jit(solution)/shard_map/ppermute | solution.py:59
  477.8 33.7 %collective-permute-start.31 = (bf16[16,64,256]{2,1,0:T(8,128)(2,1)S(1)}, bf16[16,64,256]{2,1,0:T(8,128)(2,1)S(1)}, u32[]{:S(2)}, u32[]{:S(2)}) collective-permute-start(bf16[16,64,256]{2,1,0:T(8,128)(2,1)S(1)} %get-tuple-element.131), channel_id=1, source_target_pairs={{0,2},{1,3},{2,0},{3,1},{4,6},{5,7},{6,4},{7,5},{8,10},{9,11},{10,... | collective-permute-start | bytes 1572872 | tf_op jit(solution)/shard_map/ppermute | solution.py:59
  478.4 33.3 %collective-permute-start.30 = (bf16[16,64,256]{2,1,0:T(8,128)(2,1)S(1)}, bf16[16,64,256]{2,1,0:T(8,128)(2,1)S(1)}, u32[]{:S(2)}, u32[]{:S(2)}) collective-permute-start(bf16[16,64,256]{2,1,0:T(8,128)(2,1)S(1)} %get-tuple-element.132), channel_id=1, source_target_pairs={{0,1},{1,0},{2,3},{3,2},{4,5},{5,4},{6,7},{7,6},{8,9},{9,8},{10,11... | collective-permute-start | bytes 1572872 | tf_op jit(solution)/shard_map/ppermute | solution.py:59
  (79 other events, 806.3 us)
Sparse Core Ops, SparseCore 0:
  47.1 112.3 all-gather.1

commit v4 on v3

--- a/solution.py
+++ b/solution.py
@@ -59,14 +59,43 @@
     return lax.ppermute(values, axes, [(i, i ^ mask) for i in range(count)])
 
 
-def scatter_axes(values, axes, dim, keep_wide=False):
-    count = lax.axis_size(axes)
+def begin_sum(values, axes, dim):
     mine = lax.axis_index(axes)
-    total = lax.dynamic_index_in_dim(values, mine, dim, keepdims=False).astype(f32)
-    for mask in range(1, count):
+    parts = [lax.dynamic_index_in_dim(values, mine, dim, keepdims=False)]
+    for mask in range(1, lax.axis_size(axes)):
         give = lax.dynamic_index_in_dim(values, mine ^ mask, dim, keepdims=False)
-        total = total + xor_permute(give, axes, mask).astype(f32)
-    return total if keep_wide else total.astype(values.dtype)
+        parts.append(xor_permute(give, axes, mask))
+    return parts
+
+
+def begin_near(values):
+    shape = values.shape
+    values = values.reshape((shape[0], shape[1] // 2, 2) + shape[2:])
+    mine = lax.axis_index("z") % 2
+    keep = lax.dynamic_index_in_dim(values, mine, 2, keepdims=False)
+    give = lax.dynamic_index_in_dim(values, 1 - mine, 2, keepdims=False)
+    return [keep, xor_permute(give, "z", 1)]
+
+
+def begin_far(values):
+    mine = lax.axis_index("z") // 2
+    parts = [lax.dynamic_index_in_dim(values, mine, 1, keepdims=False)]
+    for mask in range(1, values.shape[1]):
+        give = lax.dynamic_index_in_dim(values, mine ^ mask, 1, keepdims=False)
+        parts.append(xor_permute(give, "z", 2 * mask))
+    return parts
+
+
+def end_sum(parts, keep_wide=False):
+    total = parts[0].astype(f32)
+    for part in parts[1:]:
+        total = total + part.astype(f32)
+    return total if keep_wide else total.astype(parts[0].dtype)
+
+
+def hold(values, *sums):
+    tied = lax.optimization_barrier((tuple(values), tuple(parts[0] for parts in sums)))
+    return tied[0] + tuple([keep] + parts[1:] for keep, parts in zip(tied[1], sums))
 
 
 def gather_axes(values, axes):
@@ -105,45 +134,24 @@
     return matrix.astype(bf16).reshape([-1] + sizes + [CH // lax.axis_size(AXES), matrix.shape[-1]])
 
 
-def sum_core(slices):
-    return scatter_axes(slices, "c", 2)
-
-
-def sum_x(slices):
-    return scatter_axes(slices, "x", slices.ndim - 3)
-
-
-def sum_y(slices):
-    return scatter_axes(slices, "y", 2)
-
-
-def sum_z(slices):
-    return scatter_axes(slices, "z", 1, keep_wide=True)
-
-
-def sum_rows(slices):
-    merged = slices.reshape(slices.shape[:2] + (-1,) + slices.shape[-2:])
-    return scatter_axes(merged, ("y", "x"), 2)
-
-
-def split_wide(slices):
-    parts = slices.shape[-1] // D
-    if parts == 1:
-        return slices
-    cutted = slices.reshape(slices.shape[:-1] + (parts, D))
-    cutted = jnp.moveaxis(cutted, -2, 1)
-    return cutted.reshape((-1,) + slices.shape[1:-1] + (D,))
-
-
 tie = lax.optimization_barrier
 
 
-def to_tiles(slices):
+def to_tiles(slices, parts=1):
     blocks, rows, columns = slices.shape
     return (
-        slices.reshape(blocks, rows, columns // CH, CH)
-        .transpose(0, 2, 1, 3)
+        slices.reshape(parts, blocks // parts, rows, columns // CH, CH)
+        .transpose(1, 0, 3, 2, 4)
         .reshape(-1, rows, CH)
+    )
+
+
+def from_tiles(tiles, row_blocks, parts):
+    rows = tiles.shape[1]
+    return (
+        tiles.reshape(row_blocks, parts, D // CH, rows, CH)
+        .transpose(1, 0, 3, 2, 4)
+        .reshape(parts * row_blocks, rows, D)
     )
 
 
@@ -190,7 +198,7 @@
         mixed = jnp.where(mask, part / total, mixed)
         stat = jnp.where(lane == head, peak + jnp.log(total), stat)
     o_ref[...] = mixed.astype(bf16)
-    l_ref[...] = stat
+    l_ref[0] = stat.T[:8]
 
 
 def cross_forward(query, kv):
@@ -206,11 +214,11 @@
         ],
         out_specs=[
             pl.BlockSpec((rows, CH), lambda i: (i, 0)),
-            pl.BlockSpec((rows, 128), lambda i: (i, 0)),
+            pl.BlockSpec((1, 8, rows), lambda i: (i, 0, 0)),
         ],
         out_shape=[
             jax.ShapeDtypeStruct((2 * rows, CH), bf16),
-            jax.ShapeDtypeStruct((2 * rows, 128), f32),
+            jax.ShapeDtypeStruct((2, 8, rows), f32),
         ],
         compiler_params=params(),
         cost_estimate=cost(16 * TH * rows * cells * CH // 2, 8 * cells * CH, 2 * TH * rows * cells),
@@ -281,7 +289,7 @@
             pl.BlockSpec((block, CH), lambda i: (i, 1)),
             pl.BlockSpec((rows, CH), whole),
             pl.BlockSpec((rows, CH), whole),
-            pl.BlockSpec((TH, rows), whole),
+            pl.BlockSpec((8, rows), whole),
         ],
         out_specs=[
             pl.BlockSpec((rows, CH), whole),
@@ -307,47 +315,44 @@
     length = len_ref[0]
     for start, count in ROW_BLOCKS:
         stop = start + count
-        q = q_ref[start:stop, :].astype(f32) * 0.125
+        q = q_ref[0, start:stop, :].astype(f32) * 0.125
         row = lax.broadcasted_iota(jnp.int32, (count, 1), 0) + start
         bound = jnp.minimum(row, length - 1)
         allowed = lax.broadcasted_iota(jnp.int32, (count, stop), 1) <= bound
         mixed = jnp.zeros((count, CH), f32)
-        stat = l_ref[start:stop, :]
+        stat = jnp.zeros((count, 128), f32)
         lane = lax.broadcasted_iota(jnp.int32, (count, 128), 1)
         for head in range(GROUP):
             mask = head_mask((count, CH), head)
             q_head = jnp.where(mask, q, 0.0).astype(bf16)
-            scores = jnp.where(allowed, dot_nt(q_head, k_ref[:stop, :]), neg_large)
+            scores = jnp.where(allowed, dot_nt(q_head, k_ref[0, :stop, :]), neg_large)
             peak = jnp.max(scores, -1, keepdims=True)
             shifted = jnp.exp(scores - peak)
             total = jnp.sum(shifted, -1, keepdims=True)
-            part = dot_nn(shifted.astype(bf16), v_ref[:stop, :])
+            part = dot_nn(shifted.astype(bf16), v_ref[0, :stop, :])
             mixed = jnp.where(mask, part / total, mixed)
-            stat = jnp.where(lane == group * GROUP + head, peak + jnp.log(total), stat)
+            stat = jnp.where(lane == head, peak + jnp.log(total), stat)
         o_ref[start:stop, :] = mixed.astype(bf16)
-        l_ref[start:stop, :] = stat
+        l_ref[0, :, start:stop] = stat.T[:8]
 
 
 def self_forward(qkv, length):
     groups = D // CH
+    at = lambda j: (lambda i, n: (j, 0, i))
     return pl.pallas_call(
         self_forward_kernel,
         grid_spec=pltpu.PrefetchScalarGridSpec(
             num_scalar_prefetch=1,
             grid=(groups,),
-            in_specs=[
-                pl.BlockSpec((SEQ, CH), lambda i, n: (0, i)),
-                pl.BlockSpec((SEQ, CH), lambda i, n: (0, groups + i)),
-                pl.BlockSpec((SEQ, CH), lambda i, n: (0, 2 * groups + i)),
-            ],
+            in_specs=[pl.BlockSpec((1, SEQ, CH), at(j)) for j in range(3)],
             out_specs=[
                 pl.BlockSpec((SEQ, CH), lambda i, n: (0, i)),
-                pl.BlockSpec((SEQ, 128), lambda i, n: (0, 0)),
+                pl.BlockSpec((1, 8, SEQ), lambda i, n: (i, 0, 0)),
             ],
         ),
         out_shape=[
             jax.ShapeDtypeStruct((SEQ, D), bf16),
-            jax.ShapeDtypeStruct((SEQ, 128), f32),
+            jax.ShapeDtypeStruct((groups, 8, SEQ), f32),
         ],
         compiler_params=params(),
         cost_estimate=cost(4 * HEADS * SEQ * SEQ * CH, 8 * SEQ * D, HEADS * SEQ * SEQ),
@@ -363,14 +368,14 @@
     delta = delta_rows(do_ref[...], o_ref[...])
     for start, count in ROW_BLOCKS:
         stop = start + count
-        q = q_ref[start:stop, :].astype(f32) * 0.125
+        q = q_ref[0, start:stop, :].astype(f32) * 0.125
         d_out = do_ref[start:stop, :].astype(f32)
         row = lax.broadcasted_iota(jnp.int32, (1, count), 1) + start
         bound = jnp.minimum(row, length - 1)
         allowed = lax.broadcasted_iota(jnp.int32, (stop, count), 0) <= bound
         dq = jnp.zeros((count, CH), f32)
-        k = k_ref[:stop, :]
-        v = v_ref[:stop, :]
+        k = k_ref[0, :stop, :]
+        v = v_ref[0, :stop, :]
         dk = dk_s[:stop, :]
         dv = dv_s[:stop, :]
         for head in range(GROUP):
@@ -394,19 +399,18 @@
 
 def self_backward(qkv, d_out, out, log_rows, length):
     groups = D // CH
-    at = lambda j: (lambda i, n: (0, j * groups + i))
+    at = lambda j: (lambda i, n: (j, 0, i))
+    here = lambda i, n: (0, i)
     return pl.pallas_call(
         self_backward_kernel,
         grid_spec=pltpu.PrefetchScalarGridSpec(
             num_scalar_prefetch=1,
             grid=(groups,),
-            in_specs=[
-                pl.BlockSpec((SEQ, CH), at(0)),
-                pl.BlockSpec((SEQ, CH), at(1)),
-                pl.BlockSpec((SEQ, CH), at(2)),
-                pl.BlockSpec((SEQ, CH), at(0)),
-                pl.BlockSpec((SEQ, CH), at(0)),
-                pl.BlockSpec((1, GROUP, SEQ), lambda i, n: (i, 0, 0)),
+            in_specs=[pl.BlockSpec((1, SEQ, CH), at(j)) for j in range(3)]
+            + [
+                pl.BlockSpec((SEQ, CH), here),
+                pl.BlockSpec((SEQ, CH), here),
+                pl.BlockSpec((1, 8, SEQ), lambda i, n: (i, 0, 0)),
             ],
             out_specs=pl.BlockSpec((3, SEQ, CH), lambda i, n: (0, 0, i)),
             scratch_shapes=[pltpu.VMEM((SEQ, CH), f32), pltpu.VMEM((SEQ, CH), f32)],
@@ -415,6 +419,343 @@
         compiler_params=params(),
         cost_estimate=cost(8 * HEADS * SEQ * SEQ * CH, 16 * SEQ * D, HEADS * SEQ * SEQ),
     )(length, qkv, qkv, qkv, d_out, out, log_rows)
+
+
+def full(*shape):
+    return pl.BlockSpec(shape, lambda i: (0,) * len(shape))
+
+
+def part_of(first):
+    return pl.BlockSpec((3, CH, D), lambda i: (first + i, 0, 0))
+
+
+def fixed_part(index):
+    return pl.BlockSpec((3, CH, D), lambda i: (index, 0, 0))
+
+
+def square(ref):
+    return ref[...].reshape(D, D)
+
+
+def row_scale(values):
+    return lax.rsqrt(jnp.mean(values * values, -1, keepdims=True) + eps_norm)
+
+
+def pull_norm(d_normed, values, gain):
+    scale = row_scale(values)
+    d_gain = jnp.sum(d_normed * values * scale, 0, keepdims=True)
+    scaled = d_normed * gain
+    inner = jnp.mean(scaled * values, -1, keepdims=True)
+    return d_gain, scale * scaled - (scale * scale * scale) * values * inner
+
+
+def embed_kernel(
+    pool_ref, feats_ref, mixed_ref, out_w_ref, emb_ref, w_ref, gain_ref,
+    seq_ref, embed_ref, normed_ref, qkv_ref,
+):
+    @pl.when(pl.program_id(0) == 0)
+    def _():
+        updated = feats_ref[...].astype(f32) + dot_nn(mixed_ref[...], out_w_ref[...])
+        seq_ref[:CTX, :] = pool_ref[...]
+        seq_ref[CTX:, :] = updated.astype(bf16)
+        embed = dot_nn(seq_ref[...], emb_ref[0])
+        embed_ref[...] = embed
+        normed_ref[...] = (embed * row_scale(embed) * gain_ref[...]).astype(bf16)
+
+    qkv_ref[0] = dot_nn(normed_ref[...], square(w_ref)).astype(bf16)
+
+
+def embed_forward(pooled, feats, mixed, to_out, weights, gain):
+    last = weights.shape[0] - 1
+    return pl.pallas_call(
+        embed_kernel,
+        grid=(3,),
+        in_specs=[
+            full(CTX, CH),
+            full(SEQ - CTX, CH),
+            full(SEQ - CTX, CH),
+            full(CH, CH),
+            pl.BlockSpec((1, CH, D), lambda i: (last, 0, 0)),
+            part_of(0),
+            full(1, D),
+        ],
+        out_specs=[
+            full(SEQ, CH),
+            full(SEQ, D),
+            full(SEQ, D),
+            pl.BlockSpec((1, SEQ, D), lambda i: (i, 0, 0)),
+        ],
+        out_shape=[
+            jax.ShapeDtypeStruct((SEQ, CH), bf16),
+            jax.ShapeDtypeStruct((SEQ, D), f32),
+            jax.ShapeDtypeStruct((SEQ, D), bf16),
+            jax.ShapeDtypeStruct((3, SEQ, D), bf16),
+        ],
+        compiler_params=params(),
+        cost_estimate=cost(2 * SEQ * D * (CH + 3 * D), 12 * SEQ * D),
+    )(pooled, feats, mixed, to_out, weights, weights, gain)
+
+
+def up_kernel(
+    mixed_ref, embed_ref, att_ref, w_ref, gain_ref,
+    stream_ref, normed_ref, act_ref, slope_ref, pre_s,
+):
+    @pl.when(pl.program_id(0) == 0)
+    def _():
+        stream = embed_ref[...] + dot_nn(mixed_ref[...], square(att_ref))
+        stream_ref[...] = stream
+        normed_ref[...] = (stream * row_scale(stream) * gain_ref[...]).astype(bf16)
+
+    pre_s[...] = dot_nn(normed_ref[...], square(w_ref))
+    factor = (2.0 / 3.141592653589793) ** 0.5
+    cubic = 0.044715 * factor
+
+    def rows_step(index, carry):
+        here = pl.ds(pl.multiple_of(index * 16, 16), 16)
+        v = pre_s[here, :]
+        v2 = v * v
+        half = 0.5 + 0.5 * jnp.tanh(v * (factor + cubic * v2))
+        act_ref[0, here, :] = (v * half).astype(bf16)
+        bend = 2.0 * half * (1.0 - half) * (factor + 3.0 * cubic * v2)
+        slope_ref[0, here, :] = (half + v * bend).astype(bf16)
+        return carry
+
+    lax.fori_loop(0, SEQ // 16, rows_step, 0, unroll=2)
+
+
+def up_forward(mixed, embed, weights, gain):
+    return pl.pallas_call(
+        up_kernel,
+        grid=(4,),
+        in_specs=[full(SEQ, D), full(SEQ, D), fixed_part(3), part_of(4), full(1, D)],
+        out_specs=[
+            full(SEQ, D),
+            full(SEQ, D),
+            pl.BlockSpec((1, SEQ, D), lambda i: (i, 0, 0)),
+            pl.BlockSpec((1, SEQ, D), lambda i: (i, 0, 0)),
+        ],
+        out_shape=[
+            jax.ShapeDtypeStruct((SEQ, D), f32),
+            jax.ShapeDtypeStruct((SEQ, D), bf16),
+            jax.ShapeDtypeStruct((4, SEQ, D), bf16),
+            jax.ShapeDtypeStruct((4, SEQ, D), bf16),
+        ],
+        scratch_shapes=[pltpu.VMEM((SEQ, D), f32)],
+        compiler_params=params(),
+        cost_estimate=cost(10 * SEQ * D * D, 28 * SEQ * D, 4 * SEQ * D),
+    )(mixed, embed, weights, weights, gain)
+
+
+def down_kernel(act_ref, w_ref, stream_ref, out_ref):
+    part = dot_nn(act_ref[0], square(w_ref))
+
+    @pl.when(pl.program_id(0) == 0)
+    def _():
+        out_ref[...] = stream_ref[...] + part
+
+    @pl.when(pl.program_id(0) > 0)
+    def _():
+        out_ref[...] += part
+
+
+def down_forward(act, w_down, stream):
+    return pl.pallas_call(
+        down_kernel,
+        grid=(4,),
+        in_specs=[
+            pl.BlockSpec((1, SEQ, D), lambda i: (i, 0, 0)),
+            part_of(0),
+            full(SEQ, D),
+        ],
+        out_specs=full(SEQ, D),
+        out_shape=jax.ShapeDtypeStruct((SEQ, D), f32),
+        compiler_params=params(),
+        cost_estimate=cost(8 * SEQ * D * D, 24 * SEQ * D),
+    )(act, w_down, stream)
+
+
+def down_grad_kernel(act_ref, gd_ref, out_ref):
+    out_ref[...] = dot_tn(act_ref[0], gd_ref[...]).astype(bf16)
+
+
+def down_grad(act, gd):
+    return pl.pallas_call(
+        down_grad_kernel,
+        grid=(4,),
+        in_specs=[pl.BlockSpec((1, SEQ, D), lambda i: (i, 0, 0)), full(SEQ, D)],
+        out_specs=pl.BlockSpec((D, D), lambda i: (i, 0)),
+        out_shape=jax.ShapeDtypeStruct((4 * D, D), bf16),
+        compiler_params=params(),
+        cost_estimate=cost(8 * SEQ * D * D, 18 * SEQ * D),
+    )(act, gd)
+
+
+def up_grad_kernel(gd_ref, w_ref, slope_ref, normed_ref, gpre_ref, out_ref, turned_s):
+    @pl.when(pl.program_id(0) == 0)
+    def _():
+        turned_s[...] = normed_ref[...].T
+
+    gpre = (dot_nt(gd_ref[...], square(w_ref)) * slope_ref[0].astype(f32)).astype(bf16)
+    gpre_ref[0] = gpre
+    out_ref[...] = dot_nn(turned_s[...], gpre).astype(bf16)
+
+
+def up_grad(gd, w_down, slope, normed):
+    part = pl.BlockSpec((1, SEQ, D), lambda i: (i, 0, 0))
+    return pl.pallas_call(
+        up_grad_kernel,
+        grid=(4,),
+        in_specs=[full(SEQ, D), part_of(0), part, full(SEQ, D)],
+        out_specs=[part, pl.BlockSpec((D, D), lambda i: (i, 0))],
+        out_shape=[
+            jax.ShapeDtypeStruct((4, SEQ, D), bf16),
+            jax.ShapeDtypeStruct((4 * D, D), bf16),
+        ],
+        scratch_shapes=[pltpu.VMEM((D, SEQ), bf16)],
+        compiler_params=params(),
+        cost_estimate=cost(16 * SEQ * D * D, 36 * SEQ * D),
+    )(gd, w_down, slope, normed)
+
+
+def att_grad_kernel(
+    gpre_ref, w_ref, att_ref, stream_ref, gd_ref, mixed_ref, gain_ref,
+    d_stream_ref, gog_ref, att_g_ref, gain_g_ref, total_s,
+):
+    step = pl.program_id(0)
+    part = dot_nt(gpre_ref[0], square(w_ref))
+
+    @pl.when(step == 0)
+    def _():
+        total_s[...] = part
+
+    @pl.when(step > 0)
+    def _():
+        total_s[...] += part
+
+    @pl.when(step == pl.num_programs(0) - 1)
+    def _():
+        d_gain, pulled = pull_norm(total_s[...], stream_ref[...], gain_ref[...])
+        gain_g_ref[...] = d_gain
+        d_stream = gd_ref[...].astype(f32) + pulled
+        d_stream_ref[...] = d_stream
+        ga = d_stream.astype(bf16)
+        gog_ref[...] = dot_nt(ga, square(att_ref)).astype(bf16)
+        att_g_ref[...] = dot_tn(mixed_ref[...], ga).astype(bf16)
+
+
+def att_grad(gpre, weights, stream, gd, mixed, gain):
+    return pl.pallas_call(
+        att_grad_kernel,
+        grid=(4,),
+        in_specs=[
+            pl.BlockSpec((1, SEQ, D), lambda i: (i, 0, 0)),
+            part_of(4),
+            fixed_part(3),
+            full(SEQ, D),
+            full(SEQ, D),
+            full(SEQ, D),
+            full(1, D),
+        ],
+        out_specs=[full(SEQ, D), full(SEQ, D), full(D, D), full(1, D)],
+        out_shape=[
+            jax.ShapeDtypeStruct((SEQ, D), f32),
+            jax.ShapeDtypeStruct((SEQ, D), bf16),
+            jax.ShapeDtypeStruct((D, D), bf16),
+            jax.ShapeDtypeStruct((1, D), f32),
+        ],
+        scratch_shapes=[pltpu.VMEM((SEQ, D), f32)],
+        compiler_params=params(),
+        cost_estimate=cost(12 * SEQ * D * D, 32 * SEQ * D),
+    )(gpre, weights, weights, stream, gd, mixed, gain)
+
+
+def qkv_grad_kernel(normed_ref, g_ref, out_ref, turned_s):
+    @pl.when(pl.program_id(0) == 0)
+    def _():
+        turned_s[...] = normed_ref[...].T
+
+    out_ref[...] = dot_nn(turned_s[...], g_ref[0]).astype(bf16)
+
+
+def qkv_grad(normed, gqkv):
+    return pl.pallas_call(
+        qkv_grad_kernel,
+        grid=(3,),
+        in_specs=[full(SEQ, D), pl.BlockSpec((1, SEQ, D), lambda i: (i, 0, 0))],
+        out_specs=pl.BlockSpec((D, D), lambda i: (i, 0)),
+        out_shape=jax.ShapeDtypeStruct((3 * D, D), bf16),
+        scratch_shapes=[pltpu.VMEM((D, SEQ), bf16)],
+        compiler_params=params(),
+        cost_estimate=cost(6 * SEQ * D * D, 14 * SEQ * D),
+    )(normed, gqkv)
+
+
+def embed_grad_kernel(
+    g_ref, w_ref, emb_ref, embed_ref, d_stream_ref, seq_ref, mixed_ref, out_w_ref, gain_ref,
+    emb_g_ref, gupd_ref, pool_g_ref, out_g_ref, gox_ref, gain_g_ref, total_s,
+):
+    step = pl.program_id(0)
+    part = dot_nt(g_ref[0], square(w_ref))
+
+    @pl.when(step == 0)
+    def _():
+        total_s[...] = part
+
+    @pl.when(step > 0)
+    def _():
+        total_s[...] += part
+
+    @pl.when(step == pl.num_programs(0) - 1)
+    def _():
+        d_gain, pulled = pull_norm(total_s[...], embed_ref[...], gain_ref[...])
+        gain_g_ref[...] = d_gain
+        gembed = (d_stream_ref[...] + pulled).astype(bf16)
+        emb_g_ref[...] = dot_tn(seq_ref[...], gembed).astype(bf16)
+        gseq = dot_nt(gembed, emb_ref[0])
+        gupd = gseq[CTX:]
+        gb = gupd.astype(bf16)
+        pool_g_ref[...] = gseq[:CTX].astype(bf16)
+        gupd_ref[...] = gupd
+        out_g_ref[...] = dot_tn(mixed_ref[...], gb).astype(bf16)
+        gox_ref[...] = dot_nt(gb, out_w_ref[...]).astype(bf16)
+
+
+def embed_grad(gqkv, weights, embed, d_stream, seq, mixed, to_out, gain):
+    last = weights.shape[0] - 1
+    return pl.pallas_call(
+        embed_grad_kernel,
+        grid=(3,),
+        in_specs=[
+            pl.BlockSpec((1, SEQ, D), lambda i: (i, 0, 0)),
+            part_of(0),
+            pl.BlockSpec((1, CH, D), lambda i: (last, 0, 0)),
+            full(SEQ, D),
+            full(SEQ, D),
+            full(SEQ, CH),
+            full(SEQ - CTX, CH),
+            full(CH, CH),
+            full(1, D),
+        ],
+        out_specs=[
+            full(CH, D),
+            full(SEQ - CTX, CH),
+            full(CTX, CH),
+            full(CH, CH),
+            full(SEQ - CTX, CH),
+            full(1, D),
+        ],
+        out_shape=[
+            jax.ShapeDtypeStruct((CH, D), bf16),
+            jax.ShapeDtypeStruct((SEQ - CTX, CH), f32),
+            jax.ShapeDtypeStruct((CTX, CH), bf16),
+            jax.ShapeDtypeStruct((CH, CH), bf16),
+            jax.ShapeDtypeStruct((SEQ - CTX, CH), bf16),
+            jax.ShapeDtypeStruct((1, D), f32),
+        ],
+        scratch_shapes=[pltpu.VMEM((SEQ, D), f32)],
+        compiler_params=params(),
+        cost_estimate=cost(2 * SEQ * D * (3 * D + 2 * CH), 24 * SEQ * D),
+    )(gqkv, weights, weights, embed, d_stream, seq, mixed, to_out, gain)
 
 
 def patch_pick(rows, columns, patch_dim):
@@ -587,28 +928,6 @@
         compiler_params=params(),
         cost_estimate=cost(18 * CELLS * CH * CH, 8 * CELLS * CH),
     )(gz, d_hidden, conv_tiles)
-
-
-def dot(a, b):
-    return jnp.dot(a, b, preferred_element_type=f32)
-
-
-def gelu_slope(v):
-    inner = jnp.sqrt(2.0 / jnp.pi) * (v + 0.044715 * v * v * v)
-    bend = jnp.tanh(inner)
-    d_inner = jnp.sqrt(2.0 / jnp.pi) * (1.0 + 3.0 * 0.044715 * v * v)
-    return 0.5 * (1.0 + bend) + 0.5 * v * (1.0 - bend * bend) * d_inner
-
-
-def inverse_rms(values):
-    return lax.rsqrt(jnp.mean(values * values, -1, keepdims=True) + eps_norm)
-
-
-def norm_backward(d_normed, values, scale, gain):
-    d_gain = jnp.sum(d_normed * values * scale, 0)
-    scaled = d_normed * gain
-    inner = jnp.mean(scaled * values, -1, keepdims=True)
-    return d_gain, scale * scaled - (scale * scale * scale) * values * inner
 
 
 def local(
@@ -630,6 +949,9 @@
     slot_of = slot_index(tile_owner, slot_count)
 
     image = trade_rows(context_map).reshape(IMG, IMG, CH)
+    length = CTX + FT * horizon
+    valid = jnp.arange(SEQ) < length[0]
+    gd = jnp.where(valid[:, None], cotangent[0], jnp.zeros((), bf16))
 
     slices = (
         master_tiles.astype(bf16)
@@ -639,15 +961,19 @@
     slices = lax.all_to_all(slices, AXES, split_axis=0, concat_axis=0, tiled=True)
     slices = slices.reshape(devices * slot_count, rows, CH)
     slices = slices.at[slot_of].get(mode="promise_in_bounds")
-    early = gather_all(slices[:EARLY]).transpose(1, 0, 2, 3).reshape(EARLY, CH, CH)
-    later = slices[EARLY:].reshape(-1, D // CH, rows, CH).transpose(0, 2, 1, 3)
-    later = lax.all_gather(later.reshape(-1, D), AXES, axis=0, tiled=True)
-    later = later.reshape(devices, -1, rows, D)
-
-    def matrix(start, row_blocks, parts):
-        part = later[:, start : start + row_blocks * parts]
-        part = part.reshape(devices, row_blocks, parts, rows, D)
-        return part.transpose(1, 0, 3, 2, 4).reshape(row_blocks * CH, parts * D)
+    early, emb, qkv, att, up, down = jnp.split(slices, (13, 16, 43, 52, 88))
+    weights = jnp.concatenate(
+        [
+            from_tiles(qkv, 3, 3),
+            from_tiles(att, 3, 1),
+            from_tiles(up, 3, 4),
+            from_tiles(emb, 1, 1),
+        ],
+        0,
+    )
+    weights = lax.all_gather(weights, AXES, axis=1, tiled=True)
+    w_down = lax.all_gather(from_tiles(down, 12, 1), AXES, axis=1, tiled=True)
+    early = gather_all(early).transpose(1, 0, 2, 3).reshape(EARLY, CH, CH)
 
     padded = jnp.pad(image, ((1, 1), (1, 1), (0, 0)))
     wide = jnp.concatenate([padded[:, col : col + IMG] for col in range(3)], -1)
@@ -656,125 +982,110 @@
     conv_tiles = early[:9]
     to_query, to_out = early[9], early[12]
     kv_weight = jnp.concatenate([early[10], early[11]], 1)
-    w_emb = matrix(0, 1, 1)
-    w_qkv = matrix(1, 3, 3)
-    w_att = matrix(10, 3, 1)
-    w_up = matrix(13, 3, 4)
-    w_down = matrix(25, 12, 1)
-
-    slope, hidden_b, kv, pooled = token_forward(wide, conv_tiles.reshape(3, 3 * CH, CH), kv_weight)
+
+    slope_z, hidden_b, kv, pooled = token_forward(
+        wide, conv_tiles.reshape(3, 3 * CH, CH), kv_weight
+    )
     feats_b = future_feats[0]
-    length = CTX + FT * horizon
-    query = dot(feats_b, to_query).astype(bf16)
+    query = jnp.dot(feats_b, to_query, preferred_element_type=f32).astype(bf16)
     cross_mixed, cross_logs = cross_forward(query, kv)
-    updated = feats_b.astype(f32) + dot(cross_mixed, to_out)
-    seq = jnp.concatenate([pooled, updated.astype(bf16)], 0)
-
-    gain_one, gain_two = norm_gains[0], norm_gains[1]
-    embed = dot(seq, w_emb)
-    scale_one = inverse_rms(embed)
-    normed_one = (embed * scale_one * gain_one).astype(bf16)
-    qkv = dot(normed_one, w_qkv).astype(bf16)
+
+    gain_one, gain_two = norm_gains[:1], norm_gains[1:]
+    seq, embed, normed_one, qkv = embed_forward(
+        pooled, feats_b, cross_mixed, to_out, weights, gain_one
+    )
     mixed, logs = self_forward(qkv, length)
-    stream = embed + dot(mixed, w_att)
-    scale_two = inverse_rms(stream)
-    normed_two = (stream * scale_two * gain_two).astype(bf16)
-    pre = dot(normed_two, w_up)
-    act = jax.nn.gelu(pre, approximate=True).astype(bf16)
-    block_out = stream + dot(act, w_down)
-
-    valid = jnp.arange(SEQ) < length[0]
-    gd = jnp.where(valid[:, None], cotangent[0], jnp.zeros((), bf16))
-    sum_down = cut(dot(act.T, gd))
+    stream, normed_two, act, slope = up_forward(mixed, embed, weights, gain_two)
+
+    sum_down = cut(down_grad(act, gd))
     gd, sum_down = tie((gd, sum_down))
-    gpre = (dot(gd, w_down.T) * gelu_slope(pre)).astype(bf16)
-    sum_down = sum_core(sum_down)
-    sum_up = cut(dot(normed_two.T, gpre))
-    gpre, sum_up, sum_down = tie((gpre, sum_up, sum_down))
-    d_gain_two, d_stream = norm_backward(dot(gpre, w_up.T), stream, scale_two, gain_two)
-    d_stream = gd.astype(f32) + d_stream
-    ga = d_stream.astype(bf16)
-    sum_up = split_wide(sum_core(sum_up))
-    sum_down = sum_x(sum_down)
-    ga, sum_up = tie((ga, sum_up))
-    sum_up = sum_y(sum_up)
-    sum_att = cut(dot(mixed.T, ga))
-    gog = dot(ga, w_att.T).astype(bf16)
-    log_rows = logs[:, :HEADS].T.reshape(D // CH, GROUP, SEQ)
-    gqkv = self_backward(qkv, gog, mixed, log_rows, length)
-    gqkv, sum_down, sum_up, sum_att = tie((gqkv, sum_down, sum_up, sum_att))
-    sum_down = sum_y(sum_down)
-    sum_up = sum_x(sum_up)
-    sum_att = sum_core(sum_att)
-    gqkv = jnp.concatenate([gqkv[0], gqkv[1], gqkv[2]], 1)
-    sum_qkv = cut(dot(normed_one.T, gqkv))
-    gqkv, sum_qkv = tie((gqkv, sum_qkv))
-    sum_qkv = split_wide(sum_core(sum_qkv))
-    d_gain_one, d_embed = norm_backward(dot(gqkv, w_qkv.T), embed, scale_one, gain_one)
-    gembed = (d_stream + d_embed).astype(bf16)
-    sum_emb = cut(dot(seq.T, gembed))
-    gains = jnp.stack([d_gain_one, d_gain_two]).reshape(devices, 1, -1)
+    wait_down = begin_sum(sum_down, "c", 2)
+    gpre, sum_up = up_grad(gd, w_down, slope, normed_two)
+    gpre, sum_up, wait_down = hold((gpre, cut(sum_up)), wait_down)
+    wait_up = begin_sum(sum_up, "c", 2)
+    wait_down = begin_sum(end_sum(wait_down), "x", 3)
+    d_stream, gog, sum_att, gain_g_two = att_grad(gpre, weights, stream, gd, mixed, gain_two)
+    gog, sum_att, wait_up = hold((gog, cut(sum_att)), wait_up)
+    wait_up = begin_sum(end_sum(wait_up), "y", 2)
+    wait_att = begin_sum(sum_att, "c", 2)
+    gqkv = self_backward(qkv, gog, mixed, logs, length)
+    gqkv, wait_down, wait_up, wait_att = hold((gqkv,), wait_down, wait_up, wait_att)
+    wait_down = begin_sum(end_sum(wait_down), "y", 2)
+    wait_up = begin_sum(end_sum(wait_up), "x", 2)
+    sum_att = end_sum(wait_att)
+    sum_qkv = cut(qkv_grad(normed_one, gqkv))
+    gqkv, sum_qkv, sum_att = tie((gqkv, sum_qkv, sum_att))
+    wait_qkv = begin_sum(sum_qkv, "c", 2)
+    emb_g, gupd, pool_g, out_g, gox, gain_g_one = embed_grad(
+        gqkv, weights, embed, d_stream, seq, cross_mixed, to_out, gain_one
+    )
+    gains = jnp.concatenate([gain_g_one, gain_g_two], 0).reshape(devices, 1, -1)
     gain_count = gains.shape[-1]
     gains = jnp.pad(gains, ((0, 0), (0, rows - 1), (0, D - gain_count))).astype(bf16)
-    sum_emb = jnp.concatenate([sum_emb, gains.reshape((1,) + sum_emb.shape[1:])], 0)
-    gseq = dot(gembed, w_emb.T)
-    gseq, sum_emb, sum_qkv, sum_down, sum_up, sum_att = tie(
-        (gseq, sum_emb, sum_qkv, sum_down, sum_up, sum_att)
-    )
-    sum_mlp = jnp.concatenate([sum_up, sum_down], 0)
-    half = sum_qkv.shape[0] * 2 // 3
-    first = sum_qkv[:half]
-    second = jnp.concatenate([sum_qkv[half:], sum_att], 0)
-
-    gupd = gseq[CTX:]
-    gb = gupd.astype(bf16)
-    grad_out = dot(cross_mixed.T, gb)
-    gox = dot(gb, to_out.T).astype(bf16)
-    gq, gkv = cross_backward(query, kv, gox, cross_mixed, cross_logs[:, :TH].T)
-    first = sum_x(first)
-    second = sum_y(second)
-    sum_mlp = sum_z(sum_mlp)
-    sum_emb = sum_core(sum_emb)
-    gkv, first, second, sum_mlp, sum_emb = tie((gkv, first, second, sum_mlp, sum_emb))
-    grad_query = dot(feats_b.T, gq)
-
-    d_hidden, gz, grad_conv, grad_kv = token_backward(
-        gkv, slope, gseq[:CTX].astype(bf16), hidden_b, wide, kv_weight
-    )
-    first = sum_y(first)
-    second = sum_x(second)
-    sum_emb = sum_rows(sum_emb)
-    sum_early = jnp.concatenate(
+    sum_emb = cut(jnp.concatenate([emb_g, gains.reshape(CH, D)], 0))
+    gox, gupd, sum_emb, wait_qkv, wait_down, wait_up = hold(
+        (gox, gupd, sum_emb), wait_qkv, wait_down, wait_up
+    )
+    wait_mlp = begin_near(jnp.concatenate([end_sum(wait_up), end_sum(wait_down)], 0))
+    sum_qkv = end_sum(wait_qkv)
+    wait_first = begin_sum(sum_qkv[:6], "x", 3)
+    wait_second = begin_sum(jnp.concatenate([sum_qkv[6:], sum_att], 0), "y", 2)
+    wait_emb = begin_sum(sum_emb, "c", 2)
+
+    log_rows = jnp.concatenate([cross_logs[0], cross_logs[1]], 1)
+    gq, gkv = cross_backward(query, kv, gox, cross_mixed, log_rows)
+    gq, gkv, wait_first, wait_second, wait_mlp, wait_emb = hold(
+        (gq, gkv), wait_first, wait_second, wait_mlp, wait_emb
+    )
+    wait_first = begin_sum(end_sum(wait_first), "y", 2)
+    wait_second = begin_sum(end_sum(wait_second), "x", 2)
+    wait_mlp = begin_far(end_sum(wait_mlp))
+    wait_emb = begin_sum(end_sum(wait_emb), "x", 3)
+
+    d_hidden, gz, conv_g, kv_g = token_backward(gkv, slope_z, pool_g, hidden_b, wide, kv_weight)
+    query_g = jnp.dot(feats_b.T, gq, preferred_element_type=f32).astype(bf16)
+    sum_early = cut(
+        jnp.concatenate([conv_g, query_g[None], kv_g, out_g[None]], 0).reshape(EARLY * CH, CH)
+    )
+    d_hidden, gz, sum_early, wait_first, wait_second, wait_mlp, wait_emb = hold(
+        (d_hidden, gz, sum_early), wait_first, wait_second, wait_mlp, wait_emb
+    )
+    sum_early = end_sum(begin_sum(sum_early, "c", 2))
+    wait_att = begin_near(jnp.concatenate([end_sum(wait_first), end_sum(wait_second)], 0))
+    wait_emb = begin_sum(end_sum(wait_emb), "y", 2)
+    sum_mlp = end_sum(wait_mlp, keep_wide=True)
+    gz, sum_early = tie((gz, sum_early))
+    wait_early = begin_sum(
+        sum_early.reshape(sum_early.shape[:2] + (-1,) + sum_early.shape[-2:]), ("y", "x"), 2
+    )
+    context_grad = context_backward(gz, d_hidden, conv_tiles)
+    context_grad, wait_early, wait_att, wait_emb = hold(
+        (context_grad,), wait_early, wait_att, wait_emb
+    )
+    wait_early = begin_sum(end_sum(wait_early), "z", 1)
+    wait_att = begin_far(end_sum(wait_att))
+    wait_emb = begin_sum(end_sum(wait_emb), "z", 1)
+    sum_early = end_sum(wait_early, keep_wide=True)
+    sum_att = end_sum(wait_att, keep_wide=True)
+    sum_emb = end_sum(wait_emb, keep_wide=True)
+    context_rows = trade_rows(context_grad.reshape(context_map.shape))
+    future_grad = gupd + lax.dot_general(
+        gq, to_query, (((1,), (1,)), ((), ())), preferred_element_type=f32
+    )
+
+    sums = jnp.concatenate(
         [
-            grad_conv,
-            grad_query.astype(bf16)[None],
-            grad_kv,
-            grad_out.astype(bf16)[None],
+            to_tiles(sum_early),
+            to_tiles(sum_emb[:1]),
+            to_tiles(sum_att[:9], 3),
+            to_tiles(sum_att[9:]),
+            to_tiles(sum_mlp[:12], 4),
+            to_tiles(sum_mlp[12:]),
         ],
         0,
     )
-    sum_early = cut(sum_early.reshape(EARLY * CH, CH))
-    own_core = lax.axis_index("c")
-    keep = lax.dynamic_index_in_dim(sum_early, own_core, 2, keepdims=False)
-    give = lax.dynamic_index_in_dim(sum_early, own_core ^ 1, 2, keepdims=False)
-    d_hidden, gz, keep, give, first, second, sum_emb = tie(
-        (d_hidden, gz, keep, give, first, second, sum_emb)
-    )
-    sum_early = (keep.astype(f32) + xor_permute(give, "c", 1).astype(f32)).astype(bf16)
-    context_grad = context_backward(gz, d_hidden, conv_tiles)
-    context_grad, sum_early = tie((context_grad, sum_early))
-    sum_att = sum_z(jnp.concatenate([first, second], 0))
-    sum_emb = sum_z(sum_emb)
-    sum_early = sum_rows(sum_early)
-    sum_early = sum_z(sum_early)
-    context_rows = trade_rows(context_grad.reshape(context_map.shape))
-    future_grad = gupd + dot(gq, to_query.T)
-
-    sums = [sum_early, sum_emb[:1], sum_att, sum_mlp]
-    sums = jnp.concatenate([to_tiles(part) for part in sums], 0)
     gains = sum_emb[1, 0, :gain_count]
-    square = jnp.sum(sums * sums) + jnp.sum(gains * gains)
-    share = jnp.concatenate([square[None], gains])
+    share = jnp.concatenate([(jnp.sum(sums * sums) + jnp.sum(gains * gains))[None], gains])
     share_high = share.astype(bf16)
     share_low = (share - share_high.astype(f32)).astype(bf16)
     share = jnp.pad(
@@ -788,6 +1099,7 @@
     share = jnp.broadcast_to(share[None, None], (devices, 1, rows, CH))
     mine = jnp.concatenate([mine, share], 1)
     mine = lax.all_to_all(mine, AXES, split_axis=0, concat_axis=0, tiled=True)
+    block_out = down_forward(act, w_down, stream)
     shares = mine[:, slot_count, :2].astype(f32)
     shares = shares[:, 0] + shares[:, 1]
     gains = shares[:, 1 : 1 + gain_count].reshape(2, D)

time: 546 us -> 507 us (0.929); the launches traced: 536 us -> 502 us
  Pallas kernels: 121 us -> 205 us
  matrix products: 79.2 us -> 4.74 us
  waiting for transfers between devices: 150 us -> 121 us
  local copies, waits for them, and re-layouts: 60.5 us -> 45.2 us
    pallas_call x0 -> x8, Pallas kernels: none -> 84.5 us  [the longest x1 16.5 us: up_forward(): pl.pallas_call(up_kernel, grid=(4,), in_specs=[full(SEQ, D), full(SEQ, D)...]
    dot_general x21 -> x3, matrix products: 79.2 us -> 4.74 us  [the longest x1 1.95 us: local(): lax.dot_general(gq, to_query, (((1,), (1,)), ((), ())), preferred_element...]
    ppermute x45 -> x42, waiting for transfers between devices: 104 us -> 71.7 us  [xor_permute(): return lax.ppermute(values, axes, [(i, i ^ mask) for i in range(count)])]
    squeeze x22 -> x19, local copies, waits for them, and re-layouts: 7.2 us -> 18.4 us  [the longest x13 16 us: begin_sum(): give = lax.dynamic_index_in_dim(values, mine ^ mask, dim, keepdims=False)]
    slice x6 -> x7, local copies, waits for them, and re-layouts: 11.3 us -> 0.79 us  [the longest x1 0.59 us: local(): gain_one, gain_two = (norm_gains[:1], norm_gains[1:])]
    unnamed x116 -> x55, local copies, waits for them, and re-layouts: 11.5 us -> 1.92 us
    reshape x4 -> x6, local copies, waits for them, and re-layouts: 6.09 us -> 0.41 us  [the longest x2 0.28 us: to_tiles(): slices.reshape(parts, blocks // parts, rows, columns // CH, CH)]
    all_gather x1 -> x2, waiting for transfers between devices: 19.9 us -> 22.8 us  [the longest x1 15.8 us: local(): w_down = lax.all_gather(from_tiles(down, 12, 1), AXES, axis=1, tiled=True)]
  transfers between devices with their start and end apart: 48 -> 46, of which waited for: 22 -> 23; matrix products, arithmetic and copies ran while one was open for 18% -> 16% of each run, Pallas kernels for 15% -> 41%
where the time goes in v4:
time: 507 us; the launch traced here: 502 us
  Pallas kernels  205 us (40%)
  waiting for transfers between devices  121 us (24%)
  starting transfers between devices  56.3 us (11%)
  other arithmetic  50.4 us (10%)
  local copies, waits for them, and re-layouts  45.2 us (9%)
  between operations  19.2 us (4%)
    ppermute x42, waiting for transfers between devices, xor_permute(): return lax.ppermute(values, axes, [(i, i ^ mask) for i in range(count)])  71.7 us
    ppermute x42, starting transfers between devices, xor_permute(): return lax.ppermute(values, axes, [(i, i ^ mask) for i in range(count)])  45.6 us
    pallas_call x1, Pallas kernels, cross_backward(): pl.pallas_call(cross_backward_kernel, grid=(cells // block,), in_specs=[p...  27.8 us
    all_to_all x1, waiting for transfers between devices, local(): lax.all_to_all(slices, AXES, split_axis=0, concat_axis=0, tiled=True)  26.1 us
    pallas_call x1, Pallas kernels, self_backward(): pl.pallas_call(self_backward_kernel, grid_spec=pltpu.PrefetchScalarGridSp...  19.2 us
    convert_element_type x19, other arithmetic, end_sum(): return total if keep_wide else total.astype(parts[0].dtype)  18.3 us
    pallas_call x1, Pallas kernels, cross_forward(): pl.pallas_call(cross_forward_kernel, grid=(2,), in_specs=[pl.BlockSpec((r...  16.7 us
    pallas_call x1, Pallas kernels, token_backward(): pl.pallas_call(token_backward_kernel, grid=(steps,), in_specs=[pl.BlockSp...  16.7 us
  transfers between devices with their start and end apart: 46, of which 23 were waited for; matrix products, arithmetic and copies ran while one was open for 16% of the time, Pallas kernels for 41%

profile of v4, /device:TPU:0, one launch (start us, length us, event | category | flops | bytes accessed | tf_op | source)
XLA Modules:
  0.0 502.4 jit_solution(12198631001232840230)
XLA Ops:
  10.0 7.3 %all-to-all-start = ((bf16[32,8,8,256]{3,2,1,0:T(8,128)(2,1)}), bf16[32,8,8,256]{3,2,1,0:T(8,128)(2,1)S(1)}, u32[]{:S(2)}, u32[]{:S(2)}) async-start(bf16[32,8,8,256]{3,2,1,0:T(8,128)(2,1)} %copy.122), calls=%async_computation | async-start | bytes 2097152 | tf_op jit(solution)/shard_map/all_to_all | solution.py:961
  17.6 26.1 %all-to-all-done = bf16[32,8,8,256]{3,2,1,0:T(8,128)(2,1)S(1)} async-done(((bf16[32,8,8,256]{3,2,1,0:T(8,128)(2,1)}), bf16[32,8,8,256]{3,2,1,0:T(8,128)(2,1)S(1)}, u32[]{:S(2)}, u32[]{:S(2)}) %all-to-all-start) | async-done | bytes 1048608 | tf_op jit(solution)/shard_map/all_to_all | solution.py:961
  106.8 15.8 %shard_map.186 = (bf16[4096,256]{1,0:T(8,128)(2,1)}, bf16[4096,256]{1,0:T(8,128)(2,1)}, bf16[4096,512]{1,0:T(8,128)(2,1)}, bf16[256,256]{1,0:T(8,128)(2,1)}) custom-call(bf16[4224,768]{1,0:T(8,128)(2,1)} %bitcast.295, bf16[3,768,256]{2,1,0:T(8,128)(2,1)} %bitcast.314, bf16[256,512]{1,0:T(8,128)(2,1)} %pad_maximum_fusion.11.kv_w_ref), custom_call_target="tpu_custom_call" | custom-call | flops 5905580032 | bytes 14680064 | tf_op jit(solution)/shard_map/pallas_call | solution.py:793
  122.5 16.7 %shard_map.187 = (bf16[480,256]{1,0:T(8,128)(2,1)}, f32[2,8,240]{2,1,0:T(8,128)}) custom-call(bf16[480,256]{1,0:T(8,128)(2,1)} %fusion.4.q_ref, bf16[4096,512]{1,0:T(8,128)(2,1)} %get-tuple-element.85.k_ref.v_ref, bf16[4096,512]{1,0:T(8,128)(2,1)} %get-tuple-element.85.k_ref.v_ref), custom_call_target="tpu_custom_call" | custom-call | flops 8053063680 | bytes 8388608 | tf_op jit(solution)/shard_map/pallas_call | solution.py:207
  140.0 7.0 %all-gather.3.cloned.1.call-done.emb_ref.w_ref.att_ref = bf16[25,256,768]{2,1,0:T(8,128)(2,1)} async-done(((bf16[25,8,768]{2,1,0:T(8,128)(2,1)}), bf16[25,256,768]{2,1,0:T(8,128)(2,1)}) %all-gather.3.cloned.1.call-update) | async-done | bytes 9830416 | tf_op jit(solution)/shard_map/all_gather | solution.py:974
  147.0 7.4 %shard_map.188 = (bf16[736,256]{1,0:T(8,128)(2,1)}, f32[736,768]{1,0:T(8,128)}, bf16[736,768]{1,0:T(8,128)(2,1)}, bf16[3,736,768]{2,1,0:T(8,128)(2,1)}) custom-call(bf16[256,256]{1,0:T(8,128)(2,1)} %get-tuple-element.84.pool_ref, bf16[480,256]{1,0:T(8,128)(2,1)} %bitcast.311, bf16[480,256]{1,0:T(8,128)(2,1)} %get-tuple-element.86.mixed_ref.o_ref, ...), custom_call_target="tpu_custom_call" | custom-call | flops 2894069760 | bytes 6782976 | tf_op jit(solution)/shard_map/pallas_call | solution.py:470
  154.4 13.3 %shard_map.189 = (bf16[736,768]{1,0:T(8,128)(2,1)}, f32[3,8,736]{2,1,0:T(8,128)}) custom-call(s32[1]{0:T(128)} %add.388.len_ref, bf16[3,736,768]{2,1,0:T(8,128)(2,1)} %get-tuple-element.87.q_ref.k_ref.v_ref, bf16[3,736,768]{2,1,0:T(8,128)(2,1)} %get-tuple-element.87.q_ref.k_ref.v_ref, bf16[3,736,768]{2,1,0:T(8,128)(2,1)} %get-tuple-element.87.q_ref.k_ref.v_ref), custom_call_target="tpu_custom_call" | custom-call | flops 6656360448 | bytes 4521984 | tf_op jit(solution)/shard_map/pallas_call | solution.py:342
  167.7 16.5 %shard_map.190 = (f32[736,768]{1,0:T(8,128)}, bf16[736,768]{1,0:T(8,128)(2,1)}, bf16[4,736,768]{2,1,0:T(8,128)(2,1)}, bf16[4,736,768]{2,1,0:T(8,128)(2,1)}) custom-call(bf16[736,768]{1,0:T(8,128)(2,1)} %get-tuple-element.88.mixed_ref.o_ref, f32[736,768]{1,0:T(8,128)} %get-tuple-element.89.embed_ref, ...), custom_call_target="tpu_custom_call" | custom-call | flops 4341104640 | bytes 15826944 | tf_op jit(solution)/shard_map/pallas_call | solution.py:527
  184.2 7.8 %shard_map.192 = bf16[3072,768]{1,0:T(8,128)(2,1)} custom-call(bf16[4,736,768]{2,1,0:T(8,128)(2,1)} %get-tuple-element.90.act_ref, bf16[736,768]{1,0:T(8,128)(2,1)} %bitcast_select_fusion.gd_ref), custom_call_target="tpu_custom_call" | custom-call | flops 3472883712 | bytes 10174464 | tf_op jit(solution)/shard_map/pallas_call | solution.py:582
  196.7 15.8 %all-gather.5.cloned.1.call-done.w_ref = bf16[12,256,768]{2,1,0:T(8,128)(2,1)} async-done(((bf16[12,8,768]{2,1,0:T(8,128)(2,1)}), bf16[12,256,768]{2,1,0:T(8,128)(2,1)}) %all-gather.5.cloned.1.call-update) | async-done | bytes 4718608 | tf_op jit(solution)/shard_map/all_gather | solution.py:975
  212.5 11.7 %shard_map.193 = (bf16[4,736,768]{2,1,0:T(8,128)(2,1)}, bf16[3072,768]{1,0:T(8,128)(2,1)}) custom-call(bf16[736,768]{1,0:T(8,128)(2,1)} %bitcast_select_fusion.gd_ref, bf16[12,256,768]{2,1,0:T(8,128)(2,1)} %all-gather.5.cloned.1.call-done.w_ref, bf16[4,736,768]{2,1,0:T(8,128)(2,1)} %get-tuple-element.93.slope_ref, bf16[736,768]{1,0:T(8,128)(2,1)} %get-tuple-element.94.normed_ref), custom_call_target="tpu_custom_call" | custom-call | flops 6945767424 | bytes 20348928 | tf_op jit(solution)/shard_map/pallas_call | solution.py:605
  228.2 14.1 %shard_map.194 = (f32[736,768]{1,0:T(8,128)}, bf16[736,768]{1,0:T(8,128)(2,1)}, bf16[768,768]{1,0:T(8,128)(2,1)}, f32[1,768]{1,0:T(1,128)}) custom-call(bf16[4,736,768]{2,1,0:T(8,128)(2,1)} %get-tuple-element.98.gpre_ref, bf16[25,256,768]{2,1,0:T(8,128)(2,1)} %all-gather.3.cloned.1.call-done.emb_ref.w_ref.att_ref, ...), custom_call_target="tpu_custom_call" | custom-call | flops 5209325568 | bytes 18087936 | tf_op jit(solution)/shard_map/pallas_call | solution.py:647
  243.9 19.2 %shard_map.195.g_ref = bf16[3,736,768]{2,1,0:T(8,128)(2,1)} custom-call(s32[1]{0:T(128)} %add.388.len_ref, bf16[3,736,768]{2,1,0:T(8,128)(2,1)} %get-tuple-element.87.q_ref.k_ref.v_ref, bf16[3,736,768]{2,1,0:T(8,128)(2,1)} %get-tuple-element.87.q_ref.k_ref.v_ref, bf16[3,736,768]{2,1,0:T(8,128)(2,1)} %get-tuple-element.87.q_ref.k_ref.v_ref, ...), custom_call_target="tpu_custom_call" | custom-call | flops 13312720896 | bytes 9043968 | tf_op jit(solution)/shard_map/pallas_call | solution.py:404
  271.6 7.1 %shard_map.196 = bf16[2304,768]{1,0:T(8,128)(2,1)} custom-call(bf16[736,768]{1,0:T(8,128)(2,1)} %get-tuple-element.108.normed_ref, bf16[3,736,768]{2,1,0:T(8,128)(2,1)} %shard_map.195.g_ref), custom_call_target="tpu_custom_call" | custom-call | flops 2604662784 | bytes 7913472 | tf_op jit(solution)/shard_map/pallas_call | solution.py:681
  282.4 10.7 %shard_map.197 = (bf16[256,768]{1,0:T(8,128)(2,1)}, f32[480,256]{1,0:T(8,128)}, bf16[256,256]{1,0:T(8,128)(2,1)}, bf16[256,256]{1,0:T(8,128)(2,1)}, bf16[480,256]{1,0:T(8,128)(2,1)}, /*index=5*/f32[1,768]{1,0:T(1,128)}) custom-call(bf16[3,736,768]{2,1,0:T(8,128)(2,1)} %shard_map.195.g_ref, ...), custom_call_target="tpu_custom_call" | custom-call | flops 3183476736 | bytes 13565952 | tf_op jit(solution)/shard_map/pallas_call | solution.py:725
  300.4 8.9 %collective-permute-done.14 = bf16[12,4,2,8,768]{4,3,1,0,2:T(8,128)(2,1)} collective-permute-done((bf16[12,4,2,8,768]{4,3,1,0,2:T(8,128)(2,1)}, bf16[12,4,2,8,768]{4,3,1,0,2:T(8,128)(2,1)}, u32[]{:S(2)}, u32[]{:S(2)}) %collective-permute-start.14) | collective-permute-done | bytes 1179680 | tf_op jit(solution)/shard_map/ppermute | solution.py:59
  314.7 27.8 %shard_map.198 = (bf16[480,256]{1,0:T(8,128)(2,1)}, bf16[4096,512]{1,0:T(8,128)(2,1)}) custom-call(bf16[480,256]{1,0:T(8,128)(2,1)} %fusion.4.q_ref, bf16[4096,512]{1,0:T(8,128)(2,1)} %get-tuple-element.85.k_ref.v_ref, bf16[4096,512]{1,0:T(8,128)(2,1)} %get-tuple-element.85.k_ref.v_ref, bf16[480,256]{1,0:T(8,128)(2,1)} %get-tuple-element.121.do_ref, ...), custom_call_target="tpu_custom_call" | custom-call | flops 20132659200 | bytes 8388608 | tf_op jit(solution)/shard_map/pallas_call | solution.py:283
  351.5 16.7 %shard_map.199 = (f32[4096,256]{1,0:T(8,128)}, bf16[4096,256]{1,0:T(8,128)(2,1)}, bf16[9,256,256]{2,1,0:T(8,128)(2,1)}, bf16[2,256,256]{2,1,0:T(8,128)(2,1)}) custom-call(bf16[4096,512]{1,0:T(8,128)(2,1)} %get-tuple-element.130.dkv_ref, bf16[4096,256]{1,0:T(8,128)(2,1)} %get-tuple-element.131.slope_ref, bf16[256,256]{1,0:T(8,128)(2,1)} %get-tuple-element.132.pool_ref, ...), custom_call_target="tpu_custom_call" | custom-call | flops 6979321856 | bytes 20971520 | tf_op jit(solution)/shard_map/pallas_call | solution.py:854
  385.6 6.9 %collective-permute-done.41 = bf16[24,8,768]{2,1,0:T(8,128)(2,1)S(1)} collective-permute-done((bf16[24,8,768]{2,1,0:T(8,128)(2,1)S(1)}, bf16[24,8,768]{2,1,0:T(8,128)(2,1)S(1)}, u32[]{:S(2)}, u32[]{:S(2)}) %collective-permute-start.41) | collective-permute-done | bytes 294944 | tf_op jit(solution)/shard_map/ppermute | solution.py:59
  394.4 11.1 %shard_map.200 = bf16[4096,256]{1,0:T(8,128)(2,1)} custom-call(bf16[4096,256]{1,0:T(8,128)(2,1)} %get-tuple-element.146.gz_ref, f32[4096,256]{1,0:T(8,128)} %get-tuple-element.147.d_hidden_ref, bf16[9,256,256]{2,1,0:T(8,128)(2,1)} %get-tuple-element.190.conv_ref), custom_call_target="tpu_custom_call" | custom-call | flops 4831838208 | bytes 8388608 | tf_op jit(solution)/shard_map/pallas_call | solution.py:917
  443.7 9.3 %shard_map.191 = f32[736,768]{1,0:T(8,128)} custom-call(bf16[4,736,768]{2,1,0:T(8,128)(2,1)} %get-tuple-element.90.act_ref, bf16[12,256,768]{2,1,0:T(8,128)(2,1)} %all-gather.5.cloned.1.call-done.w_ref, f32[736,768]{1,0:T(8,128)} %get-tuple-element.91.stream_ref), custom_call_target="tpu_custom_call" | custom-call | flops 3472883712 | bytes 13565952 | tf_op jit(solution)/shard_map/pallas_call | solution.py:562
  454.9 12.8 %collective-permute-done.28 = bf16[16,64,256]{2,1,0:T(8,128)(2,1)S(1)} collective-permute-done((bf16[16,64,256]{2,1,0:T(8,128)(2,1)S(1)}, bf16[16,64,256]{2,1,0:T(8,128)(2,1)S(1)}, u32[]{:S(2)}, u32[]{:S(2)}) %collective-permute-start.28) | collective-permute-done | bytes 524320 | tf_op jit(solution)/shard_map/ppermute | solution.py:59
  467.8 9.9 %collective-permute-done.27 = bf16[16,64,256]{2,1,0:T(8,128)(2,1)S(1)} collective-permute-done((bf16[16,64,256]{2,1,0:T(8,128)(2,1)S(1)}, bf16[16,64,256]{2,1,0:T(8,128)(2,1)S(1)}, u32[]{:S(2)}, u32[]{:S(2)}) %collective-permute-start.27) | collective-permute-done | bytes 524320 | tf_op jit(solution)/shard_map/ppermute | solution.py:59
  487.3 6.8 %subtract_select_fusion = (f32[8,256,256]{2,1,0:T(8,128)}, f32[8,256,256]{2,1,0:T(8,128)}, f32[8,256,256]{2,1,0:T(8,128)}) fusion(f32[8,256,256]{2,1,0:T(8,128)} %param.16, pred[8]{0:T(512)(128)(4,1)S(1)} %compare_bitcast_fusion, f32[8,256,256]{2,1,0:T(8,128)} %param.17, f32[8,256,256]{2,1,0:T(8,128)} %param.18, ...), kind=kLoop, calls=%fused_computation.24 | loop fusion | flops 10485760 | bytes 13632004 | tf_op jit(solution)/shard_map/jit(_where)/select_n | solution.py:1124
  (279 shorter events, 176.3 us)
Async XLA Ops:
  10.0 33.7 %all-to-all-start = ((bf16[32,8,8,256]{3,2,1,0:T(8,128)(2,1)}), bf16[32,8,8,256]{3,2,1,0:T(8,128)(2,1)S(1)}, u32[]{:S(2)}, u32[]{:S(2)}) async-start(bf16[32,8,8,256]{3,2,1,0:T(8,128)(2,1)} %copy.122), calls=%async_computation | async-start | bytes 2097152 | tf_op jit(solution)/shard_map/all_to_all | solution.py:961
  17.3 129.7 %all-gather.3.cloned.1.call-start = ((), (), s32[]{:S(2)}) async-start(), calls=%async_computation.2 | async-start | bytes 10137600 | tf_op jit(solution)/shard_map/all_gather | solution.py:974
  50.0 162.5 %all-gather.5.cloned.1.call-start = ((), (), s32[]{:S(2)}) async-start(), calls=%async_computation.3 | async-start | bytes 4866048 | tf_op jit(solution)/shard_map/all_gather | solution.py:975
  54.2 27.2 %collective-permute-start.1 = (bf16[16,64,256]{2,1,0:T(8,128)(2,1)}, bf16[16,64,256]{2,1,0:T(8,128)(2,1)S(1)}, u32[]{:S(2)}, u32[]{:S(2)}) collective-permute-start(bf16[16,64,256]{2,1,0:T(8,128)(2,1)} %get-tuple-element.186), channel_id=1, source_target_pairs={{0,2},{1,3},{2,0},{3,1},{4,6},{5,7},{6,4},{7,5},{8,10},{9,11},{10,... | collective-permute-start | bytes 1572872 | tf_op jit(solution)/shard_map/ppermute | solution.py:59
  54.8 26.7 %collective-permute-start = (bf16[16,64,256]{2,1,0:T(8,128)(2,1)S(1)}, bf16[16,64,256]{2,1,0:T(8,128)(2,1)S(1)}, u32[]{:S(2)}, u32[]{:S(2)}) collective-permute-start(bf16[16,64,256]{2,1,0:T(8,128)(2,1)S(1)} %get-tuple-element.184), channel_id=1, source_target_pairs={{0,1},{1,0},{2,3},{3,2},{4,5},{5,4},{6,7},{7,6},{8,9},{9,8},{10,11... | collective-permute-start | bytes 1572872 | tf_op jit(solution)/shard_map/ppermute | solution.py:59
  196.4 66.7 %collective-permute-start.10 = (bf16[12,4,2,2,8,768]{5,4,3,2,1,0:T(8,128)(2,1)}, bf16[12,4,2,2,8,768]{5,4,3,2,1,0:T(8,128)(2,1)}, u32[]{:S(2)}, u32[]{:S(2)}) collective-permute-start(bf16[12,4,2,2,8,768]{5,4,3,2,1,0:T(8,128)(2,1)} %get-tuple-element.165), channel_id=1, source_target_pairs={{0,4},{4,0},{1,5},{5,1},{2,6},{6,2},{3,7},{7,3},{8,12},{12,8},{9,1... | collective-permute-start | bytes 7077896 | tf_op jit(solution)/shard_map/ppermute | solution.py:59
  227.2 38.5 %collective-permute-start.11 = (bf16[12,4,2,2,8,768]{5,4,3,2,1,0:T(8,128)(2,1)S(1)}, bf16[12,4,2,2,8,768]{5,4,3,2,1,0:T(8,128)(2,1)}, u32[]{:S(2)}, u32[]{:S(2)}) collective-permute-start(bf16[12,4,2,2,8,768]{5,4,3,2,1,0:T(8,128)(2,1)S(1)} %get-tuple-element.163), channel_id=1, source_target_pairs={{0,4},{4,0},{1,5},{5,1},{2,6},{6,2},{3,7},{7,3},{8,12},{12,8},{9,1... | collective-permute-start | bytes 7077896 | tf_op jit(solution)/shard_map/ppermute | solution.py:59
  243.6 35.1 %collective-permute-start.12 = (bf16[3,4,2,2,8,768]{5,4,3,2,1,0:T(8,128)(2,1)S(1)}, bf16[3,4,2,2,8,768]{5,4,3,2,1,0:T(8,128)(2,1)}, u32[]{:S(2)}, u32[]{:S(2)}) collective-permute-start(bf16[3,4,2,2,8,768]{5,4,3,2,1,0:T(8,128)(2,1)S(1)} %get-tuple-element.202), channel_id=1, source_target_pairs={{0,4},{4,0},{1,5},{5,1},{2,6},{6,2},{3,7},{7,3},{8,12},{12,8},{9,1... | collective-permute-start | bytes 1769480 | tf_op jit(solution)/shard_map/ppermute | solution.py:59
  270.2 28.4 %collective-permute-start.13 = (bf16[12,4,2,8,768]{4,3,1,0,2:T(8,128)(2,1)}, bf16[12,4,2,8,768]{4,3,1,0,2:T(8,128)(2,1)}, u32[]{:S(2)}, u32[]{:S(2)}) collective-permute-start(bf16[12,4,2,8,768]{4,3,1,0,2:T(8,128)(2,1)} %bitcast.275), channel_id=1, source_target_pairs={{0,1},{1,0},{2,3},{3,2},{4,5},{5,4},{6,7},{7,6},{8,9},{9,8},{10,11... | collective-permute-start | bytes 3538952 | tf_op jit(solution)/shard_map/ppermute | solution.py:59
  281.1 28.2 %collective-permute-start.14 = (bf16[12,4,2,8,768]{4,3,1,0,2:T(8,128)(2,1)}, bf16[12,4,2,8,768]{4,3,1,0,2:T(8,128)(2,1)}, u32[]{:S(2)}, u32[]{:S(2)}) collective-permute-start(bf16[12,4,2,8,768]{4,3,1,0,2:T(8,128)(2,1)} %bitcast.274), channel_id=1, source_target_pairs={{0,2},{2,0},{1,3},{3,1},{4,6},{6,4},{5,7},{7,5},{8,10},{10,8},{9,1... | collective-permute-start | bytes 3538952 | tf_op jit(solution)/shard_map/ppermute | solution.py:59
  297.5 45.0 %collective-permute-start.15 = (bf16[9,4,2,2,8,768]{5,4,3,2,1,0:T(8,128)(2,1)}, bf16[9,4,2,2,8,768]{5,4,3,2,1,0:T(8,128)(2,1)}, u32[]{:S(2)}, u32[]{:S(2)}) collective-permute-start(bf16[9,4,2,2,8,768]{5,4,3,2,1,0:T(8,128)(2,1)} %get-tuple-element.170), channel_id=1, source_target_pairs={{0,4},{4,0},{1,5},{5,1},{2,6},{6,2},{3,7},{7,3},{8,12},{12,8},{9,1... | collective-permute-start | bytes 5308424 | tf_op jit(solution)/shard_map/ppermute | solution.py:59
  311.9 33.1 %collective-permute-start.17 = (bf16[12,4,8,768]{3,2,1,0:T(8,128)(2,1)S(1)}, bf16[12,4,8,768]{3,2,1,0:T(8,128)(2,1)S(1)}, u32[]{:S(2)}, u32[]{:S(2)}) collective-permute-start(bf16[12,4,8,768]{3,2,1,0:T(8,128)(2,1)S(1)} %get-tuple-element.200), channel_id=1, source_target_pairs={{0,2},{2,0},{1,3},{3,1},{4,6},{6,4},{5,7},{7,5},{8,10},{10,8},{9,1... | collective-permute-start | bytes 1769480 | tf_op jit(solution)/shard_map/ppermute | solution.py:59
  313.1 32.1 %collective-permute-start.16 = (bf16[12,4,8,768]{3,2,1,0:T(8,128)(2,1)}, bf16[12,4,8,768]{3,2,1,0:T(8,128)(2,1)S(1)}, u32[]{:S(2)}, u32[]{:S(2)}) collective-permute-start(bf16[12,4,8,768]{3,2,1,0:T(8,128)(2,1)} %get-tuple-element.198), channel_id=1, source_target_pairs={{0,1},{1,0},{2,3},{3,2},{4,5},{5,4},{6,7},{7,6},{8,9},{9,8},{10,11... | collective-permute-start | bytes 1769480 | tf_op jit(solution)/shard_map/ppermute | solution.py:59
  314.7 34.3 %collective-permute-start.21 = (bf16[2,4,2,2,8,768]{5,4,3,2,1,0:T(8,128)(2,1)}, bf16[2,4,2,2,8,768]{5,4,3,2,1,0:T(8,128)(2,1)}, u32[]{:S(2)}, u32[]{:S(2)}) collective-permute-start(bf16[2,4,2,2,8,768]{5,4,3,2,1,0:T(8,128)(2,1)} %get-tuple-element.212), channel_id=1, source_target_pairs={{0,4},{4,0},{1,5},{5,1},{2,6},{6,2},{3,7},{7,3},{8,12},{12,8},{9,1... | collective-permute-start | bytes 1179656 | tf_op jit(solution)/shard_map/ppermute | solution.py:59
  345.8 24.0 %collective-permute-start.18 = (bf16[6,4,2,8,768]{4,3,1,0,2:T(8,128)(2,1)S(1)}, bf16[6,4,2,8,768]{4,3,1,0,2:T(8,128)(2,1)S(1)}, u32[]{:S(2)}, u32[]{:S(2)}) collective-permute-start(bf16[6,4,2,8,768]{4,3,1,0,2:T(8,128)(2,1)S(1)} %bitcast.325), channel_id=1, source_target_pairs={{0,1},{1,0},{2,3},{3,2},{4,5},{5,4},{6,7},{7,6},{8,9},{9,8},{10,11... | collective-permute-start | bytes 1769480 | tf_op jit(solution)/shard_map/ppermute | solution.py:59
  347.1 22.9 %collective-permute-start.19 = (bf16[6,4,2,8,768]{4,3,1,0,2:T(8,128)(2,1)S(1)}, bf16[6,4,2,8,768]{4,3,1,0,2:T(8,128)(2,1)S(1)}, u32[]{:S(2)}, u32[]{:S(2)}) collective-permute-start(bf16[6,4,2,8,768]{4,3,1,0,2:T(8,128)(2,1)S(1)} %bitcast.324), channel_id=1, source_target_pairs={{0,2},{2,0},{1,3},{3,1},{4,6},{6,4},{5,7},{7,5},{8,10},{10,8},{9,1... | collective-permute-start | bytes 1769480 | tf_op jit(solution)/shard_map/ppermute | solution.py:59
  348.0 22.3 %collective-permute-start.20 = (bf16[24,2,8,768]{3,2,1,0:T(8,128)(2,1)S(1)}, bf16[24,2,8,768]{3,2,1,0:T(8,128)(2,1)S(1)}, u32[]{:S(2)}, u32[]{:S(2)}) collective-permute-start(bf16[24,2,8,768]{3,2,1,0:T(8,128)(2,1)S(1)} %get-tuple-element.192), channel_id=1, source_target_pairs={{0,8},{8,0},{16,24},{24,16},{1,9},{9,1},{17,25},{25,17},{2,10},{10... | collective-permute-start | bytes 1769480 | tf_op jit(solution)/shard_map/ppermute | solution.py:59
  350.9 23.1 %collective-permute-start.25 = (bf16[2,4,2,8,768]{4,3,0,1,2:T(8,128)(2,1)}, bf16[2,4,2,8,768]{4,3,0,1,2:T(8,128)(2,1)}, u32[]{:S(2)}, u32[]{:S(2)}) collective-permute-start(bf16[2,4,2,8,768]{4,3,0,1,2:T(8,128)(2,1)} %bitcast.286), channel_id=1, source_target_pairs={{0,1},{1,0},{2,3},{3,2},{4,5},{5,4},{6,7},{7,6},{8,9},{9,8},{10,11... | collective-permute-start | bytes 589832 | tf_op jit(solution)/shard_map/ppermute | solution.py:59
  375.7 30.0 %collective-permute-start.35 = (bf16[2,4,8,768]{3,2,0,1:T(8,128)(2,1)}, bf16[2,4,8,768]{3,2,0,1:T(8,128)(2,1)}, u32[]{:S(2)}, u32[]{:S(2)}) collective-permute-start(bf16[2,4,8,768]{3,2,0,1:T(8,128)(2,1)} %get-tuple-element.235), channel_id=1, source_target_pairs={{0,2},{2,0},{1,3},{3,1},{4,6},{6,4},{5,7},{7,5},{8,10},{10,8},{9,1... | collective-permute-start | bytes 294920 | tf_op jit(solution)/shard_map/ppermute | solution.py:59
  383.6 29.8 %collective-permute-start.39 = (bf16[12,2,8,768]{3,2,1,0:T(8,128)(2,1)}, bf16[12,2,8,768]{3,2,1,0:T(8,128)(2,1)}, u32[]{:S(2)}, u32[]{:S(2)}) collective-permute-start(bf16[12,2,8,768]{3,2,1,0:T(8,128)(2,1)} %get-tuple-element.218), channel_id=1, source_target_pairs={{0,8},{8,0},{16,24},{24,16},{1,9},{9,1},{17,25},{25,17},{2,10},{10... | collective-permute-start | bytes 884744 | tf_op jit(solution)/shard_map/ppermute | solution.py:59
  436.4 48.7 %all-to-all-start.1 = ((bf16[32,9,8,256]{3,2,1,0:T(8,128)(2,1)}), bf16[32,9,8,256]{3,2,1,0:T(8,128)(2,1)S(1)}, u32[]{:S(2)}, u32[]{:S(2)}) async-start(bf16[32,9,8,256]{3,2,1,0:T(8,128)(2,1)} %pad_maximum_fusion.6), calls=%async_computation.1 | async-start | bytes 2359296 | tf_op jit(solution)/shard_map/all_to_all | solution.py:1101
  440.1 27.6 %collective-permute-start.28 = (bf16[16,64,256]{2,1,0:T(8,128)(2,1)S(1)}, bf16[16,64,256]{2,1,0:T(8,128)(2,1)S(1)}, u32[]{:S(2)}, u32[]{:S(2)}) collective-permute-start(bf16[16,64,256]{2,1,0:T(8,128)(2,1)S(1)} %get-tuple-element.177), channel_id=1, source_target_pairs={{0,3},{1,2},{2,1},{3,0},{4,7},{5,6},{6,5},{7,4},{8,11},{9,10},{10,... | collective-permute-start | bytes 1572872 | tf_op jit(solution)/shard_map/ppermute | solution.py:59
  442.8 34.9 %collective-permute-start.27 = (bf16[16,64,256]{2,1,0:T(8,128)(2,1)S(1)}, bf16[16,64,256]{2,1,0:T(8,128)(2,1)S(1)}, u32[]{:S(2)}, u32[]{:S(2)}) collective-permute-start(bf16[16,64,256]{2,1,0:T(8,128)(2,1)S(1)} %get-tuple-element.178), channel_id=1, source_target_pairs={{0,2},{1,3},{2,0},{3,1},{4,6},{5,7},{6,4},{7,5},{8,10},{9,11},{10,... | collective-permute-start | bytes 1572872 | tf_op jit(solution)/shard_map/ppermute | solution.py:59
  443.4 35.1 %collective-permute-start.26 = (bf16[16,64,256]{2,1,0:T(8,128)(2,1)S(1)}, bf16[16,64,256]{2,1,0:T(8,128)(2,1)S(1)}, u32[]{:S(2)}, u32[]{:S(2)}) collective-permute-start(bf16[16,64,256]{2,1,0:T(8,128)(2,1)S(1)} %get-tuple-element.179), channel_id=1, source_target_pairs={{0,1},{1,0},{2,3},{3,2},{4,5},{5,4},{6,7},{7,6},{8,9},{9,8},{10,11... | collective-permute-start | bytes 1572872 | tf_op jit(solution)/shard_map/ppermute | solution.py:59
  (45 other events, 453.0 us)
Sparse Core Ops, SparseCore 0:
  50.2 96.8 all-gather.2
  149.8 62.6 all-gather.4

commit v5 on v4

--- a/solution.py
+++ b/solution.py
@@ -1,3 +1,5 @@
+import functools
+
 import jax
 import jax.numpy as jnp
 from jax import lax
@@ -59,34 +61,39 @@
     return lax.ppermute(values, axes, [(i, i ^ mask) for i in range(count)])
 
 
-def begin_sum(values, axes, dim):
+def advance(parts, axes, dim):
     mine = lax.axis_index(axes)
-    parts = [lax.dynamic_index_in_dim(values, mine, dim, keepdims=False)]
-    for mask in range(1, lax.axis_size(axes)):
-        give = lax.dynamic_index_in_dim(values, mine ^ mask, dim, keepdims=False)
-        parts.append(xor_permute(give, axes, mask))
-    return parts
-
-
-def begin_near(values):
-    shape = values.shape
-    values = values.reshape((shape[0], shape[1] // 2, 2) + shape[2:])
+    cuts = []
+    for mask in range(lax.axis_size(axes)):
+        cuts.append(add_up([lax.dynamic_index_in_dim(p, mine ^ mask, dim, False) for p in parts]))
+    return cuts
+
+
+def advance_near(parts):
     mine = lax.axis_index("z") % 2
-    keep = lax.dynamic_index_in_dim(values, mine, 2, keepdims=False)
-    give = lax.dynamic_index_in_dim(values, 1 - mine, 2, keepdims=False)
-    return [keep, xor_permute(give, "z", 1)]
-
-
-def begin_far(values):
+    shape = parts[0].shape
+    parts = [p.reshape((shape[0], shape[1] // 2, 2) + shape[2:]) for p in parts]
+    return [
+        add_up([lax.dynamic_index_in_dim(p, mine ^ mask, 2, False) for p in parts])
+        for mask in range(2)
+    ]
+
+
+def advance_far(parts):
     mine = lax.axis_index("z") // 2
-    parts = [lax.dynamic_index_in_dim(values, mine, 1, keepdims=False)]
-    for mask in range(1, values.shape[1]):
-        give = lax.dynamic_index_in_dim(values, mine ^ mask, 1, keepdims=False)
-        parts.append(xor_permute(give, "z", 2 * mask))
-    return parts
-
-
-def end_sum(parts, keep_wide=False):
+    return [
+        add_up([lax.dynamic_index_in_dim(p, mine ^ mask, 1, False) for p in parts])
+        for mask in range(parts[0].shape[1])
+    ]
+
+
+def send(cuts, axes, unit=1):
+    return [cuts[0]] + [
+        xor_permute(cut, axes, unit * mask) for mask, cut in enumerate(cuts) if mask > 0
+    ]
+
+
+def add_up(parts, keep_wide=False):
     total = parts[0].astype(f32)
     for part in parts[1:]:
         total = total + part.astype(f32)
@@ -119,19 +126,31 @@
 
 
 def trade_rows(values):
+    mine = lax.axis_index(("y", "x"))
     count = lax.axis_size(("y", "x"))
-    mine = lax.axis_index(("y", "x"))
-    pieces = [lax.dynamic_index_in_dim(values, mine, 0, keepdims=False)]
-    for mask in range(1, count):
-        give = lax.dynamic_index_in_dim(values, mine ^ mask, 0, keepdims=False)
-        pieces.append(xor_permute(give, ("y", "x"), mask))
-    order = jnp.arange(count) ^ mine
+    cuts = [lax.dynamic_index_in_dim(values, mine ^ mask, 0, False) for mask in range(count)]
+    return send(cuts, ("y", "x"))
+
+
+def row_order(pieces):
+    order = jnp.arange(len(pieces)) ^ lax.axis_index(("y", "x"))
     return jnp.stack(pieces).at[order].get(mode="promise_in_bounds")
 
 
-def cut(matrix):
-    sizes = [lax.axis_size(axis) for axis in AXES]
-    return matrix.astype(bf16).reshape([-1] + sizes + [CH // lax.axis_size(AXES), matrix.shape[-1]])
+def slice_shape():
+    z, c, y, x = [lax.axis_size(axis) for axis in AXES]
+    return (z, y, x, CH // (z * c * y * x))
+
+
+def cut_core(matrix):
+    z, y, x, rows = slice_shape()
+    parts = matrix.astype(bf16).reshape(-1, z, 2, y, x, rows, matrix.shape[-1])
+    own = lax.axis_index("c")
+    return [lax.dynamic_index_in_dim(parts, own ^ other, 2, False) for other in range(2)]
+
+
+def core_parts(parts):
+    return [part.reshape((-1,) + slice_shape() + part.shape[-1:]) for part in parts]
 
 
 tie = lax.optimization_barrier
@@ -437,6 +456,27 @@
     return ref[...].reshape(D, D)
 
 
+def write_cores(core, matrix, keep_ref, give_ref, span):
+    parts = matrix.reshape(-1, 2, span, matrix.shape[-1])
+    first, second = parts[:, 0], parts[:, 1]
+    keep = jnp.where(core == 0, first, second)
+    give = jnp.where(core == 0, second, first)
+    keep_ref[...] = keep.reshape(keep_ref.shape).astype(bf16)
+    give_ref[...] = give.reshape(give_ref.shape).astype(bf16)
+
+
+def core_span():
+    return CH // (2 * lax.axis_size("z"))
+
+
+def core_here():
+    return lax.axis_index("c").astype(jnp.int32).reshape(1)
+
+
+CORE_SPEC = pl.BlockSpec(memory_space=pltpu.SMEM)
+HALF = D // 2
+
+
 def row_scale(values):
     return lax.rsqrt(jnp.mean(values * values, -1, keepdims=True) + eps_norm)
 
@@ -574,52 +614,55 @@
     )(act, w_down, stream)
 
 
-def down_grad_kernel(act_ref, gd_ref, out_ref):
-    out_ref[...] = dot_tn(act_ref[0], gd_ref[...]).astype(bf16)
+def down_grad_kernel(core_ref, act_ref, gd_ref, keep_ref, give_ref, *, span):
+    total = dot_tn(act_ref[0], gd_ref[...])
+    write_cores(core_ref[0], total, keep_ref, give_ref, span)
 
 
 def down_grad(act, gd):
-    return pl.pallas_call(
-        down_grad_kernel,
+    half = pl.BlockSpec((HALF, D), lambda i: (i, 0))
+    return pl.pallas_call(
+        functools.partial(down_grad_kernel, span=core_span()),
         grid=(4,),
-        in_specs=[pl.BlockSpec((1, SEQ, D), lambda i: (i, 0, 0)), full(SEQ, D)],
-        out_specs=pl.BlockSpec((D, D), lambda i: (i, 0)),
-        out_shape=jax.ShapeDtypeStruct((4 * D, D), bf16),
+        in_specs=[CORE_SPEC, pl.BlockSpec((1, SEQ, D), lambda i: (i, 0, 0)), full(SEQ, D)],
+        out_specs=[half, half],
+        out_shape=[jax.ShapeDtypeStruct((4 * HALF, D), bf16)] * 2,
         compiler_params=params(),
         cost_estimate=cost(8 * SEQ * D * D, 18 * SEQ * D),
-    )(act, gd)
-
-
-def up_grad_kernel(gd_ref, w_ref, slope_ref, normed_ref, gpre_ref, out_ref, turned_s):
+    )(core_here(), act, gd)
+
+
+def up_grad_kernel(
+    core_ref, gd_ref, w_ref, slope_ref, normed_ref, gpre_ref, keep_ref, give_ref, turned_s, *, span
+):
     @pl.when(pl.program_id(0) == 0)
     def _():
         turned_s[...] = normed_ref[...].T
 
     gpre = (dot_nt(gd_ref[...], square(w_ref)) * slope_ref[0].astype(f32)).astype(bf16)
     gpre_ref[0] = gpre
-    out_ref[...] = dot_nn(turned_s[...], gpre).astype(bf16)
+    write_cores(core_ref[0], dot_nn(turned_s[...], gpre), keep_ref, give_ref, span)
 
 
 def up_grad(gd, w_down, slope, normed):
     part = pl.BlockSpec((1, SEQ, D), lambda i: (i, 0, 0))
-    return pl.pallas_call(
-        up_grad_kernel,
+    half = pl.BlockSpec((HALF, D), lambda i: (i, 0))
+    return pl.pallas_call(
+        functools.partial(up_grad_kernel, span=core_span()),
         grid=(4,),
-        in_specs=[full(SEQ, D), part_of(0), part, full(SEQ, D)],
-        out_specs=[part, pl.BlockSpec((D, D), lambda i: (i, 0))],
-        out_shape=[
-            jax.ShapeDtypeStruct((4, SEQ, D), bf16),
-            jax.ShapeDtypeStruct((4 * D, D), bf16),
-        ],
+        in_specs=[CORE_SPEC, full(SEQ, D), part_of(0), part, full(SEQ, D)],
+        out_specs=[part, half, half],
+        out_shape=[jax.ShapeDtypeStruct((4, SEQ, D), bf16)]
+        + [jax.ShapeDtypeStruct((4 * HALF, D), bf16)] * 2,
         scratch_shapes=[pltpu.VMEM((D, SEQ), bf16)],
         compiler_params=params(),
         cost_estimate=cost(16 * SEQ * D * D, 36 * SEQ * D),
-    )(gd, w_down, slope, normed)
+    )(core_here(), gd, w_down, slope, normed)
 
 
 def att_grad_kernel(
-    gpre_ref, w_ref, att_ref, stream_ref, gd_ref, mixed_ref, gain_ref,
-    d_stream_ref, gog_ref, att_g_ref, gain_g_ref, total_s,
+    core_ref, gpre_ref, w_ref, att_ref, stream_ref, gd_ref, mixed_ref, gain_ref,
+    d_stream_ref, gog_ref, keep_ref, give_ref, gain_g_ref, total_s, *, span
 ):
     step = pl.program_id(0)
     part = dot_nt(gpre_ref[0], square(w_ref))
@@ -640,14 +683,15 @@
         d_stream_ref[...] = d_stream
         ga = d_stream.astype(bf16)
         gog_ref[...] = dot_nt(ga, square(att_ref)).astype(bf16)
-        att_g_ref[...] = dot_tn(mixed_ref[...], ga).astype(bf16)
+        write_cores(core_ref[0], dot_tn(mixed_ref[...], ga), keep_ref, give_ref, span)
 
 
 def att_grad(gpre, weights, stream, gd, mixed, gain):
     return pl.pallas_call(
-        att_grad_kernel,
+        functools.partial(att_grad_kernel, span=core_span()),
         grid=(4,),
         in_specs=[
+            CORE_SPEC,
             pl.BlockSpec((1, SEQ, D), lambda i: (i, 0, 0)),
             part_of(4),
             fixed_part(3),
@@ -656,38 +700,40 @@
             full(SEQ, D),
             full(1, D),
         ],
-        out_specs=[full(SEQ, D), full(SEQ, D), full(D, D), full(1, D)],
+        out_specs=[full(SEQ, D), full(SEQ, D), full(HALF, D), full(HALF, D), full(1, D)],
         out_shape=[
             jax.ShapeDtypeStruct((SEQ, D), f32),
             jax.ShapeDtypeStruct((SEQ, D), bf16),
-            jax.ShapeDtypeStruct((D, D), bf16),
+            jax.ShapeDtypeStruct((HALF, D), bf16),
+            jax.ShapeDtypeStruct((HALF, D), bf16),
             jax.ShapeDtypeStruct((1, D), f32),
         ],
         scratch_shapes=[pltpu.VMEM((SEQ, D), f32)],
         compiler_params=params(),
         cost_estimate=cost(12 * SEQ * D * D, 32 * SEQ * D),
-    )(gpre, weights, weights, stream, gd, mixed, gain)
-
-
-def qkv_grad_kernel(normed_ref, g_ref, out_ref, turned_s):
+    )(core_here(), gpre, weights, weights, stream, gd, mixed, gain)
+
+
+def qkv_grad_kernel(core_ref, normed_ref, g_ref, keep_ref, give_ref, turned_s, *, span):
     @pl.when(pl.program_id(0) == 0)
     def _():
         turned_s[...] = normed_ref[...].T
 
-    out_ref[...] = dot_nn(turned_s[...], g_ref[0]).astype(bf16)
+    write_cores(core_ref[0], dot_nn(turned_s[...], g_ref[0]), keep_ref, give_ref, span)
 
 
 def qkv_grad(normed, gqkv):
-    return pl.pallas_call(
-        qkv_grad_kernel,
+    half = pl.BlockSpec((HALF, D), lambda i: (i, 0))
+    return pl.pallas_call(
+        functools.partial(qkv_grad_kernel, span=core_span()),
         grid=(3,),
-        in_specs=[full(SEQ, D), pl.BlockSpec((1, SEQ, D), lambda i: (i, 0, 0))],
-        out_specs=pl.BlockSpec((D, D), lambda i: (i, 0)),
-        out_shape=jax.ShapeDtypeStruct((3 * D, D), bf16),
+        in_specs=[CORE_SPEC, full(SEQ, D), pl.BlockSpec((1, SEQ, D), lambda i: (i, 0, 0))],
+        out_specs=[half, half],
+        out_shape=[jax.ShapeDtypeStruct((3 * HALF, D), bf16)] * 2,
         scratch_shapes=[pltpu.VMEM((D, SEQ), bf16)],
         compiler_params=params(),
         cost_estimate=cost(6 * SEQ * D * D, 14 * SEQ * D),
-    )(normed, gqkv)
+    )(core_here(), normed, gqkv)
 
 
 def embed_grad_kernel(
@@ -816,8 +862,8 @@
 
 
 def token_backward_kernel(
-    dkv_ref, slope_ref, pool_ref, hidden_ref, x_ref, kv_w_ref,
-    d_hidden_ref, gz_ref, conv_ref, kv_g_ref, conv_s, kv_s,
+    core_ref, dkv_ref, slope_ref, pool_ref, hidden_ref, x_ref, kv_w_ref,
+    d_hidden_ref, gz_ref, keep_ref, give_ref, conv_s, kv_s, *, span
 ):
     step = pl.program_id(0)
 
@@ -839,11 +885,13 @@
 
     @pl.when(step == pl.num_programs(0) - 1)
     def _():
+        tiles = []
         for row in range(3):
             for col in range(3):
-                conv_ref[3 * row + col] = conv_s[row, :, col * CH : (col + 1) * CH].T.astype(bf16)
-        kv_g_ref[0] = kv_s[:, :CH].astype(bf16)
-        kv_g_ref[1] = kv_s[:, CH:].astype(bf16)
+                tiles.append(conv_s[row, :, col * CH : (col + 1) * CH].T)
+        tiles = tiles + [kv_s[:, :CH], kv_s[:, CH:]]
+        for at, tile in enumerate(tiles):
+            write_cores(core_ref[0], tile, keep_ref.at[at], give_ref.at[at], span)
 
 
 def token_backward(dkv, slope, d_pool, hidden_b, wide, kv_weight):
@@ -852,9 +900,10 @@
     whole_3 = lambda i: (0, 0, 0)
     block = lambda i: (i, 0)
     return pl.pallas_call(
-        token_backward_kernel,
+        functools.partial(token_backward_kernel, span=core_span()),
         grid=(steps,),
         in_specs=[
+            CORE_SPEC,
             pl.BlockSpec((BLOCK, 2 * CH), block),
             pl.BlockSpec((BLOCK, CH), block),
             pl.BlockSpec((CTX // steps, CH), block),
@@ -865,19 +914,19 @@
         out_specs=[
             pl.BlockSpec((BLOCK, CH), block),
             pl.BlockSpec((BLOCK, CH), block),
-            pl.BlockSpec((9, CH, CH), whole_3),
-            pl.BlockSpec((2, CH, CH), whole_3),
+            pl.BlockSpec((11, CH // 2, CH), whole_3),
+            pl.BlockSpec((11, CH // 2, CH), whole_3),
         ],
         out_shape=[
             jax.ShapeDtypeStruct((CELLS, CH), f32),
             jax.ShapeDtypeStruct((CELLS, CH), bf16),
-            jax.ShapeDtypeStruct((9, CH, CH), bf16),
-            jax.ShapeDtypeStruct((2, CH, CH), bf16),
+            jax.ShapeDtypeStruct((11, CH // 2, CH), bf16),
+            jax.ShapeDtypeStruct((11, CH // 2, CH), bf16),
         ],
         scratch_shapes=[pltpu.VMEM((3, CH, 3 * CH), f32), pltpu.VMEM((CH, 2 * CH), f32)],
         compiler_params=params(),
         cost_estimate=cost(26 * CELLS * CH * CH, 20 * CELLS * CH),
-    )(dkv, slope, d_pool, hidden_b, wide, kv_weight)
+    )(core_here(), dkv, slope, d_pool, hidden_b, wide, kv_weight)
 
 
 def context_backward_kernel(gz_ref, d_hidden_ref, conv_ref, out_ref, wide_s):
@@ -948,7 +997,7 @@
     rows = CH // devices
     slot_of = slot_index(tile_owner, slot_count)
 
-    image = trade_rows(context_map).reshape(IMG, IMG, CH)
+    pieces = trade_rows(context_map)
     length = CTX + FT * horizon
     valid = jnp.arange(SEQ) < length[0]
     gd = jnp.where(valid[:, None], cotangent[0], jnp.zeros((), bf16))
@@ -959,6 +1008,8 @@
         .transpose(1, 0, 2, 3)
     )
     slices = lax.all_to_all(slices, AXES, split_axis=0, concat_axis=0, tiled=True)
+    slices, pieces, gd = tie((slices, pieces, gd))
+    image = row_order(pieces).reshape(IMG, IMG, CH)
     slices = slices.reshape(devices * slot_count, rows, CH)
     slices = slices.at[slot_of].get(mode="promise_in_bounds")
     early, emb, qkv, att, up, down = jnp.split(slices, (13, 16, 43, 52, 88))
@@ -997,86 +1048,98 @@
     mixed, logs = self_forward(qkv, length)
     stream, normed_two, act, slope = up_forward(mixed, embed, weights, gain_two)
 
-    sum_down = cut(down_grad(act, gd))
-    gd, sum_down = tie((gd, sum_down))
-    wait_down = begin_sum(sum_down, "c", 2)
-    gpre, sum_up = up_grad(gd, w_down, slope, normed_two)
-    gpre, sum_up, wait_down = hold((gpre, cut(sum_up)), wait_down)
-    wait_up = begin_sum(sum_up, "c", 2)
-    wait_down = begin_sum(end_sum(wait_down), "x", 3)
-    d_stream, gog, sum_att, gain_g_two = att_grad(gpre, weights, stream, gd, mixed, gain_two)
-    gog, sum_att, wait_up = hold((gog, cut(sum_att)), wait_up)
-    wait_up = begin_sum(end_sum(wait_up), "y", 2)
-    wait_att = begin_sum(sum_att, "c", 2)
+    down = core_parts(down_grad(act, gd))
+    gd, down = tie((gd, down))
+    down = send(down, "c")
+    gpre, up_keep, up_give = up_grad(gd, w_down, slope, normed_two)
+    gpre, up, down = hold((gpre, core_parts([up_keep, up_give])), down)
+    down = advance(down, "x", 3)
+    gpre, up, down = tie((gpre, up, down))
+    up, down = send(up, "c"), send(down, "x")
+    d_stream, gog, att_keep, att_give, gain_g_two = att_grad(
+        gpre, weights, stream, gd, mixed, gain_two
+    )
+    gog, att, up = hold((gog, core_parts([att_keep, att_give])), up)
+    up = advance(up, "y", 2)
+    gog, att, up = tie((gog, att, up))
+    up, att = send(up, "y"), send(att, "c")
     gqkv = self_backward(qkv, gog, mixed, logs, length)
-    gqkv, wait_down, wait_up, wait_att = hold((gqkv,), wait_down, wait_up, wait_att)
-    wait_down = begin_sum(end_sum(wait_down), "y", 2)
-    wait_up = begin_sum(end_sum(wait_up), "x", 2)
-    sum_att = end_sum(wait_att)
-    sum_qkv = cut(qkv_grad(normed_one, gqkv))
-    gqkv, sum_qkv, sum_att = tie((gqkv, sum_qkv, sum_att))
-    wait_qkv = begin_sum(sum_qkv, "c", 2)
+    gqkv, down, att = hold((gqkv,), down, att)
+    down = advance(down, "y", 2)
+    gqkv, down = tie((gqkv, down))
+    down = send(down, "y")
+    qkv_keep, qkv_give = qkv_grad(normed_one, gqkv)
+    gqkv, qkv, up = hold((gqkv, core_parts([qkv_keep, qkv_give])), up)
+    up = advance(up, "x", 2)
+    gqkv, qkv, up = tie((gqkv, qkv, up))
+    qkv, up = send(qkv, "c"), send(up, "x")
     emb_g, gupd, pool_g, out_g, gox, gain_g_one = embed_grad(
         gqkv, weights, embed, d_stream, seq, cross_mixed, to_out, gain_one
     )
     gains = jnp.concatenate([gain_g_one, gain_g_two], 0).reshape(devices, 1, -1)
     gain_count = gains.shape[-1]
     gains = jnp.pad(gains, ((0, 0), (0, rows - 1), (0, D - gain_count))).astype(bf16)
-    sum_emb = cut(jnp.concatenate([emb_g, gains.reshape(CH, D)], 0))
-    gox, gupd, sum_emb, wait_qkv, wait_down, wait_up = hold(
-        (gox, gupd, sum_emb), wait_qkv, wait_down, wait_up
-    )
-    wait_mlp = begin_near(jnp.concatenate([end_sum(wait_up), end_sum(wait_down)], 0))
-    sum_qkv = end_sum(wait_qkv)
-    wait_first = begin_sum(sum_qkv[:6], "x", 3)
-    wait_second = begin_sum(jnp.concatenate([sum_qkv[6:], sum_att], 0), "y", 2)
-    wait_emb = begin_sum(sum_emb, "c", 2)
+    emb = cut_core(jnp.concatenate([emb_g, gains.reshape(CH, D)], 0))
+    gox, gupd, emb, qkv, up, down = hold((gox, gupd, emb), qkv, up, down)
+    mlp = advance_near([jnp.concatenate(part, 0) for part in zip(up, down)])
+    first = advance([part[:6] for part in qkv], "x", 3)
+    second = advance([jnp.concatenate([p[6:], q], 0) for p, q in zip(qkv, att)], "y", 2)
+    gox, mlp, first, second, emb = tie((gox, mlp, first, second, emb))
+    mlp, emb = send(mlp, "z"), send(emb, "c")
+    first, second = send(first, "x"), send(second, "y")
 
     log_rows = jnp.concatenate([cross_logs[0], cross_logs[1]], 1)
     gq, gkv = cross_backward(query, kv, gox, cross_mixed, log_rows)
-    gq, gkv, wait_first, wait_second, wait_mlp, wait_emb = hold(
-        (gq, gkv), wait_first, wait_second, wait_mlp, wait_emb
-    )
-    wait_first = begin_sum(end_sum(wait_first), "y", 2)
-    wait_second = begin_sum(end_sum(wait_second), "x", 2)
-    wait_mlp = begin_far(end_sum(wait_mlp))
-    wait_emb = begin_sum(end_sum(wait_emb), "x", 3)
-
-    d_hidden, gz, conv_g, kv_g = token_backward(gkv, slope_z, pool_g, hidden_b, wide, kv_weight)
-    query_g = jnp.dot(feats_b.T, gq, preferred_element_type=f32).astype(bf16)
-    sum_early = cut(
-        jnp.concatenate([conv_g, query_g[None], kv_g, out_g[None]], 0).reshape(EARLY * CH, CH)
-    )
-    d_hidden, gz, sum_early, wait_first, wait_second, wait_mlp, wait_emb = hold(
-        (d_hidden, gz, sum_early), wait_first, wait_second, wait_mlp, wait_emb
-    )
-    sum_early = end_sum(begin_sum(sum_early, "c", 2))
-    wait_att = begin_near(jnp.concatenate([end_sum(wait_first), end_sum(wait_second)], 0))
-    wait_emb = begin_sum(end_sum(wait_emb), "y", 2)
-    sum_mlp = end_sum(wait_mlp, keep_wide=True)
-    gz, sum_early = tie((gz, sum_early))
-    wait_early = begin_sum(
-        sum_early.reshape(sum_early.shape[:2] + (-1,) + sum_early.shape[-2:]), ("y", "x"), 2
-    )
-    context_grad = context_backward(gz, d_hidden, conv_tiles)
-    context_grad, wait_early, wait_att, wait_emb = hold(
-        (context_grad,), wait_early, wait_att, wait_emb
-    )
-    wait_early = begin_sum(end_sum(wait_early), "z", 1)
-    wait_att = begin_far(end_sum(wait_att))
-    wait_emb = begin_sum(end_sum(wait_emb), "z", 1)
-    sum_early = end_sum(wait_early, keep_wide=True)
-    sum_att = end_sum(wait_att, keep_wide=True)
-    sum_emb = end_sum(wait_emb, keep_wide=True)
-    context_rows = trade_rows(context_grad.reshape(context_map.shape))
+    gq, gkv, mlp, first, second, emb = hold((gq, gkv), mlp, first, second, emb)
+    mlp, emb = advance_far(mlp), advance(emb, "x", 3)
+    first, second = advance(first, "y", 2), advance(second, "x", 2)
+    query_g = cut_core(jnp.dot(feats_b.T, gq, preferred_element_type=f32))
+    out_g = cut_core(out_g)
+    gkv, mlp, first, second, emb, query_g, out_g = tie(
+        (gkv, mlp, first, second, emb, query_g, out_g)
+    )
+    mlp, emb = send(mlp, "z", 2), send(emb, "x")
+    first, second = send(first, "y"), send(second, "x")
+
+    d_hidden, gz, token_keep, token_give = token_backward(
+        gkv, slope_z, pool_g, hidden_b, wide, kv_weight
+    )
+    early = [
+        jnp.concatenate([token[:9], q.reshape(1, CH // 2, CH), token[9:], o.reshape(1, CH // 2, CH)], 0)
+        for token, q, o in zip((token_keep, token_give), query_g, out_g)
+    ]
+    d_hidden, early, mlp, first, second, emb = hold(
+        (d_hidden, core_parts(early)), mlp, first, second, emb
+    )
+    att = advance_near([jnp.concatenate(part, 0) for part in zip(first, second)])
+    emb = advance(emb, "y", 2)
+    early, att, emb = tie((early, att, emb))
+    early = send(early, "c")
+    att, emb = send(att, "z"), send(emb, "y")
+    sum_mlp = add_up(mlp, keep_wide=True)
     future_grad = gupd + lax.dot_general(
         gq, to_query, (((1,), (1,)), ((), ())), preferred_element_type=f32
     )
+    future_grad, gz, early = hold((future_grad, gz), early)
+    shape = early[0].shape
+    early = advance([p.reshape(shape[:2] + (-1,) + shape[4:]) for p in early], ("y", "x"), 2)
+    gz, early = tie((gz, early))
+    early = send(early, ("y", "x"))
+    context_grad = context_backward(gz, d_hidden, conv_tiles)
+    context_grad, early, att, emb = hold((context_grad,), early, att, emb)
+    att = advance_far(att)
+    early = advance(early, "z", 1)
+    emb = advance(emb, "z", 1)
+    early = [jnp.concatenate([e, to_tiles(m)], 0) for e, m in zip(early, emb)]
+    context_grad, early, att = tie((context_grad, early, att))
+    early, att = send(early, "z"), send(att, "z", 2)
+    pieces = trade_rows(context_grad.reshape(context_map.shape))
+    sum_early = add_up(early, keep_wide=True)
+    sum_att = add_up(att, keep_wide=True)
 
     sums = jnp.concatenate(
         [
-            to_tiles(sum_early),
-            to_tiles(sum_emb[:1]),
+            sum_early[: EARLY + 3],
             to_tiles(sum_att[:9], 3),
             to_tiles(sum_att[9:]),
             to_tiles(sum_mlp[:12], 4),
@@ -1084,7 +1147,7 @@
         ],
         0,
     )
-    gains = sum_emb[1, 0, :gain_count]
+    gains = sum_early[EARLY + 3, 0, :gain_count]
     share = jnp.concatenate([(jnp.sum(sums * sums) + jnp.sum(gains * gains))[None], gains])
     share_high = share.astype(bf16)
     share_low = (share - share_high.astype(f32)).astype(bf16)
@@ -1117,7 +1180,7 @@
     )
     return (
         block_out[None],
-        context_rows.reshape(context_map.shape).astype(f32),
+        row_order(pieces).reshape(context_map.shape).astype(f32),
         future_grad[None],
         jnp.where(used > 0, new_first, 0.0),
         jnp.where(used > 0, new_second, 0.0),

time: 507 us -> 539 us (1.063)
  waiting for transfers between devices: 121 us -> 167 us
  local copies, waits for them, and re-layouts: 45.2 us -> 35.1 us
    ppermute x42 -> x39, waiting for transfers between devices: 71.7 us -> 125 us  [xor_permute(): return lax.ppermute(values, axes, [(i, i ^ mask) for i in range(count)])]
    all_to_all x1, waiting for transfers between devices: 26.1 us -> 0.01 us  [local(): lax.all_to_all(slices, AXES, split_axis=0, concat_axis=0, tiled=True)]
    all_gather x1, waiting for transfers between devices: 7.04 us -> 24.5 us  [local(): weights = lax.all_gather(weights, AXES, axis=1, tiled=True)]
    squeeze x17 -> x4, local copies, waits for them, and re-layouts: 16.9 us -> 1.83 us  [the longest x1 0.96 us: trade_rows(): lax.dynamic_index_in_dim(values, mine ^ mask, 0, False)]
    optimization_barrier x0 -> x7, local copies, waits for them, and re-layouts: none -> 7.89 us  [the longest x1 3.51 us: local(): gd, down = tie((gd, down))]
    slice x3 -> x10, local copies, waits for them, and re-layouts: 0.14 us -> 5.7 us  [the longest x2 1.9 us: local(): token[9:]]
    ppermute x42 -> x39, starting transfers between devices: 45.6 us -> 40.2 us  [xor_permute(): return lax.ppermute(values, axes, [(i, i ^ mask) for i in range(count)])]
    convert_element_type x20 -> x22, other arithmetic: 20.9 us -> 20.4 us  [the longest x21 17.8 us: add_up(): return total if keep_wide else total.astype(parts[0].dtype)]
  transfers between devices with their start and end apart: 46 -> 43, of which waited for: 23 -> 23; matrix products, arithmetic and copies ran while one was open for 16% -> 11% of each run, Pallas kernels for 41% -> 35%
where the time goes in v5:
time: 539 us; the launch traced here: 535 us
  Pallas kernels  205 us (38%)
  waiting for transfers between devices  167 us (31%)
  other arithmetic  51.4 us (10%)
  starting transfers between devices  51.4 us (10%)
  local copies, waits for them, and re-layouts  35.1 us (7%)
  between operations  19.1 us (4%)
    ppermute x39, waiting for transfers between devices, xor_permute(): return lax.ppermute(values, axes, [(i, i ^ mask) for i in range(count)])  125 us
    ppermute x39, starting transfers between devices, xor_permute(): return lax.ppermute(values, axes, [(i, i ^ mask) for i in range(count)])  40.2 us
    pallas_call x1, Pallas kernels, cross_backward(): pl.pallas_call(cross_backward_kernel, grid=(cells // block,), in_specs=[p...  27.7 us
    all_gather x1, waiting for transfers between devices, local(): weights = lax.all_gather(weights, AXES, axis=1, tiled=True)  24.5 us
    pallas_call x1, Pallas kernels, self_backward(): pl.pallas_call(self_backward_kernel, grid_spec=pltpu.PrefetchScalarGridSp...  19.2 us
    convert_element_type x21, other arithmetic, add_up(): return total if keep_wide else total.astype(parts[0].dtype)  17.8 us
    all_gather x1, waiting for transfers between devices, local(): w_down = lax.all_gather(from_tiles(down, 12, 1), AXES, axis=1, tiled=True)  16.7 us
    pallas_call x1, Pallas kernels, cross_forward(): pl.pallas_call(cross_forward_kernel, grid=(2,), in_specs=[pl.BlockSpec((r...  16.6 us
  transfers between devices with their start and end apart: 43, of which 23 were waited for; matrix products, arithmetic and copies ran while one was open for 11% of the time, Pallas kernels for 35%

profile of v5, /device:TPU:0, one launch (start us, length us, event | category | flops | bytes accessed | tf_op | source)
XLA Modules:
  0.0 534.5 jit_solution(781345218636014063)
XLA Ops:
  10.0 7.3 %all-to-all-start = ((bf16[32,8,8,256]{3,2,1,0:T(8,128)(2,1)}), bf16[32,8,8,256]{3,2,1,0:T(8,128)(2,1)S(1)}, u32[]{:S(2)}, u32[]{:S(2)}) async-start(bf16[32,8,8,256]{3,2,1,0:T(8,128)(2,1)} %copy.190), calls=%async_computation | async-start | bytes 2097152 | tf_op jit(solution)/shard_map/all_to_all | solution.py:1010
  24.6 18.1 %collective-permute-done = bf16[16,64,256]{2,1,0:T(8,128)(2,1)S(1)} collective-permute-done((bf16[16,64,256]{2,1,0:T(8,128)(2,1)S(1)}, bf16[16,64,256]{2,1,0:T(8,128)(2,1)S(1)}, u32[]{:S(2)}, u32[]{:S(2)}) %collective-permute-start) | collective-permute-done | bytes 524320 | tf_op jit(solution)/shard_map/ppermute | solution.py:61
  43.6 11.3 %collective-permute-done.2 = bf16[16,64,256]{2,1,0:T(8,128)(2,1)} collective-permute-done((bf16[16,64,256]{2,1,0:T(8,128)(2,1)S(1)}, bf16[16,64,256]{2,1,0:T(8,128)(2,1)}, u32[]{:S(2)}, u32[]{:S(2)}) %collective-permute-start.2) | collective-permute-done | bytes 524320 | tf_op jit(solution)/shard_map/ppermute | solution.py:61
  92.8 15.8 %shard_map.186 = (bf16[4096,256]{1,0:T(8,128)(2,1)}, bf16[4096,256]{1,0:T(8,128)(2,1)}, bf16[4096,512]{1,0:T(8,128)(2,1)}, bf16[256,256]{1,0:T(8,128)(2,1)}) custom-call(bf16[4224,768]{1,0:T(8,128)(2,1)} %bitcast.301, bf16[3,768,256]{2,1,0:T(8,128)(2,1)} %bitcast.329, bf16[256,512]{1,0:T(8,128)(2,1)} %pad_maximum_fusion.14.kv_w_ref), custom_call_target="tpu_custom_call" | custom-call | flops 5905580032 | bytes 14680064 | tf_op jit(solution)/shard_map/pallas_call | solution.py:839
  108.6 16.6 %shard_map.187 = (bf16[480,256]{1,0:T(8,128)(2,1)}, f32[2,8,240]{2,1,0:T(8,128)}) custom-call(bf16[480,256]{1,0:T(8,128)(2,1)} %fusion.6.q_ref, bf16[4096,512]{1,0:T(8,128)(2,1)} %get-tuple-element.165.k_ref.v_ref, bf16[4096,512]{1,0:T(8,128)(2,1)} %get-tuple-element.165.k_ref.v_ref), custom_call_target="tpu_custom_call" | custom-call | flops 8053063680 | bytes 8388608 | tf_op jit(solution)/shard_map/pallas_call | solution.py:226
  125.2 24.5 %all-gather.3.cloned.1.call-done.emb_ref.w_ref.att_ref = bf16[25,256,768]{2,1,0:T(8,128)(2,1)} async-done(((bf16[25,8,768]{2,1,0:T(8,128)(2,1)}), bf16[25,256,768]{2,1,0:T(8,128)(2,1)}) %all-gather.3.cloned.1.call-update) | async-done | bytes 9830416 | tf_op jit(solution)/shard_map/all_gather | solution.py:1025
  149.7 7.3 %shard_map.188 = (bf16[736,256]{1,0:T(8,128)(2,1)}, f32[736,768]{1,0:T(8,128)}, bf16[736,768]{1,0:T(8,128)(2,1)}, bf16[3,736,768]{2,1,0:T(8,128)(2,1)}) custom-call(bf16[256,256]{1,0:T(8,128)(2,1)} %get-tuple-element.164.pool_ref, bf16[480,256]{1,0:T(8,128)(2,1)} %bitcast.323, bf16[480,256]{1,0:T(8,128)(2,1)} %get-tuple-element.166.mixed_ref.o_ref, ...), custom_call_target="tpu_custom_call" | custom-call | flops 2894069760 | bytes 6782976 | tf_op jit(solution)/shard_map/pallas_call | solution.py:510
  157.0 13.3 %shard_map.189 = (bf16[736,768]{1,0:T(8,128)(2,1)}, f32[3,8,736]{2,1,0:T(8,128)}) custom-call(s32[1]{0:T(128)} %add.584.len_ref, bf16[3,736,768]{2,1,0:T(8,128)(2,1)} %get-tuple-element.167.q_ref.k_ref.v_ref, bf16[3,736,768]{2,1,0:T(8,128)(2,1)} %get-tuple-element.167.q_ref.k_ref.v_ref, bf16[3,736,768]{2,1,0:T(8,128)(2,1)} %get-tuple-element.167.q_ref.k_ref.v_ref), custom_call_target="tpu_custom_call" | custom-call | flops 6656360448 | bytes 4521984 | tf_op jit(solution)/shard_map/pallas_call | solution.py:361
  170.3 16.5 %shard_map.190 = (f32[736,768]{1,0:T(8,128)}, bf16[736,768]{1,0:T(8,128)(2,1)}, bf16[4,736,768]{2,1,0:T(8,128)(2,1)}, bf16[4,736,768]{2,1,0:T(8,128)(2,1)}) custom-call(bf16[736,768]{1,0:T(8,128)(2,1)} %get-tuple-element.168.mixed_ref.o_ref, f32[736,768]{1,0:T(8,128)} %get-tuple-element.169.embed_ref, ...), custom_call_target="tpu_custom_call" | custom-call | flops 4341104640 | bytes 15826944 | tf_op jit(solution)/shard_map/pallas_call | solution.py:567
  186.8 7.9 %shard_map.192 = (bf16[1536,768]{1,0:T(8,128)(2,1)}, bf16[1536,768]{1,0:T(8,128)(2,1)}) custom-call(s32[1]{0:T(128)} %bitcast.52.core_ref, bf16[4,736,768]{2,1,0:T(8,128)(2,1)} %get-tuple-element.170.act_ref, bf16[736,768]{1,0:T(8,128)(2,1)} %bitcast_select_fusion.gd_ref), custom_call_target="tpu_custom_call" | custom-call | flops 3472883712 | bytes 10174464 | tf_op jit(solution)/shard_map/pallas_call | solution.py:624
  198.5 16.7 %all-gather.5.cloned.1.call-done.w_ref = bf16[12,256,768]{2,1,0:T(8,128)(2,1)} async-done(((bf16[12,8,768]{2,1,0:T(8,128)(2,1)}), bf16[12,256,768]{2,1,0:T(8,128)(2,1)}) %all-gather.5.cloned.1.call-update) | async-done | bytes 4718608 | tf_op jit(solution)/shard_map/all_gather | solution.py:1026
  215.2 12.0 %shard_map.193 = (bf16[4,736,768]{2,1,0:T(8,128)(2,1)}, bf16[1536,768]{1,0:T(8,128)(2,1)}, bf16[1536,768]{1,0:T(8,128)(2,1)}) custom-call(s32[1]{0:T(128)} %bitcast.52.core_ref, bf16[736,768]{1,0:T(8,128)(2,1)} %bitcast_select_fusion.gd_ref, bf16[12,256,768]{2,1,0:T(8,128)(2,1)} %all-gather.5.cloned.1.call-done.w_ref, ...), custom_call_target="tpu_custom_call" | custom-call | flops 6945767424 | bytes 20348928 | tf_op jit(solution)/shard_map/pallas_call | solution.py:650
  232.8 14.3 %shard_map.194 = (f32[736,768]{1,0:T(8,128)}, bf16[736,768]{1,0:T(8,128)(2,1)}, bf16[384,768]{1,0:T(8,128)(2,1)}, bf16[384,768]{1,0:T(8,128)(2,1)}, f32[1,768]{1,0:T(1,128)}) custom-call(s32[1]{0:T(128)} %bitcast.52.core_ref, bf16[4,736,768]{2,1,0:T(8,128)(2,1)} %get-tuple-element.187.gpre_ref, ...), custom_call_target="tpu_custom_call" | custom-call | flops 5209325568 | bytes 18087936 | tf_op jit(solution)/shard_map/pallas_call | solution.py:690
  253.2 19.2 %shard_map.195.g_ref = bf16[3,736,768]{2,1,0:T(8,128)(2,1)} custom-call(s32[1]{0:T(128)} %add.584.len_ref, bf16[3,736,768]{2,1,0:T(8,128)(2,1)} %get-tuple-element.167.q_ref.k_ref.v_ref, bf16[3,736,768]{2,1,0:T(8,128)(2,1)} %get-tuple-element.167.q_ref.k_ref.v_ref, bf16[3,736,768]{2,1,0:T(8,128)(2,1)} %get-tuple-element.167.q_ref.k_ref.v_ref, ...), custom_call_target="tpu_custom_call" | custom-call | flops 13312720896 | bytes 9043968 | tf_op jit(solution)/shard_map/pallas_call | solution.py:423
  291.3 10.8 %shard_map.197 = (bf16[256,768]{1,0:T(8,128)(2,1)}, f32[480,256]{1,0:T(8,128)}, bf16[256,256]{1,0:T(8,128)(2,1)}, bf16[256,256]{1,0:T(8,128)(2,1)}, bf16[480,256]{1,0:T(8,128)(2,1)}, /*index=5*/f32[1,768]{1,0:T(1,128)}) custom-call(bf16[3,736,768]{2,1,0:T(8,128)(2,1)} %shard_map.195.g_ref, ...), custom_call_target="tpu_custom_call" | custom-call | flops 3183476736 | bytes 13565952 | tf_op jit(solution)/shard_map/pallas_call | solution.py:771
  307.2 11.5 %collective-permute-done.14 = bf16[12,4,8,768]{3,2,1,0:T(8,128)(2,1)S(1)} collective-permute-done((bf16[12,4,8,768]{3,2,1,0:T(8,128)(2,1)}, bf16[12,4,8,768]{3,2,1,0:T(8,128)(2,1)S(1)}, u32[]{:S(2)}, u32[]{:S(2)}) %collective-permute-start.14) | collective-permute-done | bytes 589856 | tf_op jit(solution)/shard_map/ppermute | solution.py:61
  326.5 27.7 %shard_map.198 = (bf16[480,256]{1,0:T(8,128)(2,1)}, bf16[4096,512]{1,0:T(8,128)(2,1)}) custom-call(bf16[480,256]{1,0:T(8,128)(2,1)} %fusion.6.q_ref, bf16[4096,512]{1,0:T(8,128)(2,1)} %get-tuple-element.165.k_ref.v_ref, bf16[4096,512]{1,0:T(8,128)(2,1)} %get-tuple-element.165.k_ref.v_ref, bf16[480,256]{1,0:T(8,128)(2,1)} %get-tuple-element.237.do_ref, ...), custom_call_target="tpu_custom_call" | custom-call | flops 20132659200 | bytes 8388608 | tf_op jit(solution)/shard_map/pallas_call | solution.py:302
  358.6 11.6 %collective-permute-done.19 = bf16[6,4,2,8,768]{4,3,1,0,2:T(8,128)(2,1)S(1)} collective-permute-done((bf16[6,4,2,8,768]{4,3,1,0,2:T(8,128)(2,1)}, bf16[6,4,2,8,768]{4,3,1,0,2:T(8,128)(2,1)S(1)}, u32[]{:S(2)}, u32[]{:S(2)}) %collective-permute-start.19) | collective-permute-done | bytes 589856 | tf_op jit(solution)/shard_map/ppermute | solution.py:61
  371.3 16.5 %shard_map.199 = (f32[4096,256]{1,0:T(8,128)}, bf16[4096,256]{1,0:T(8,128)(2,1)}, bf16[11,128,256]{2,1,0:T(8,128)(2,1)}, bf16[11,128,256]{2,1,0:T(8,128)(2,1)}) custom-call(s32[1]{0:T(128)} %bitcast.52.core_ref, bf16[4096,512]{1,0:T(8,128)(2,1)} %get-tuple-element.256.dkv_ref, bf16[4096,256]{1,0:T(8,128)(2,1)} %get-tuple-element.257.slope_ref, ...), custom_call_target="tpu_custom_call" | custom-call | flops 6979321856 | bytes 20971520 | tf_op jit(solution)/shard_map/pallas_call | solution.py:902
  410.9 10.4 %collective-permute-done.38 = bf16[24,8,768]{2,1,0:T(8,128)(2,1)} collective-permute-done((bf16[24,8,768]{2,1,0:T(8,128)(2,1)}, bf16[24,8,768]{2,1,0:T(8,128)(2,1)}, u32[]{:S(2)}, u32[]{:S(2)}) %collective-permute-start.38) | collective-permute-done | bytes 294944 | tf_op jit(solution)/shard_map/ppermute | solution.py:61
  423.8 11.1 %shard_map.200 = bf16[4096,256]{1,0:T(8,128)(2,1)} custom-call(bf16[4096,256]{1,0:T(8,128)(2,1)} %get-tuple-element.284.gz_ref, f32[4096,256]{1,0:T(8,128)} %get-tuple-element.285.d_hidden_ref, bf16[9,256,256]{2,1,0:T(8,128)(2,1)} %get-tuple-element.346.conv_ref), custom_call_target="tpu_custom_call" | custom-call | flops 4831838208 | bytes 8388608 | tf_op jit(solution)/shard_map/pallas_call | solution.py:966
  477.0 9.3 %shard_map.191 = f32[736,768]{1,0:T(8,128)} custom-call(bf16[4,736,768]{2,1,0:T(8,128)(2,1)} %get-tuple-element.170.act_ref, bf16[12,256,768]{2,1,0:T(8,128)(2,1)} %all-gather.5.cloned.1.call-done.w_ref, f32[736,768]{1,0:T(8,128)} %get-tuple-element.171.stream_ref), custom_call_target="tpu_custom_call" | custom-call | flops 3472883712 | bytes 13565952 | tf_op jit(solution)/shard_map/pallas_call | solution.py:602
  486.3 13.6 %collective-permute-done.33 = bf16[16,64,256]{2,1,0:T(8,128)(2,1)S(1)} collective-permute-done((bf16[16,64,256]{2,1,0:T(8,128)(2,1)}, bf16[16,64,256]{2,1,0:T(8,128)(2,1)S(1)}, u32[]{:S(2)}, u32[]{:S(2)}) %collective-permute-start.33) | collective-permute-done | bytes 524320 | tf_op jit(solution)/shard_map/ppermute | solution.py:61
  499.9 10.3 %collective-permute-done.32 = bf16[16,64,256]{2,1,0:T(8,128)(2,1)S(1)} collective-permute-done((bf16[16,64,256]{2,1,0:T(8,128)(2,1)}, bf16[16,64,256]{2,1,0:T(8,128)(2,1)S(1)}, u32[]{:S(2)}, u32[]{:S(2)}) %collective-permute-start.32) | collective-permute-done | bytes 524320 | tf_op jit(solution)/shard_map/ppermute | solution.py:61
  (279 shorter events, 181.6 us)
Async XLA Ops:
  10.0 44.9 %all-to-all-start = ((bf16[32,8,8,256]{3,2,1,0:T(8,128)(2,1)}), bf16[32,8,8,256]{3,2,1,0:T(8,128)(2,1)S(1)}, u32[]{:S(2)}, u32[]{:S(2)}) async-start(bf16[32,8,8,256]{3,2,1,0:T(8,128)(2,1)} %copy.190), calls=%async_computation | async-start | bytes 2097152 | tf_op jit(solution)/shard_map/all_to_all | solution.py:1010
  17.3 132.4 %all-gather.3.cloned.1.call-start = ((), (), s32[]{:S(2)}) async-start(), calls=%async_computation.2 | async-start | bytes 10137600 | tf_op jit(solution)/shard_map/all_gather | solution.py:1025
  18.4 24.4 %collective-permute-start = (bf16[16,64,256]{2,1,0:T(8,128)(2,1)S(1)}, bf16[16,64,256]{2,1,0:T(8,128)(2,1)S(1)}, u32[]{:S(2)}, u32[]{:S(2)}) collective-permute-start(bf16[16,64,256]{2,1,0:T(8,128)(2,1)S(1)} %get-tuple-element.336), channel_id=1, source_target_pairs={{0,1},{1,0},{2,3},{3,2},{4,5},{5,4},{6,7},{7,6},{8,9},{9,8},{10,11... | collective-permute-start | bytes 1572872 | tf_op jit(solution)/shard_map/ppermute | solution.py:61
  20.1 22.6 %collective-permute-start.1 = (bf16[16,64,256]{2,1,0:T(8,128)(2,1)S(1)}, bf16[16,64,256]{2,1,0:T(8,128)(2,1)S(1)}, u32[]{:S(2)}, u32[]{:S(2)}) collective-permute-start(bf16[16,64,256]{2,1,0:T(8,128)(2,1)S(1)} %get-tuple-element.338), channel_id=1, source_target_pairs={{0,2},{1,3},{2,0},{3,1},{4,6},{5,7},{6,4},{7,5},{8,10},{9,11},{10,... | collective-permute-start | bytes 1572872 | tf_op jit(solution)/shard_map/ppermute | solution.py:61
  21.6 33.3 %collective-permute-start.2 = (bf16[16,64,256]{2,1,0:T(8,128)(2,1)S(1)}, bf16[16,64,256]{2,1,0:T(8,128)(2,1)}, u32[]{:S(2)}, u32[]{:S(2)}) collective-permute-start(bf16[16,64,256]{2,1,0:T(8,128)(2,1)S(1)} %get-tuple-element.335), channel_id=1, source_target_pairs={{0,3},{1,2},{2,1},{3,0},{4,7},{5,6},{6,5},{7,4},{8,11},{9,10},{10,... | collective-permute-start | bytes 1572872 | tf_op jit(solution)/shard_map/ppermute | solution.py:61
  57.1 158.1 %all-gather.5.cloned.1.call-start = ((), (), s32[]{:S(2)}) async-start(), calls=%async_computation.3 | async-start | bytes 4866048 | tf_op jit(solution)/shard_map/all_gather | solution.py:1026
  198.2 29.0 %collective-permute-start.10 = (bf16[12,4,2,2,8,768]{5,4,1,0,2,3:T(8,128)(2,1)}, bf16[12,4,2,2,8,768]{5,4,1,0,2,3:T(8,128)(2,1)}, u32[]{:S(2)}, u32[]{:S(2)}) collective-permute-start(bf16[12,4,2,2,8,768]{5,4,1,0,2,3:T(8,128)(2,1)} %copy.195), channel_id=1, source_target_pairs={{0,4},{4,0},{1,5},{5,1},{2,6},{6,2},{3,7},{7,3},{8,12},{12,8},{9,1... | collective-permute-start | bytes 7077896 | tf_op jit(solution)/shard_map/ppermute | solution.py:61
  232.5 16.0 %collective-permute-start.11 = (bf16[12,4,2,2,8,768]{5,4,1,0,3,2:T(8,128)(2,1)}, bf16[12,4,2,2,8,768]{5,4,1,0,3,2:T(8,128)(2,1)}, u32[]{:S(2)}, u32[]{:S(2)}) collective-permute-start(bf16[12,4,2,2,8,768]{5,4,1,0,3,2:T(8,128)(2,1)} %copy.198), channel_id=1, source_target_pairs={{0,4},{4,0},{1,5},{5,1},{2,6},{6,2},{3,7},{7,3},{8,12},{12,8},{9,1... | collective-permute-start | bytes 7077896 | tf_op jit(solution)/shard_map/ppermute | solution.py:61
  247.1 28.4 %collective-permute-start.12 = (bf16[12,4,2,8,768]{4,3,1,0,2:T(8,128)(2,1)}, bf16[12,4,2,8,768]{4,3,1,0,2:T(8,128)(2,1)}, u32[]{:S(2)}, u32[]{:S(2)}) collective-permute-start(bf16[12,4,2,8,768]{4,3,1,0,2:T(8,128)(2,1)} %get-tuple-element.203), channel_id=1, source_target_pairs={{0,1},{1,0},{2,3},{3,2},{4,5},{5,4},{6,7},{7,6},{8,9},{9,8},{10,11... | collective-permute-start | bytes 3538952 | tf_op jit(solution)/shard_map/ppermute | solution.py:61
  251.9 32.9 %collective-permute-start.13 = (bf16[12,4,2,8,768]{4,3,1,0,2:T(8,128)(2,1)}, bf16[12,4,2,8,768]{4,3,1,0,2:T(8,128)(2,1)S(1)}, u32[]{:S(2)}, u32[]{:S(2)}) collective-permute-start(bf16[12,4,2,8,768]{4,3,1,0,2:T(8,128)(2,1)} %get-tuple-element.213), channel_id=1, source_target_pairs={{0,2},{2,0},{1,3},{3,1},{4,6},{6,4},{5,7},{7,5},{8,10},{10,8},{9,1... | collective-permute-start | bytes 3538952 | tf_op jit(solution)/shard_map/ppermute | solution.py:61
  288.0 32.2 %collective-permute-start.16 = (bf16[9,4,2,2,8,768]{5,4,1,0,2,3:T(8,128)(2,1)}, bf16[9,4,2,2,8,768]{5,4,1,0,2,3:T(8,128)(2,1)}, u32[]{:S(2)}, u32[]{:S(2)}) collective-permute-start(bf16[9,4,2,2,8,768]{5,4,1,0,2,3:T(8,128)(2,1)} %copy.206), channel_id=1, source_target_pairs={{0,4},{4,0},{1,5},{5,1},{2,6},{6,2},{3,7},{7,3},{8,12},{12,8},{9,1... | collective-permute-start | bytes 5308424 | tf_op jit(solution)/shard_map/ppermute | solution.py:61
  288.7 18.5 %collective-permute-start.15 = (bf16[12,4,8,768]{3,2,1,0:T(8,128)(2,1)}, bf16[12,4,8,768]{3,2,1,0:T(8,128)(2,1)}, u32[]{:S(2)}, u32[]{:S(2)}) collective-permute-start(bf16[12,4,8,768]{3,2,1,0:T(8,128)(2,1)} %get-tuple-element.230), channel_id=1, source_target_pairs={{0,2},{2,0},{1,3},{3,1},{4,6},{6,4},{5,7},{7,5},{8,10},{10,8},{9,1... | collective-permute-start | bytes 1769480 | tf_op jit(solution)/shard_map/ppermute | solution.py:61
  291.0 33.1 %collective-permute-start.17 = (bf16[3,4,2,2,8,768]{5,4,1,0,2,3:T(8,128)(2,1)}, bf16[3,4,2,2,8,768]{5,4,1,0,2,3:T(8,128)(2,1)}, u32[]{:S(2)}, u32[]{:S(2)}) collective-permute-start(bf16[3,4,2,2,8,768]{5,4,1,0,2,3:T(8,128)(2,1)} %copy.209), channel_id=1, source_target_pairs={{0,4},{4,0},{1,5},{5,1},{2,6},{6,2},{3,7},{7,3},{8,12},{12,8},{9,1... | collective-permute-start | bytes 1769480 | tf_op jit(solution)/shard_map/ppermute | solution.py:61
  326.4 31.3 %collective-permute-start.18 = (bf16[24,2,8,768]{3,2,1,0:T(8,128)(2,1)S(1)}, bf16[24,2,8,768]{3,2,1,0:T(8,128)(2,1)S(1)}, u32[]{:S(2)}, u32[]{:S(2)}) collective-permute-start(bf16[24,2,8,768]{3,2,1,0:T(8,128)(2,1)S(1)} %fusion.12), channel_id=1, source_target_pairs={{0,8},{8,0},{16,24},{24,16},{1,9},{9,1},{17,25},{25,17},{2,10},{10... | collective-permute-start | bytes 1769480 | tf_op jit(solution)/shard_map/ppermute | solution.py:61
  326.5 31.0 %collective-permute-start.21 = (bf16[2,4,2,2,8,768]{5,4,3,2,1,0:T(8,128)(2,1)}, bf16[2,4,2,2,8,768]{5,4,3,2,1,0:T(8,128)(2,1)S(1)}, u32[]{:S(2)}, u32[]{:S(2)}) collective-permute-start(bf16[2,4,2,2,8,768]{5,4,3,2,1,0:T(8,128)(2,1)} %get-tuple-element.254), channel_id=1, source_target_pairs={{0,4},{4,0},{1,5},{5,1},{2,6},{6,2},{3,7},{7,3},{8,12},{12,8},{9,1... | collective-permute-start | bytes 1179656 | tf_op jit(solution)/shard_map/ppermute | solution.py:61
  354.2 16.0 %collective-permute-start.19 = (bf16[6,4,2,8,768]{4,3,1,0,2:T(8,128)(2,1)}, bf16[6,4,2,8,768]{4,3,1,0,2:T(8,128)(2,1)S(1)}, u32[]{:S(2)}, u32[]{:S(2)}) collective-permute-start(bf16[6,4,2,8,768]{4,3,1,0,2:T(8,128)(2,1)} %get-tuple-element.250), channel_id=1, source_target_pairs={{0,1},{1,0},{2,3},{3,2},{4,5},{5,4},{6,7},{7,6},{8,9},{9,8},{10,11... | collective-permute-start | bytes 1769480 | tf_op jit(solution)/shard_map/ppermute | solution.py:61
  404.3 18.1 %collective-permute-start.25 = (bf16[13,4,2,2,8,256]{5,4,3,2,1,0:T(8,128)(2,1)}, bf16[13,4,2,2,8,256]{5,4,3,2,1,0:T(8,128)(2,1)}, u32[]{:S(2)}, u32[]{:S(2)}) collective-permute-start(bf16[13,4,2,2,8,256]{5,4,3,2,1,0:T(8,128)(2,1)} %pad_maximum_fusion.9), channel_id=1, source_target_pairs={{0,4},{4,0},{1,5},{5,1},{2,6},{6,2},{3,7},{7,3},{8,12},{12,8},{9,1... | collective-permute-start | bytes 2555912 | tf_op jit(solution)/shard_map/ppermute | solution.py:61
  404.3 17.1 %collective-permute-start.38 = (bf16[24,8,768]{2,1,0:T(8,128)(2,1)}, bf16[24,8,768]{2,1,0:T(8,128)(2,1)}, u32[]{:S(2)}, u32[]{:S(2)}) collective-permute-start(bf16[24,8,768]{2,1,0:T(8,128)(2,1)} %fusion.29), channel_id=1, source_target_pairs={{0,16},{8,24},{16,0},{24,8},{1,17},{9,25},{17,1},{25,9},{2,18},{10... | collective-permute-start | bytes 884744 | tf_op jit(solution)/shard_map/ppermute | solution.py:61
  408.1 30.4 %collective-permute-start.29 = (bf16[2,4,8,768]{3,2,1,0:T(8,128)(2,1)S(1)}, bf16[2,4,8,768]{3,2,1,0:T(8,128)(2,1)S(1)}, u32[]{:S(2)}, u32[]{:S(2)}) collective-permute-start(bf16[2,4,8,768]{3,2,1,0:T(8,128)(2,1)S(1)} %copy-done.20), channel_id=1, source_target_pairs={{0,2},{2,0},{1,3},{3,1},{4,6},{6,4},{5,7},{7,5},{8,10},{10,8},{9,1... | collective-permute-start | bytes 294920 | tf_op jit(solution)/shard_map/ppermute | solution.py:61
  409.4 29.1 %collective-permute-start.30 = (bf16[12,2,8,768]{3,2,1,0:T(8,128)(2,1)S(1)}, bf16[12,2,8,768]{3,2,1,0:T(8,128)(2,1)S(1)}, u32[]{:S(2)}, u32[]{:S(2)}) collective-permute-start(bf16[12,2,8,768]{3,2,1,0:T(8,128)(2,1)S(1)} %copy-done.18), channel_id=1, source_target_pairs={{0,8},{8,0},{16,24},{24,16},{1,9},{9,1},{17,25},{25,17},{2,10},{10... | collective-permute-start | bytes 884744 | tf_op jit(solution)/shard_map/ppermute | solution.py:61
  468.0 49.2 %all-to-all-start.1 = ((bf16[32,9,8,256]{3,2,1,0:T(8,128)(2,1)}), bf16[32,9,8,256]{3,2,1,0:T(8,128)(2,1)S(1)}, u32[]{:S(2)}, u32[]{:S(2)}) async-start(bf16[32,9,8,256]{3,2,1,0:T(8,128)(2,1)} %pad_maximum_fusion.6), calls=%async_computation.1 | async-start | bytes 2359296 | tf_op jit(solution)/shard_map/all_to_all | solution.py:1164
  473.3 26.6 %collective-permute-start.33 = (bf16[16,64,256]{2,1,0:T(8,128)(2,1)}, bf16[16,64,256]{2,1,0:T(8,128)(2,1)S(1)}, u32[]{:S(2)}, u32[]{:S(2)}) collective-permute-start(bf16[16,64,256]{2,1,0:T(8,128)(2,1)} %get-tuple-element.329), channel_id=1, source_target_pairs={{0,3},{1,2},{2,1},{3,0},{4,7},{5,6},{6,5},{7,4},{8,11},{9,10},{10,... | collective-permute-start | bytes 1572872 | tf_op jit(solution)/shard_map/ppermute | solution.py:61
  476.0 34.2 %collective-permute-start.32 = (bf16[16,64,256]{2,1,0:T(8,128)(2,1)}, bf16[16,64,256]{2,1,0:T(8,128)(2,1)S(1)}, u32[]{:S(2)}, u32[]{:S(2)}) collective-permute-start(bf16[16,64,256]{2,1,0:T(8,128)(2,1)} %get-tuple-element.330), channel_id=1, source_target_pairs={{0,2},{1,3},{2,0},{3,1},{4,6},{5,7},{6,4},{7,5},{8,10},{9,11},{10,... | collective-permute-start | bytes 1572872 | tf_op jit(solution)/shard_map/ppermute | solution.py:61
  476.6 34.0 %collective-permute-start.31 = (bf16[16,64,256]{2,1,0:T(8,128)(2,1)}, bf16[16,64,256]{2,1,0:T(8,128)(2,1)S(1)}, u32[]{:S(2)}, u32[]{:S(2)}) collective-permute-start(bf16[16,64,256]{2,1,0:T(8,128)(2,1)} %get-tuple-element.331), channel_id=1, source_target_pairs={{0,1},{1,0},{2,3},{3,2},{4,5},{5,4},{6,7},{7,6},{8,9},{9,8},{10,11... | collective-permute-start | bytes 1572872 | tf_op jit(solution)/shard_map/ppermute | solution.py:61
  (52 other events, 474.6 us)
Sparse Core Ops, SparseCore 0:
  57.2 92.4 all-gather.2
  152.5 62.6 all-gather.4

commit v6 on v5

--- a/solution.py
+++ b/solution.py
@@ -101,8 +101,8 @@
 
 
 def hold(values, *sums):
-    tied = lax.optimization_barrier((tuple(values), tuple(parts[0] for parts in sums)))
-    return tied[0] + tuple([keep] + parts[1:] for keep, parts in zip(tied[1], sums))
+    tied = lax.optimization_barrier((tuple(values), tuple(tuple(parts) for parts in sums)))
+    return tied[0] + tuple(list(parts) for parts in tied[1])
 
 
 def gather_axes(values, axes):
@@ -1076,11 +1076,13 @@
     emb_g, gupd, pool_g, out_g, gox, gain_g_one = embed_grad(
         gqkv, weights, embed, d_stream, seq, cross_mixed, to_out, gain_one
     )
+    gox, gupd, emb_g, gain_g_one, qkv, up, down = hold(
+        (gox, gupd, emb_g, gain_g_one), qkv, up, down
+    )
     gains = jnp.concatenate([gain_g_one, gain_g_two], 0).reshape(devices, 1, -1)
     gain_count = gains.shape[-1]
     gains = jnp.pad(gains, ((0, 0), (0, rows - 1), (0, D - gain_count))).astype(bf16)
     emb = cut_core(jnp.concatenate([emb_g, gains.reshape(CH, D)], 0))
-    gox, gupd, emb, qkv, up, down = hold((gox, gupd, emb), qkv, up, down)
     mlp = advance_near([jnp.concatenate(part, 0) for part in zip(up, down)])
     first = advance([part[:6] for part in qkv], "x", 3)
     second = advance([jnp.concatenate([p[6:], q], 0) for p, q in zip(qkv, att)], "y", 2)
@@ -1104,13 +1106,14 @@
     d_hidden, gz, token_keep, token_give = token_backward(
         gkv, slope_z, pool_g, hidden_b, wide, kv_weight
     )
-    early = [
-        jnp.concatenate([token[:9], q.reshape(1, CH // 2, CH), token[9:], o.reshape(1, CH // 2, CH)], 0)
-        for token, q, o in zip((token_keep, token_give), query_g, out_g)
-    ]
-    d_hidden, early, mlp, first, second, emb = hold(
-        (d_hidden, core_parts(early)), mlp, first, second, emb
-    )
+    d_hidden, token_keep, token_give, mlp, first, second, emb = hold(
+        (d_hidden, token_keep, token_give), mlp, first, second, emb
+    )
+    early = []
+    for token, q, o in zip((token_keep, token_give), query_g, out_g):
+        q, o = (part.reshape(1, CH // 2, CH) for part in (q, o))
+        early.append(jnp.concatenate([token[:9], q, token[9:], o], 0))
+    early = core_parts(early)
     att = advance_near([jnp.concatenate(part, 0) for part in zip(first, second)])
     emb = advance(emb, "y", 2)
     early, att, emb = tie((early, att, emb))
@@ -1161,6 +1164,7 @@
     mine = mine.reshape(devices, slot_count, rows, CH)
     share = jnp.broadcast_to(share[None, None], (devices, 1, rows, CH))
     mine = jnp.concatenate([mine, share], 1)
+    mine, act, pieces[-1] = tie((mine, act, pieces[-1]))
     mine = lax.all_to_all(mine, AXES, split_axis=0, concat_axis=0, tiled=True)
     block_out = down_forward(act, w_down, stream)
     shares = mine[:, slot_count, :2].astype(f32)

time: 539 us -> 475 us (0.88)
  waiting for transfers between devices: 167 us -> 106 us
    ppermute x39, waiting for transfers between devices: 125 us -> 69.4 us  [xor_permute(): return lax.ppermute(values, axes, [(i, i ^ mask) for i in range(count)])]
    all_gather x1, waiting for transfers between devices: 24.5 us -> 18.9 us  [local(): weights = lax.all_gather(weights, AXES, axis=1, tiled=True)]
  transfers between devices with their start and end apart: 43 -> 43, of which waited for: 23 -> 13; matrix products, arithmetic and copies ran while one was open for 11% -> 10% of each run, Pallas kernels for 35% -> 44%
where the time goes in v6:
time: 475 us; the launch traced here: 470 us
  Pallas kernels  206 us (43%)
  waiting for transfers between devices  106 us (22%)
  starting transfers between devices  51.1 us (11%)
  other arithmetic  49.6 us (10%)
  local copies, waits for them, and re-layouts  35.3 us (7%)
  between operations  19.3 us (4%)
    ppermute x39, waiting for transfers between devices, xor_permute(): return lax.ppermute(values, axes, [(i, i ^ mask) for i in range(count)])  69.4 us
    ppermute x39, starting transfers between devices, xor_permute(): return lax.ppermute(values, axes, [(i, i ^ mask) for i in range(count)])  40.7 us
    pallas_call x1, Pallas kernels, cross_backward(): pl.pallas_call(cross_backward_kernel, grid=(cells // block,), in_specs=[p...  27.7 us
    pallas_call x1, Pallas kernels, self_backward(): pl.pallas_call(self_backward_kernel, grid_spec=pltpu.PrefetchScalarGridSp...  19.3 us
    all_gather x1, waiting for transfers between devices, local(): weights = lax.all_gather(weights, AXES, axis=1, tiled=True)  18.9 us
    pallas_call x1, Pallas kernels, cross_forward(): pl.pallas_call(cross_forward_kernel, grid=(2,), in_specs=[pl.BlockSpec((r...  16.9 us
    all_gather x1, waiting for transfers between devices, local(): w_down = lax.all_gather(from_tiles(down, 12, 1), AXES, axis=1, tiled=True)  16.7 us
    pallas_call x1, Pallas kernels, up_forward(): pl.pallas_call(up_kernel, grid=(4,), in_specs=[full(SEQ, D), full(SEQ, D)...  16.5 us
  transfers between devices with their start and end apart: 43, of which 13 were waited for; matrix products, arithmetic and copies ran while one was open for 10% of the time, Pallas kernels for 44%

profile of v6, /device:TPU:0, one launch (start us, length us, event | category | flops | bytes accessed | tf_op | source)
XLA Modules:
  0.0 470.0 jit_solution(5146660526716044478)
XLA Ops:
  10.0 7.3 %all-to-all-start = ((bf16[32,8,8,256]{3,2,1,0:T(8,128)(2,1)}), bf16[32,8,8,256]{3,2,1,0:T(8,128)(2,1)S(1)}, u32[]{:S(2)}, u32[]{:S(2)}) async-start(bf16[32,8,8,256]{3,2,1,0:T(8,128)(2,1)} %copy.190), calls=%async_computation | async-start | bytes 2097152 | tf_op jit(solution)/shard_map/all_to_all | solution.py:1010
  24.6 18.1 %collective-permute-done = bf16[16,64,256]{2,1,0:T(8,128)(2,1)S(1)} collective-permute-done((bf16[16,64,256]{2,1,0:T(8,128)(2,1)S(1)}, bf16[16,64,256]{2,1,0:T(8,128)(2,1)S(1)}, u32[]{:S(2)}, u32[]{:S(2)}) %collective-permute-start) | collective-permute-done | bytes 524320 | tf_op jit(solution)/shard_map/ppermute | solution.py:61
  43.6 11.3 %collective-permute-done.2 = bf16[16,64,256]{2,1,0:T(8,128)(2,1)} collective-permute-done((bf16[16,64,256]{2,1,0:T(8,128)(2,1)S(1)}, bf16[16,64,256]{2,1,0:T(8,128)(2,1)}, u32[]{:S(2)}, u32[]{:S(2)}) %collective-permute-start.2) | collective-permute-done | bytes 524320 | tf_op jit(solution)/shard_map/ppermute | solution.py:61
  93.6 15.8 %shard_map.186 = (bf16[4096,256]{1,0:T(8,128)(2,1)}, bf16[4096,256]{1,0:T(8,128)(2,1)}, bf16[4096,512]{1,0:T(8,128)(2,1)}, bf16[256,256]{1,0:T(8,128)(2,1)}) custom-call(bf16[4224,768]{1,0:T(8,128)(2,1)} %bitcast.297, bf16[3,768,256]{2,1,0:T(8,128)(2,1)} %bitcast.325, bf16[256,512]{1,0:T(8,128)(2,1)} %pad_maximum_fusion.14.kv_w_ref), custom_call_target="tpu_custom_call" | custom-call | flops 5905580032 | bytes 14680064 | tf_op jit(solution)/shard_map/pallas_call | solution.py:839
  109.4 16.9 %shard_map.187 = (bf16[480,256]{1,0:T(8,128)(2,1)}, f32[2,8,240]{2,1,0:T(8,128)}) custom-call(bf16[480,256]{1,0:T(8,128)(2,1)} %fusion.6.q_ref, bf16[4096,512]{1,0:T(8,128)(2,1)} %get-tuple-element.190.k_ref.v_ref, bf16[4096,512]{1,0:T(8,128)(2,1)} %get-tuple-element.190.k_ref.v_ref), custom_call_target="tpu_custom_call" | custom-call | flops 8053063680 | bytes 8388608 | tf_op jit(solution)/shard_map/pallas_call | solution.py:226
  126.3 18.9 %all-gather.3.cloned.1.call-done.emb_ref.w_ref.att_ref = bf16[25,256,768]{2,1,0:T(8,128)(2,1)} async-done(((bf16[25,8,768]{2,1,0:T(8,128)(2,1)}), bf16[25,256,768]{2,1,0:T(8,128)(2,1)}) %all-gather.3.cloned.1.call-update) | async-done | bytes 9830416 | tf_op jit(solution)/shard_map/all_gather | solution.py:1025
  145.2 7.3 %shard_map.188 = (bf16[736,256]{1,0:T(8,128)(2,1)}, f32[736,768]{1,0:T(8,128)}, bf16[736,768]{1,0:T(8,128)(2,1)}, bf16[3,736,768]{2,1,0:T(8,128)(2,1)}) custom-call(bf16[256,256]{1,0:T(8,128)(2,1)} %get-tuple-element.189.pool_ref, bf16[480,256]{1,0:T(8,128)(2,1)} %bitcast.319, bf16[480,256]{1,0:T(8,128)(2,1)} %get-tuple-element.191.mixed_ref.o_ref, ...), custom_call_target="tpu_custom_call" | custom-call | flops 2894069760 | bytes 6782976 | tf_op jit(solution)/shard_map/pallas_call | solution.py:510
  152.6 13.3 %shard_map.189 = (bf16[736,768]{1,0:T(8,128)(2,1)}, f32[3,8,736]{2,1,0:T(8,128)}) custom-call(s32[1]{0:T(128)} %add.584.len_ref, bf16[3,736,768]{2,1,0:T(8,128)(2,1)} %get-tuple-element.192.q_ref.k_ref.v_ref, bf16[3,736,768]{2,1,0:T(8,128)(2,1)} %get-tuple-element.192.q_ref.k_ref.v_ref, bf16[3,736,768]{2,1,0:T(8,128)(2,1)} %get-tuple-element.192.q_ref.k_ref.v_ref), custom_call_target="tpu_custom_call" | custom-call | flops 6656360448 | bytes 4521984 | tf_op jit(solution)/shard_map/pallas_call | solution.py:361
  165.8 16.5 %shard_map.190 = (f32[736,768]{1,0:T(8,128)}, bf16[736,768]{1,0:T(8,128)(2,1)}, bf16[4,736,768]{2,1,0:T(8,128)(2,1)}, bf16[4,736,768]{2,1,0:T(8,128)(2,1)}) custom-call(bf16[736,768]{1,0:T(8,128)(2,1)} %get-tuple-element.194.mixed_ref.o_ref, f32[736,768]{1,0:T(8,128)} %get-tuple-element.195.embed_ref, ...), custom_call_target="tpu_custom_call" | custom-call | flops 4341104640 | bytes 15826944 | tf_op jit(solution)/shard_map/pallas_call | solution.py:567
  182.3 7.9 %shard_map.191 = (bf16[1536,768]{1,0:T(8,128)(2,1)}, bf16[1536,768]{1,0:T(8,128)(2,1)}) custom-call(s32[1]{0:T(128)} %bitcast.48.core_ref, bf16[4,736,768]{2,1,0:T(8,128)(2,1)} %get-tuple-element.354.act_ref, bf16[736,768]{1,0:T(8,128)(2,1)} %bitcast_select_fusion.gd_ref), custom_call_target="tpu_custom_call" | custom-call | flops 3472883712 | bytes 10174464 | tf_op jit(solution)/shard_map/pallas_call | solution.py:624
  194.0 16.7 %all-gather.5.cloned.1.call-done.w_ref = bf16[12,256,768]{2,1,0:T(8,128)(2,1)} async-done(((bf16[12,8,768]{2,1,0:T(8,128)(2,1)}), bf16[12,256,768]{2,1,0:T(8,128)(2,1)}) %all-gather.5.cloned.1.call-update) | async-done | bytes 4718608 | tf_op jit(solution)/shard_map/all_gather | solution.py:1026
  210.7 11.9 %shard_map.192 = (bf16[4,736,768]{2,1,0:T(8,128)(2,1)}, bf16[1536,768]{1,0:T(8,128)(2,1)}, bf16[1536,768]{1,0:T(8,128)(2,1)}) custom-call(s32[1]{0:T(128)} %bitcast.48.core_ref, bf16[736,768]{1,0:T(8,128)(2,1)} %bitcast_select_fusion.gd_ref, bf16[12,256,768]{2,1,0:T(8,128)(2,1)} %all-gather.5.cloned.1.call-done.w_ref, ...), custom_call_target="tpu_custom_call" | custom-call | flops 6945767424 | bytes 20348928 | tf_op jit(solution)/shard_map/pallas_call | solution.py:650
  222.7 3.6 fusion.3
  229.7 14.3 %shard_map.193 = (f32[736,768]{1,0:T(8,128)}, bf16[736,768]{1,0:T(8,128)(2,1)}, bf16[384,768]{1,0:T(8,128)(2,1)}, bf16[384,768]{1,0:T(8,128)(2,1)}, f32[1,768]{1,0:T(1,128)}) custom-call(s32[1]{0:T(128)} %bitcast.48.core_ref, bf16[4,736,768]{2,1,0:T(8,128)(2,1)} %get-tuple-element.212.gpre_ref, ...), custom_call_target="tpu_custom_call" | custom-call | flops 5209325568 | bytes 18087936 | tf_op jit(solution)/shard_map/pallas_call | solution.py:690
  248.9 19.3 %shard_map.194.g_ref = bf16[3,736,768]{2,1,0:T(8,128)(2,1)} custom-call(s32[1]{0:T(128)} %add.584.len_ref, bf16[3,736,768]{2,1,0:T(8,128)(2,1)} %get-tuple-element.192.q_ref.k_ref.v_ref, bf16[3,736,768]{2,1,0:T(8,128)(2,1)} %get-tuple-element.192.q_ref.k_ref.v_ref, bf16[3,736,768]{2,1,0:T(8,128)(2,1)} %get-tuple-element.192.q_ref.k_ref.v_ref, ...), custom_call_target="tpu_custom_call" | custom-call | flops 13312720896 | bytes 9043968 | tf_op jit(solution)/shard_map/pallas_call | solution.py:423
  269.7 6.8 %shard_map.195 = (bf16[1152,768]{1,0:T(8,128)(2,1)}, bf16[1152,768]{1,0:T(8,128)(2,1)}) custom-call(s32[1]{0:T(128)} %bitcast.48.core_ref, bf16[736,768]{1,0:T(8,128)(2,1)} %get-tuple-element.234.normed_ref, bf16[3,736,768]{2,1,0:T(8,128)(2,1)} %shard_map.194.g_ref), custom_call_target="tpu_custom_call" | custom-call | flops 2604662784 | bytes 7913472 | tf_op jit(solution)/shard_map/pallas_call | solution.py:727
  283.2 10.9 %shard_map.196 = (bf16[256,768]{1,0:T(8,128)(2,1)}, f32[480,256]{1,0:T(8,128)}, bf16[256,256]{1,0:T(8,128)(2,1)}, bf16[256,256]{1,0:T(8,128)(2,1)}, bf16[480,256]{1,0:T(8,128)(2,1)}, /*index=5*/f32[1,768]{1,0:T(1,128)}) custom-call(bf16[3,736,768]{2,1,0:T(8,128)(2,1)} %shard_map.194.g_ref, ...), custom_call_target="tpu_custom_call" | custom-call | flops 3183476736 | bytes 13565952 | tf_op jit(solution)/shard_map/pallas_call | solution.py:771
  308.5 27.7 %shard_map.197 = (bf16[480,256]{1,0:T(8,128)(2,1)}, bf16[4096,512]{1,0:T(8,128)(2,1)}) custom-call(bf16[480,256]{1,0:T(8,128)(2,1)} %fusion.6.q_ref, bf16[4096,512]{1,0:T(8,128)(2,1)} %get-tuple-element.190.k_ref.v_ref, bf16[4096,512]{1,0:T(8,128)(2,1)} %get-tuple-element.190.k_ref.v_ref, bf16[480,256]{1,0:T(8,128)(2,1)} %get-tuple-element.270.do_ref, ...), custom_call_target="tpu_custom_call" | custom-call | flops 20132659200 | bytes 8388608 | tf_op jit(solution)/shard_map/pallas_call | solution.py:302
  344.2 16.4 %shard_map.198 = (f32[4096,256]{1,0:T(8,128)}, bf16[4096,256]{1,0:T(8,128)(2,1)}, bf16[11,128,256]{2,1,0:T(8,128)(2,1)}, bf16[11,128,256]{2,1,0:T(8,128)(2,1)}) custom-call(s32[1]{0:T(128)} %bitcast.48.core_ref, bf16[4096,512]{1,0:T(8,128)(2,1)} %get-tuple-element.293.dkv_ref, bf16[4096,256]{1,0:T(8,128)(2,1)} %get-tuple-element.294.slope_ref, ...), custom_call_target="tpu_custom_call" | custom-call | flops 6979321856 | bytes 20971520 | tf_op jit(solution)/shard_map/pallas_call | solution.py:902
  375.3 11.1 %shard_map.199 = bf16[4096,256]{1,0:T(8,128)(2,1)} custom-call(bf16[4096,256]{1,0:T(8,128)(2,1)} %get-tuple-element.326.gz_ref, f32[4096,256]{1,0:T(8,128)} %get-tuple-element.327.d_hidden_ref, bf16[9,256,256]{2,1,0:T(8,128)(2,1)} %get-tuple-element.396.conv_ref), custom_call_target="tpu_custom_call" | custom-call | flops 4831838208 | bytes 8388608 | tf_op jit(solution)/shard_map/pallas_call | solution.py:966
  395.6 5.6 %collective-permute-done.33 = bf16[19,8,256]{2,1,0:T(8,128)(2,1)S(1)} collective-permute-done((bf16[19,8,256]{2,1,0:T(8,128)(2,1)S(1)}, bf16[19,8,256]{2,1,0:T(8,128)(2,1)S(1)}, u32[]{:S(2)}, u32[]{:S(2)}) %collective-permute-start.33) | collective-permute-done | bytes 77856 | tf_op jit(solution)/shard_map/ppermute | solution.py:61
  413.6 22.4 %collective-permute-done.37 = bf16[16,64,256]{2,1,0:T(8,128)(2,1)} collective-permute-done((bf16[16,64,256]{2,1,0:T(8,128)(2,1)S(1)}, bf16[16,64,256]{2,1,0:T(8,128)(2,1)}, u32[]{:S(2)}, u32[]{:S(2)}) %collective-permute-start.37) | collective-permute-done | bytes 524320 | tf_op jit(solution)/shard_map/ppermute | solution.py:61
  443.9 9.4 %shard_map.200 = f32[736,768]{1,0:T(8,128)} custom-call(bf16[4,736,768]{2,1,0:T(8,128)(2,1)} %get-tuple-element.354.act_ref, bf16[12,256,768]{2,1,0:T(8,128)(2,1)} %all-gather.5.cloned.1.call-done.w_ref, f32[736,768]{1,0:T(8,128)} %get-tuple-element.213.stream_ref), custom_call_target="tpu_custom_call" | custom-call | flops 3472883712 | bytes 13565952 | tf_op jit(solution)/shard_map/pallas_call | solution.py:602
  455.5 6.2 %subtract_select_fusion = (f32[8,256,256]{2,1,0:T(8,128)}, f32[8,256,256]{2,1,0:T(8,128)}, f32[8,256,256]{2,1,0:T(8,128)}) fusion(f32[8,256,256]{2,1,0:T(8,128)S(1)} %copy-done, pred[8]{0:T(512)(128)(4,1)S(1)} %compare_bitcast_fusion, f32[8,256,256]{2,1,0:T(8,128)} %param.17, f32[8,256,256]{2,1,0:T(8,128)} %param.18, ...), kind=kLoop, calls=%fused_computation.19 | loop fusion | flops 10485760 | bytes 13632004 | tf_op jit(solution)/shard_map/jit(_where)/select_n | solution.py:1191
  (312 shorter events, 134.9 us)
Async XLA Ops:
  10.0 44.9 %all-to-all-start = ((bf16[32,8,8,256]{3,2,1,0:T(8,128)(2,1)}), bf16[32,8,8,256]{3,2,1,0:T(8,128)(2,1)S(1)}, u32[]{:S(2)}, u32[]{:S(2)}) async-start(bf16[32,8,8,256]{3,2,1,0:T(8,128)(2,1)} %copy.190), calls=%async_computation | async-start | bytes 2097152 | tf_op jit(solution)/shard_map/all_to_all | solution.py:1010
  17.3 127.9 %all-gather.3.cloned.1.call-start = ((), (), s32[]{:S(2)}) async-start(), calls=%async_computation.2 | async-start | bytes 10137600 | tf_op jit(solution)/shard_map/all_gather | solution.py:1025
  18.4 24.4 %collective-permute-start = (bf16[16,64,256]{2,1,0:T(8,128)(2,1)S(1)}, bf16[16,64,256]{2,1,0:T(8,128)(2,1)S(1)}, u32[]{:S(2)}, u32[]{:S(2)}) collective-permute-start(bf16[16,64,256]{2,1,0:T(8,128)(2,1)S(1)} %get-tuple-element.386), channel_id=1, source_target_pairs={{0,1},{1,0},{2,3},{3,2},{4,5},{5,4},{6,7},{7,6},{8,9},{9,8},{10,11... | collective-permute-start | bytes 1572872 | tf_op jit(solution)/shard_map/ppermute | solution.py:61
  20.1 22.6 %collective-permute-start.1 = (bf16[16,64,256]{2,1,0:T(8,128)(2,1)S(1)}, bf16[16,64,256]{2,1,0:T(8,128)(2,1)S(1)}, u32[]{:S(2)}, u32[]{:S(2)}) collective-permute-start(bf16[16,64,256]{2,1,0:T(8,128)(2,1)S(1)} %get-tuple-element.388), channel_id=1, source_target_pairs={{0,2},{1,3},{2,0},{3,1},{4,6},{5,7},{6,4},{7,5},{8,10},{9,11},{10,... | collective-permute-start | bytes 1572872 | tf_op jit(solution)/shard_map/ppermute | solution.py:61
  21.6 33.3 %collective-permute-start.2 = (bf16[16,64,256]{2,1,0:T(8,128)(2,1)S(1)}, bf16[16,64,256]{2,1,0:T(8,128)(2,1)}, u32[]{:S(2)}, u32[]{:S(2)}) collective-permute-start(bf16[16,64,256]{2,1,0:T(8,128)(2,1)S(1)} %get-tuple-element.385), channel_id=1, source_target_pairs={{0,3},{1,2},{2,1},{3,0},{4,7},{5,6},{6,5},{7,4},{8,11},{9,10},{10,... | collective-permute-start | bytes 1572872 | tf_op jit(solution)/shard_map/ppermute | solution.py:61
  57.1 153.6 %all-gather.5.cloned.1.call-start = ((), (), s32[]{:S(2)}) async-start(), calls=%async_computation.3 | async-start | bytes 4866048 | tf_op jit(solution)/shard_map/all_gather | solution.py:1026
  193.8 28.9 %collective-permute-start.10 = (bf16[12,4,2,2,8,768]{5,4,1,0,2,3:T(8,128)(2,1)}, bf16[12,4,2,2,8,768]{5,4,1,0,2,3:T(8,128)(2,1)}, u32[]{:S(2)}, u32[]{:S(2)}) collective-permute-start(bf16[12,4,2,2,8,768]{5,4,1,0,2,3:T(8,128)(2,1)} %copy.194), channel_id=1, source_target_pairs={{0,4},{4,0},{1,5},{5,1},{2,6},{6,2},{3,7},{7,3},{8,12},{12,8},{9,1... | collective-permute-start | bytes 7077896 | tf_op jit(solution)/shard_map/ppermute | solution.py:61
  228.2 40.0 %collective-permute-start.12 = (bf16[12,4,2,8,768]{4,3,1,0,2:T(8,128)(2,1)}, bf16[12,4,2,8,768]{4,3,1,0,2:T(8,128)(2,1)S(1)}, u32[]{:S(2)}, u32[]{:S(2)}) collective-permute-start(bf16[12,4,2,8,768]{4,3,1,0,2:T(8,128)(2,1)} %get-tuple-element.227), channel_id=1, source_target_pairs={{0,1},{1,0},{2,3},{3,2},{4,5},{5,4},{6,7},{7,6},{8,9},{9,8},{10,11... | collective-permute-start | bytes 3538952 | tf_op jit(solution)/shard_map/ppermute | solution.py:61
  247.6 20.7 %collective-permute-start.13 = (bf16[3,4,2,2,8,768]{5,4,1,0,2,3:T(8,128)(2,1)S(1)}, bf16[3,4,2,2,8,768]{5,4,1,0,2,3:T(8,128)(2,1)S(1)}, u32[]{:S(2)}, u32[]{:S(2)}) collective-permute-start(bf16[3,4,2,2,8,768]{5,4,1,0,2,3:T(8,128)(2,1)S(1)} %copy.200), channel_id=1, source_target_pairs={{0,4},{4,0},{1,5},{5,1},{2,6},{6,2},{3,7},{7,3},{8,12},{12,8},{9,1... | collective-permute-start | bytes 1769480 | tf_op jit(solution)/shard_map/ppermute | solution.py:61
  247.6 28.9 %collective-permute-start.14 = (bf16[12,4,2,8,768]{4,3,1,0,2:T(8,128)(2,1)}, bf16[12,4,2,8,768]{4,3,1,0,2:T(8,128)(2,1)}, u32[]{:S(2)}, u32[]{:S(2)}) collective-permute-start(bf16[12,4,2,8,768]{4,3,1,0,2:T(8,128)(2,1)} %get-tuple-element.238), channel_id=1, source_target_pairs={{0,2},{2,0},{1,3},{3,1},{4,6},{6,4},{5,7},{7,5},{8,10},{10,8},{9,1... | collective-permute-start | bytes 3538952 | tf_op jit(solution)/shard_map/ppermute | solution.py:61
  280.8 16.7 %collective-permute-start.15 = (bf16[9,4,2,2,8,768]{5,4,1,0,2,3:T(8,128)(2,1)}, bf16[9,4,2,2,8,768]{5,4,1,0,2,3:T(8,128)(2,1)S(1)}, u32[]{:S(2)}, u32[]{:S(2)}) collective-permute-start(bf16[9,4,2,2,8,768]{5,4,1,0,2,3:T(8,128)(2,1)} %copy.201), channel_id=1, source_target_pairs={{0,4},{4,0},{1,5},{5,1},{2,6},{6,2},{3,7},{7,3},{8,12},{12,8},{9,1... | collective-permute-start | bytes 5308424 | tf_op jit(solution)/shard_map/ppermute | solution.py:61
  306.4 29.8 %collective-permute-start.18 = (bf16[24,2,8,768]{3,2,1,0:T(8,128)(2,1)S(1)}, bf16[24,2,8,768]{3,2,1,0:T(8,128)(2,1)S(1)}, u32[]{:S(2)}, u32[]{:S(2)}) collective-permute-start(bf16[24,2,8,768]{3,2,1,0:T(8,128)(2,1)S(1)} %fusion.12), channel_id=1, source_target_pairs={{0,8},{8,0},{16,24},{24,16},{1,9},{9,1},{17,25},{25,17},{2,10},{10... | collective-permute-start | bytes 1769480 | tf_op jit(solution)/shard_map/ppermute | solution.py:61
  306.5 29.7 %collective-permute-start.19 = (bf16[6,4,2,8,768]{4,3,1,0,2:T(8,128)(2,1)S(1)}, bf16[6,4,2,8,768]{4,3,1,0,2:T(8,128)(2,1)S(1)}, u32[]{:S(2)}, u32[]{:S(2)}) collective-permute-start(bf16[6,4,2,8,768]{4,3,1,0,2:T(8,128)(2,1)S(1)} %get-tuple-element.277), channel_id=1, source_target_pairs={{0,1},{1,0},{2,3},{3,2},{4,5},{5,4},{6,7},{7,6},{8,9},{9,8},{10,11... | collective-permute-start | bytes 1769480 | tf_op jit(solution)/shard_map/ppermute | solution.py:61
  307.4 28.8 %collective-permute-start.20 = (bf16[6,4,2,8,768]{4,3,1,0,2:T(8,128)(2,1)S(1)}, bf16[6,4,2,8,768]{4,3,1,0,2:T(8,128)(2,1)S(1)}, u32[]{:S(2)}, u32[]{:S(2)}) collective-permute-start(bf16[6,4,2,8,768]{4,3,1,0,2:T(8,128)(2,1)S(1)} %get-tuple-element.279), channel_id=1, source_target_pairs={{0,2},{2,0},{1,3},{3,1},{4,6},{6,4},{5,7},{7,5},{8,10},{10,8},{9,1... | collective-permute-start | bytes 1769480 | tf_op jit(solution)/shard_map/ppermute | solution.py:61
  308.5 27.7 %collective-permute-start.21 = (bf16[2,4,2,2,8,768]{5,4,3,2,1,0:T(8,128)(2,1)S(1)}, bf16[2,4,2,2,8,768]{5,4,3,2,1,0:T(8,128)(2,1)}, u32[]{:S(2)}, u32[]{:S(2)}) collective-permute-start(bf16[2,4,2,2,8,768]{5,4,3,2,1,0:T(8,128)(2,1)S(1)} %get-tuple-element.281), channel_id=1, source_target_pairs={{0,4},{4,0},{1,5},{5,1},{2,6},{6,2},{3,7},{7,3},{8,12},{12,8},{9,1... | collective-permute-start | bytes 1179656 | tf_op jit(solution)/shard_map/ppermute | solution.py:61
  339.2 21.5 %collective-permute-start.25 = (bf16[2,4,2,8,768]{4,3,1,0,2:T(8,128)(2,1)S(1)}, bf16[2,4,2,8,768]{4,3,1,0,2:T(8,128)(2,1)S(1)}, u32[]{:S(2)}, u32[]{:S(2)}) collective-permute-start(bf16[2,4,2,8,768]{4,3,1,0,2:T(8,128)(2,1)S(1)} %copy.212), channel_id=1, source_target_pairs={{0,1},{1,0},{2,3},{3,2},{4,5},{5,4},{6,7},{7,6},{8,9},{9,8},{10,11... | collective-permute-start | bytes 589832 | tf_op jit(solution)/shard_map/ppermute | solution.py:61
  340.4 20.3 %collective-permute-start.22 = (bf16[24,8,768]{2,1,0:T(8,128)(2,1)S(1)}, bf16[24,8,768]{2,1,0:T(8,128)(2,1)S(1)}, u32[]{:S(2)}, u32[]{:S(2)}) collective-permute-start(bf16[24,8,768]{2,1,0:T(8,128)(2,1)S(1)} %fusion.29), channel_id=1, source_target_pairs={{0,16},{8,24},{16,0},{24,8},{1,17},{9,25},{17,1},{25,9},{2,18},{10... | collective-permute-start | bytes 884744 | tf_op jit(solution)/shard_map/ppermute | solution.py:61
  342.1 18.6 %collective-permute-start.23 = (bf16[6,4,8,768]{3,2,1,0:T(8,128)(2,1)S(1)}, bf16[6,4,8,768]{3,2,1,0:T(8,128)(2,1)S(1)}, u32[]{:S(2)}, u32[]{:S(2)}) collective-permute-start(bf16[6,4,8,768]{3,2,1,0:T(8,128)(2,1)S(1)} %get-tuple-element.304), channel_id=1, source_target_pairs={{0,2},{2,0},{1,3},{3,1},{4,6},{6,4},{5,7},{7,5},{8,10},{10,8},{9,1... | collective-permute-start | bytes 884744 | tf_op jit(solution)/shard_map/ppermute | solution.py:61
  343.1 17.6 %collective-permute-start.24 = (bf16[6,4,8,768]{3,2,1,0:T(8,128)(2,1)S(1)}, bf16[6,4,8,768]{3,2,1,0:T(8,128)(2,1)S(1)}, u32[]{:S(2)}, u32[]{:S(2)}) collective-permute-start(bf16[6,4,8,768]{3,2,1,0:T(8,128)(2,1)S(1)} %get-tuple-element.306), channel_id=1, source_target_pairs={{0,1},{1,0},{2,3},{3,2},{4,5},{5,4},{6,7},{7,6},{8,9},{9,8},{10,11... | collective-permute-start | bytes 884744 | tf_op jit(solution)/shard_map/ppermute | solution.py:61
  367.8 18.7 %collective-permute-start.30 = (bf16[12,2,8,768]{3,2,1,0:T(8,128)(2,1)S(1)}, bf16[12,2,8,768]{3,2,1,0:T(8,128)(2,1)S(1)}, u32[]{:S(2)}, u32[]{:S(2)}) collective-permute-start(bf16[12,2,8,768]{3,2,1,0:T(8,128)(2,1)S(1)} %copy-done.30), channel_id=1, source_target_pairs={{0,8},{8,0},{16,24},{24,16},{1,9},{9,1},{17,25},{25,17},{2,10},{10... | collective-permute-start | bytes 884744 | tf_op jit(solution)/shard_map/ppermute | solution.py:61
  369.2 17.3 %collective-permute-start.31 = (bf16[2,4,8,768]{3,2,1,0:T(8,128)(2,1)}, bf16[2,4,8,768]{3,2,1,0:T(8,128)(2,1)S(1)}, u32[]{:S(2)}, u32[]{:S(2)}) collective-permute-start(bf16[2,4,8,768]{3,2,1,0:T(8,128)(2,1)} %fusion.43), channel_id=1, source_target_pairs={{0,2},{2,0},{1,3},{3,1},{4,6},{6,4},{5,7},{7,5},{8,10},{10,8},{9,1... | collective-permute-start | bytes 294920 | tf_op jit(solution)/shard_map/ppermute | solution.py:61
  406.9 46.4 %all-to-all-start.1 = ((bf16[32,9,8,256]{3,2,1,0:T(8,128)(2,1)}), bf16[32,9,8,256]{3,2,1,0:T(8,128)(2,1)S(1)}, u32[]{:S(2)}, u32[]{:S(2)}) async-start(bf16[32,9,8,256]{3,2,1,0:T(8,128)(2,1)} %pad_maximum_fusion.6), calls=%async_computation.1 | async-start | bytes 2359296 | tf_op jit(solution)/shard_map/all_to_all | solution.py:1168
  410.0 26.0 %collective-permute-start.37 = (bf16[16,64,256]{2,1,0:T(8,128)(2,1)S(1)}, bf16[16,64,256]{2,1,0:T(8,128)(2,1)}, u32[]{:S(2)}, u32[]{:S(2)}) collective-permute-start(bf16[16,64,256]{2,1,0:T(8,128)(2,1)S(1)} %copy-done.29), channel_id=1, source_target_pairs={{0,1},{1,0},{2,3},{3,2},{4,5},{5,4},{6,7},{7,6},{8,9},{9,8},{10,11... | collective-permute-start | bytes 1572872 | tf_op jit(solution)/shard_map/ppermute | solution.py:61
  411.9 24.1 %collective-permute-start.38 = (bf16[16,64,256]{2,1,0:T(8,128)(2,1)S(1)}, bf16[16,64,256]{2,1,0:T(8,128)(2,1)}, u32[]{:S(2)}, u32[]{:S(2)}) collective-permute-start(bf16[16,64,256]{2,1,0:T(8,128)(2,1)S(1)} %copy-done.28), channel_id=1, source_target_pairs={{0,2},{1,3},{2,0},{3,1},{4,6},{5,7},{6,4},{7,5},{8,10},{9,11},{10,... | collective-permute-start | bytes 1572872 | tf_op jit(solution)/shard_map/ppermute | solution.py:61
  (69 other events, 507.6 us)
Sparse Core Ops, SparseCore 0:
  57.2 87.9 all-gather.2
  148.0 62.6 all-gather.4

commit v7 on v6

--- a/solution.py
+++ b/solution.py
@@ -35,8 +35,10 @@
 BLOCK = 512
 GROUP = 4
 EARLY = 13
-VMEM_BYTES = 56 * 1024 * 1024
+VMEM_BYTES = 28 * 1024 * 1024
+MLP_BYTES = 44 * 1024 * 1024
 ROW_BLOCKS = ((0, 256), (256, 256), (512, 224))
+CORE_SPEC = pl.BlockSpec(memory_space=pltpu.SMEM)
 bf16 = jnp.bfloat16
 f32 = jnp.float32
 
@@ -61,30 +63,29 @@
     return lax.ppermute(values, axes, [(i, i ^ mask) for i in range(count)])
 
 
+def pick(parts, index, dim):
+    if parts[0].shape[dim] == 2:
+        total = add_up(parts)
+        first, second = (lax.index_in_dim(total, at, dim, False) for at in range(2))
+        return jnp.where(index == 0, first, second)
+    return add_up([lax.dynamic_index_in_dim(part, index, dim, False) for part in parts])
+
+
 def advance(parts, axes, dim):
     mine = lax.axis_index(axes)
-    cuts = []
-    for mask in range(lax.axis_size(axes)):
-        cuts.append(add_up([lax.dynamic_index_in_dim(p, mine ^ mask, dim, False) for p in parts]))
-    return cuts
+    return [pick(parts, mine ^ mask, dim) for mask in range(lax.axis_size(axes))]
 
 
 def advance_near(parts):
     mine = lax.axis_index("z") % 2
     shape = parts[0].shape
     parts = [p.reshape((shape[0], shape[1] // 2, 2) + shape[2:]) for p in parts]
-    return [
-        add_up([lax.dynamic_index_in_dim(p, mine ^ mask, 2, False) for p in parts])
-        for mask in range(2)
-    ]
+    return [pick(parts, mine ^ mask, 2) for mask in range(2)]
 
 
 def advance_far(parts):
     mine = lax.axis_index("z") // 2
-    return [
-        add_up([lax.dynamic_index_in_dim(p, mine ^ mask, 1, False) for p in parts])
-        for mask in range(parts[0].shape[1])
-    ]
+    return [pick(parts, mine ^ mask, 1) for mask in range(parts[0].shape[1])]
 
 
 def send(cuts, axes, unit=1):
@@ -106,23 +107,76 @@
 
 
 def gather_axes(values, axes):
-    pieces = [values]
-    for mask in range(1, lax.axis_size(axes)):
-        pieces.append(xor_permute(values, axes, mask))
-    return jnp.stack(pieces)
-
-
-def gather_all(values):
-    shape = values.shape
-    values = gather_axes(values, "z")
-    values = gather_axes(values, ("y", "x"))
-    values = gather_axes(values, "c")
-    cores, rows, depth = values.shape[:3]
-    order = jnp.arange(depth * cores * rows)
-    z, c, row = order // (cores * rows), (order // rows) % cores, order % rows
-    own = lax.axis_index("z"), lax.axis_index("c"), lax.axis_index(("y", "x"))
-    at = ((c ^ own[1]) * rows + (row ^ own[2])) * depth + (z ^ own[0])
-    return values.reshape((-1,) + shape).at[at].get(mode="promise_in_bounds")
+    return [values] + [
+        xor_permute(values, axes, mask) for mask in range(1, lax.axis_size(axes))
+    ]
+
+
+def joined(pieces):
+    return jnp.stack(pieces, 1)
+
+
+def device_order(values, axes):
+    sizes = [lax.axis_size(axis) for axis in AXES]
+    own = [lax.axis_index(axis) for axis in AXES]
+    places = jnp.unravel_index(jnp.arange(lax.axis_size(AXES)), sizes)
+    at = 0
+    for axis in axes:
+        which = AXES.index(axis)
+        at = at * sizes[which] + (places[which] ^ own[which])
+    values = values.reshape((values.shape[0], -1) + values.shape[-2:])
+    values = values.at[:, at].get(mode="promise_in_bounds")
+    return values.reshape(values.shape[0], -1, values.shape[-1])
+
+
+def place_kernel(own_ref, low_ref, low_other_ref, high_ref, high_other_ref, out_ref, *, half, sizes):
+    z_count, c_count, y_count, x_count = sizes
+    own_z, own_c, own_y, own_x = (own_ref[axis] for axis in range(4))
+    step = pl.program_id(0)
+
+    def place(near_ref, far_ref, x_first):
+        for z in range(z_count):
+            for y in range(y_count):
+                for x in range(x_count):
+                    if x_first:
+                        at = (x ^ own_x) * y_count + (y ^ own_y)
+                    else:
+                        at = (y ^ own_y) * x_count + (x ^ own_x)
+                    at = at * z_count + (z ^ own_z)
+                    near, far = near_ref[0, at], far_ref[0, at]
+                    for c in range(c_count):
+                        to = ((z * c_count + c) * y_count + y) * x_count + x
+                        out_ref[0, to] = jnp.where(own_c == c, near, far)
+
+    @pl.when(step < half)
+    def _():
+        place(low_ref, low_other_ref, False)
+
+    @pl.when(step >= half)
+    def _():
+        place(high_ref, high_other_ref, True)
+
+
+def place_rows(low, high):
+    sizes = tuple(lax.axis_size(axis) for axis in AXES)
+    half, rows = low[0].shape[0], low[0].shape[-2]
+    count = half + high[0].shape[0]
+    own = jnp.stack([lax.axis_index(axis) for axis in AXES]).astype(jnp.int32)
+    pieces = [part.reshape(part.shape[0], -1, rows, D) for part in low + high]
+    block = (1,) + pieces[0].shape[1:]
+    early = pl.BlockSpec(block, lambda i: (jnp.minimum(i, half - 1), 0, 0, 0))
+    later = pl.BlockSpec(block, lambda i: (jnp.maximum(i - half, 0), 0, 0, 0))
+    devices = CH // rows
+    out = pl.pallas_call(
+        functools.partial(place_kernel, half=half, sizes=sizes),
+        grid=(count,),
+        in_specs=[CORE_SPEC, early, early, later, later],
+        out_specs=pl.BlockSpec((1, devices, rows, D), lambda i: (i, 0, 0, 0)),
+        out_shape=jax.ShapeDtypeStruct((count, devices, rows, D), bf16),
+        compiler_params=params(),
+        cost_estimate=cost(0, 4 * count * CH * D),
+    )(own, *pieces)
+    return out.reshape(count, CH, D)
 
 
 def trade_rows(values):
@@ -132,9 +186,58 @@
     return send(cuts, ("y", "x"))
 
 
+def row_order_kernel(row_ref, *refs):
+    at = pl.program_id(0) ^ row_ref[0]
+    values = refs[0][...]
+    for mask in range(1, len(refs) - 1):
+        values = jnp.where(at == mask, refs[mask][...], values)
+    refs[-1][0] = values.astype(f32)
+
+
 def row_order(pieces):
-    order = jnp.arange(len(pieces)) ^ lax.axis_index(("y", "x"))
-    return jnp.stack(pieces).at[order].get(mode="promise_in_bounds")
+    count = len(pieces)
+    cells = pieces[0].size // CH
+    return pl.pallas_call(
+        row_order_kernel,
+        grid=(count,),
+        in_specs=[CORE_SPEC] + [pl.BlockSpec((cells, CH), lambda i: (0, 0))] * count,
+        out_specs=pl.BlockSpec((1, cells, CH), lambda i: (i, 0, 0)),
+        out_shape=jax.ShapeDtypeStruct((count, cells, CH), f32),
+        compiler_params=params(),
+        cost_estimate=cost(0, 6 * count * cells * CH),
+    )(row_here(), *[piece.reshape(cells, CH) for piece in pieces])
+
+
+def widen_kernel(row_ref, *refs):
+    out_ref = refs[-1]
+    cells = refs[0].shape[0]
+    col = lax.broadcasted_iota(jnp.int32, (cells, CH), 0) % IMG
+    out_ref[0:IMG, :] = jnp.zeros((IMG, 3 * CH), bf16)
+    out_ref[CELLS + IMG :, :] = jnp.zeros((IMG, 3 * CH), bf16)
+    for at in range(len(refs) - 1):
+        values = refs[at][...]
+        for mask in range(1, len(refs) - 1):
+            values = jnp.where(row_ref[0] == mask, refs[at ^ mask][...], values)
+        here = slice(IMG + at * cells, IMG + (at + 1) * cells)
+        out_ref[here, CH : 2 * CH] = values
+        values = values.astype(f32)
+        left = jnp.where(col == 0, 0.0, pltpu.roll(values, 1, 0))
+        right = jnp.where(col == IMG - 1, 0.0, pltpu.roll(values, cells - 1, 0))
+        out_ref[here, 0:CH] = left.astype(bf16)
+        out_ref[here, 2 * CH :] = right.astype(bf16)
+
+
+def widen(pieces):
+    cells = pieces[0].size // CH
+    vmem = pl.BlockSpec(memory_space=pltpu.VMEM)
+    return pl.pallas_call(
+        widen_kernel,
+        in_specs=[CORE_SPEC] + [vmem] * len(pieces),
+        out_specs=vmem,
+        out_shape=lasting((CELLS + 2 * IMG, 3 * CH), bf16),
+        compiler_params=params(),
+        cost_estimate=cost(0, 8 * CELLS * CH),
+    )(row_here(), *[piece.reshape(cells, CH) for piece in pieces])
 
 
 def slice_shape():
@@ -194,6 +297,13 @@
     return pl.CostEstimate(
         flops=int(flops), bytes_accessed=int(moved), transcendentals=int(transcendentals)
     )
+
+
+def stay(values):
+    return pltpu.with_memory_space_constraint(values, pltpu.HBM)
+
+
+lasting = pltpu.HBM
 
 
 def params():
@@ -259,7 +369,8 @@
 
 
 def cross_backward_kernel(
-    q_ref, k_ref, v_ref, do_ref, o_ref, l_ref, dq_ref, dkv_ref, q_s, do_s, delta_s, dq_s
+    q_ref, k_ref, v_ref, do_ref, o_ref, l_ref, feats_ref, gupd_ref, query_w_ref,
+    dkv_ref, query_g_ref, future_ref, q_s, do_s, delta_s, dq_s,
 ):
     step = pl.program_id(0)
     rows = q_ref.shape[0]
@@ -291,10 +402,12 @@
 
     @pl.when(step == pl.num_programs(0) - 1)
     def _():
-        dq_ref[...] = (dq_s[...] * 0.125).astype(bf16)
-
-
-def cross_backward(query, kv, d_out, out, log_rows):
+        gq = (dq_s[...] * 0.125).astype(bf16)
+        query_g_ref[...] = dot_tn(feats_ref[...], gq).astype(bf16)
+        future_ref[...] = gupd_ref[...] + dot_nt(gq, query_w_ref[...])
+
+
+def cross_backward(query, kv, d_out, out, log_rows, feats, gupd, to_query):
     rows = query.shape[0]
     cells = kv.shape[0]
     block = 1024
@@ -309,14 +422,19 @@
             pl.BlockSpec((rows, CH), whole),
             pl.BlockSpec((rows, CH), whole),
             pl.BlockSpec((8, rows), whole),
+            pl.BlockSpec((rows, CH), whole),
+            pl.BlockSpec((rows, CH), whole),
+            pl.BlockSpec((CH, CH), whole),
         ],
         out_specs=[
+            pl.BlockSpec((block, 2 * CH), lambda i: (i, 0)),
+            pl.BlockSpec((CH, CH), whole),
             pl.BlockSpec((rows, CH), whole),
-            pl.BlockSpec((block, 2 * CH), lambda i: (i, 0)),
         ],
         out_shape=[
-            jax.ShapeDtypeStruct((rows, CH), bf16),
             jax.ShapeDtypeStruct((cells, 2 * CH), bf16),
+            jax.ShapeDtypeStruct((CH, CH), bf16),
+            jax.ShapeDtypeStruct((rows, CH), f32),
         ],
         scratch_shapes=[
             pltpu.VMEM((TH, rows, CH), bf16),
@@ -326,7 +444,7 @@
         ],
         compiler_params=params(),
         cost_estimate=cost(10 * TH * rows * cells * CH, 8 * cells * CH, TH * rows * cells),
-    )(query, kv, kv, d_out, out, log_rows)
+    )(query, kv, kv, d_out, out, log_rows, feats, gupd, to_query)
 
 
 def self_forward_kernel(len_ref, q_ref, k_ref, v_ref, o_ref, l_ref):
@@ -469,11 +587,14 @@
     return CH // (2 * lax.axis_size("z"))
 
 
+def row_here():
+    return lax.axis_index(("y", "x")).astype(jnp.int32).reshape(1)
+
+
 def core_here():
     return lax.axis_index("c").astype(jnp.int32).reshape(1)
 
 
-CORE_SPEC = pl.BlockSpec(memory_space=pltpu.SMEM)
 HALF = D // 2
 
 
@@ -526,192 +647,99 @@
             pl.BlockSpec((1, SEQ, D), lambda i: (i, 0, 0)),
         ],
         out_shape=[
-            jax.ShapeDtypeStruct((SEQ, CH), bf16),
-            jax.ShapeDtypeStruct((SEQ, D), f32),
-            jax.ShapeDtypeStruct((SEQ, D), bf16),
+            lasting((SEQ, CH), bf16),
+            lasting((SEQ, D), f32),
+            lasting((SEQ, D), bf16),
             jax.ShapeDtypeStruct((3, SEQ, D), bf16),
         ],
         compiler_params=params(),
         cost_estimate=cost(2 * SEQ * D * (CH + 3 * D), 12 * SEQ * D),
-    )(pooled, feats, mixed, to_out, weights, weights, gain)
-
-
-def up_kernel(
-    mixed_ref, embed_ref, att_ref, w_ref, gain_ref,
-    stream_ref, normed_ref, act_ref, slope_ref, pre_s,
+    )(pooled, feats, mixed, to_out, stay(weights), stay(weights), gain)
+
+
+def mlp_kernel(
+    core_ref, mixed_ref, embed_ref, att_ref, up_ref, down_ref, gain_ref, gd_ref,
+    out_ref, d_stream_ref, gog_ref, up_keep_ref, up_give_ref, down_keep_ref, down_give_ref,
+    att_keep_ref, att_give_ref, gain_g_ref,
+    stream_s, normed_s, turned_s, act_s, gpre_s, total_s, *, span
 ):
-    @pl.when(pl.program_id(0) == 0)
+    step = pl.program_id(0)
+    core = core_ref[0]
+
+    @pl.when(step == 0)
     def _():
         stream = embed_ref[...] + dot_nn(mixed_ref[...], square(att_ref))
-        stream_ref[...] = stream
-        normed_ref[...] = (stream * row_scale(stream) * gain_ref[...]).astype(bf16)
-
-    pre_s[...] = dot_nn(normed_ref[...], square(w_ref))
+        stream_s[...] = stream
+        out_ref[...] = stream
+        total_s[...] = jnp.zeros_like(total_s)
+        normed = stream * row_scale(stream) * gain_ref[...]
+        normed_s[...] = normed.astype(bf16)
+        turned_s[...] = normed.T.astype(bf16)
+
     factor = (2.0 / 3.141592653589793) ** 0.5
     cubic = 0.044715 * factor
-
-    def rows_step(index, carry):
-        here = pl.ds(pl.multiple_of(index * 16, 16), 16)
-        v = pre_s[here, :]
+    rows = SEQ // 4
+    for start in range(0, SEQ, rows):
+        here = slice(start, start + rows)
+        v = dot_nn(normed_s[here, :], square(up_ref))
         v2 = v * v
         half = 0.5 + 0.5 * jnp.tanh(v * (factor + cubic * v2))
-        act_ref[0, here, :] = (v * half).astype(bf16)
-        bend = 2.0 * half * (1.0 - half) * (factor + 3.0 * cubic * v2)
-        slope_ref[0, here, :] = (half + v * bend).astype(bf16)
-        return carry
-
-    lax.fori_loop(0, SEQ // 16, rows_step, 0, unroll=2)
-
-
-def up_forward(mixed, embed, weights, gain):
-    return pl.pallas_call(
-        up_kernel,
-        grid=(4,),
-        in_specs=[full(SEQ, D), full(SEQ, D), fixed_part(3), part_of(4), full(1, D)],
-        out_specs=[
-            full(SEQ, D),
-            full(SEQ, D),
-            pl.BlockSpec((1, SEQ, D), lambda i: (i, 0, 0)),
-            pl.BlockSpec((1, SEQ, D), lambda i: (i, 0, 0)),
-        ],
-        out_shape=[
-            jax.ShapeDtypeStruct((SEQ, D), f32),
-            jax.ShapeDtypeStruct((SEQ, D), bf16),
-            jax.ShapeDtypeStruct((4, SEQ, D), bf16),
-            jax.ShapeDtypeStruct((4, SEQ, D), bf16),
-        ],
-        scratch_shapes=[pltpu.VMEM((SEQ, D), f32)],
-        compiler_params=params(),
-        cost_estimate=cost(10 * SEQ * D * D, 28 * SEQ * D, 4 * SEQ * D),
-    )(mixed, embed, weights, weights, gain)
-
-
-def down_kernel(act_ref, w_ref, stream_ref, out_ref):
-    part = dot_nn(act_ref[0], square(w_ref))
-
-    @pl.when(pl.program_id(0) == 0)
-    def _():
-        out_ref[...] = stream_ref[...] + part
-
-    @pl.when(pl.program_id(0) > 0)
-    def _():
-        out_ref[...] += part
-
-
-def down_forward(act, w_down, stream):
-    return pl.pallas_call(
-        down_kernel,
-        grid=(4,),
-        in_specs=[
-            pl.BlockSpec((1, SEQ, D), lambda i: (i, 0, 0)),
-            part_of(0),
-            full(SEQ, D),
-        ],
-        out_specs=full(SEQ, D),
-        out_shape=jax.ShapeDtypeStruct((SEQ, D), f32),
-        compiler_params=params(),
-        cost_estimate=cost(8 * SEQ * D * D, 24 * SEQ * D),
-    )(act, w_down, stream)
-
-
-def down_grad_kernel(core_ref, act_ref, gd_ref, keep_ref, give_ref, *, span):
-    total = dot_tn(act_ref[0], gd_ref[...])
-    write_cores(core_ref[0], total, keep_ref, give_ref, span)
-
-
-def down_grad(act, gd):
-    half = pl.BlockSpec((HALF, D), lambda i: (i, 0))
-    return pl.pallas_call(
-        functools.partial(down_grad_kernel, span=core_span()),
-        grid=(4,),
-        in_specs=[CORE_SPEC, pl.BlockSpec((1, SEQ, D), lambda i: (i, 0, 0)), full(SEQ, D)],
-        out_specs=[half, half],
-        out_shape=[jax.ShapeDtypeStruct((4 * HALF, D), bf16)] * 2,
-        compiler_params=params(),
-        cost_estimate=cost(8 * SEQ * D * D, 18 * SEQ * D),
-    )(core_here(), act, gd)
-
-
-def up_grad_kernel(
-    core_ref, gd_ref, w_ref, slope_ref, normed_ref, gpre_ref, keep_ref, give_ref, turned_s, *, span
-):
-    @pl.when(pl.program_id(0) == 0)
-    def _():
-        turned_s[...] = normed_ref[...].T
-
-    gpre = (dot_nt(gd_ref[...], square(w_ref)) * slope_ref[0].astype(f32)).astype(bf16)
-    gpre_ref[0] = gpre
-    write_cores(core_ref[0], dot_nn(turned_s[...], gpre), keep_ref, give_ref, span)
-
-
-def up_grad(gd, w_down, slope, normed):
-    part = pl.BlockSpec((1, SEQ, D), lambda i: (i, 0, 0))
-    half = pl.BlockSpec((HALF, D), lambda i: (i, 0))
-    return pl.pallas_call(
-        functools.partial(up_grad_kernel, span=core_span()),
-        grid=(4,),
-        in_specs=[CORE_SPEC, full(SEQ, D), part_of(0), part, full(SEQ, D)],
-        out_specs=[part, half, half],
-        out_shape=[jax.ShapeDtypeStruct((4, SEQ, D), bf16)]
-        + [jax.ShapeDtypeStruct((4 * HALF, D), bf16)] * 2,
-        scratch_shapes=[pltpu.VMEM((D, SEQ), bf16)],
-        compiler_params=params(),
-        cost_estimate=cost(16 * SEQ * D * D, 36 * SEQ * D),
-    )(core_here(), gd, w_down, slope, normed)
-
-
-def att_grad_kernel(
-    core_ref, gpre_ref, w_ref, att_ref, stream_ref, gd_ref, mixed_ref, gain_ref,
-    d_stream_ref, gog_ref, keep_ref, give_ref, gain_g_ref, total_s, *, span
-):
-    step = pl.program_id(0)
-    part = dot_nt(gpre_ref[0], square(w_ref))
-
-    @pl.when(step == 0)
-    def _():
-        total_s[...] = part
-
-    @pl.when(step > 0)
-    def _():
-        total_s[...] += part
+        act = (v * half).astype(bf16)
+        act_s[here, :] = act
+        slope = half + v * (2.0 * half * (1.0 - half) * (factor + 3.0 * cubic * v2))
+        gpre = (dot_nt(gd_ref[here, :], square(down_ref)) * slope).astype(bf16)
+        gpre_s[here, :] = gpre
+        out_ref[here, :] += dot_nn(act, square(down_ref))
+        total_s[here, :] += dot_nt(gpre, square(up_ref))
+    write_cores(core, dot_tn(act_s[...], gd_ref[...]), down_keep_ref, down_give_ref, span)
+    write_cores(core, dot_nn(turned_s[...], gpre_s[...]), up_keep_ref, up_give_ref, span)
 
     @pl.when(step == pl.num_programs(0) - 1)
     def _():
-        d_gain, pulled = pull_norm(total_s[...], stream_ref[...], gain_ref[...])
+        d_gain, pulled = pull_norm(total_s[...], stream_s[...], gain_ref[...])
         gain_g_ref[...] = d_gain
         d_stream = gd_ref[...].astype(f32) + pulled
         d_stream_ref[...] = d_stream
         ga = d_stream.astype(bf16)
         gog_ref[...] = dot_nt(ga, square(att_ref)).astype(bf16)
-        write_cores(core_ref[0], dot_tn(mixed_ref[...], ga), keep_ref, give_ref, span)
-
-
-def att_grad(gpre, weights, stream, gd, mixed, gain):
+        write_cores(core, dot_tn(mixed_ref[...], ga), att_keep_ref, att_give_ref, span)
+
+
+def mlp_block(mixed, embed, weights, mlp, gain, gd):
+    half = pl.BlockSpec((HALF, D), lambda i: (i, 0))
     return pl.pallas_call(
-        functools.partial(att_grad_kernel, span=core_span()),
+        functools.partial(mlp_kernel, span=core_span()),
         grid=(4,),
         in_specs=[
             CORE_SPEC,
-            pl.BlockSpec((1, SEQ, D), lambda i: (i, 0, 0)),
-            part_of(4),
-            fixed_part(3),
             full(SEQ, D),
             full(SEQ, D),
+            fixed_part(3),
+            part_of(0),
+            part_of(4),
+            full(1, D),
             full(SEQ, D),
-            full(1, D),
-        ],
-        out_specs=[full(SEQ, D), full(SEQ, D), full(HALF, D), full(HALF, D), full(1, D)],
+        ],
+        out_specs=[full(SEQ, D)] * 3 + [half] * 4 + [full(HALF, D)] * 2 + [full(1, D)],
         out_shape=[
-            jax.ShapeDtypeStruct((SEQ, D), f32),
+            lasting((SEQ, D), f32),
+            lasting((SEQ, D), f32),
             jax.ShapeDtypeStruct((SEQ, D), bf16),
-            jax.ShapeDtypeStruct((HALF, D), bf16),
-            jax.ShapeDtypeStruct((HALF, D), bf16),
-            jax.ShapeDtypeStruct((1, D), f32),
-        ],
-        scratch_shapes=[pltpu.VMEM((SEQ, D), f32)],
-        compiler_params=params(),
-        cost_estimate=cost(12 * SEQ * D * D, 32 * SEQ * D),
-    )(core_here(), gpre, weights, weights, stream, gd, mixed, gain)
+        ]
+        + [jax.ShapeDtypeStruct((4 * HALF, D), bf16)] * 4
+        + [jax.ShapeDtypeStruct((HALF, D), bf16)] * 2
+        + [jax.ShapeDtypeStruct((1, D), f32)],
+        scratch_shapes=[
+            pltpu.VMEM((SEQ, D), f32),
+            pltpu.VMEM((SEQ, D), bf16),
+            pltpu.VMEM((D, SEQ), bf16),
+            pltpu.VMEM((SEQ, D), bf16),
+            pltpu.VMEM((SEQ, D), bf16),
+            pltpu.VMEM((SEQ, D), f32),
+        ],
+        compiler_params=pltpu.CompilerParams(vmem_limit_bytes=MLP_BYTES),
+        cost_estimate=cost(54 * SEQ * D * D, 60 * SEQ * D, 4 * SEQ * D),
+    )(core_here(), mixed, embed, stay(weights), stay(mlp), stay(mlp), gain, gd)
 
 
 def qkv_grad_kernel(core_ref, normed_ref, g_ref, keep_ref, give_ref, turned_s, *, span):
@@ -737,8 +765,9 @@
 
 
 def embed_grad_kernel(
-    g_ref, w_ref, emb_ref, embed_ref, d_stream_ref, seq_ref, mixed_ref, out_w_ref, gain_ref,
-    emb_g_ref, gupd_ref, pool_g_ref, out_g_ref, gox_ref, gain_g_ref, total_s,
+    core_ref, g_ref, w_ref, emb_ref, embed_ref, d_stream_ref, seq_ref, mixed_ref, out_w_ref,
+    gain_ref, gain_g_ref,
+    keep_ref, give_ref, gupd_ref, pool_g_ref, out_g_ref, gox_ref, total_s, *, span, rows
 ):
     step = pl.program_id(0)
     part = dot_nt(g_ref[0], square(w_ref))
@@ -754,9 +783,11 @@
     @pl.when(step == pl.num_programs(0) - 1)
     def _():
         d_gain, pulled = pull_norm(total_s[...], embed_ref[...], gain_ref[...])
-        gain_g_ref[...] = d_gain
         gembed = (d_stream_ref[...] + pulled).astype(bf16)
-        emb_g_ref[...] = dot_tn(seq_ref[...], gembed).astype(bf16)
+        at = lax.broadcasted_iota(jnp.int32, (CH, D), 0)
+        gains = jnp.where(at == 0, d_gain, jnp.where(at == rows, gain_g_ref[...], 0.0))
+        for index, values in enumerate((dot_tn(seq_ref[...], gembed), gains)):
+            write_cores(core_ref[0], values, keep_ref.at[index], give_ref.at[index], span)
         gseq = dot_nt(gembed, emb_ref[0])
         gupd = gseq[CTX:]
         gb = gupd.astype(bf16)
@@ -766,12 +797,13 @@
         gox_ref[...] = dot_nt(gb, out_w_ref[...]).astype(bf16)
 
 
-def embed_grad(gqkv, weights, embed, d_stream, seq, mixed, to_out, gain):
+def embed_grad(gqkv, weights, embed, d_stream, seq, mixed, to_out, gain, gain_g):
     last = weights.shape[0] - 1
     return pl.pallas_call(
-        embed_grad_kernel,
+        functools.partial(embed_grad_kernel, span=core_span(), rows=CH // lax.axis_size(AXES)),
         grid=(3,),
         in_specs=[
+            CORE_SPEC,
             pl.BlockSpec((1, SEQ, D), lambda i: (i, 0, 0)),
             part_of(0),
             pl.BlockSpec((1, CH, D), lambda i: (last, 0, 0)),
@@ -781,27 +813,31 @@
             full(SEQ - CTX, CH),
             full(CH, CH),
             full(1, D),
+            full(1, D),
         ],
         out_specs=[
-            full(CH, D),
+            full(2, CH // 2, D),
+            full(2, CH // 2, D),
             full(SEQ - CTX, CH),
             full(CTX, CH),
             full(CH, CH),
             full(SEQ - CTX, CH),
-            full(1, D),
         ],
         out_shape=[
-            jax.ShapeDtypeStruct((CH, D), bf16),
+            jax.ShapeDtypeStruct((2, CH // 2, D), bf16),
+            jax.ShapeDtypeStruct((2, CH // 2, D), bf16),
             jax.ShapeDtypeStruct((SEQ - CTX, CH), f32),
             jax.ShapeDtypeStruct((CTX, CH), bf16),
             jax.ShapeDtypeStruct((CH, CH), bf16),
             jax.ShapeDtypeStruct((SEQ - CTX, CH), bf16),
-            jax.ShapeDtypeStruct((1, D), f32),
         ],
         scratch_shapes=[pltpu.VMEM((SEQ, D), f32)],
         compiler_params=params(),
         cost_estimate=cost(2 * SEQ * D * (3 * D + 2 * CH), 24 * SEQ * D),
-    )(gqkv, weights, weights, embed, d_stream, seq, mixed, to_out, gain)
+    )(
+        core_here(), gqkv, stay(weights), stay(weights), stay(embed), stay(d_stream), stay(seq), stay(mixed), to_out,
+        gain, gain_g,
+    )
 
 
 def patch_pick(rows, columns, patch_dim):
@@ -851,18 +887,18 @@
             pl.BlockSpec((CTX // steps, CH), block),
         ],
         out_shape=[
-            jax.ShapeDtypeStruct((CELLS, CH), bf16),
-            jax.ShapeDtypeStruct((CELLS, CH), bf16),
+            lasting((CELLS, CH), bf16),
+            lasting((CELLS, CH), bf16),
             jax.ShapeDtypeStruct((CELLS, 2 * CH), bf16),
             jax.ShapeDtypeStruct((CTX, CH), bf16),
         ],
         compiler_params=params(),
         cost_estimate=cost(22 * CELLS * CH * CH, 14 * CELLS * CH, CELLS * CH),
-    )(wide, conv_rows, kv_weight)
+    )(stay(wide), conv_rows, kv_weight)
 
 
 def token_backward_kernel(
-    core_ref, dkv_ref, slope_ref, pool_ref, hidden_ref, x_ref, kv_w_ref,
+    core_ref, dkv_ref, slope_ref, pool_ref, hidden_ref, x_ref, kv_w_ref, query_g_ref, out_g_ref,
     d_hidden_ref, gz_ref, keep_ref, give_ref, conv_s, kv_s, *, span
 ):
     step = pl.program_id(0)
@@ -889,12 +925,12 @@
         for row in range(3):
             for col in range(3):
                 tiles.append(conv_s[row, :, col * CH : (col + 1) * CH].T)
-        tiles = tiles + [kv_s[:, :CH], kv_s[:, CH:]]
+        tiles = tiles + [query_g_ref[...], kv_s[:, :CH], kv_s[:, CH:], out_g_ref[...]]
         for at, tile in enumerate(tiles):
-            write_cores(core_ref[0], tile, keep_ref.at[at], give_ref.at[at], span)
-
-
-def token_backward(dkv, slope, d_pool, hidden_b, wide, kv_weight):
+            write_cores(core_ref[0], tile.astype(f32), keep_ref.at[at], give_ref.at[at], span)
+
+
+def token_backward(dkv, slope, d_pool, hidden_b, wide, kv_weight, query_g, out_g):
     steps = CELLS // BLOCK
     whole = lambda i: (0, 0)
     whole_3 = lambda i: (0, 0, 0)
@@ -910,23 +946,25 @@
             pl.BlockSpec((BLOCK, CH), block),
             pl.BlockSpec(wide.shape, whole),
             pl.BlockSpec((CH, 2 * CH), whole),
+            pl.BlockSpec((CH, CH), whole),
+            pl.BlockSpec((CH, CH), whole),
         ],
         out_specs=[
             pl.BlockSpec((BLOCK, CH), block),
             pl.BlockSpec((BLOCK, CH), block),
-            pl.BlockSpec((11, CH // 2, CH), whole_3),
-            pl.BlockSpec((11, CH // 2, CH), whole_3),
+            pl.BlockSpec((EARLY, CH // 2, CH), whole_3),
+            pl.BlockSpec((EARLY, CH // 2, CH), whole_3),
         ],
         out_shape=[
             jax.ShapeDtypeStruct((CELLS, CH), f32),
             jax.ShapeDtypeStruct((CELLS, CH), bf16),
-            jax.ShapeDtypeStruct((11, CH // 2, CH), bf16),
-            jax.ShapeDtypeStruct((11, CH // 2, CH), bf16),
+            jax.ShapeDtypeStruct((EARLY, CH // 2, CH), bf16),
+            jax.ShapeDtypeStruct((EARLY, CH // 2, CH), bf16),
         ],
         scratch_shapes=[pltpu.VMEM((3, CH, 3 * CH), f32), pltpu.VMEM((CH, 2 * CH), f32)],
         compiler_params=params(),
         cost_estimate=cost(26 * CELLS * CH * CH, 20 * CELLS * CH),
-    )(core_here(), dkv, slope, d_pool, hidden_b, wide, kv_weight)
+    )(core_here(), dkv, stay(slope), d_pool, stay(hidden_b), stay(wide), kv_weight, query_g, out_g)
 
 
 def context_backward_kernel(gz_ref, d_hidden_ref, conv_ref, out_ref, wide_s):
@@ -997,7 +1035,6 @@
     rows = CH // devices
     slot_of = slot_index(tile_owner, slot_count)
 
-    pieces = trade_rows(context_map)
     length = CTX + FT * horizon
     valid = jnp.arange(SEQ) < length[0]
     gd = jnp.where(valid[:, None], cotangent[0], jnp.zeros((), bf16))
@@ -1008,173 +1045,167 @@
         .transpose(1, 0, 2, 3)
     )
     slices = lax.all_to_all(slices, AXES, split_axis=0, concat_axis=0, tiled=True)
-    slices, pieces, gd = tie((slices, pieces, gd))
-    image = row_order(pieces).reshape(IMG, IMG, CH)
+    slices, gd = tie((slices, gd))
     slices = slices.reshape(devices * slot_count, rows, CH)
     slices = slices.at[slot_of].get(mode="promise_in_bounds")
     early, emb, qkv, att, up, down = jnp.split(slices, (13, 16, 43, 52, 88))
-    weights = jnp.concatenate(
-        [
-            from_tiles(qkv, 3, 3),
-            from_tiles(att, 3, 1),
-            from_tiles(up, 3, 4),
-            from_tiles(emb, 1, 1),
-        ],
-        0,
-    )
-    weights = lax.all_gather(weights, AXES, axis=1, tiled=True)
-    w_down = lax.all_gather(from_tiles(down, 12, 1), AXES, axis=1, tiled=True)
-    early = gather_all(early).transpose(1, 0, 2, 3).reshape(EARLY, CH, CH)
-
-    padded = jnp.pad(image, ((1, 1), (1, 1), (0, 0)))
-    wide = jnp.concatenate([padded[:, col : col + IMG] for col in range(3)], -1)
-    wide = wide.reshape((IMG + 2) * IMG, 3 * CH)
+    mlp = jnp.concatenate([from_tiles(up, 3, 4), from_tiles(down, 12, 1)], 0)
+    mlp = lax.all_gather(mlp, AXES, axis=1, tiled=True)
+    early = gather_axes(early, "z")
+    core = jnp.concatenate([from_tiles(qkv, 3, 3), from_tiles(att, 3, 1), from_tiles(emb, 1, 1)], 0)
+    core, early = tie((core, early))
+    early = gather_axes(joined(early), ("y", "x"))
+    core = gather_axes(core, "z")
+    pieces = trade_rows(context_map)
+    early = joined(gather_axes(joined(early), "c"))
+    early = device_order(early, ("c", "y", "x", "z"))
+    wide = widen(pieces)
+    core = joined(core)
+    low, high = gather_axes(core[:6], "x"), gather_axes(core[6:], "y")
 
     conv_tiles = early[:9]
     to_query, to_out = early[9], early[12]
     kv_weight = jnp.concatenate([early[10], early[11]], 1)
 
+    wide, low, high = hold((wide,), low, high)
+    low, high = joined(low), joined(high)
+    wide, low, high = tie((wide, low, high))
+    low, high = gather_axes(low, "y"), gather_axes(high, "x")
     slope_z, hidden_b, kv, pooled = token_forward(
         wide, conv_tiles.reshape(3, 3 * CH, CH), kv_weight
     )
+    kv, low, high = hold((kv,), low, high)
+    low, high = joined(low), joined(high)
     feats_b = future_feats[0]
     query = jnp.dot(feats_b, to_query, preferred_element_type=f32).astype(bf16)
+    kv, low, high = tie((kv, low, high))
+    low, high = gather_axes(low, "c"), gather_axes(high, "c")
     cross_mixed, cross_logs = cross_forward(query, kv)
+    cross_mixed, low, high = hold((cross_mixed,), low, high)
+    weights = place_rows(low, high)
 
     gain_one, gain_two = norm_gains[:1], norm_gains[1:]
     seq, embed, normed_one, qkv = embed_forward(
         pooled, feats_b, cross_mixed, to_out, weights, gain_one
     )
     mixed, logs = self_forward(qkv, length)
-    stream, normed_two, act, slope = up_forward(mixed, embed, weights, gain_two)
-
-    down = core_parts(down_grad(act, gd))
-    gd, down = tie((gd, down))
-    down = send(down, "c")
-    gpre, up_keep, up_give = up_grad(gd, w_down, slope, normed_two)
-    gpre, up, down = hold((gpre, core_parts([up_keep, up_give])), down)
-    down = advance(down, "x", 3)
-    gpre, up, down = tie((gpre, up, down))
-    up, down = send(up, "c"), send(down, "x")
-    d_stream, gog, att_keep, att_give, gain_g_two = att_grad(
-        gpre, weights, stream, gd, mixed, gain_two
-    )
-    gog, att, up = hold((gog, core_parts([att_keep, att_give])), up)
-    up = advance(up, "y", 2)
-    gog, att, up = tie((gog, att, up))
-    up, att = send(up, "y"), send(att, "c")
+    (
+        block_out, d_stream, gog, up_keep, up_give, down_keep, down_give, att_keep, att_give,
+        gain_g_two,
+    ) = mlp_block(mixed, embed, weights, mlp, gain_two, gd)
+    gog, up, down, att = tie(
+        (
+            gog,
+            core_parts([up_keep, up_give]),
+            core_parts([down_keep, down_give]),
+            core_parts([att_keep, att_give]),
+        )
+    )
+    up, down, att = send(up, "c"), send(down, "c"), send(att, "c")
     gqkv = self_backward(qkv, gog, mixed, logs, length)
-    gqkv, down, att = hold((gqkv,), down, att)
-    down = advance(down, "y", 2)
-    gqkv, down = tie((gqkv, down))
-    down = send(down, "y")
+    gqkv, up, down, att = hold((gqkv,), up, down, att)
+    up, down = advance(up, "y", 2), advance(down, "x", 3)
+    gqkv, up, down = tie((gqkv, up, down))
+    up, down = send(up, "y"), send(down, "x")
     qkv_keep, qkv_give = qkv_grad(normed_one, gqkv)
-    gqkv, qkv, up = hold((gqkv, core_parts([qkv_keep, qkv_give])), up)
-    up = advance(up, "x", 2)
-    gqkv, qkv, up = tie((gqkv, qkv, up))
-    qkv, up = send(qkv, "c"), send(up, "x")
-    emb_g, gupd, pool_g, out_g, gox, gain_g_one = embed_grad(
-        gqkv, weights, embed, d_stream, seq, cross_mixed, to_out, gain_one
-    )
-    gox, gupd, emb_g, gain_g_one, qkv, up, down = hold(
-        (gox, gupd, emb_g, gain_g_one), qkv, up, down
-    )
-    gains = jnp.concatenate([gain_g_one, gain_g_two], 0).reshape(devices, 1, -1)
-    gain_count = gains.shape[-1]
-    gains = jnp.pad(gains, ((0, 0), (0, rows - 1), (0, D - gain_count))).astype(bf16)
-    emb = cut_core(jnp.concatenate([emb_g, gains.reshape(CH, D)], 0))
-    mlp = advance_near([jnp.concatenate(part, 0) for part in zip(up, down)])
+    gqkv, qkv_keep, qkv_give = tie((gqkv, qkv_keep, qkv_give))
+    qkv = send(core_parts([qkv_keep, qkv_give]), "c")
+    emb_keep, emb_give, gupd, pool_g, out_g, gox = embed_grad(
+        gqkv, weights, embed, d_stream, seq, cross_mixed, to_out, gain_one, gain_g_two
+    )
+    gox, gupd, emb_keep, emb_give, qkv, up, down = hold(
+        (gox, gupd, emb_keep, emb_give), qkv, up, down
+    )
+    up, down = advance(up, "x", 2), advance(down, "y", 2)
     first = advance([part[:6] for part in qkv], "x", 3)
     second = advance([jnp.concatenate([p[6:], q], 0) for p, q in zip(qkv, att)], "y", 2)
-    gox, mlp, first, second, emb = tie((gox, mlp, first, second, emb))
-    mlp, emb = send(mlp, "z"), send(emb, "c")
+    emb = core_parts([emb_keep, emb_give])
+    gox, up, down, first, second, emb = tie((gox, up, down, first, second, emb))
+    up, down, emb = send(up, "x"), send(down, "y"), send(emb, "c")
     first, second = send(first, "x"), send(second, "y")
 
     log_rows = jnp.concatenate([cross_logs[0], cross_logs[1]], 1)
-    gq, gkv = cross_backward(query, kv, gox, cross_mixed, log_rows)
-    gq, gkv, mlp, first, second, emb = hold((gq, gkv), mlp, first, second, emb)
-    mlp, emb = advance_far(mlp), advance(emb, "x", 3)
+    gkv, query_g, future_grad = cross_backward(
+        query, kv, gox, cross_mixed, log_rows, feats_b, gupd, to_query
+    )
+    gkv, up, down, first, second, emb = hold((gkv,), up, down, first, second, emb)
+    mlp = advance_near([jnp.concatenate(part, 0) for part in zip(up, down)])
+    emb = advance(emb, "x", 3)
     first, second = advance(first, "y", 2), advance(second, "x", 2)
-    query_g = cut_core(jnp.dot(feats_b.T, gq, preferred_element_type=f32))
-    out_g = cut_core(out_g)
-    gkv, mlp, first, second, emb, query_g, out_g = tie(
-        (gkv, mlp, first, second, emb, query_g, out_g)
-    )
-    mlp, emb = send(mlp, "z", 2), send(emb, "x")
+    gkv, mlp, first, second, emb = tie((gkv, mlp, first, second, emb))
+    mlp, emb = send(mlp, "z"), send(emb, "x")
     first, second = send(first, "y"), send(second, "x")
 
-    d_hidden, gz, token_keep, token_give = token_backward(
-        gkv, slope_z, pool_g, hidden_b, wide, kv_weight
-    )
-    d_hidden, token_keep, token_give, mlp, first, second, emb = hold(
-        (d_hidden, token_keep, token_give), mlp, first, second, emb
-    )
-    early = []
-    for token, q, o in zip((token_keep, token_give), query_g, out_g):
-        q, o = (part.reshape(1, CH // 2, CH) for part in (q, o))
-        early.append(jnp.concatenate([token[:9], q, token[9:], o], 0))
-    early = core_parts(early)
+    d_hidden, gz, early_keep, early_give = token_backward(
+        gkv, slope_z, pool_g, hidden_b, wide, kv_weight, query_g, out_g
+    )
+    d_hidden, gz, early_keep, early_give, mlp, first, second, emb = hold(
+        (d_hidden, gz, early_keep, early_give), mlp, first, second, emb
+    )
+    early = core_parts([early_keep, early_give])
+    early, mlp, first, second, emb = tie((early, mlp, first, second, emb))
+    early = send(early, "c")
     att = advance_near([jnp.concatenate(part, 0) for part in zip(first, second)])
-    emb = advance(emb, "y", 2)
-    early, att, emb = tie((early, att, emb))
-    early = send(early, "c")
-    att, emb = send(att, "z"), send(emb, "y")
-    sum_mlp = add_up(mlp, keep_wide=True)
-    future_grad = gupd + lax.dot_general(
-        gq, to_query, (((1,), (1,)), ((), ())), preferred_element_type=f32
-    )
-    future_grad, gz, early = hold((future_grad, gz), early)
+    emb, mlp = advance(emb, "y", 2), advance_far(mlp)
+    att, emb, mlp = send(att, "z"), send(emb, "y"), send(mlp, "z", 2)
+    gz, early, att, emb = hold((gz,), early, att, emb)
     shape = early[0].shape
     early = advance([p.reshape(shape[:2] + (-1,) + shape[4:]) for p in early], ("y", "x"), 2)
-    gz, early = tie((gz, early))
-    early = send(early, ("y", "x"))
+    att = advance_far(att)
+    gz, early, att = tie((gz, early, att))
+    early, att = send(early, ("y", "x")), send(att, "z", 2)
     context_grad = context_backward(gz, d_hidden, conv_tiles)
-    context_grad, early, att, emb = hold((context_grad,), early, att, emb)
-    att = advance_far(att)
+    context_grad, early, att, mlp = hold((context_grad,), early, att, mlp)
     early = advance(early, "z", 1)
     emb = advance(emb, "z", 1)
     early = [jnp.concatenate([e, to_tiles(m)], 0) for e, m in zip(early, emb)]
-    context_grad, early, att = tie((context_grad, early, att))
-    early, att = send(early, "z"), send(att, "z", 2)
+    context_grad, early = tie((context_grad, early))
+    early = send(early, "z")
     pieces = trade_rows(context_grad.reshape(context_map.shape))
+    sum_mlp = add_up(mlp, keep_wide=True)
+    square_mlp = jnp.sum(sum_mlp * sum_mlp)
+    half = sum_mlp.shape[0] // 2
+    mlp = jnp.concatenate([to_tiles(sum_mlp[:half], 4), to_tiles(sum_mlp[half:])], 0).astype(bf16)
     sum_early = add_up(early, keep_wide=True)
     sum_att = add_up(att, keep_wide=True)
 
+    gains = sum_early[EARLY + 3 :, 0]
+    square = square_mlp + jnp.sum(sum_att * sum_att) + jnp.sum(sum_early * sum_early)
+    share = jnp.concatenate([gains, jnp.broadcast_to(square, (1, CH))], 0)
+    share_high = share.astype(bf16)
+    share_low = (share - share_high.astype(f32)).astype(bf16)
+    share = jnp.concatenate([share_high, share_low], 0)
+    extra = max(1, share.shape[0] // rows)
+    share = jnp.pad(share, ((0, extra * rows - share.shape[0]), (0, 0)))
     sums = jnp.concatenate(
         [
-            sum_early[: EARLY + 3],
-            to_tiles(sum_att[:9], 3),
-            to_tiles(sum_att[9:]),
-            to_tiles(sum_mlp[:12], 4),
-            to_tiles(sum_mlp[12:]),
+            sum_early[: EARLY + 3].astype(bf16),
+            to_tiles(sum_att[:9], 3).astype(bf16),
+            to_tiles(sum_att[9:]).astype(bf16),
+            mlp,
+            share.reshape(extra, rows, CH),
         ],
         0,
-    )
-    gains = sum_early[EARLY + 3, 0, :gain_count]
-    share = jnp.concatenate([(jnp.sum(sums * sums) + jnp.sum(gains * gains))[None], gains])
-    share_high = share.astype(bf16)
-    share_low = (share - share_high.astype(f32)).astype(bf16)
-    share = jnp.pad(
-        jnp.stack([share_high, share_low]), ((0, rows - 2), (0, CH - 1 - gain_count))
     )
     slots = jnp.arange(devices * slot_count)
     found = slot_of[None, :] == slots[:, None]
-    tile_of = jnp.sum(jnp.where(found, jnp.arange(found.shape[1])[None], 0), 1)
-    mine = sums.astype(bf16).at[tile_of].get(mode="promise_in_bounds")
-    mine = mine.reshape(devices, slot_count, rows, CH)
-    share = jnp.broadcast_to(share[None, None], (devices, 1, rows, CH))
-    mine = jnp.concatenate([mine, share], 1)
-    mine, act, pieces[-1] = tie((mine, act, pieces[-1]))
+    tiles = found.shape[1]
+    tile_of = jnp.sum(jnp.where(found, jnp.arange(tiles)[None], 0), 1)
+    tile_of = tile_of.reshape(devices, slot_count)
+    shared = jnp.broadcast_to(tiles + jnp.arange(extra)[None], (devices, extra))
+    tile_of = jnp.concatenate([tile_of, shared], 1).reshape(-1)
+    mine = sums.at[tile_of].get(mode="promise_in_bounds")
+    mine = mine.reshape(devices, slot_count + extra, rows, CH)
+    mine, pieces[-1] = tie((mine, pieces[-1]))
     mine = lax.all_to_all(mine, AXES, split_axis=0, concat_axis=0, tiled=True)
-    block_out = down_forward(act, w_down, stream)
-    shares = mine[:, slot_count, :2].astype(f32)
-    shares = shares[:, 0] + shares[:, 1]
-    gains = shares[:, 1 : 1 + gain_count].reshape(2, D)
+    shares = mine[:, slot_count:].reshape(devices, -1, CH).astype(f32)
+    shares = shares[:, :4] + shares[:, 4:8]
+    gains = shares[:2, :3].reshape(2, D)
     mine = mine[:, :slot_count].transpose(1, 0, 2, 3).reshape(slot_count, CH, CH).astype(f32)
 
     used = jnp.any(found, 1).astype(f32).reshape(devices, slot_count)
     used = lax.dynamic_index_in_dim(used, lax.axis_index(AXES), 0, keepdims=False)[:, None, None]
-    grad_norm = jnp.sqrt(jnp.sum(shares[:, 0]))
+    grad_norm = jnp.sqrt(jnp.sum(shares[:, 3, 0]))
     factor = jnp.minimum(1.0, clip_level / (grad_norm + 1e-06))
     new_first, new_second, new_master = adam_step(
         master_tiles, mine * factor, moment_first, moment_second, learn_rate, decay_rate
@@ -1184,7 +1215,7 @@
     )
     return (
         block_out[None],
-        row_order(pieces).reshape(context_map.shape).astype(f32),
+        row_order(pieces).reshape(context_map.shape),
         future_grad[None],
         jnp.where(used > 0, new_first, 0.0),
         jnp.where(used > 0, new_second, 0.0),

time: 475 us -> 458 us (0.964)
  Pallas kernels: 206 us -> 172 us
  waiting for transfers between devices: 106 us -> 118 us
  other arithmetic: 49.6 us -> 38.7 us
  local copies, waits for them, and re-layouts: 35.3 us -> 43.3 us
  starting transfers between devices: 51.1 us -> 58.9 us
    all_gather x2 -> x1, waiting for transfers between devices: 35.6 us -> 0.01 us  [local(): mlp = lax.all_gather(mlp, AXES, axis=1, tiled=True)]
    all_to_all x1, waiting for transfers between devices: 0.01 us -> 24.3 us  [local(): lax.all_to_all(slices, AXES, split_axis=0, concat_axis=0, tiled=True)]
    ppermute x39 -> x48, waiting for transfers between devices: 69.4 us -> 93.4 us  [xor_permute(): return lax.ppermute(values, axes, [(i, i ^ mask) for i in range(count)])]
    pallas_call x6 -> x5, Pallas kernels: 70.9 us -> 53.3 us  [the longest x1 36.1 us: mlp_block(): pl.pallas_call(functools.partial(mlp_kernel, span=core_span()), grid=(4,)...]
    unnamed x97 -> x90, local copies, waits for them, and re-layouts: 6.16 us -> 20.5 us
    ppermute x39 -> x48, starting transfers between devices: 40.7 us -> 48.9 us  [xor_permute(): return lax.ppermute(values, axes, [(i, i ^ mask) for i in range(count)])]
    concatenate x10 -> x2, other arithmetic: 6.93 us -> 0.75 us  [the longest x1 0.74 us: local(): mlp = jnp.concatenate([from_tiles(up, 3, 4), from_tiles(down, 12, 1)], 0)]
    convert_element_type x21 -> x16, other arithmetic: 16 us -> 13.2 us  [add_up(): return total if keep_wide else total.astype(parts[0].dtype)]
  transfers between devices with their start and end apart: 43 -> 51, of which waited for: 13 -> 17; matrix products, arithmetic and copies ran while one was open for 10% -> 5% of each run, Pallas kernels for 44% -> 29%
where the time goes in v7:
time: 458 us; the launch traced here: 453 us
  Pallas kernels  172 us (38%)
  waiting for transfers between devices  118 us (26%)
  starting transfers between devices  58.9 us (13%)
  local copies, waits for them, and re-layouts  43.3 us (9%)
  other arithmetic  38.7 us (8%)
  between operations  20.3 us (4%)
    ppermute x48, waiting for transfers between devices, xor_permute(): return lax.ppermute(values, axes, [(i, i ^ mask) for i in range(count)])  93.4 us
    ppermute x48, starting transfers between devices, xor_permute(): return lax.ppermute(values, axes, [(i, i ^ mask) for i in range(count)])  48.9 us
    pallas_call x1, Pallas kernels, mlp_block(): pl.pallas_call(functools.partial(mlp_kernel, span=core_span()), grid=(4,)...  36.1 us
    pallas_call x1, Pallas kernels, cross_backward(): pl.pallas_call(cross_backward_kernel, grid=(cells // block,), in_specs=[p...  26.3 us
    all_to_all x1, waiting for transfers between devices, local(): lax.all_to_all(slices, AXES, split_axis=0, concat_axis=0, tiled=True)  24.3 us
    unnamed x90, local copies, waits for them, and re-layouts  20.5 us
    pallas_call x1, Pallas kernels, self_backward(): pl.pallas_call(self_backward_kernel, grid_spec=pltpu.PrefetchScalarGridSp...  17.4 us
    pallas_call x1, Pallas kernels, token_forward(): pl.pallas_call(token_forward_kernel, grid=(steps,), in_specs=[pl.BlockSpe...  16.4 us
  transfers between devices with their start and end apart: 51, of which 17 were waited for; matrix products, arithmetic and copies ran while one was open for 5% of the time, Pallas kernels for 29%

profile of v7, /device:TPU:0, one launch (start us, length us, event | category | flops | bytes accessed | tf_op | source)
XLA Modules:
  0.0 452.6 jit_solution(10912519796566995155)
XLA Ops:
  10.0 7.3 %all-to-all-start = ((bf16[32,8,8,256]{3,2,1,0:T(8,128)(2,1)}), bf16[32,8,8,256]{3,2,1,0:T(8,128)(2,1)S(1)}, u32[]{:S(2)}, u32[]{:S(2)}) async-start(bf16[32,8,8,256]{3,2,1,0:T(8,128)(2,1)} %copy.277), calls=%async_computation | async-start | bytes 2097152 | tf_op jit(solution)/shard_map/all_to_all | solution.py:1047
  19.5 24.3 %all-to-all-done = bf16[32,8,8,256]{3,2,1,0:T(8,128)(2,1)S(1)} async-done(((bf16[32,8,8,256]{3,2,1,0:T(8,128)(2,1)}), bf16[32,8,8,256]{3,2,1,0:T(8,128)(2,1)S(1)}, u32[]{:S(2)}, u32[]{:S(2)}) %all-to-all-start) | async-done | bytes 1048608 | tf_op jit(solution)/shard_map/all_to_all | solution.py:1047
  69.2 9.4 %collective-permute-done.7 = bf16[13,8,768]{2,1,0:T(8,128)(2,1)S(1)} collective-permute-done((bf16[13,8,768]{2,1,0:T(8,128)(2,1)S(1)}, bf16[13,8,768]{2,1,0:T(8,128)(2,1)S(1)}, u32[]{:S(2)}, u32[]{:S(2)}) %collective-permute-start.7) | collective-permute-done | bytes 159776 | tf_op jit(solution)/shard_map/ppermute | solution.py:63
  82.3 11.3 %collective-permute-done.1 = bf16[16,64,256]{2,1,0:T(8,128)(2,1)S(1)} collective-permute-done((bf16[16,64,256]{2,1,0:T(8,128)(2,1)S(1)}, bf16[16,64,256]{2,1,0:T(8,128)(2,1)S(1)}, u32[]{:S(2)}, u32[]{:S(2)}) %collective-permute-start.1) | collective-permute-done | bytes 524320 | tf_op jit(solution)/shard_map/ppermute | solution.py:63
  93.6 9.2 %collective-permute-done.2 = bf16[16,64,256]{2,1,0:T(8,128)(2,1)S(1)} collective-permute-done((bf16[16,64,256]{2,1,0:T(8,128)(2,1)S(1)}, bf16[16,64,256]{2,1,0:T(8,128)(2,1)S(1)}, u32[]{:S(2)}, u32[]{:S(2)}) %collective-permute-start.2) | collective-permute-done | bytes 524320 | tf_op jit(solution)/shard_map/ppermute | solution.py:63
  102.8 4.1 shard_map.186.x_ref
  113.9 16.4 %shard_map.187 = (bf16[4096,256]{1,0:T(8,128)(2,1)}, bf16[4096,256]{1,0:T(8,128)(2,1)}, bf16[4096,512]{1,0:T(8,128)(2,1)S(1)}, bf16[256,256]{1,0:T(8,128)(2,1)S(1)}) custom-call(bf16[4224,768]{1,0:T(8,128)(2,1)} %shard_map.186.x_ref, bf16[3,768,256]{2,1,0:T(8,128)(2,1)S(1)} %bitcast.349, bf16[256,512]{1,0:T(8,128)(2,1)S(1)} %pad_maximum_fusion.11.kv_w_ref), custom_call_target="tpu_custom_call" | custom-call | flops 5905580032 | bytes 14680064 | tf_op jit(solution)/shard_map/pallas_call | solution.py:875
  136.9 14.0 %shard_map.188 = (bf16[480,256]{1,0:T(8,128)(2,1)S(1)}, f32[2,8,240]{2,1,0:T(8,128)S(1)}) custom-call(bf16[480,256]{1,0:T(8,128)(2,1)S(1)} %fusion.2.q_ref, bf16[4096,512]{1,0:T(8,128)(2,1)S(1)} %get-tuple-element.239.k_ref.v_ref, bf16[4096,512]{1,0:T(8,128)(2,1)S(1)} %get-tuple-element.239.k_ref.v_ref), custom_call_target="tpu_custom_call" | custom-call | flops 8053063680 | bytes 8388608 | tf_op jit(solution)/shard_map/pallas_call | solution.py:336
  154.9 6.8 %shard_map.190 = (bf16[736,256]{1,0:T(8,128)(2,1)}, f32[736,768]{1,0:T(8,128)}, bf16[736,768]{1,0:T(8,128)(2,1)}, bf16[3,736,768]{2,1,0:T(8,128)(2,1)S(1)}) custom-call(bf16[256,256]{1,0:T(8,128)(2,1)S(1)} %get-tuple-element.230.pool_ref, bf16[480,256]{1,0:T(8,128)(2,1)S(1)} %bitcast.350, bf16[480,256]{1,0:T(8,128)(2,1)S(1)} %get-tuple-element.243.mixed_ref.o_ref, ...), custom_call_target="tpu_custom_call" | custom-call | flops 2894069760 | bytes 6782976 | tf_op jit(solution)/shard_map/pallas_call | solution.py:631
  161.7 11.7 %shard_map.191 = (bf16[736,768]{1,0:T(8,128)(2,1)S(1)}, f32[3,8,736]{2,1,0:T(8,128)S(1)}) custom-call(s32[1]{0:T(128)} %add.370.len_ref, bf16[3,736,768]{2,1,0:T(8,128)(2,1)S(1)} %get-tuple-element.248.q_ref.k_ref.v_ref, bf16[3,736,768]{2,1,0:T(8,128)(2,1)S(1)} %get-tuple-element.248.q_ref.k_ref.v_ref, ...), custom_call_target="tpu_custom_call" | custom-call | flops 6656360448 | bytes 4521984 | tf_op jit(solution)/shard_map/pallas_call | solution.py:479
  180.9 36.1 %shard_map.192 = (f32[736,768]{1,0:T(8,128)}, f32[736,768]{1,0:T(8,128)}, bf16[736,768]{1,0:T(8,128)(2,1)S(1)}, bf16[1536,768]{1,0:T(8,128)(2,1)S(1)}, bf16[1536...) custom-call(s32[1]{0:T(128)} %bitcast.core_ref, ...), custom_call_target="tpu_custom_call" | custom-call | flops 23441965056 | bytes 33914880 | tf_op jit(solution)/shard_map/pallas_call | solution.py:710
  217.0 4.1 copy.289
  229.9 17.4 %shard_map.193.g_ref = bf16[3,736,768]{2,1,0:T(8,128)(2,1)S(1)} custom-call(s32[1]{0:T(128)} %add.370.len_ref, bf16[3,736,768]{2,1,0:T(8,128)(2,1)S(1)} %copy-done.15, bf16[3,736,768]{2,1,0:T(8,128)(2,1)S(1)} %copy-done.15, bf16[3,736,768]{2,1,0:T(8,128)(2,1)S(1)} %copy-done.15, bf16[736,768]{1,0:T(8,128)(2,1)S(1)} %copy-done.23, ...), custom_call_target="tpu_custom_call" | custom-call | flops 13312720896 | bytes 9043968 | tf_op jit(solution)/shard_map/pallas_call | solution.py:541
  247.4 3.7 add_convert_fusion
  266.0 9.2 %shard_map.195 = (bf16[2,128,768]{2,1,0:T(8,128)(2,1)S(1)}, bf16[2,128,768]{2,1,0:T(8,128)(2,1)S(1)}, f32[480,256]{1,0:T(8,128)S(1)}, bf16[256,256]{1,0:T(8,128)...) custom-call(s32[1]{0:T(128)} %bitcast.core_ref, bf16[3,736,768]{2,1,0:T(8,128)(2,1)S(1)} %copy-done.2, ...), custom_call_target="tpu_custom_call" | custom-call | flops 3183476736 | bytes 13565952 | tf_op jit(solution)/shard_map/pallas_call | solution.py:802
  275.2 15.4 %collective-permute-done.23 = bf16[12,4,2,8,768]{4,3,1,0,2:T(8,128)(2,1)} collective-permute-done((bf16[12,4,2,8,768]{4,3,1,0,2:T(8,128)(2,1)}, bf16[12,4,2,8,768]{4,3,1,0,2:T(8,128)(2,1)}, u32[]{:S(2)}, u32[]{:S(2)}) %collective-permute-start.23) | collective-permute-done | bytes 1179680 | tf_op jit(solution)/shard_map/ppermute | solution.py:63
  304.5 26.3 %shard_map.196 = (bf16[4096,512]{1,0:T(8,128)(2,1)S(1)}, bf16[256,256]{1,0:T(8,128)(2,1)S(1)}, f32[480,256]{1,0:T(8,128)}) custom-call(bf16[480,256]{1,0:T(8,128)(2,1)S(1)} %copy-done.13, bf16[4096,512]{1,0:T(8,128)(2,1)S(1)} %copy-done.18, bf16[4096,512]{1,0:T(8,128)(2,1)S(1)} %copy-done.18, bf16[480,256]{1,0:T(8,128)(2,1)S(1)} %get-tuple-element.302.do_ref, ...), custom_call_target="tpu_custom_call" | custom-call | flops 20132659200 | bytes 8388608 | tf_op jit(solution)/shard_map/pallas_call | solution.py:415
  336.0 14.6 %shard_map.197 = (f32[4096,256]{1,0:T(8,128)S(1)}, bf16[4096,256]{1,0:T(8,128)(2,1)S(1)}, bf16[13,128,256]{2,1,0:T(8,128)(2,1)S(1)}, bf16[13,128,256]{2,1,0:T(8,128)(2,1)S(1)}) custom-call(s32[1]{0:T(128)} %bitcast.core_ref, bf16[4096,512]{1,0:T(8,128)(2,1)S(1)} %get-tuple-element.327.dkv_ref, bf16[4096,256]{1,0:T(8,128)(2,1)} %get-tuple-element.328.slope_ref, ...), custom_call_target="tpu_custom_call" | custom-call | flops 6979321856 | bytes 20971520 | tf_op jit(solution)/shard_map/pallas_call | solution.py:938
  353.7 4.9 %collective-permute-done.36 = bf16[2,4,8,768]{3,2,1,0:T(8,128)(2,1)S(1)} collective-permute-done((bf16[2,4,8,768]{3,2,1,0:T(8,128)(2,1)S(1)}, bf16[2,4,8,768]{3,2,1,0:T(8,128)(2,1)S(1)}, u32[]{:S(2)}, u32[]{:S(2)}) %collective-permute-start.36) | collective-permute-done | bytes 98336 | tf_op jit(solution)/shard_map/ppermute | solution.py:63
  358.6 5.3 %collective-permute-done.35 = bf16[12,2,8,768]{3,2,1,0:T(8,128)(2,1)S(1)} collective-permute-done((bf16[12,2,8,768]{3,2,1,0:T(8,128)(2,1)S(1)}, bf16[12,2,8,768]{3,2,1,0:T(8,128)(2,1)S(1)}, u32[]{:S(2)}, u32[]{:S(2)}) %collective-permute-start.35) | collective-permute-done | bytes 294944 | tf_op jit(solution)/shard_map/ppermute | solution.py:63
  368.9 4.8 %collective-permute-start.40 = (bf16[12,8,768]{2,1,0:T(8,128)(2,1)S(1)}, bf16[12,8,768]{2,1,0:T(8,128)(2,1)S(1)}, u32[]{:S(2)}, u32[]{:S(2)}) collective-permute-start(bf16[12,8,768]{2,1,0:T(8,128)(2,1)S(1)} %select_bitcast_fusion.19), channel_id=1, source_target_pairs={{0,16},{8,24},{16,0},{24,8},{1,17},{9,25},{17,1},{25,9},{2,18},{10... | collective-permute-start | bytes 442376 | tf_op jit(solution)/shard_map/ppermute | solution.py:63
  373.7 7.7 %shard_map.198 = bf16[4096,256]{1,0:T(8,128)(2,1)S(1)} custom-call(bf16[4096,256]{1,0:T(8,128)(2,1)S(1)} %get-tuple-element.369.gz_ref, f32[4096,256]{1,0:T(8,128)S(1)} %get-tuple-element.370.d_hidden_ref, bf16[9,256,256]{2,1,0:T(8,128)(2,1)S(1)} %copy-done.4), custom_call_target="tpu_custom_call" | custom-call | flops 4831838208 | bytes 8388608 | tf_op jit(solution)/shard_map/pallas_call | solution.py:1004
  409.6 22.4 %collective-permute-done.42 = bf16[16,64,256]{2,1,0:T(8,128)(2,1)S(1)} collective-permute-done((bf16[16,64,256]{2,1,0:T(8,128)(2,1)}, bf16[16,64,256]{2,1,0:T(8,128)(2,1)S(1)}, u32[]{:S(2)}, u32[]{:S(2)}) %collective-permute-start.42) | collective-permute-done | bytes 524320 | tf_op jit(solution)/shard_map/ppermute | solution.py:63
  437.3 6.8 %subtract_select_fusion = (f32[8,256,256]{2,1,0:T(8,128)}, f32[8,256,256]{2,1,0:T(8,128)}, f32[8,256,256]{2,1,0:T(8,128)}) fusion(f32[8,256,256]{2,1,0:T(8,128)} %param.20, pred[8]{0:T(512)(128)(4,1)S(1)} %compare_bitcast_fusion, f32[8,256,256]{2,1,0:T(8,128)} %param.21, f32[8,256,256]{2,1,0:T(8,128)} %param.22, ...), kind=kLoop, calls=%fused_computation.14 | loop fusion | flops 10485760 | bytes 13632004 | tf_op jit(solution)/shard_map/jit(_where)/select_n | solution.py:1222
  (311 shorter events, 139.0 us)
Async XLA Ops:
  10.0 33.7 %all-to-all-start = ((bf16[32,8,8,256]{3,2,1,0:T(8,128)(2,1)}), bf16[32,8,8,256]{3,2,1,0:T(8,128)(2,1)S(1)}, u32[]{:S(2)}, u32[]{:S(2)}) async-start(bf16[32,8,8,256]{3,2,1,0:T(8,128)(2,1)} %copy.277), calls=%async_computation | async-start | bytes 2097152 | tf_op jit(solution)/shard_map/all_to_all | solution.py:1047
  17.3 159.4 %all-gather.2.cloned.1.call-start = ((), (), s32[]{:S(2)}) async-start(), calls=%async_computation.2 | async-start | bytes 9732096 | tf_op jit(solution)/shard_map/all_gather | solution.py:1053
  57.4 23.0 %collective-permute-start = (bf16[16,64,256]{2,1,0:T(8,128)(2,1)S(1)}, bf16[16,64,256]{2,1,0:T(8,128)(2,1)S(1)}, u32[]{:S(2)}, u32[]{:S(2)}) collective-permute-start(bf16[16,64,256]{2,1,0:T(8,128)(2,1)S(1)} %get-tuple-element.421), channel_id=1, source_target_pairs={{0,1},{1,0},{2,3},{3,2},{4,5},{5,4},{6,7},{7,6},{8,9},{9,8},{10,11... | collective-permute-start | bytes 1572872 | tf_op jit(solution)/shard_map/ppermute | solution.py:63
  68.1 40.4 %collective-permute-start.14 = (bf16[13,4,4,8,256]{4,3,0,2,1:T(8,128)(2,1)S(1)}, bf16[13,4,4,8,256]{4,3,0,2,1:T(8,128)(2,1)S(1)}, u32[]{:S(2)}, u32[]{:S(2)}) collective-permute-start(bf16[13,4,4,8,256]{4,3,0,2,1:T(8,128)(2,1)S(1)} %get-tuple-element.441), channel_id=1, source_target_pairs={{0,4},{4,0},{1,5},{5,1},{2,6},{6,2},{3,7},{7,3},{8,12},{12,8},{9,1... | collective-permute-start | bytes 2555912 | tf_op jit(solution)/shard_map/ppermute | solution.py:63
  68.2 25.5 %collective-permute-start.1 = (bf16[16,64,256]{2,1,0:T(8,128)(2,1)S(1)}, bf16[16,64,256]{2,1,0:T(8,128)(2,1)S(1)}, u32[]{:S(2)}, u32[]{:S(2)}) collective-permute-start(bf16[16,64,256]{2,1,0:T(8,128)(2,1)S(1)} %get-tuple-element.423), channel_id=1, source_target_pairs={{0,2},{1,3},{2,0},{3,1},{4,6},{5,7},{6,4},{7,5},{8,10},{9,11},{10,... | collective-permute-start | bytes 1572872 | tf_op jit(solution)/shard_map/ppermute | solution.py:63
  78.6 24.2 %collective-permute-start.2 = (bf16[16,64,256]{2,1,0:T(8,128)(2,1)S(1)}, bf16[16,64,256]{2,1,0:T(8,128)(2,1)S(1)}, u32[]{:S(2)}, u32[]{:S(2)}) collective-permute-start(bf16[16,64,256]{2,1,0:T(8,128)(2,1)S(1)} %get-tuple-element.420), channel_id=1, source_target_pairs={{0,3},{1,2},{2,1},{3,0},{4,7},{5,6},{6,5},{7,4},{8,11},{9,10},{10,... | collective-permute-start | bytes 1572872 | tf_op jit(solution)/shard_map/ppermute | solution.py:63
  79.6 27.6 %collective-permute-start.10 = (bf16[7,4,8,768]{3,2,1,0:T(8,128)(2,1)S(1)}, bf16[7,4,8,768]{3,2,1,0:T(8,128)(2,1)S(1)}, u32[]{:S(2)}, u32[]{:S(2)}) collective-permute-start(bf16[7,4,8,768]{3,2,1,0:T(8,128)(2,1)S(1)} %pad_maximum_fusion.6), channel_id=1, source_target_pairs={{0,2},{2,0},{1,3},{3,1},{4,6},{6,4},{5,7},{7,5},{8,10},{10,8},{9,1... | collective-permute-start | bytes 1032200 | tf_op jit(solution)/shard_map/ppermute | solution.py:63
  80.5 26.8 %collective-permute-start.9 = (bf16[6,4,8,768]{3,2,1,0:T(8,128)(2,1)S(1)}, bf16[6,4,8,768]{3,2,1,0:T(8,128)(2,1)S(1)}, u32[]{:S(2)}, u32[]{:S(2)}) collective-permute-start(bf16[6,4,8,768]{3,2,1,0:T(8,128)(2,1)S(1)} %pad_maximum_fusion.9), channel_id=1, source_target_pairs={{0,1},{1,0},{2,3},{3,2},{4,5},{5,4},{6,7},{7,6},{8,9},{9,8},{10,11... | collective-permute-start | bytes 884744 | tf_op jit(solution)/shard_map/ppermute | solution.py:63
  107.4 25.3 %collective-permute-start.16 = (bf16[7,2,4,8,768]{4,3,2,1,0:T(8,128)(2,1)S(1)}, bf16[7,2,4,8,768]{4,3,2,1,0:T(8,128)(2,1)}, u32[]{:S(2)}, u32[]{:S(2)}) collective-permute-start(bf16[7,2,4,8,768]{4,3,2,1,0:T(8,128)(2,1)S(1)} %pad_maximum_fusion.4), channel_id=1, source_target_pairs={{0,1},{1,0},{2,3},{3,2},{4,5},{5,4},{6,7},{7,6},{8,9},{9,8},{10,11... | collective-permute-start | bytes 2064392 | tf_op jit(solution)/shard_map/ppermute | solution.py:63
  221.2 26.2 %collective-permute-start.19 = (bf16[12,4,2,2,8,768]{5,4,1,0,3,2:T(8,128)(2,1)}, bf16[12,4,2,2,8,768]{5,4,1,0,3,2:T(8,128)(2,1)}, u32[]{:S(2)}, u32[]{:S(2)}) collective-permute-start(bf16[12,4,2,2,8,768]{5,4,1,0,3,2:T(8,128)(2,1)} %copy.289), channel_id=1, source_target_pairs={{0,4},{4,0},{1,5},{5,1},{2,6},{6,2},{3,7},{7,3},{8,12},{12,8},{9,1... | collective-permute-start | bytes 7077896 | tf_op jit(solution)/shard_map/ppermute | solution.py:63
  222.9 24.5 %collective-permute-start.20 = (bf16[12,4,2,2,8,768]{5,4,1,0,2,3:T(8,128)(2,1)}, bf16[12,4,2,2,8,768]{5,4,1,0,2,3:T(8,128)(2,1)}, u32[]{:S(2)}, u32[]{:S(2)}) collective-permute-start(bf16[12,4,2,2,8,768]{5,4,1,0,2,3:T(8,128)(2,1)} %copy.290), channel_id=1, source_target_pairs={{0,4},{4,0},{1,5},{5,1},{2,6},{6,2},{3,7},{7,3},{8,12},{12,8},{9,1... | collective-permute-start | bytes 7077896 | tf_op jit(solution)/shard_map/ppermute | solution.py:63
  224.5 22.8 %collective-permute-start.21 = (bf16[3,4,2,2,8,768]{5,4,1,0,2,3:T(8,128)(2,1)S(1)}, bf16[3,4,2,2,8,768]{5,4,1,0,2,3:T(8,128)(2,1)S(1)}, u32[]{:S(2)}, u32[]{:S(2)}) collective-permute-start(bf16[3,4,2,2,8,768]{5,4,1,0,2,3:T(8,128)(2,1)S(1)} %copy.291), channel_id=1, source_target_pairs={{0,4},{4,0},{1,5},{5,1},{2,6},{6,2},{3,7},{7,3},{8,12},{12,8},{9,1... | collective-permute-start | bytes 1769480 | tf_op jit(solution)/shard_map/ppermute | solution.py:63
  261.9 28.7 %collective-permute-start.22 = (bf16[9,4,2,2,8,768]{5,4,1,0,2,3:T(8,128)(2,1)}, bf16[9,4,2,2,8,768]{5,4,1,0,2,3:T(8,128)(2,1)}, u32[]{:S(2)}, u32[]{:S(2)}) collective-permute-start(bf16[9,4,2,2,8,768]{5,4,1,0,2,3:T(8,128)(2,1)} %copy.294), channel_id=1, source_target_pairs={{0,4},{4,0},{1,5},{5,1},{2,6},{6,2},{3,7},{7,3},{8,12},{12,8},{9,1... | collective-permute-start | bytes 5308424 | tf_op jit(solution)/shard_map/ppermute | solution.py:63
  262.4 28.2 %collective-permute-start.23 = (bf16[12,4,2,8,768]{4,3,1,0,2:T(8,128)(2,1)}, bf16[12,4,2,8,768]{4,3,1,0,2:T(8,128)(2,1)}, u32[]{:S(2)}, u32[]{:S(2)}) collective-permute-start(bf16[12,4,2,8,768]{4,3,1,0,2:T(8,128)(2,1)} %get-tuple-element.288), channel_id=1, source_target_pairs={{0,2},{2,0},{1,3},{3,1},{4,6},{6,4},{5,7},{7,5},{8,10},{10,8},{9,1... | collective-permute-start | bytes 3538952 | tf_op jit(solution)/shard_map/ppermute | solution.py:63
  262.4 28.2 %collective-permute-start.24 = (bf16[12,4,2,8,768]{4,3,1,0,2:T(8,128)(2,1)}, bf16[12,4,2,8,768]{4,3,1,0,2:T(8,128)(2,1)}, u32[]{:S(2)}, u32[]{:S(2)}) collective-permute-start(bf16[12,4,2,8,768]{4,3,1,0,2:T(8,128)(2,1)} %get-tuple-element.290), channel_id=1, source_target_pairs={{0,1},{1,0},{2,3},{3,2},{4,5},{5,4},{6,7},{7,6},{8,9},{9,8},{10,11... | collective-permute-start | bytes 3538952 | tf_op jit(solution)/shard_map/ppermute | solution.py:63
  300.4 30.5 %collective-permute-start.25 = (bf16[12,4,8,768]{3,2,1,0:T(8,128)(2,1)S(1)}, bf16[12,4,8,768]{3,2,1,0:T(8,128)(2,1)S(1)}, u32[]{:S(2)}, u32[]{:S(2)}) collective-permute-start(bf16[12,4,8,768]{3,2,1,0:T(8,128)(2,1)S(1)} %get-tuple-element.307), channel_id=1, source_target_pairs={{0,1},{1,0},{2,3},{3,2},{4,5},{5,4},{6,7},{7,6},{8,9},{9,8},{10,11... | collective-permute-start | bytes 1769480 | tf_op jit(solution)/shard_map/ppermute | solution.py:63
  301.3 29.6 %collective-permute-start.26 = (bf16[12,4,8,768]{3,2,1,0:T(8,128)(2,1)S(1)}, bf16[12,4,8,768]{3,2,1,0:T(8,128)(2,1)S(1)}, u32[]{:S(2)}, u32[]{:S(2)}) collective-permute-start(bf16[12,4,8,768]{3,2,1,0:T(8,128)(2,1)S(1)} %get-tuple-element.309), channel_id=1, source_target_pairs={{0,2},{2,0},{1,3},{3,1},{4,6},{6,4},{5,7},{7,5},{8,10},{10,8},{9,1... | collective-permute-start | bytes 1769480 | tf_op jit(solution)/shard_map/ppermute | solution.py:63
  302.5 28.4 %collective-permute-start.27 = (bf16[6,4,2,8,768]{4,3,1,0,2:T(8,128)(2,1)S(1)}, bf16[6,4,2,8,768]{4,3,1,0,2:T(8,128)(2,1)S(1)}, u32[]{:S(2)}, u32[]{:S(2)}) collective-permute-start(bf16[6,4,2,8,768]{4,3,1,0,2:T(8,128)(2,1)S(1)} %get-tuple-element.311), channel_id=1, source_target_pairs={{0,1},{1,0},{2,3},{3,2},{4,5},{5,4},{6,7},{7,6},{8,9},{9,8},{10,11... | collective-permute-start | bytes 1769480 | tf_op jit(solution)/shard_map/ppermute | solution.py:63
  304.2 26.7 %collective-permute-start.28 = (bf16[6,4,2,8,768]{4,3,1,0,2:T(8,128)(2,1)S(1)}, bf16[6,4,2,8,768]{4,3,1,0,2:T(8,128)(2,1)S(1)}, u32[]{:S(2)}, u32[]{:S(2)}) collective-permute-start(bf16[6,4,2,8,768]{4,3,1,0,2:T(8,128)(2,1)S(1)} %select_bitcast_fusion.5), channel_id=1, source_target_pairs={{0,2},{2,0},{1,3},{3,1},{4,6},{6,4},{5,7},{7,5},{8,10},{10,8},{9,1... | collective-permute-start | bytes 1769480 | tf_op jit(solution)/shard_map/ppermute | solution.py:63
  304.5 26.4 %collective-permute-start.29 = (bf16[2,4,2,2,8,768]{5,4,3,2,1,0:T(8,128)(2,1)S(1)}, bf16[2,4,2,2,8,768]{5,4,3,2,1,0:T(8,128)(2,1)S(1)}, u32[]{:S(2)}, u32[]{:S(2)}) collective-permute-start(bf16[2,4,2,2,8,768]{5,4,3,2,1,0:T(8,128)(2,1)S(1)} %bitcast.363), channel_id=1, source_target_pairs={{0,4},{4,0},{1,5},{5,1},{2,6},{6,2},{3,7},{7,3},{8,12},{12,8},{9,1... | collective-permute-start | bytes 1179656 | tf_op jit(solution)/shard_map/ppermute | solution.py:63
  351.1 30.4 %collective-permute-start.41 = (bf16[24,8,768]{2,1,0:T(8,128)(2,1)S(1)}, bf16[24,8,768]{2,1,0:T(8,128)(2,1)S(1)}, u32[]{:S(2)}, u32[]{:S(2)}) collective-permute-start(bf16[24,8,768]{2,1,0:T(8,128)(2,1)S(1)} %select_bitcast_fusion.12), channel_id=1, source_target_pairs={{0,16},{8,24},{16,0},{24,8},{1,17},{9,25},{17,1},{25,9},{2,18},{10... | collective-permute-start | bytes 884744 | tf_op jit(solution)/shard_map/ppermute | solution.py:63
  403.5 31.7 %all-to-all-start.1 = ((bf16[32,9,8,256]{3,2,1,0:T(8,128)(2,1)}), bf16[32,9,8,256]{3,2,1,0:T(8,128)(2,1)S(1)}, u32[]{:S(2)}, u32[]{:S(2)}) async-start(bf16[32,9,8,256]{3,2,1,0:T(8,128)(2,1)} %bitcast.173), calls=%async_computation.1 | async-start | bytes 2359296 | tf_op jit(solution)/shard_map/all_to_all | solution.py:1200
  406.1 25.9 %collective-permute-start.42 = (bf16[16,64,256]{2,1,0:T(8,128)(2,1)}, bf16[16,64,256]{2,1,0:T(8,128)(2,1)S(1)}, u32[]{:S(2)}, u32[]{:S(2)}) collective-permute-start(bf16[16,64,256]{2,1,0:T(8,128)(2,1)} %get-tuple-element.414), channel_id=1, source_target_pairs={{0,1},{1,0},{2,3},{3,2},{4,5},{5,4},{6,7},{7,6},{8,9},{9,8},{10,11... | collective-permute-start | bytes 1572872 | tf_op jit(solution)/shard_map/ppermute | solution.py:63
  407.8 24.2 %collective-permute-start.43 = (bf16[16,64,256]{2,1,0:T(8,128)(2,1)}, bf16[16,64,256]{2,1,0:T(8,128)(2,1)S(1)}, u32[]{:S(2)}, u32[]{:S(2)}) collective-permute-start(bf16[16,64,256]{2,1,0:T(8,128)(2,1)} %get-tuple-element.413), channel_id=1, source_target_pairs={{0,2},{1,3},{2,0},{3,1},{4,6},{5,7},{6,4},{7,5},{8,10},{9,11},{10,... | collective-permute-start | bytes 1572872 | tf_op jit(solution)/shard_map/ppermute | solution.py:63
  (69 other events, 773.5 us)
Sparse Core Ops, SparseCore 0:
  45.4 109.8 all-gather.1

commit v8 on v7

--- a/solution.py
+++ b/solution.py
@@ -243,17 +243,6 @@
 def slice_shape():
     z, c, y, x = [lax.axis_size(axis) for axis in AXES]
     return (z, y, x, CH // (z * c * y * x))
-
-
-def cut_core(matrix):
-    z, y, x, rows = slice_shape()
-    parts = matrix.astype(bf16).reshape(-1, z, 2, y, x, rows, matrix.shape[-1])
-    own = lax.axis_index("c")
-    return [lax.dynamic_index_in_dim(parts, own ^ other, 2, False) for other in range(2)]
-
-
-def core_parts(parts):
-    return [part.reshape((-1,) + slice_shape() + part.shape[-1:]) for part in parts]
 
 
 tie = lax.optimization_barrier
@@ -534,7 +523,7 @@
     out_ref[2] = dv_s[...].astype(bf16)
 
 
-def self_backward(qkv, d_out, out, log_rows, length):
+def self_backward(qkv, d_out, out, log_rows, length, count):
     groups = D // CH
     at = lambda j: (lambda i, n: (j, 0, i))
     here = lambda i, n: (0, i)
@@ -542,7 +531,7 @@
         self_backward_kernel,
         grid_spec=pltpu.PrefetchScalarGridSpec(
             num_scalar_prefetch=1,
-            grid=(groups,),
+            grid=(count,),
             in_specs=[pl.BlockSpec((1, SEQ, CH), at(j)) for j in range(3)]
             + [
                 pl.BlockSpec((SEQ, CH), here),
@@ -552,10 +541,12 @@
             out_specs=pl.BlockSpec((3, SEQ, CH), lambda i, n: (0, 0, i)),
             scratch_shapes=[pltpu.VMEM((SEQ, CH), f32), pltpu.VMEM((SEQ, CH), f32)],
         ),
-        out_shape=jax.ShapeDtypeStruct((3, SEQ, D), bf16),
+        out_shape=jax.ShapeDtypeStruct((3, SEQ, count * CH), bf16),
         compiler_params=params(),
-        cost_estimate=cost(8 * HEADS * SEQ * SEQ * CH, 16 * SEQ * D, HEADS * SEQ * SEQ),
-    )(length, qkv, qkv, qkv, d_out, out, log_rows)
+        cost_estimate=cost(
+            8 * HEADS * SEQ * SEQ * CH * count // groups, 16 * SEQ * D, HEADS * SEQ * SEQ
+        ),
+    )(length, stay(qkv), stay(qkv), stay(qkv), d_out, stay(out), log_rows)
 
 
 def full(*shape):
@@ -574,17 +565,50 @@
     return ref[...].reshape(D, D)
 
 
-def write_cores(core, matrix, keep_ref, give_ref, span):
-    parts = matrix.reshape(-1, 2, span, matrix.shape[-1])
+def write_cores(core, matrix, keep_refs, sizes, order, at=0):
+    z, y, x, rows = sizes
+    columns = matrix.shape[-1]
+    if rows % 8:
+        parts = matrix.reshape(-1, 2, y * x * rows, columns)
+    else:
+        parts = matrix.reshape(-1, 2, y, x, rows, columns)
     first, second = parts[:, 0], parts[:, 1]
-    keep = jnp.where(core == 0, first, second)
-    give = jnp.where(core == 0, second, first)
-    keep_ref[...] = keep.reshape(keep_ref.shape).astype(bf16)
-    give_ref[...] = give.reshape(give_ref.shape).astype(bf16)
-
-
-def core_span():
-    return CH // (2 * lax.axis_size("z"))
+    halves = (jnp.where(core == 0, first, second), jnp.where(core == 0, second, first))
+    for ref, half in zip(keep_refs, halves):
+        here = slice(at * z, at * z + half.shape[0])
+        if rows % 8:
+            ref[here] = half.astype(bf16)
+            continue
+        for row in range(y):
+            for col in range(x):
+                to = (col, row) if order == "xy" else (row, col)
+                ref[to[0], to[1], here] = half[:, row, col].astype(bf16)
+
+
+def core_shape(count, order, columns=D):
+    z, y, x, rows = slice_shape()
+    if rows % 8:
+        return (count * z, y * x * rows, columns)
+    cuts = (x, y) if order == "xy" else (y, x)
+    return cuts + (count * z, rows, columns)
+
+
+def core_block(count, order, at, columns=D):
+    shape = core_shape(count, order, columns)
+    return pl.BlockSpec(shape, lambda i: (0,) * (len(shape) - 3) + (at(i), 0, 0))
+
+
+def core_cuts(parts, order):
+    z, y, x, rows = slice_shape()
+    if rows % 8 == 0:
+        return list(parts)
+    parts = [part.reshape(-1, y, x, rows, part.shape[-1]) for part in parts]
+    dims = (2, 1, 0, 3, 4) if order == "xy" else (1, 2, 0, 3, 4)
+    return [part.transpose(dims) for part in parts]
+
+
+def split_z(slices):
+    return slices.reshape((-1, lax.axis_size("z")) + slices.shape[1:])
 
 
 def row_here():
@@ -593,9 +617,6 @@
 
 def core_here():
     return lax.axis_index("c").astype(jnp.int32).reshape(1)
-
-
-HALF = D // 2
 
 
 def row_scale(values):
@@ -661,7 +682,7 @@
     core_ref, mixed_ref, embed_ref, att_ref, up_ref, down_ref, gain_ref, gd_ref,
     out_ref, d_stream_ref, gog_ref, up_keep_ref, up_give_ref, down_keep_ref, down_give_ref,
     att_keep_ref, att_give_ref, gain_g_ref,
-    stream_s, normed_s, turned_s, act_s, gpre_s, total_s, *, span
+    stream_s, normed_s, turned_s, act_s, gpre_s, total_s, *, sizes
 ):
     step = pl.program_id(0)
     core = core_ref[0]
@@ -678,7 +699,7 @@
 
     factor = (2.0 / 3.141592653589793) ** 0.5
     cubic = 0.044715 * factor
-    rows = SEQ // 4
+    rows = SEQ // 2
     for start in range(0, SEQ, rows):
         here = slice(start, start + rows)
         v = dot_nn(normed_s[here, :], square(up_ref))
@@ -691,8 +712,9 @@
         gpre_s[here, :] = gpre
         out_ref[here, :] += dot_nn(act, square(down_ref))
         total_s[here, :] += dot_nt(gpre, square(up_ref))
-    write_cores(core, dot_tn(act_s[...], gd_ref[...]), down_keep_ref, down_give_ref, span)
-    write_cores(core, dot_nn(turned_s[...], gpre_s[...]), up_keep_ref, up_give_ref, span)
+    down_refs, up_refs = (down_keep_ref, down_give_ref), (up_keep_ref, up_give_ref)
+    write_cores(core, dot_tn(act_s[...], gd_ref[...]), down_refs, sizes, "xy")
+    write_cores(core, dot_nn(turned_s[...], gpre_s[...]), up_refs, sizes, "yx")
 
     @pl.when(step == pl.num_programs(0) - 1)
     def _():
@@ -702,13 +724,16 @@
         d_stream_ref[...] = d_stream
         ga = d_stream.astype(bf16)
         gog_ref[...] = dot_nt(ga, square(att_ref)).astype(bf16)
-        write_cores(core, dot_tn(mixed_ref[...], ga), att_keep_ref, att_give_ref, span)
+        att_refs = (att_keep_ref, att_give_ref)
+        write_cores(core, dot_tn(mixed_ref[...], ga), att_refs, sizes, "yx")
 
 
 def mlp_block(mixed, embed, weights, mlp, gain, gd):
-    half = pl.BlockSpec((HALF, D), lambda i: (i, 0))
+    up_part = core_block(3, "yx", lambda i: i)
+    down_part = core_block(3, "xy", lambda i: i)
+    att_part = core_block(3, "yx", lambda i: 0)
     return pl.pallas_call(
-        functools.partial(mlp_kernel, span=core_span()),
+        functools.partial(mlp_kernel, sizes=slice_shape()),
         grid=(4,),
         in_specs=[
             CORE_SPEC,
@@ -720,14 +745,19 @@
             full(1, D),
             full(SEQ, D),
         ],
-        out_specs=[full(SEQ, D)] * 3 + [half] * 4 + [full(HALF, D)] * 2 + [full(1, D)],
+        out_specs=[full(SEQ, D)] * 3
+        + [up_part] * 2
+        + [down_part] * 2
+        + [att_part] * 2
+        + [full(1, D)],
         out_shape=[
             lasting((SEQ, D), f32),
             lasting((SEQ, D), f32),
             jax.ShapeDtypeStruct((SEQ, D), bf16),
         ]
-        + [jax.ShapeDtypeStruct((4 * HALF, D), bf16)] * 4
-        + [jax.ShapeDtypeStruct((HALF, D), bf16)] * 2
+        + [jax.ShapeDtypeStruct(core_shape(12, "yx"), bf16)] * 2
+        + [jax.ShapeDtypeStruct(core_shape(12, "xy"), bf16)] * 2
+        + [jax.ShapeDtypeStruct(core_shape(3, "yx"), bf16)] * 2
         + [jax.ShapeDtypeStruct((1, D), f32)],
         scratch_shapes=[
             pltpu.VMEM((SEQ, D), f32),
@@ -742,52 +772,47 @@
     )(core_here(), mixed, embed, stay(weights), stay(mlp), stay(mlp), gain, gd)
 
 
-def qkv_grad_kernel(core_ref, normed_ref, g_ref, keep_ref, give_ref, turned_s, *, span):
-    @pl.when(pl.program_id(0) == 0)
-    def _():
-        turned_s[...] = normed_ref[...].T
-
-    write_cores(core_ref[0], dot_nn(turned_s[...], g_ref[0]), keep_ref, give_ref, span)
-
-
-def qkv_grad(normed, gqkv):
-    half = pl.BlockSpec((HALF, D), lambda i: (i, 0))
-    return pl.pallas_call(
-        functools.partial(qkv_grad_kernel, span=core_span()),
-        grid=(3,),
-        in_specs=[CORE_SPEC, full(SEQ, D), pl.BlockSpec((1, SEQ, D), lambda i: (i, 0, 0))],
-        out_specs=[half, half],
-        out_shape=[jax.ShapeDtypeStruct((3 * HALF, D), bf16)] * 2,
-        scratch_shapes=[pltpu.VMEM((D, SEQ), bf16)],
-        compiler_params=params(),
-        cost_estimate=cost(6 * SEQ * D * D, 14 * SEQ * D),
-    )(core_here(), normed, gqkv)
-
-
 def embed_grad_kernel(
-    core_ref, g_ref, w_ref, emb_ref, embed_ref, d_stream_ref, seq_ref, mixed_ref, out_w_ref,
+    core_ref, len_ref, q_ref, k_ref, v_ref, do_ref, o_ref, l_ref,
+    g_ref, normed_ref, w_ref, emb_ref, embed_ref, d_stream_ref, seq_ref, mixed_ref, out_w_ref,
     gain_ref, gain_g_ref,
-    keep_ref, give_ref, gupd_ref, pool_g_ref, out_g_ref, gox_ref, total_s, *, span, rows
+    qk_keep_ref, qk_give_ref, v_keep_ref, v_give_ref, keep_ref, give_ref,
+    gupd_ref, pool_g_ref, out_g_ref, gox_ref,
+    dk_s, dv_s, last_s, turned_s, total_s, *, sizes
 ):
     step = pl.program_id(0)
-    part = dot_nt(g_ref[0], square(w_ref))
+    core = core_ref[0]
 
     @pl.when(step == 0)
     def _():
-        total_s[...] = part
+        self_backward_kernel(
+            len_ref, q_ref, k_ref, v_ref, do_ref, o_ref, l_ref, last_s, dk_s, dv_s
+        )
+        turned_s[...] = normed_ref[...].T
+        total_s[...] = jnp.zeros_like(total_s)
 
     @pl.when(step > 0)
     def _():
-        total_s[...] += part
-
-    @pl.when(step == pl.num_programs(0) - 1)
+        g = jnp.concatenate([g_ref[0], last_s[step - 1]], 1)
+        total_s[...] += dot_nt(g, square(w_ref))
+        grad = dot_nn(turned_s[...], g)
+
+        @pl.when(step < 3)
+        def _():
+            write_cores(core, grad, (qk_keep_ref, qk_give_ref), sizes, "xy")
+
+        @pl.when(step == 3)
+        def _():
+            write_cores(core, grad, (v_keep_ref, v_give_ref), sizes, "yx")
+
+    @pl.when(step == 3)
     def _():
         d_gain, pulled = pull_norm(total_s[...], embed_ref[...], gain_ref[...])
         gembed = (d_stream_ref[...] + pulled).astype(bf16)
         at = lax.broadcasted_iota(jnp.int32, (CH, D), 0)
-        gains = jnp.where(at == 0, d_gain, jnp.where(at == rows, gain_g_ref[...], 0.0))
+        gains = jnp.where(at == 0, d_gain, jnp.where(at == sizes[-1], gain_g_ref[...], 0.0))
         for index, values in enumerate((dot_tn(seq_ref[...], gembed), gains)):
-            write_cores(core_ref[0], values, keep_ref.at[index], give_ref.at[index], span)
+            write_cores(core, values, (keep_ref, give_ref), sizes, "xy", index)
         gseq = dot_nt(gembed, emb_ref[0])
         gupd = gseq[CTX:]
         gb = gupd.astype(bf16)
@@ -797,15 +822,34 @@
         gox_ref[...] = dot_nt(gb, out_w_ref[...]).astype(bf16)
 
 
-def embed_grad(gqkv, weights, embed, d_stream, seq, mixed, to_out, gain, gain_g):
+def embed_grad(
+    length, qkv, gog, out, log_rows, gqkv, normed, weights, embed, d_stream, seq, mixed, to_out,
+    gain, gain_g,
+):
     last = weights.shape[0] - 1
+    group = D // CH - 1
+    done = gqkv.shape[-1]
+    part = lambda i: jnp.maximum(i - 1, 0)
+    at = lambda j: pl.BlockSpec((1, SEQ, CH), lambda i: (j, 0, group))
+    here = pl.BlockSpec((SEQ, CH), lambda i: (0, group))
+    qk_part = core_block(3, "xy", lambda i: jnp.clip(i - 1, 0, 1))
+    v_part = core_block(3, "yx", lambda i: 0)
+    emb_part = core_block(2, "xy", lambda i: 0)
     return pl.pallas_call(
-        functools.partial(embed_grad_kernel, span=core_span(), rows=CH // lax.axis_size(AXES)),
-        grid=(3,),
+        functools.partial(embed_grad_kernel, sizes=slice_shape()),
+        grid=(4,),
         in_specs=[
             CORE_SPEC,
-            pl.BlockSpec((1, SEQ, D), lambda i: (i, 0, 0)),
-            part_of(0),
+            CORE_SPEC,
+            at(0),
+            at(1),
+            at(2),
+            here,
+            here,
+            pl.BlockSpec((1, 8, SEQ), lambda i: (group, 0, 0)),
+            pl.BlockSpec((1, SEQ, done), lambda i: (part(i), 0, 0)),
+            full(SEQ, D),
+            pl.BlockSpec((3, CH, D), lambda i: (part(i), 0, 0)),
             pl.BlockSpec((1, CH, D), lambda i: (last, 0, 0)),
             full(SEQ, D),
             full(SEQ, D),
@@ -816,27 +860,38 @@
             full(1, D),
         ],
         out_specs=[
-            full(2, CH // 2, D),
-            full(2, CH // 2, D),
+            qk_part,
+            qk_part,
+            v_part,
+            v_part,
+            emb_part,
+            emb_part,
             full(SEQ - CTX, CH),
             full(CTX, CH),
             full(CH, CH),
             full(SEQ - CTX, CH),
         ],
-        out_shape=[
-            jax.ShapeDtypeStruct((2, CH // 2, D), bf16),
-            jax.ShapeDtypeStruct((2, CH // 2, D), bf16),
+        out_shape=[jax.ShapeDtypeStruct(core_shape(6, "xy"), bf16)] * 2
+        + [jax.ShapeDtypeStruct(core_shape(3, "yx"), bf16)] * 2
+        + [jax.ShapeDtypeStruct(core_shape(2, "xy"), bf16)] * 2
+        + [
             jax.ShapeDtypeStruct((SEQ - CTX, CH), f32),
             jax.ShapeDtypeStruct((CTX, CH), bf16),
             jax.ShapeDtypeStruct((CH, CH), bf16),
             jax.ShapeDtypeStruct((SEQ - CTX, CH), bf16),
         ],
-        scratch_shapes=[pltpu.VMEM((SEQ, D), f32)],
-        compiler_params=params(),
-        cost_estimate=cost(2 * SEQ * D * (3 * D + 2 * CH), 24 * SEQ * D),
+        scratch_shapes=[
+            pltpu.VMEM((SEQ, CH), f32),
+            pltpu.VMEM((SEQ, CH), f32),
+            pltpu.VMEM((3, SEQ, CH), bf16),
+            pltpu.VMEM((D, SEQ), bf16),
+            pltpu.VMEM((SEQ, D), f32),
+        ],
+        compiler_params=pltpu.CompilerParams(vmem_limit_bytes=MLP_BYTES),
+        cost_estimate=cost(2 * SEQ * D * (6 * D + 2 * CH) + 32 * SEQ * SEQ * CH, 50 * SEQ * D),
     )(
-        core_here(), gqkv, stay(weights), stay(weights), stay(embed), stay(d_stream), stay(seq), stay(mixed), to_out,
-        gain, gain_g,
+        core_here(), length, stay(qkv), stay(qkv), stay(qkv), gog, stay(out), log_rows, gqkv, normed, stay(weights),
+        stay(weights), stay(embed), stay(d_stream), stay(seq), stay(mixed), to_out, gain, gain_g,
     )
 
 
@@ -899,7 +954,7 @@
 
 def token_backward_kernel(
     core_ref, dkv_ref, slope_ref, pool_ref, hidden_ref, x_ref, kv_w_ref, query_g_ref, out_g_ref,
-    d_hidden_ref, gz_ref, keep_ref, give_ref, conv_s, kv_s, *, span
+    d_hidden_ref, gz_ref, keep_ref, give_ref, conv_s, kv_s, *, sizes
 ):
     step = pl.program_id(0)
 
@@ -927,16 +982,15 @@
                 tiles.append(conv_s[row, :, col * CH : (col + 1) * CH].T)
         tiles = tiles + [query_g_ref[...], kv_s[:, :CH], kv_s[:, CH:], out_g_ref[...]]
         for at, tile in enumerate(tiles):
-            write_cores(core_ref[0], tile.astype(f32), keep_ref.at[at], give_ref.at[at], span)
+            write_cores(core_ref[0], tile.astype(f32), (keep_ref, give_ref), sizes, "yx", at)
 
 
 def token_backward(dkv, slope, d_pool, hidden_b, wide, kv_weight, query_g, out_g):
     steps = CELLS // BLOCK
     whole = lambda i: (0, 0)
-    whole_3 = lambda i: (0, 0, 0)
     block = lambda i: (i, 0)
     return pl.pallas_call(
-        functools.partial(token_backward_kernel, span=core_span()),
+        functools.partial(token_backward_kernel, sizes=slice_shape()),
         grid=(steps,),
         in_specs=[
             CORE_SPEC,
@@ -952,14 +1006,14 @@
         out_specs=[
             pl.BlockSpec((BLOCK, CH), block),
             pl.BlockSpec((BLOCK, CH), block),
-            pl.BlockSpec((EARLY, CH // 2, CH), whole_3),
-            pl.BlockSpec((EARLY, CH // 2, CH), whole_3),
+            core_block(EARLY, "yx", lambda i: 0, CH),
+            core_block(EARLY, "yx", lambda i: 0, CH),
         ],
         out_shape=[
             jax.ShapeDtypeStruct((CELLS, CH), f32),
             jax.ShapeDtypeStruct((CELLS, CH), bf16),
-            jax.ShapeDtypeStruct((EARLY, CH // 2, CH), bf16),
-            jax.ShapeDtypeStruct((EARLY, CH // 2, CH), bf16),
+            jax.ShapeDtypeStruct(core_shape(EARLY, "yx", CH), bf16),
+            jax.ShapeDtypeStruct(core_shape(EARLY, "yx", CH), bf16),
         ],
         scratch_shapes=[pltpu.VMEM((3, CH, 3 * CH), f32), pltpu.VMEM((CH, 2 * CH), f32)],
         compiler_params=params(),
@@ -1045,7 +1099,17 @@
         .transpose(1, 0, 2, 3)
     )
     slices = lax.all_to_all(slices, AXES, split_axis=0, concat_axis=0, tiled=True)
-    slices, gd = tie((slices, gd))
+    extra = max(1, 8 // rows)
+    tiles = tile_owner.shape[0]
+    span = slot_count + extra
+    place = jnp.arange(devices * span)
+    device, at = place // span, place % span
+    found = slot_of[None, :] == jnp.where(at < slot_count, device * slot_count + at, -1)[:, None]
+    tile_of = jnp.sum(jnp.where(found, jnp.arange(tiles)[None], 0), 1)
+    tile_of = jnp.where(at < slot_count, tile_of, tiles + at - slot_count)
+    mine_at = lax.axis_index(AXES) * slot_count + jnp.arange(slot_count)
+    used = jnp.any(slot_of[None, :] == mine_at[:, None], 1).astype(f32)
+    slices, gd, tile_of, used = tie((slices, gd, tile_of, used))
     slices = slices.reshape(devices * slot_count, rows, CH)
     slices = slices.at[slot_of].get(mode="promise_in_bounds")
     early, emb, qkv, att, up, down = jnp.split(slices, (13, 16, 43, 52, 88))
@@ -1093,48 +1157,43 @@
         block_out, d_stream, gog, up_keep, up_give, down_keep, down_give, att_keep, att_give,
         gain_g_two,
     ) = mlp_block(mixed, embed, weights, mlp, gain_two, gd)
-    gog, up, down, att = tie(
-        (
-            gog,
-            core_parts([up_keep, up_give]),
-            core_parts([down_keep, down_give]),
-            core_parts([att_keep, att_give]),
-        )
-    )
+    up = core_cuts([up_keep, up_give], "yx")
+    down = core_cuts([down_keep, down_give], "xy")
+    att = core_cuts([att_keep, att_give], "yx")
+    gog, up, down, att = tie((gog, up, down, att))
     up, down, att = send(up, "c"), send(down, "c"), send(att, "c")
-    gqkv = self_backward(qkv, gog, mixed, logs, length)
+    gqkv = self_backward(qkv, gog, mixed, logs, length, 2)
     gqkv, up, down, att = hold((gqkv,), up, down, att)
-    up, down = advance(up, "y", 2), advance(down, "x", 3)
+    up, down = advance(up, "y", 0), advance(down, "x", 0)
     gqkv, up, down = tie((gqkv, up, down))
     up, down = send(up, "y"), send(down, "x")
-    qkv_keep, qkv_give = qkv_grad(normed_one, gqkv)
-    gqkv, qkv_keep, qkv_give = tie((gqkv, qkv_keep, qkv_give))
-    qkv = send(core_parts([qkv_keep, qkv_give]), "c")
-    emb_keep, emb_give, gupd, pool_g, out_g, gox = embed_grad(
-        gqkv, weights, embed, d_stream, seq, cross_mixed, to_out, gain_one, gain_g_two
-    )
-    gox, gupd, emb_keep, emb_give, qkv, up, down = hold(
-        (gox, gupd, emb_keep, emb_give), qkv, up, down
-    )
-    up, down = advance(up, "x", 2), advance(down, "y", 2)
-    first = advance([part[:6] for part in qkv], "x", 3)
-    second = advance([jnp.concatenate([p[6:], q], 0) for p, q in zip(qkv, att)], "y", 2)
-    emb = core_parts([emb_keep, emb_give])
+    (
+        qk_keep, qk_give, v_keep, v_give, emb_keep, emb_give, gupd, pool_g, out_g, gox,
+    ) = embed_grad(
+        length, qkv, gog, mixed, logs, gqkv, normed_one, weights, embed, d_stream, seq,
+        cross_mixed, to_out, gain_one, gain_g_two,
+    )
+    first = core_cuts([qk_keep, qk_give], "xy")
+    second = core_cuts([v_keep, v_give], "yx")
+    emb = core_cuts([emb_keep, emb_give], "xy")
+    gox, gupd, first, second, emb, up, down = hold((gox, gupd, first, second, emb), up, down)
+    up, down = advance(up, "x", 0), advance(down, "y", 0)
     gox, up, down, first, second, emb = tie((gox, up, down, first, second, emb))
     up, down, emb = send(up, "x"), send(down, "y"), send(emb, "c")
-    first, second = send(first, "x"), send(second, "y")
+    first, second = send(first, "c"), send(second, "c")
 
     log_rows = jnp.concatenate([cross_logs[0], cross_logs[1]], 1)
     gkv, query_g, future_grad = cross_backward(
         query, kv, gox, cross_mixed, log_rows, feats_b, gupd, to_query
     )
     gkv, up, down, first, second, emb = hold((gkv,), up, down, first, second, emb)
-    mlp = advance_near([jnp.concatenate(part, 0) for part in zip(up, down)])
-    emb = advance(emb, "x", 3)
-    first, second = advance(first, "y", 2), advance(second, "x", 2)
+    mlp = advance_near([split_z(jnp.concatenate(part, 0)) for part in zip(up, down)])
+    emb = advance(emb, "x", 0)
+    second = [jnp.concatenate([p, q], 2) for p, q in zip(second, att)]
+    first, second = advance(first, "x", 0), advance(second, "y", 0)
     gkv, mlp, first, second, emb = tie((gkv, mlp, first, second, emb))
     mlp, emb = send(mlp, "z"), send(emb, "x")
-    first, second = send(first, "y"), send(second, "x")
+    first, second = send(first, "x"), send(second, "y")
 
     d_hidden, gz, early_keep, early_give = token_backward(
         gkv, slope_z, pool_g, hidden_b, wide, kv_weight, query_g, out_g
@@ -1142,25 +1201,26 @@
     d_hidden, gz, early_keep, early_give, mlp, first, second, emb = hold(
         (d_hidden, gz, early_keep, early_give), mlp, first, second, emb
     )
-    early = core_parts([early_keep, early_give])
+    early = core_cuts([early_keep, early_give], "yx")
     early, mlp, first, second, emb = tie((early, mlp, first, second, emb))
     early = send(early, "c")
-    att = advance_near([jnp.concatenate(part, 0) for part in zip(first, second)])
-    emb, mlp = advance(emb, "y", 2), advance_far(mlp)
-    att, emb, mlp = send(att, "z"), send(emb, "y"), send(mlp, "z", 2)
-    gz, early, att, emb = hold((gz,), early, att, emb)
-    shape = early[0].shape
-    early = advance([p.reshape(shape[:2] + (-1,) + shape[4:]) for p in early], ("y", "x"), 2)
-    att = advance_far(att)
+    first, second = advance(first, "y", 0), advance(second, "x", 0)
+    emb, mlp = advance(emb, "y", 0), advance_far(mlp)
+    first, second = send(first, "y"), send(second, "x")
+    emb, mlp = send(emb, "y"), send(mlp, "z", 2)
+    gz, early, first, second, emb = hold((gz,), early, first, second, emb)
+    early = advance([p.reshape((-1,) + p.shape[2:]) for p in early], ("y", "x"), 0)
+    att = advance_near([split_z(jnp.concatenate(part, 0)) for part in zip(first, second)])
     gz, early, att = tie((gz, early, att))
-    early, att = send(early, ("y", "x")), send(att, "z", 2)
+    early, att = send(early, ("y", "x")), send(att, "z")
     context_grad = context_backward(gz, d_hidden, conv_tiles)
     context_grad, early, att, mlp = hold((context_grad,), early, att, mlp)
-    early = advance(early, "z", 1)
-    emb = advance(emb, "z", 1)
+    early = advance([split_z(part) for part in early], "z", 1)
+    emb = advance([split_z(part) for part in emb], "z", 1)
     early = [jnp.concatenate([e, to_tiles(m)], 0) for e, m in zip(early, emb)]
-    context_grad, early = tie((context_grad, early))
-    early = send(early, "z")
+    att = advance_far(att)
+    context_grad, early, att = tie((context_grad, early, att))
+    early, att = send(early, "z"), send(att, "z", 2)
     pieces = trade_rows(context_grad.reshape(context_map.shape))
     sum_mlp = add_up(mlp, keep_wide=True)
     square_mlp = jnp.sum(sum_mlp * sum_mlp)
@@ -1175,7 +1235,6 @@
     share_high = share.astype(bf16)
     share_low = (share - share_high.astype(f32)).astype(bf16)
     share = jnp.concatenate([share_high, share_low], 0)
-    extra = max(1, share.shape[0] // rows)
     share = jnp.pad(share, ((0, extra * rows - share.shape[0]), (0, 0)))
     sums = jnp.concatenate(
         [
@@ -1187,13 +1246,6 @@
         ],
         0,
     )
-    slots = jnp.arange(devices * slot_count)
-    found = slot_of[None, :] == slots[:, None]
-    tiles = found.shape[1]
-    tile_of = jnp.sum(jnp.where(found, jnp.arange(tiles)[None], 0), 1)
-    tile_of = tile_of.reshape(devices, slot_count)
-    shared = jnp.broadcast_to(tiles + jnp.arange(extra)[None], (devices, extra))
-    tile_of = jnp.concatenate([tile_of, shared], 1).reshape(-1)
     mine = sums.at[tile_of].get(mode="promise_in_bounds")
     mine = mine.reshape(devices, slot_count + extra, rows, CH)
     mine, pieces[-1] = tie((mine, pieces[-1]))
@@ -1203,8 +1255,7 @@
     gains = shares[:2, :3].reshape(2, D)
     mine = mine[:, :slot_count].transpose(1, 0, 2, 3).reshape(slot_count, CH, CH).astype(f32)
 
-    used = jnp.any(found, 1).astype(f32).reshape(devices, slot_count)
-    used = lax.dynamic_index_in_dim(used, lax.axis_index(AXES), 0, keepdims=False)[:, None, None]
+    used = used[:, None, None]
     grad_norm = jnp.sqrt(jnp.sum(shares[:, 3, 0]))
     factor = jnp.minimum(1.0, clip_level / (grad_norm + 1e-06))
     new_first, new_second, new_master = adam_step(

time: 458 us -> 429 us (0.937)
  local copies, waits for them, and re-layouts: 43.3 us -> 31 us
  other arithmetic: 38.7 us -> 33.7 us
    optimization_barrier x3 -> x0, local copies, waits for them, and re-layouts: 6.94 us -> none  [local(): tie((gog, core_parts([up_keep, up_give]), core_parts([down_keep, down_giv...]
    convert_element_type x16, other arithmetic: 13.2 us -> 6.89 us  [add_up(): return total if keep_wide else total.astype(parts[0].dtype)]
    ppermute x48 -> x49, starting transfers between devices: 48.9 us -> 45.1 us  [xor_permute(): return lax.ppermute(values, axes, [(i, i ^ mask) for i in range(count)])]
    ppermute x48 -> x49, waiting for transfers between devices: 93.4 us -> 90.2 us  [xor_permute(): return lax.ppermute(values, axes, [(i, i ^ mask) for i in range(count)])]
    pallas_call x4 -> x3, Pallas kernels: 63.6 us -> 65.4 us  [the longest x1 32.3 us: mlp_block(): pl.pallas_call(functools.partial(mlp_kernel, sizes=slice_shape()), grid=(...]
    unnamed x90 -> x109, local copies, waits for them, and re-layouts: 20.5 us -> 19.1 us
  transfers between devices with their start and end apart: 51 -> 52, of which waited for: 17 -> 19; matrix products, arithmetic and copies ran while one was open for 5% -> 6% of each run, Pallas kernels for 29% -> 32%
where the time goes in v8:
time: 429 us; the launch traced here: 424 us
  Pallas kernels  170 us (40%)
  waiting for transfers between devices  114 us (27%)
  starting transfers between devices  56 us (13%)
  other arithmetic  33.7 us (8%)
  local copies, waits for them, and re-layouts  31 us (7%)
  between operations  20 us (5%)
    ppermute x49, waiting for transfers between devices, xor_permute(): return lax.ppermute(values, axes, [(i, i ^ mask) for i in range(count)])  90.2 us
    ppermute x49, starting transfers between devices, xor_permute(): return lax.ppermute(values, axes, [(i, i ^ mask) for i in range(count)])  45.1 us
    pallas_call x1, Pallas kernels, mlp_block(): pl.pallas_call(functools.partial(mlp_kernel, sizes=slice_shape()), grid=(...  32.3 us
    pallas_call x1, Pallas kernels, cross_backward(): pl.pallas_call(cross_backward_kernel, grid=(cells // block,), in_specs=[p...  26.5 us
    all_to_all x1, waiting for transfers between devices, local(): lax.all_to_all(slices, AXES, split_axis=0, concat_axis=0, tiled=True)  22.7 us
    unnamed x109, local copies, waits for them, and re-layouts  19.1 us
    pallas_call x1, Pallas kernels, embed_grad(): pl.pallas_call(functools.partial(embed_grad_kernel, sizes=slice_shape()),...  18.7 us
    pallas_call x1, Pallas kernels, token_forward(): pl.pallas_call(token_forward_kernel, grid=(steps,), in_specs=[pl.BlockSpe...  16.3 us
  transfers between devices with their start and end apart: 52, of which 19 were waited for; matrix products, arithmetic and copies ran while one was open for 6% of the time, Pallas kernels for 32%

profile of v8, /device:TPU:0, one launch (start us, length us, event | category | flops | bytes accessed | tf_op | source)
XLA Modules:
  0.0 424.0 jit_solution(16246167427597740531)
XLA Ops:
  10.0 7.3 %all-to-all-start = ((bf16[32,8,8,256]{3,2,1,0:T(8,128)(2,1)}), bf16[32,8,8,256]{3,2,1,0:T(8,128)(2,1)S(1)}, u32[]{:S(2)}, u32[]{:S(2)}) async-start(bf16[32,8,8,256]{3,2,1,0:T(8,128)(2,1)} %copy.146), calls=%async_computation | async-start | bytes 2097152 | tf_op jit(solution)/shard_map/all_to_all | solution.py:1101
  21.0 22.7 %all-to-all-done = bf16[32,8,8,256]{3,2,1,0:T(8,128)(2,1)S(1)} async-done(((bf16[32,8,8,256]{3,2,1,0:T(8,128)(2,1)}), bf16[32,8,8,256]{3,2,1,0:T(8,128)(2,1)S(1)}, u32[]{:S(2)}, u32[]{:S(2)}) %all-to-all-start) | async-done | bytes 1048608 | tf_op jit(solution)/shard_map/all_to_all | solution.py:1101
  69.3 9.4 %collective-permute-done.7 = bf16[13,8,768]{2,1,0:T(8,128)(2,1)S(1)} collective-permute-done((bf16[13,8,768]{2,1,0:T(8,128)(2,1)S(1)}, bf16[13,8,768]{2,1,0:T(8,128)(2,1)S(1)}, u32[]{:S(2)}, u32[]{:S(2)}) %collective-permute-start.7) | collective-permute-done | bytes 159776 | tf_op jit(solution)/shard_map/ppermute | solution.py:63
  82.3 11.4 %collective-permute-done.1 = bf16[16,64,256]{2,1,0:T(8,128)(2,1)S(1)} collective-permute-done((bf16[16,64,256]{2,1,0:T(8,128)(2,1)S(1)}, bf16[16,64,256]{2,1,0:T(8,128)(2,1)S(1)}, u32[]{:S(2)}, u32[]{:S(2)}) %collective-permute-start.1) | collective-permute-done | bytes 524320 | tf_op jit(solution)/shard_map/ppermute | solution.py:63
  93.7 9.1 %collective-permute-done.2 = bf16[16,64,256]{2,1,0:T(8,128)(2,1)S(1)} collective-permute-done((bf16[16,64,256]{2,1,0:T(8,128)(2,1)S(1)}, bf16[16,64,256]{2,1,0:T(8,128)(2,1)S(1)}, u32[]{:S(2)}, u32[]{:S(2)}) %collective-permute-start.2) | collective-permute-done | bytes 524320 | tf_op jit(solution)/shard_map/ppermute | solution.py:63
  102.8 4.1 shard_map.186.x_ref
  114.0 16.3 %shard_map.187 = (bf16[4096,256]{1,0:T(8,128)(2,1)}, bf16[4096,256]{1,0:T(8,128)(2,1)}, bf16[4096,512]{1,0:T(8,128)(2,1)S(1)}, bf16[256,256]{1,0:T(8,128)(2,1)S(1)}) custom-call(bf16[4224,768]{1,0:T(8,128)(2,1)} %shard_map.186.x_ref, bf16[3,768,256]{2,1,0:T(8,128)(2,1)S(1)} %bitcast.306, bf16[256,512]{1,0:T(8,128)(2,1)S(1)} %pad_maximum_fusion.11.kv_w_ref), custom_call_target="tpu_custom_call" | custom-call | flops 5905580032 | bytes 14680064 | tf_op jit(solution)/shard_map/pallas_call | solution.py:930
  130.3 4.4 %collective-permute-done.16 = bf16[7,2,4,8,768]{4,3,2,1,0:T(8,128)(2,1)} collective-permute-done((bf16[7,2,4,8,768]{4,3,2,1,0:T(8,128)(2,1)}, bf16[7,2,4,8,768]{4,3,2,1,0:T(8,128)(2,1)}, u32[]{:S(2)}, u32[]{:S(2)}) %collective-permute-start.16) | collective-permute-done | bytes 688160 | tf_op jit(solution)/shard_map/ppermute | solution.py:63
  138.9 14.0 %shard_map.188 = (bf16[480,256]{1,0:T(8,128)(2,1)S(1)}, f32[2,8,240]{2,1,0:T(8,128)S(1)}) custom-call(bf16[480,256]{1,0:T(8,128)(2,1)S(1)} %fusion.2.q_ref, bf16[4096,512]{1,0:T(8,128)(2,1)S(1)} %get-tuple-element.246.k_ref.v_ref, bf16[4096,512]{1,0:T(8,128)(2,1)S(1)} %get-tuple-element.246.k_ref.v_ref), custom_call_target="tpu_custom_call" | custom-call | flops 8053063680 | bytes 8388608 | tf_op jit(solution)/shard_map/pallas_call | solution.py:325
  156.8 6.8 %shard_map.190 = (bf16[736,256]{1,0:T(8,128)(2,1)}, f32[736,768]{1,0:T(8,128)}, bf16[736,768]{1,0:T(8,128)(2,1)}, bf16[3,736,768]{2,1,0:T(8,128)(2,1)S(1)}) custom-call(bf16[256,256]{1,0:T(8,128)(2,1)S(1)} %get-tuple-element.237.pool_ref, bf16[480,256]{1,0:T(8,128)(2,1)S(1)} %bitcast.307, bf16[480,256]{1,0:T(8,128)(2,1)S(1)} %get-tuple-element.250.mixed_ref.o_ref, ...), custom_call_target="tpu_custom_call" | custom-call | flops 2894069760 | bytes 6782976 | tf_op jit(solution)/shard_map/pallas_call | solution.py:652
  163.6 11.5 %shard_map.191 = (bf16[736,768]{1,0:T(8,128)(2,1)S(1)}, f32[3,8,736]{2,1,0:T(8,128)S(1)}) custom-call(s32[1]{0:T(128)} %add.398.len_ref, bf16[3,736,768]{2,1,0:T(8,128)(2,1)S(1)} %get-tuple-element.255.q_ref.k_ref.v_ref, bf16[3,736,768]{2,1,0:T(8,128)(2,1)S(1)} %get-tuple-element.255.q_ref.k_ref.v_ref, ...), custom_call_target="tpu_custom_call" | custom-call | flops 6656360448 | bytes 4521984 | tf_op jit(solution)/shard_map/pallas_call | solution.py:468
  183.4 32.3 %shard_map.192 = (f32[736,768]{1,0:T(8,128)}, f32[736,768]{1,0:T(8,128)}, bf16[736,768]{1,0:T(8,128)(2,1)S(1)}, bf16[2,2,48,8,768]{4,3,2,1,0:T(8,128)(2,1)S(1)},...) custom-call(s32[1]{0:T(128)} %bitcast.core_ref, ...), custom_call_target="tpu_custom_call" | custom-call | flops 23441965056 | bytes 33914880 | tf_op jit(solution)/shard_map/pallas_call | solution.py:735
  222.9 13.2 %shard_map.193.g_ref = bf16[3,736,512]{2,1,0:T(8,128)(2,1)S(1)} custom-call(s32[1]{0:T(128)} %add.398.len_ref, bf16[3,736,768]{2,1,0:T(8,128)(2,1)} %copy-done.18, bf16[3,736,768]{2,1,0:T(8,128)(2,1)} %copy-done.18, bf16[3,736,768]{2,1,0:T(8,128)(2,1)} %copy-done.18, bf16[736,768]{1,0:T(8,128)(2,1)S(1)} %copy-done.25, bf16[736,768]{1,0:T(8,128)(2,1)} %copy-done.22, ...), custom_call_target="tpu_custom_call" | custom-call | flops 8875147264 | bytes 9043968 | tf_op jit(solution)/shard_map/pallas_call | solution.py:530
  243.3 18.7 %shard_map.194 = (bf16[2,2,24,8,768]{4,3,2,1,0:T(8,128)(2,1)S(1)}, bf16[2,2,24,8,768]{4,3,2,1,0:T(8,128)(2,1)S(1)}, bf16[2,2,12,8,768]{4,3,2,1,0:T(8,128)(2,1)S(...) custom-call(s32[1]{0:T(128)} %bitcast.core_ref, ...), custom_call_target="tpu_custom_call" | custom-call | flops 10225713152 | bytes 28262400 | tf_op jit(solution)/shard_map/pallas_call | solution.py:838
  262.0 8.3 %collective-permute-done.22 = bf16[2,48,8,768]{3,2,1,0:T(8,128)(2,1)S(1)} collective-permute-done((bf16[2,48,8,768]{3,2,1,0:T(8,128)(2,1)S(1)}, bf16[2,48,8,768]{3,2,1,0:T(8,128)(2,1)S(1)}, u32[]{:S(2)}, u32[]{:S(2)}) %collective-permute-start.22) | collective-permute-done | bytes 1179680 | tf_op jit(solution)/shard_map/ppermute | solution.py:63
  273.8 26.5 %shard_map.195 = (bf16[4096,512]{1,0:T(8,128)(2,1)S(1)}, bf16[256,256]{1,0:T(8,128)(2,1)S(1)}, f32[480,256]{1,0:T(8,128)}) custom-call(bf16[480,256]{1,0:T(8,128)(2,1)S(1)} %copy-done.11, bf16[4096,512]{1,0:T(8,128)(2,1)S(1)} %copy-done.28, bf16[4096,512]{1,0:T(8,128)(2,1)S(1)} %copy-done.28, bf16[480,256]{1,0:T(8,128)(2,1)S(1)} %get-tuple-element.308.do_ref, ...), custom_call_target="tpu_custom_call" | custom-call | flops 20132659200 | bytes 8388608 | tf_op jit(solution)/shard_map/pallas_call | solution.py:404
  306.0 14.4 %shard_map.196 = (f32[4096,256]{1,0:T(8,128)S(1)}, bf16[4096,256]{1,0:T(8,128)(2,1)S(1)}, bf16[2,2,52,8,256]{4,3,2,1,0:T(8,128)(2,1)S(1)}, bf16[2,2,52,8,256]{4,3,2,1,0:T(8,128)(2,1)S(1)}) custom-call(s32[1]{0:T(128)} %bitcast.core_ref, bf16[4096,512]{1,0:T(8,128)(2,1)S(1)} %get-tuple-element.335.dkv_ref, bf16[4096,256]{1,0:T(8,128)(2,1)} %get-tuple-element.336.slope_ref, ...), custom_call_target="tpu_custom_call" | custom-call | flops 6979321856 | bytes 20971520 | tf_op jit(solution)/shard_map/pallas_call | solution.py:992
  327.2 3.8 collective-permute-done.35
  331.0 3.6 collective-permute-done.34
  340.3 8.0 %shard_map.197 = bf16[4096,256]{1,0:T(8,128)(2,1)S(1)} custom-call(bf16[4096,256]{1,0:T(8,128)(2,1)S(1)} %get-tuple-element.379.gz_ref, f32[4096,256]{1,0:T(8,128)S(1)} %get-tuple-element.380.d_hidden_ref, bf16[9,256,256]{2,1,0:T(8,128)(2,1)S(1)} %get-tuple-element.442.conv_ref), custom_call_target="tpu_custom_call" | custom-call | flops 4831838208 | bytes 8388608 | tf_op jit(solution)/shard_map/pallas_call | solution.py:1058
  360.4 5.4 %collective-permute-done.45 = bf16[19,8,256]{2,1,0:T(8,128)(2,1)} collective-permute-done((bf16[19,8,256]{2,1,0:T(8,128)(2,1)}, bf16[19,8,256]{2,1,0:T(8,128)(2,1)}, u32[]{:S(2)}, u32[]{:S(2)}) %collective-permute-start.45) | collective-permute-done | bytes 77856 | tf_op jit(solution)/shard_map/ppermute | solution.py:63
  373.6 3.6 all-to-all-start.1
  380.4 22.6 %collective-permute-done.42 = bf16[16,64,256]{2,1,0:T(8,128)(2,1)S(1)} collective-permute-done((bf16[16,64,256]{2,1,0:T(8,128)(2,1)S(1)}, bf16[16,64,256]{2,1,0:T(8,128)(2,1)S(1)}, u32[]{:S(2)}, u32[]{:S(2)}) %collective-permute-start.42) | collective-permute-done | bytes 524320 | tf_op jit(solution)/shard_map/ppermute | solution.py:63
  409.3 6.5 %subtract_select_fusion = (f32[8,256,256]{2,1,0:T(8,128)}, f32[8,256,256]{2,1,0:T(8,128)}, f32[8,256,256]{2,1,0:T(8,128)}) fusion(f32[8,256,256]{2,1,0:T(8,128)S(1)} %copy-done.34, pred[8]{0:T(512)(128)(4,1)S(1)} %broadcast_compare_fusion, f32[8,256,256]{2,1,0:T(8,128)} %param.21, f32[8,256,256]{2,1,0:T(8,128)} %param.22, ...), kind=kLoop, calls=%fused_computation.14 | loop fusion | flops 10485760 | bytes 13631500 | tf_op jit(solution)/shard_map/jit(_where)/select_n | solution.py:1273
  (312 shorter events, 120.4 us)
Async XLA Ops:
  10.0 33.7 %all-to-all-start = ((bf16[32,8,8,256]{3,2,1,0:T(8,128)(2,1)}), bf16[32,8,8,256]{3,2,1,0:T(8,128)(2,1)S(1)}, u32[]{:S(2)}, u32[]{:S(2)}) async-start(bf16[32,8,8,256]{3,2,1,0:T(8,128)(2,1)} %copy.146), calls=%async_computation | async-start | bytes 2097152 | tf_op jit(solution)/shard_map/all_to_all | solution.py:1101
  17.3 161.2 %all-gather.2.cloned.1.call-start = ((), (), s32[]{:S(2)}) async-start(), calls=%async_computation.2 | async-start | bytes 9732096 | tf_op jit(solution)/shard_map/all_gather | solution.py:1117
  57.5 23.0 %collective-permute-start = (bf16[16,64,256]{2,1,0:T(8,128)(2,1)S(1)}, bf16[16,64,256]{2,1,0:T(8,128)(2,1)S(1)}, u32[]{:S(2)}, u32[]{:S(2)}) collective-permute-start(bf16[16,64,256]{2,1,0:T(8,128)(2,1)S(1)} %get-tuple-element.431), channel_id=1, source_target_pairs={{0,1},{1,0},{2,3},{3,2},{4,5},{5,4},{6,7},{7,6},{8,9},{9,8},{10,11... | collective-permute-start | bytes 1572872 | tf_op jit(solution)/shard_map/ppermute | solution.py:63
  68.1 41.1 %collective-permute-start.14 = (bf16[13,4,4,8,256]{4,3,0,2,1:T(8,128)(2,1)S(1)}, bf16[13,4,4,8,256]{4,3,0,2,1:T(8,128)(2,1)S(1)}, u32[]{:S(2)}, u32[]{:S(2)}) collective-permute-start(bf16[13,4,4,8,256]{4,3,0,2,1:T(8,128)(2,1)S(1)} %get-tuple-element.460), channel_id=1, source_target_pairs={{0,4},{4,0},{1,5},{5,1},{2,6},{6,2},{3,7},{7,3},{8,12},{12,8},{9,1... | collective-permute-start | bytes 2555912 | tf_op jit(solution)/shard_map/ppermute | solution.py:63
  68.2 25.5 %collective-permute-start.1 = (bf16[16,64,256]{2,1,0:T(8,128)(2,1)S(1)}, bf16[16,64,256]{2,1,0:T(8,128)(2,1)S(1)}, u32[]{:S(2)}, u32[]{:S(2)}) collective-permute-start(bf16[16,64,256]{2,1,0:T(8,128)(2,1)S(1)} %get-tuple-element.433), channel_id=1, source_target_pairs={{0,2},{1,3},{2,0},{3,1},{4,6},{5,7},{6,4},{7,5},{8,10},{9,11},{10,... | collective-permute-start | bytes 1572872 | tf_op jit(solution)/shard_map/ppermute | solution.py:63
  78.6 24.2 %collective-permute-start.2 = (bf16[16,64,256]{2,1,0:T(8,128)(2,1)S(1)}, bf16[16,64,256]{2,1,0:T(8,128)(2,1)S(1)}, u32[]{:S(2)}, u32[]{:S(2)}) collective-permute-start(bf16[16,64,256]{2,1,0:T(8,128)(2,1)S(1)} %get-tuple-element.430), channel_id=1, source_target_pairs={{0,3},{1,2},{2,1},{3,0},{4,7},{5,6},{6,5},{7,4},{8,11},{9,10},{10,... | collective-permute-start | bytes 1572872 | tf_op jit(solution)/shard_map/ppermute | solution.py:63
  79.6 27.7 %collective-permute-start.10 = (bf16[7,4,8,768]{3,2,1,0:T(8,128)(2,1)S(1)}, bf16[7,4,8,768]{3,2,1,0:T(8,128)(2,1)S(1)}, u32[]{:S(2)}, u32[]{:S(2)}) collective-permute-start(bf16[7,4,8,768]{3,2,1,0:T(8,128)(2,1)S(1)} %pad_maximum_fusion.6), channel_id=1, source_target_pairs={{0,2},{2,0},{1,3},{3,1},{4,6},{6,4},{5,7},{7,5},{8,10},{10,8},{9,1... | collective-permute-start | bytes 1032200 | tf_op jit(solution)/shard_map/ppermute | solution.py:63
  80.5 26.8 %collective-permute-start.9 = (bf16[6,4,8,768]{3,2,1,0:T(8,128)(2,1)S(1)}, bf16[6,4,8,768]{3,2,1,0:T(8,128)(2,1)S(1)}, u32[]{:S(2)}, u32[]{:S(2)}) collective-permute-start(bf16[6,4,8,768]{3,2,1,0:T(8,128)(2,1)S(1)} %pad_maximum_fusion.9), channel_id=1, source_target_pairs={{0,1},{1,0},{2,3},{3,2},{4,5},{5,4},{6,7},{7,6},{8,9},{9,8},{10,11... | collective-permute-start | bytes 884744 | tf_op jit(solution)/shard_map/ppermute | solution.py:63
  108.2 26.4 %collective-permute-start.16 = (bf16[7,2,4,8,768]{4,3,2,1,0:T(8,128)(2,1)}, bf16[7,2,4,8,768]{4,3,2,1,0:T(8,128)(2,1)}, u32[]{:S(2)}, u32[]{:S(2)}) collective-permute-start(bf16[7,2,4,8,768]{4,3,2,1,0:T(8,128)(2,1)} %pad_maximum_fusion.4), channel_id=1, source_target_pairs={{0,1},{1,0},{2,3},{3,2},{4,5},{5,4},{6,7},{7,6},{8,9},{9,8},{10,11... | collective-permute-start | bytes 2064392 | tf_op jit(solution)/shard_map/ppermute | solution.py:63
  108.3 22.1 %collective-permute-start.15 = (bf16[6,2,4,8,768]{4,3,2,0,1:T(8,128)(2,1)S(1)}, bf16[6,2,4,8,768]{4,3,2,0,1:T(8,128)(2,1)}, u32[]{:S(2)}, u32[]{:S(2)}) collective-permute-start(bf16[6,2,4,8,768]{4,3,2,0,1:T(8,128)(2,1)S(1)} %pad_maximum_fusion.5), channel_id=1, source_target_pairs={{0,2},{2,0},{1,3},{3,1},{4,6},{6,4},{5,7},{7,5},{8,10},{10,8},{9,1... | collective-permute-start | bytes 1769480 | tf_op jit(solution)/shard_map/ppermute | solution.py:63
  241.8 28.4 %collective-permute-start.22 = (bf16[2,48,8,768]{3,2,1,0:T(8,128)(2,1)S(1)}, bf16[2,48,8,768]{3,2,1,0:T(8,128)(2,1)S(1)}, u32[]{:S(2)}, u32[]{:S(2)}) collective-permute-start(bf16[2,48,8,768]{3,2,1,0:T(8,128)(2,1)S(1)} %get-tuple-element.294), channel_id=1, source_target_pairs={{0,2},{2,0},{1,3},{3,1},{4,6},{6,4},{5,7},{7,5},{8,10},{10,8},{9,1... | collective-permute-start | bytes 3538952 | tf_op jit(solution)/shard_map/ppermute | solution.py:63
  241.9 28.4 %collective-permute-start.23 = (bf16[2,48,8,768]{3,2,1,0:T(8,128)(2,1)S(1)}, bf16[2,48,8,768]{3,2,1,0:T(8,128)(2,1)S(1)}, u32[]{:S(2)}, u32[]{:S(2)}) collective-permute-start(bf16[2,48,8,768]{3,2,1,0:T(8,128)(2,1)S(1)} %get-tuple-element.296), channel_id=1, source_target_pairs={{0,1},{1,0},{2,3},{3,2},{4,5},{5,4},{6,7},{7,6},{8,9},{9,8},{10,11... | collective-permute-start | bytes 3538952 | tf_op jit(solution)/shard_map/ppermute | solution.py:63
  271.2 29.2 %collective-permute-start.26 = (bf16[2,2,24,8,768]{4,3,2,1,0:T(8,128)(2,1)S(1)}, bf16[2,2,24,8,768]{4,3,2,1,0:T(8,128)(2,1)S(1)}, u32[]{:S(2)}, u32[]{:S(2)}) collective-permute-start(bf16[2,2,24,8,768]{4,3,2,1,0:T(8,128)(2,1)S(1)} %get-tuple-element.317), channel_id=1, source_target_pairs={{0,4},{4,0},{1,5},{5,1},{2,6},{6,2},{3,7},{7,3},{8,12},{12,8},{9,1... | collective-permute-start | bytes 3538952 | tf_op jit(solution)/shard_map/ppermute | solution.py:63
  271.3 29.1 %collective-permute-start.24 = (bf16[48,8,768]{2,1,0:T(8,128)(2,1)S(1)}, bf16[48,8,768]{2,1,0:T(8,128)(2,1)S(1)}, u32[]{:S(2)}, u32[]{:S(2)}) collective-permute-start(bf16[48,8,768]{2,1,0:T(8,128)(2,1)S(1)} %get-tuple-element.313), channel_id=1, source_target_pairs={{0,1},{1,0},{2,3},{3,2},{4,5},{5,4},{6,7},{7,6},{8,9},{9,8},{10,11... | collective-permute-start | bytes 1769480 | tf_op jit(solution)/shard_map/ppermute | solution.py:63
  271.6 28.7 %collective-permute-start.25 = (bf16[48,8,768]{2,1,0:T(8,128)(2,1)S(1)}, bf16[48,8,768]{2,1,0:T(8,128)(2,1)S(1)}, u32[]{:S(2)}, u32[]{:S(2)}) collective-permute-start(bf16[48,8,768]{2,1,0:T(8,128)(2,1)S(1)} %get-tuple-element.315), channel_id=1, source_target_pairs={{0,2},{2,0},{1,3},{3,1},{4,6},{6,4},{5,7},{7,5},{8,10},{10,8},{9,1... | collective-permute-start | bytes 1769480 | tf_op jit(solution)/shard_map/ppermute | solution.py:63
  273.3 27.1 %collective-permute-start.27 = (bf16[2,2,12,8,768]{4,3,2,1,0:T(8,128)(2,1)S(1)}, bf16[2,2,12,8,768]{4,3,2,1,0:T(8,128)(2,1)S(1)}, u32[]{:S(2)}, u32[]{:S(2)}) collective-permute-start(bf16[2,2,12,8,768]{4,3,2,1,0:T(8,128)(2,1)S(1)} %get-tuple-element.319), channel_id=1, source_target_pairs={{0,4},{4,0},{1,5},{5,1},{2,6},{6,2},{3,7},{7,3},{8,12},{12,8},{9,1... | collective-permute-start | bytes 1769480 | tf_op jit(solution)/shard_map/ppermute | solution.py:63
  273.3 27.1 %collective-permute-start.28 = (bf16[2,2,8,8,768]{4,3,2,1,0:T(8,128)(2,1)S(1)}, bf16[2,2,8,8,768]{4,3,2,1,0:T(8,128)(2,1)S(1)}, u32[]{:S(2)}, u32[]{:S(2)}) collective-permute-start(bf16[2,2,8,8,768]{4,3,2,1,0:T(8,128)(2,1)S(1)} %get-tuple-element.321), channel_id=1, source_target_pairs={{0,4},{4,0},{1,5},{5,1},{2,6},{6,2},{3,7},{7,3},{8,12},{12,8},{9,1... | collective-permute-start | bytes 1179656 | tf_op jit(solution)/shard_map/ppermute | solution.py:63
  302.8 19.6 %collective-permute-start.29 = (bf16[24,2,8,768]{3,2,0,1:T(8,128)(2,1)S(1)}, bf16[24,2,8,768]{3,2,0,1:T(8,128)(2,1)S(1)}, u32[]{:S(2)}, u32[]{:S(2)}) collective-permute-start(bf16[24,2,8,768]{3,2,0,1:T(8,128)(2,1)S(1)} %get-tuple-element.346), channel_id=1, source_target_pairs={{0,8},{8,0},{16,24},{24,16},{1,9},{9,1},{17,25},{25,17},{2,10},{10... | collective-permute-start | bytes 1769480 | tf_op jit(solution)/shard_map/ppermute | solution.py:63
  302.9 19.5 %collective-permute-start.30 = (bf16[2,24,8,768]{3,2,1,0:T(8,128)(2,1)S(1)}, bf16[2,24,8,768]{3,2,1,0:T(8,128)(2,1)S(1)}, u32[]{:S(2)}, u32[]{:S(2)}) collective-permute-start(bf16[2,24,8,768]{3,2,1,0:T(8,128)(2,1)S(1)} %get-tuple-element.348), channel_id=1, source_target_pairs={{0,1},{1,0},{2,3},{3,2},{4,5},{5,4},{6,7},{7,6},{8,9},{9,8},{10,11... | collective-permute-start | bytes 1769480 | tf_op jit(solution)/shard_map/ppermute | solution.py:63
  304.7 17.7 %collective-permute-start.31 = (bf16[2,24,8,768]{3,2,1,0:T(8,128)(2,1)S(1)}, bf16[2,24,8,768]{3,2,1,0:T(8,128)(2,1)S(1)}, u32[]{:S(2)}, u32[]{:S(2)}) collective-permute-start(bf16[2,24,8,768]{3,2,1,0:T(8,128)(2,1)S(1)} %get-tuple-element.350), channel_id=1, source_target_pairs={{0,2},{2,0},{1,3},{3,1},{4,6},{6,4},{5,7},{7,5},{8,10},{10,8},{9,1... | collective-permute-start | bytes 1769480 | tf_op jit(solution)/shard_map/ppermute | solution.py:63
  327.1 21.3 %collective-permute-start.41 = (bf16[24,8,768]{2,1,0:T(8,128)(2,1)S(1)}, bf16[24,8,768]{2,1,0:T(8,128)(2,1)S(1)}, u32[]{:S(2)}, u32[]{:S(2)}) collective-permute-start(bf16[24,8,768]{2,1,0:T(8,128)(2,1)S(1)} %get-tuple-element.463), channel_id=1, source_target_pairs={{0,16},{8,24},{16,0},{24,8},{1,17},{9,25},{17,1},{25,9},{2,18},{10... | collective-permute-start | bytes 884744 | tf_op jit(solution)/shard_map/ppermute | solution.py:63
  373.6 32.6 %all-to-all-start.1 = ((bf16[32,9,8,256]{3,2,1,0:T(8,128)(2,1)}), bf16[32,9,8,256]{3,2,1,0:T(8,128)(2,1)}, u32[]{:S(2)}, u32[]{:S(2)}) async-start(bf16[32,9,8,256]{3,2,1,0:T(8,128)(2,1)} %bitcast.152), calls=%async_computation.1 | async-start | bytes 2359296 | tf_op jit(solution)/shard_map/all_to_all | solution.py:1252
  377.2 25.9 %collective-permute-start.42 = (bf16[16,64,256]{2,1,0:T(8,128)(2,1)S(1)}, bf16[16,64,256]{2,1,0:T(8,128)(2,1)S(1)}, u32[]{:S(2)}, u32[]{:S(2)}) collective-permute-start(bf16[16,64,256]{2,1,0:T(8,128)(2,1)S(1)} %copy-done.43), channel_id=1, source_target_pairs={{0,1},{1,0},{2,3},{3,2},{4,5},{5,4},{6,7},{7,6},{8,9},{9,8},{10,11... | collective-permute-start | bytes 1572872 | tf_op jit(solution)/shard_map/ppermute | solution.py:63
  379.0 24.1 %collective-permute-start.43 = (bf16[16,64,256]{2,1,0:T(8,128)(2,1)S(1)}, bf16[16,64,256]{2,1,0:T(8,128)(2,1)S(1)}, u32[]{:S(2)}, u32[]{:S(2)}) collective-permute-start(bf16[16,64,256]{2,1,0:T(8,128)(2,1)S(1)} %copy-done.42), channel_id=1, source_target_pairs={{0,2},{1,3},{2,0},{3,1},{4,6},{5,7},{6,4},{7,5},{8,10},{9,11},{10,... | collective-permute-start | bytes 1572872 | tf_op jit(solution)/shard_map/ppermute | solution.py:63
  (79 other events, 601.4 us)
Sparse Core Ops, SparseCore 0:
  45.4 110.8 all-gather.1

commit v9 on v8

--- a/solution.py
+++ b/solution.py
@@ -477,7 +477,7 @@
             ],
         ),
         out_shape=[
-            jax.ShapeDtypeStruct((SEQ, D), bf16),
+            lasting((SEQ, D), bf16),
             jax.ShapeDtypeStruct((groups, 8, SEQ), f32),
         ],
         compiler_params=params(),
@@ -546,7 +546,7 @@
         cost_estimate=cost(
             8 * HEADS * SEQ * SEQ * CH * count // groups, 16 * SEQ * D, HEADS * SEQ * SEQ
         ),
-    )(length, stay(qkv), stay(qkv), stay(qkv), d_out, stay(out), log_rows)
+    )(length, stay(qkv), stay(qkv), stay(qkv), stay(d_out), stay(out), log_rows)
 
 
 def full(*shape):
@@ -671,7 +671,7 @@
             lasting((SEQ, CH), bf16),
             lasting((SEQ, D), f32),
             lasting((SEQ, D), bf16),
-            jax.ShapeDtypeStruct((3, SEQ, D), bf16),
+            lasting((3, SEQ, D), bf16),
         ],
         compiler_params=params(),
         cost_estimate=cost(2 * SEQ * D * (CH + 3 * D), 12 * SEQ * D),
@@ -753,11 +753,11 @@
         out_shape=[
             lasting((SEQ, D), f32),
             lasting((SEQ, D), f32),
-            jax.ShapeDtypeStruct((SEQ, D), bf16),
+            lasting((SEQ, D), bf16),
         ]
         + [jax.ShapeDtypeStruct(core_shape(12, "yx"), bf16)] * 2
         + [jax.ShapeDtypeStruct(core_shape(12, "xy"), bf16)] * 2
-        + [jax.ShapeDtypeStruct(core_shape(3, "yx"), bf16)] * 2
+        + [lasting(core_shape(3, "yx"), bf16)] * 2
         + [jax.ShapeDtypeStruct((1, D), f32)],
         scratch_shapes=[
             pltpu.VMEM((SEQ, D), f32),
@@ -769,7 +769,9 @@
         ],
         compiler_params=pltpu.CompilerParams(vmem_limit_bytes=MLP_BYTES),
         cost_estimate=cost(54 * SEQ * D * D, 60 * SEQ * D, 4 * SEQ * D),
-    )(core_here(), mixed, embed, stay(weights), stay(mlp), stay(mlp), gain, gd)
+    )(
+        core_here(), stay(mixed), stay(embed), stay(weights), stay(mlp), stay(mlp), gain, stay(gd)
+    )
 
 
 def embed_grad_kernel(
@@ -890,7 +892,7 @@
         compiler_params=pltpu.CompilerParams(vmem_limit_bytes=MLP_BYTES),
         cost_estimate=cost(2 * SEQ * D * (6 * D + 2 * CH) + 32 * SEQ * SEQ * CH, 50 * SEQ * D),
     )(
-        core_here(), length, stay(qkv), stay(qkv), stay(qkv), gog, stay(out), log_rows, gqkv, normed, stay(weights),
+        core_here(), length, stay(qkv), stay(qkv), stay(qkv), stay(gog), stay(out), log_rows, gqkv, normed, stay(weights),
         stay(weights), stay(embed), stay(d_stream), stay(seq), stay(mixed), to_out, gain, gain_g,
     )
 
@@ -1114,7 +1116,6 @@
     slices = slices.at[slot_of].get(mode="promise_in_bounds")
     early, emb, qkv, att, up, down = jnp.split(slices, (13, 16, 43, 52, 88))
     mlp = jnp.concatenate([from_tiles(up, 3, 4), from_tiles(down, 12, 1)], 0)
-    mlp = lax.all_gather(mlp, AXES, axis=1, tiled=True)
     early = gather_axes(early, "z")
     core = jnp.concatenate([from_tiles(qkv, 3, 3), from_tiles(att, 3, 1), from_tiles(emb, 1, 1)], 0)
     core, early = tie((core, early))
@@ -1131,7 +1132,8 @@
     to_query, to_out = early[9], early[12]
     kv_weight = jnp.concatenate([early[10], early[11]], 1)
 
-    wide, low, high = hold((wide,), low, high)
+    wide, mlp, low, high = hold((wide, mlp), low, high)
+    mlp = lax.all_gather(mlp, AXES, axis=1, tiled=True)
     low, high = joined(low), joined(high)
     wide, low, high = tie((wide, low, high))
     low, high = gather_axes(low, "y"), gather_axes(high, "x")

time: 429 us -> 415 us (0.967)
  waiting for transfers between devices: 114 us -> 91.6 us
  starting transfers between devices: 56 us -> 61.6 us
    ppermute x49, waiting for transfers between devices: 90.2 us -> 65.7 us  [xor_permute(): return lax.ppermute(values, axes, [(i, i ^ mask) for i in range(count)])]
    all_gather x1, waiting for transfers between devices: 0.01 us -> 9.92 us  [local(): mlp = lax.all_gather(mlp, AXES, axis=1, tiled=True)]
    unnamed x109 -> x91, local copies, waits for them, and re-layouts: 19.1 us -> 10.5 us
    all_to_all x1, waiting for transfers between devices: 22.7 us -> 15.3 us  [local(): lax.all_to_all(slices, AXES, split_axis=0, concat_axis=0, tiled=True)]
    ppermute x49, starting transfers between devices: 45.1 us -> 50.6 us  [xor_permute(): return lax.ppermute(values, axes, [(i, i ^ mask) for i in range(count)])]
  transfers between devices with their start and end apart: 52 -> 52, of which waited for: 19 -> 19; matrix products, arithmetic and copies ran while one was open for 6% -> 8% of each run, Pallas kernels for 32% -> 34%
where the time goes in v9:
time: 415 us; the launch traced here: 410 us
  Pallas kernels  172 us (41%)
  waiting for transfers between devices  91.6 us (22%)
  starting transfers between devices  61.6 us (15%)
  other arithmetic  35.4 us (9%)
  local copies, waits for them, and re-layouts  28.9 us (7%)
  between operations  19.8 us (5%)
    ppermute x49, waiting for transfers between devices, xor_permute(): return lax.ppermute(values, axes, [(i, i ^ mask) for i in range(count)])  65.7 us
    ppermute x49, starting transfers between devices, xor_permute(): return lax.ppermute(values, axes, [(i, i ^ mask) for i in range(count)])  50.6 us
    pallas_call x1, Pallas kernels, mlp_block(): pl.pallas_call(functools.partial(mlp_kernel, sizes=slice_shape()), grid=(...  34.3 us
    pallas_call x1, Pallas kernels, cross_backward(): pl.pallas_call(cross_backward_kernel, grid=(cells // block,), in_specs=[p...  26.5 us
    pallas_call x1, Pallas kernels, embed_grad(): pl.pallas_call(functools.partial(embed_grad_kernel, sizes=slice_shape()),...  18.8 us
    all_to_all x1, waiting for transfers between devices, local(): lax.all_to_all(slices, AXES, split_axis=0, concat_axis=0, tiled=True)  15.3 us
    pallas_call x1, Pallas kernels, token_forward(): pl.pallas_call(token_forward_kernel, grid=(steps,), in_specs=[pl.BlockSpe...  15.2 us
    pallas_call x1, Pallas kernels, token_backward(): pl.pallas_call(functools.partial(token_backward_kernel, sizes=slice_shape...  14.4 us
  transfers between devices with their start and end apart: 52, of which 19 were waited for; matrix products, arithmetic and copies ran while one was open for 8% of the time, Pallas kernels for 34%

profile of v9, /device:TPU:0, one launch (start us, length us, event | category | flops | bytes accessed | tf_op | source)
XLA Modules:
  0.0 409.9 jit_solution(18429272188943349422)
XLA Ops:
  10.0 7.3 %all-to-all-start = ((bf16[32,8,8,256]{3,2,1,0:T(8,128)(2,1)}), bf16[32,8,8,256]{3,2,1,0:T(8,128)(2,1)S(1)}, u32[]{:S(2)}, u32[]{:S(2)}) async-start(bf16[32,8,8,256]{3,2,1,0:T(8,128)(2,1)} %copy.146), calls=%async_computation | async-start | bytes 2097152 | tf_op jit(solution)/shard_map/all_to_all | solution.py:1103
  28.5 15.3 %all-to-all-done = bf16[32,8,8,256]{3,2,1,0:T(8,128)(2,1)S(1)} async-done(((bf16[32,8,8,256]{3,2,1,0:T(8,128)(2,1)}), bf16[32,8,8,256]{3,2,1,0:T(8,128)(2,1)S(1)}, u32[]{:S(2)}, u32[]{:S(2)}) %all-to-all-start) | async-done | bytes 1048608 | tf_op jit(solution)/shard_map/all_to_all | solution.py:1103
  52.9 3.0 collective-permute-done.4
  61.2 4.0 shard_map.186.x_ref
  65.4 5.0 %collective-permute-done.7 = bf16[13,8,768]{2,1,0:T(8,128)(2,1)S(1)} collective-permute-done((bf16[13,8,768]{2,1,0:T(8,128)(2,1)S(1)}, bf16[13,8,768]{2,1,0:T(8,128)(2,1)S(1)}, u32[]{:S(2)}, u32[]{:S(2)}) %collective-permute-start.7) | collective-permute-done | bytes 159776 | tf_op jit(solution)/shard_map/ppermute | solution.py:63
  74.4 5.5 %collective-permute-done.9 = bf16[6,4,8,768]{3,2,1,0:T(8,128)(2,1)S(1)} collective-permute-done((bf16[6,4,8,768]{3,2,1,0:T(8,128)(2,1)S(1)}, bf16[6,4,8,768]{3,2,1,0:T(8,128)(2,1)S(1)}, u32[]{:S(2)}, u32[]{:S(2)}) %collective-permute-start.9) | collective-permute-done | bytes 294944 | tf_op jit(solution)/shard_map/ppermute | solution.py:63
  83.5 2.8 collective-permute-done.11
  97.1 15.2 %shard_map.187 = (bf16[4096,256]{1,0:T(8,128)(2,1)}, bf16[4096,256]{1,0:T(8,128)(2,1)}, bf16[4096,512]{1,0:T(8,128)(2,1)S(1)}, bf16[256,256]{1,0:T(8,128)(2,1)S(1)}) custom-call(bf16[4224,768]{1,0:T(8,128)(2,1)} %shard_map.186.x_ref, bf16[3,768,256]{2,1,0:T(8,128)(2,1)S(1)} %bitcast.306, bf16[256,512]{1,0:T(8,128)(2,1)S(1)} %pad_maximum_fusion.11.kv_w_ref), custom_call_target="tpu_custom_call" | custom-call | flops 5905580032 | bytes 14680064 | tf_op jit(solution)/shard_map/pallas_call | solution.py:932
  116.9 14.0 %shard_map.188 = (bf16[480,256]{1,0:T(8,128)(2,1)S(1)}, f32[2,8,240]{2,1,0:T(8,128)S(1)}) custom-call(bf16[480,256]{1,0:T(8,128)(2,1)S(1)} %fusion.2.q_ref, bf16[4096,512]{1,0:T(8,128)(2,1)S(1)} %get-tuple-element.247.k_ref.v_ref, bf16[4096,512]{1,0:T(8,128)(2,1)S(1)} %get-tuple-element.247.k_ref.v_ref), custom_call_target="tpu_custom_call" | custom-call | flops 8053063680 | bytes 8388608 | tf_op jit(solution)/shard_map/pallas_call | solution.py:325
  134.9 7.7 %shard_map.190 = (bf16[736,256]{1,0:T(8,128)(2,1)}, f32[736,768]{1,0:T(8,128)}, bf16[736,768]{1,0:T(8,128)(2,1)}, bf16[3,736,768]{2,1,0:T(8,128)(2,1)}) custom-call(bf16[256,256]{1,0:T(8,128)(2,1)S(1)} %get-tuple-element.238.pool_ref, bf16[480,256]{1,0:T(8,128)(2,1)S(1)} %bitcast.307, bf16[480,256]{1,0:T(8,128)(2,1)S(1)} %get-tuple-element.251.mixed_ref.o_ref, ...), custom_call_target="tpu_custom_call" | custom-call | flops 2894069760 | bytes 6782976 | tf_op jit(solution)/shard_map/pallas_call | solution.py:652
  144.6 12.2 %shard_map.191 = (bf16[736,768]{1,0:T(8,128)(2,1)}, f32[3,8,736]{2,1,0:T(8,128)S(1)}) custom-call(s32[1]{0:T(128)} %add.398.len_ref, bf16[3,736,768]{2,1,0:T(8,128)(2,1)S(1)} %copy-done.17, bf16[3,736,768]{2,1,0:T(8,128)(2,1)S(1)} %copy-done.17, bf16[3,736,768]{2,1,0:T(8,128)(2,1)S(1)} %copy-done.17), custom_call_target="tpu_custom_call" | custom-call | flops 6656360448 | bytes 4521984 | tf_op jit(solution)/shard_map/pallas_call | solution.py:468
  157.4 9.9 %all-gather.2.cloned.1.call-done.up_ref.down_ref = bf16[24,256,768]{2,1,0:T(8,128)(2,1)} async-done(((bf16[24,8,768]{2,1,0:T(8,128)(2,1)}), bf16[24,256,768]{2,1,0:T(8,128)(2,1)}) %all-gather.2.cloned.1.call-update) | async-done | bytes 9437200 | tf_op jit(solution)/shard_map/all_gather | solution.py:1136
  168.0 34.3 %shard_map.192 = (f32[736,768]{1,0:T(8,128)}, f32[736,768]{1,0:T(8,128)}, bf16[736,768]{1,0:T(8,128)(2,1)}, bf16[2,2,48,8,768]{4,3,2,1,0:T(8,128)(2,1)S(1)}, bf1...) custom-call(s32[1]{0:T(128)} %bitcast.core_ref, ...), custom_call_target="tpu_custom_call" | custom-call | flops 23441965056 | bytes 33914880 | tf_op jit(solution)/shard_map/pallas_call | solution.py:735
  207.2 13.3 %shard_map.193.g_ref = bf16[3,736,512]{2,1,0:T(8,128)(2,1)S(1)} custom-call(s32[1]{0:T(128)} %add.398.len_ref, bf16[3,736,768]{2,1,0:T(8,128)(2,1)} %get-tuple-element.256.q_ref.k_ref.v_ref, bf16[3,736,768]{2,1,0:T(8,128)(2,1)} %get-tuple-element.256.q_ref.k_ref.v_ref, bf16[3,736,768]{2,1,0:T(8,128)(2,1)} %get-tuple-element.256.q_ref.k_ref.v_ref, ...), custom_call_target="tpu_custom_call" | custom-call | flops 8875147264 | bytes 9043968 | tf_op jit(solution)/shard_map/pallas_call | solution.py:530
  229.2 18.8 %shard_map.194 = (bf16[2,2,24,8,768]{4,3,2,1,0:T(8,128)(2,1)S(1)}, bf16[2,2,24,8,768]{4,3,2,1,0:T(8,128)(2,1)S(1)}, bf16[2,2,12,8,768]{4,3,2,1,0:T(8,128)(2,1)S(...) custom-call(s32[1]{0:T(128)} %bitcast.core_ref, ...), custom_call_target="tpu_custom_call" | custom-call | flops 10225713152 | bytes 28262400 | tf_op jit(solution)/shard_map/pallas_call | solution.py:840
  248.0 6.4 %collective-permute-done.22 = bf16[2,48,8,768]{3,2,1,0:T(8,128)(2,1)S(1)} collective-permute-done((bf16[2,48,8,768]{3,2,1,0:T(8,128)(2,1)S(1)}, bf16[2,48,8,768]{3,2,1,0:T(8,128)(2,1)S(1)}, u32[]{:S(2)}, u32[]{:S(2)}) %collective-permute-start.22) | collective-permute-done | bytes 1179680 | tf_op jit(solution)/shard_map/ppermute | solution.py:63
  259.1 26.5 %shard_map.195 = (bf16[4096,512]{1,0:T(8,128)(2,1)S(1)}, bf16[256,256]{1,0:T(8,128)(2,1)S(1)}, f32[480,256]{1,0:T(8,128)}) custom-call(bf16[480,256]{1,0:T(8,128)(2,1)S(1)} %copy-done.10, bf16[4096,512]{1,0:T(8,128)(2,1)S(1)} %copy-done.20, bf16[4096,512]{1,0:T(8,128)(2,1)S(1)} %copy-done.20, bf16[480,256]{1,0:T(8,128)(2,1)S(1)} %get-tuple-element.310.do_ref, ...), custom_call_target="tpu_custom_call" | custom-call | flops 20132659200 | bytes 8388608 | tf_op jit(solution)/shard_map/pallas_call | solution.py:404
  291.7 14.4 %shard_map.196 = (f32[4096,256]{1,0:T(8,128)S(1)}, bf16[4096,256]{1,0:T(8,128)(2,1)S(1)}, bf16[2,2,52,8,256]{4,3,2,1,0:T(8,128)(2,1)S(1)}, bf16[2,2,52,8,256]{4,3,2,1,0:T(8,128)(2,1)S(1)}) custom-call(s32[1]{0:T(128)} %bitcast.core_ref, bf16[4096,512]{1,0:T(8,128)(2,1)S(1)} %get-tuple-element.337.dkv_ref, bf16[4096,256]{1,0:T(8,128)(2,1)} %get-tuple-element.338.slope_ref, ...), custom_call_target="tpu_custom_call" | custom-call | flops 6979321856 | bytes 20971520 | tf_op jit(solution)/shard_map/pallas_call | solution.py:994
  312.9 4.4 %collective-permute-done.35 = bf16[24,8,768]{2,1,0:T(8,128)(2,1)S(1)} collective-permute-done((bf16[24,8,768]{2,1,0:T(8,128)(2,1)S(1)}, bf16[24,8,768]{2,1,0:T(8,128)(2,1)S(1)}, u32[]{:S(2)}, u32[]{:S(2)}) %collective-permute-start.35) | collective-permute-done | bytes 294944 | tf_op jit(solution)/shard_map/ppermute | solution.py:63
  325.6 8.0 %shard_map.197 = bf16[4096,256]{1,0:T(8,128)(2,1)S(1)} custom-call(bf16[4096,256]{1,0:T(8,128)(2,1)S(1)} %get-tuple-element.381.gz_ref, f32[4096,256]{1,0:T(8,128)S(1)} %get-tuple-element.382.d_hidden_ref, bf16[9,256,256]{2,1,0:T(8,128)(2,1)S(1)} %get-tuple-element.444.conv_ref), custom_call_target="tpu_custom_call" | custom-call | flops 4831838208 | bytes 8388608 | tf_op jit(solution)/shard_map/pallas_call | solution.py:1060
  346.0 5.4 %collective-permute-done.45 = bf16[19,8,256]{2,1,0:T(8,128)(2,1)} collective-permute-done((bf16[19,8,256]{2,1,0:T(8,128)(2,1)}, bf16[19,8,256]{2,1,0:T(8,128)(2,1)}, u32[]{:S(2)}, u32[]{:S(2)}) %collective-permute-start.45) | collective-permute-done | bytes 77856 | tf_op jit(solution)/shard_map/ppermute | solution.py:63
  359.3 3.7 all-to-all-start.1
  366.3 22.6 %collective-permute-done.42 = bf16[16,64,256]{2,1,0:T(8,128)(2,1)S(1)} collective-permute-done((bf16[16,64,256]{2,1,0:T(8,128)(2,1)S(1)}, bf16[16,64,256]{2,1,0:T(8,128)(2,1)S(1)}, u32[]{:S(2)}, u32[]{:S(2)}) %collective-permute-start.42) | collective-permute-done | bytes 524320 | tf_op jit(solution)/shard_map/ppermute | solution.py:63
  395.1 6.5 %subtract_select_fusion = (f32[8,256,256]{2,1,0:T(8,128)}, f32[8,256,256]{2,1,0:T(8,128)}, f32[8,256,256]{2,1,0:T(8,128)}) fusion(f32[8,256,256]{2,1,0:T(8,128)S(1)} %copy-done.26, pred[8]{0:T(512)(128)(4,1)S(1)} %broadcast_compare_fusion, f32[8,256,256]{2,1,0:T(8,128)} %param.21, f32[8,256,256]{2,1,0:T(8,128)} %param.22, ...), kind=kLoop, calls=%fused_computation.14 | loop fusion | flops 10485760 | bytes 13631500 | tf_op jit(solution)/shard_map/jit(_where)/select_n | solution.py:1275
  (294 shorter events, 123.8 us)
Async XLA Ops:
  10.0 33.7 %all-to-all-start = ((bf16[32,8,8,256]{3,2,1,0:T(8,128)(2,1)}), bf16[32,8,8,256]{3,2,1,0:T(8,128)(2,1)S(1)}, u32[]{:S(2)}, u32[]{:S(2)}) async-start(bf16[32,8,8,256]{3,2,1,0:T(8,128)(2,1)} %copy.146), calls=%async_computation | async-start | bytes 2097152 | tf_op jit(solution)/shard_map/all_to_all | solution.py:1103
  17.3 150.0 %all-gather.2.cloned.1.call-start = ((), (), s32[]{:S(2)}) async-start(), calls=%async_computation.2 | async-start | bytes 9732096 | tf_op jit(solution)/shard_map/all_gather | solution.py:1136
  20.1 39.4 %collective-permute-start = (bf16[16,64,256]{2,1,0:T(8,128)(2,1)}, bf16[16,64,256]{2,1,0:T(8,128)(2,1)S(1)}, u32[]{:S(2)}, u32[]{:S(2)}) collective-permute-start(bf16[16,64,256]{2,1,0:T(8,128)(2,1)} %get-tuple-element.433), channel_id=1, source_target_pairs={{0,1},{1,0},{2,3},{3,2},{4,5},{5,4},{6,7},{7,6},{8,9},{9,8},{10,11... | collective-permute-start | bytes 1572872 | tf_op jit(solution)/shard_map/ppermute | solution.py:63
  21.9 39.3 %collective-permute-start.1 = (bf16[16,64,256]{2,1,0:T(8,128)(2,1)}, bf16[16,64,256]{2,1,0:T(8,128)(2,1)S(1)}, u32[]{:S(2)}, u32[]{:S(2)}) collective-permute-start(bf16[16,64,256]{2,1,0:T(8,128)(2,1)} %get-tuple-element.435), channel_id=1, source_target_pairs={{0,2},{1,3},{2,0},{3,1},{4,6},{5,7},{6,4},{7,5},{8,10},{9,11},{10,... | collective-permute-start | bytes 1572872 | tf_op jit(solution)/shard_map/ppermute | solution.py:63
  23.3 37.8 %collective-permute-start.2 = (bf16[16,64,256]{2,1,0:T(8,128)(2,1)}, bf16[16,64,256]{2,1,0:T(8,128)(2,1)S(1)}, u32[]{:S(2)}, u32[]{:S(2)}) collective-permute-start(bf16[16,64,256]{2,1,0:T(8,128)(2,1)} %get-tuple-element.432), channel_id=1, source_target_pairs={{0,3},{1,2},{2,1},{3,0},{4,7},{5,6},{6,5},{7,4},{8,11},{9,10},{10,... | collective-permute-start | bytes 1572872 | tf_op jit(solution)/shard_map/ppermute | solution.py:63
  90.8 21.5 %collective-permute-start.16 = (bf16[7,2,4,8,768]{4,3,2,1,0:T(8,128)(2,1)}, bf16[7,2,4,8,768]{4,3,2,1,0:T(8,128)(2,1)}, u32[]{:S(2)}, u32[]{:S(2)}) collective-permute-start(bf16[7,2,4,8,768]{4,3,2,1,0:T(8,128)(2,1)} %pad_maximum_fusion.4), channel_id=1, source_target_pairs={{0,1},{1,0},{2,3},{3,2},{4,5},{5,4},{6,7},{7,6},{8,9},{9,8},{10,11... | collective-permute-start | bytes 2064392 | tf_op jit(solution)/shard_map/ppermute | solution.py:63
  91.5 20.7 %collective-permute-start.15 = (bf16[6,2,4,8,768]{4,3,2,0,1:T(8,128)(2,1)S(1)}, bf16[6,2,4,8,768]{4,3,2,0,1:T(8,128)(2,1)}, u32[]{:S(2)}, u32[]{:S(2)}) collective-permute-start(bf16[6,2,4,8,768]{4,3,2,0,1:T(8,128)(2,1)S(1)} %pad_maximum_fusion.5), channel_id=1, source_target_pairs={{0,2},{2,0},{1,3},{3,1},{4,6},{6,4},{5,7},{7,5},{8,10},{10,8},{9,1... | collective-permute-start | bytes 1769480 | tf_op jit(solution)/shard_map/ppermute | solution.py:63
  204.3 16.3 %collective-permute-start.19 = (bf16[2,2,48,8,768]{4,3,2,1,0:T(8,128)(2,1)}, bf16[2,2,48,8,768]{4,3,2,1,0:T(8,128)(2,1)}, u32[]{:S(2)}, u32[]{:S(2)}) collective-permute-start(bf16[2,2,48,8,768]{4,3,2,1,0:T(8,128)(2,1)} %get-tuple-element.272), channel_id=1, source_target_pairs={{0,4},{4,0},{1,5},{5,1},{2,6},{6,2},{3,7},{7,3},{8,12},{12,8},{9,1... | collective-permute-start | bytes 7077896 | tf_op jit(solution)/shard_map/ppermute | solution.py:63
  226.2 28.2 %collective-permute-start.22 = (bf16[2,48,8,768]{3,2,1,0:T(8,128)(2,1)S(1)}, bf16[2,48,8,768]{3,2,1,0:T(8,128)(2,1)S(1)}, u32[]{:S(2)}, u32[]{:S(2)}) collective-permute-start(bf16[2,48,8,768]{3,2,1,0:T(8,128)(2,1)S(1)} %get-tuple-element.296), channel_id=1, source_target_pairs={{0,2},{2,0},{1,3},{3,1},{4,6},{6,4},{5,7},{7,5},{8,10},{10,8},{9,1... | collective-permute-start | bytes 3538952 | tf_op jit(solution)/shard_map/ppermute | solution.py:63
  227.8 27.9 %collective-permute-start.23 = (bf16[2,48,8,768]{3,2,1,0:T(8,128)(2,1)S(1)}, bf16[2,48,8,768]{3,2,1,0:T(8,128)(2,1)S(1)}, u32[]{:S(2)}, u32[]{:S(2)}) collective-permute-start(bf16[2,48,8,768]{3,2,1,0:T(8,128)(2,1)S(1)} %get-tuple-element.298), channel_id=1, source_target_pairs={{0,1},{1,0},{2,3},{3,2},{4,5},{5,4},{6,7},{7,6},{8,9},{9,8},{10,11... | collective-permute-start | bytes 3538952 | tf_op jit(solution)/shard_map/ppermute | solution.py:63
  256.4 29.2 %collective-permute-start.26 = (bf16[2,2,24,8,768]{4,3,2,1,0:T(8,128)(2,1)S(1)}, bf16[2,2,24,8,768]{4,3,2,1,0:T(8,128)(2,1)S(1)}, u32[]{:S(2)}, u32[]{:S(2)}) collective-permute-start(bf16[2,2,24,8,768]{4,3,2,1,0:T(8,128)(2,1)S(1)} %get-tuple-element.319), channel_id=1, source_target_pairs={{0,4},{4,0},{1,5},{5,1},{2,6},{6,2},{3,7},{7,3},{8,12},{12,8},{9,1... | collective-permute-start | bytes 3538952 | tf_op jit(solution)/shard_map/ppermute | solution.py:63
  256.5 29.1 %collective-permute-start.24 = (bf16[48,8,768]{2,1,0:T(8,128)(2,1)S(1)}, bf16[48,8,768]{2,1,0:T(8,128)(2,1)S(1)}, u32[]{:S(2)}, u32[]{:S(2)}) collective-permute-start(bf16[48,8,768]{2,1,0:T(8,128)(2,1)S(1)} %get-tuple-element.315), channel_id=1, source_target_pairs={{0,1},{1,0},{2,3},{3,2},{4,5},{5,4},{6,7},{7,6},{8,9},{9,8},{10,11... | collective-permute-start | bytes 1769480 | tf_op jit(solution)/shard_map/ppermute | solution.py:63
  258.0 27.7 %collective-permute-start.25 = (bf16[48,8,768]{2,1,0:T(8,128)(2,1)S(1)}, bf16[48,8,768]{2,1,0:T(8,128)(2,1)S(1)}, u32[]{:S(2)}, u32[]{:S(2)}) collective-permute-start(bf16[48,8,768]{2,1,0:T(8,128)(2,1)S(1)} %get-tuple-element.317), channel_id=1, source_target_pairs={{0,2},{2,0},{1,3},{3,1},{4,6},{6,4},{5,7},{7,5},{8,10},{10,8},{9,1... | collective-permute-start | bytes 1769480 | tf_op jit(solution)/shard_map/ppermute | solution.py:63
  258.6 27.1 %collective-permute-start.27 = (bf16[2,2,12,8,768]{4,3,2,1,0:T(8,128)(2,1)S(1)}, bf16[2,2,12,8,768]{4,3,2,1,0:T(8,128)(2,1)S(1)}, u32[]{:S(2)}, u32[]{:S(2)}) collective-permute-start(bf16[2,2,12,8,768]{4,3,2,1,0:T(8,128)(2,1)S(1)} %get-tuple-element.321), channel_id=1, source_target_pairs={{0,4},{4,0},{1,5},{5,1},{2,6},{6,2},{3,7},{7,3},{8,12},{12,8},{9,1... | collective-permute-start | bytes 1769480 | tf_op jit(solution)/shard_map/ppermute | solution.py:63
  258.6 27.1 %collective-permute-start.28 = (bf16[2,2,8,8,768]{4,3,2,1,0:T(8,128)(2,1)S(1)}, bf16[2,2,8,8,768]{4,3,2,1,0:T(8,128)(2,1)S(1)}, u32[]{:S(2)}, u32[]{:S(2)}) collective-permute-start(bf16[2,2,8,8,768]{4,3,2,1,0:T(8,128)(2,1)S(1)} %get-tuple-element.323), channel_id=1, source_target_pairs={{0,4},{4,0},{1,5},{5,1},{2,6},{6,2},{3,7},{7,3},{8,12},{12,8},{9,1... | collective-permute-start | bytes 1179656 | tf_op jit(solution)/shard_map/ppermute | solution.py:63
  288.1 19.6 %collective-permute-start.29 = (bf16[24,2,8,768]{3,2,0,1:T(8,128)(2,1)S(1)}, bf16[24,2,8,768]{3,2,0,1:T(8,128)(2,1)S(1)}, u32[]{:S(2)}, u32[]{:S(2)}) collective-permute-start(bf16[24,2,8,768]{3,2,0,1:T(8,128)(2,1)S(1)} %get-tuple-element.348), channel_id=1, source_target_pairs={{0,8},{8,0},{16,24},{24,16},{1,9},{9,1},{17,25},{25,17},{2,10},{10... | collective-permute-start | bytes 1769480 | tf_op jit(solution)/shard_map/ppermute | solution.py:63
  288.2 19.5 %collective-permute-start.30 = (bf16[2,24,8,768]{3,2,1,0:T(8,128)(2,1)S(1)}, bf16[2,24,8,768]{3,2,1,0:T(8,128)(2,1)S(1)}, u32[]{:S(2)}, u32[]{:S(2)}) collective-permute-start(bf16[2,24,8,768]{3,2,1,0:T(8,128)(2,1)S(1)} %get-tuple-element.350), channel_id=1, source_target_pairs={{0,1},{1,0},{2,3},{3,2},{4,5},{5,4},{6,7},{7,6},{8,9},{9,8},{10,11... | collective-permute-start | bytes 1769480 | tf_op jit(solution)/shard_map/ppermute | solution.py:63
  288.9 18.8 %collective-permute-start.31 = (bf16[2,24,8,768]{3,2,1,0:T(8,128)(2,1)S(1)}, bf16[2,24,8,768]{3,2,1,0:T(8,128)(2,1)S(1)}, u32[]{:S(2)}, u32[]{:S(2)}) collective-permute-start(bf16[2,24,8,768]{3,2,1,0:T(8,128)(2,1)S(1)} %get-tuple-element.352), channel_id=1, source_target_pairs={{0,2},{2,0},{1,3},{3,1},{4,6},{6,4},{5,7},{7,5},{8,10},{10,8},{9,1... | collective-permute-start | bytes 1769480 | tf_op jit(solution)/shard_map/ppermute | solution.py:63
  290.3 17.4 %collective-permute-start.32 = (bf16[2,8,8,768]{3,2,1,0:T(8,128)(2,1)S(1)}, bf16[2,8,8,768]{3,2,1,0:T(8,128)(2,1)S(1)}, u32[]{:S(2)}, u32[]{:S(2)}) collective-permute-start(bf16[2,8,8,768]{3,2,1,0:T(8,128)(2,1)S(1)} %get-tuple-element.354), channel_id=1, source_target_pairs={{0,1},{1,0},{2,3},{3,2},{4,5},{5,4},{6,7},{7,6},{8,9},{9,8},{10,11... | collective-permute-start | bytes 589832 | tf_op jit(solution)/shard_map/ppermute | solution.py:63
  311.2 22.4 %collective-permute-start.41 = (bf16[24,8,768]{2,1,0:T(8,128)(2,1)S(1)}, bf16[24,8,768]{2,1,0:T(8,128)(2,1)S(1)}, u32[]{:S(2)}, u32[]{:S(2)}) collective-permute-start(bf16[24,8,768]{2,1,0:T(8,128)(2,1)S(1)} %get-tuple-element.465), channel_id=1, source_target_pairs={{0,16},{8,24},{16,0},{24,8},{1,17},{9,25},{17,1},{25,9},{2,18},{10... | collective-permute-start | bytes 884744 | tf_op jit(solution)/shard_map/ppermute | solution.py:63
  336.6 16.5 %collective-permute-start.47 = (bf16[12,8,768]{2,1,0:T(8,128)(2,1)}, bf16[12,8,768]{2,1,0:T(8,128)(2,1)}, u32[]{:S(2)}, u32[]{:S(2)}) collective-permute-start(bf16[12,8,768]{2,1,0:T(8,128)(2,1)} %get-tuple-element.406), channel_id=1, source_target_pairs={{0,16},{8,24},{16,0},{24,8},{1,17},{9,25},{17,1},{25,9},{2,18},{10... | collective-permute-start | bytes 442376 | tf_op jit(solution)/shard_map/ppermute | solution.py:63
  359.3 32.8 %all-to-all-start.1 = ((bf16[32,9,8,256]{3,2,1,0:T(8,128)(2,1)}), bf16[32,9,8,256]{3,2,1,0:T(8,128)(2,1)}, u32[]{:S(2)}, u32[]{:S(2)}) async-start(bf16[32,9,8,256]{3,2,1,0:T(8,128)(2,1)} %bitcast.152), calls=%async_computation.1 | async-start | bytes 2359296 | tf_op jit(solution)/shard_map/all_to_all | solution.py:1254
  363.0 25.9 %collective-permute-start.42 = (bf16[16,64,256]{2,1,0:T(8,128)(2,1)S(1)}, bf16[16,64,256]{2,1,0:T(8,128)(2,1)S(1)}, u32[]{:S(2)}, u32[]{:S(2)}) collective-permute-start(bf16[16,64,256]{2,1,0:T(8,128)(2,1)S(1)} %copy-done.34), channel_id=1, source_target_pairs={{0,1},{1,0},{2,3},{3,2},{4,5},{5,4},{6,7},{7,6},{8,9},{9,8},{10,11... | collective-permute-start | bytes 1572872 | tf_op jit(solution)/shard_map/ppermute | solution.py:63
  364.8 24.1 %collective-permute-start.43 = (bf16[16,64,256]{2,1,0:T(8,128)(2,1)S(1)}, bf16[16,64,256]{2,1,0:T(8,128)(2,1)S(1)}, u32[]{:S(2)}, u32[]{:S(2)}) collective-permute-start(bf16[16,64,256]{2,1,0:T(8,128)(2,1)S(1)} %copy-done.33), channel_id=1, source_target_pairs={{0,2},{1,3},{2,0},{3,1},{4,6},{5,7},{6,4},{7,5},{8,10},{9,11},{10,... | collective-permute-start | bytes 1572872 | tf_op jit(solution)/shard_map/ppermute | solution.py:63
  (70 other events, 521.8 us)
Sparse Core Ops, SparseCore 0:
  80.0 87.2 all-gather.1

commit v10 on v9

--- a/solution.py
+++ b/solution.py
@@ -36,7 +36,7 @@
 GROUP = 4
 EARLY = 13
 VMEM_BYTES = 28 * 1024 * 1024
-MLP_BYTES = 44 * 1024 * 1024
+MLP_BYTES = 40 * 1024 * 1024
 ROW_BLOCKS = ((0, 256), (256, 256), (512, 224))
 CORE_SPEC = pl.BlockSpec(memory_space=pltpu.SMEM)
 bf16 = jnp.bfloat16
@@ -320,11 +320,11 @@
 
 
 def cross_forward(query, kv):
-    rows = query.shape[0] // 2
+    rows = query.shape[0] // 1
     cells = kv.shape[0]
     return pl.pallas_call(
         cross_forward_kernel,
-        grid=(2,),
+        grid=(1,),
         in_specs=[
             pl.BlockSpec((rows, CH), lambda i: (i, 0)),
             pl.BlockSpec((cells, CH), lambda i: (0, 0)),
@@ -335,8 +335,8 @@
             pl.BlockSpec((1, 8, rows), lambda i: (i, 0, 0)),
         ],
         out_shape=[
-            jax.ShapeDtypeStruct((2 * rows, CH), bf16),
-            jax.ShapeDtypeStruct((2, 8, rows), f32),
+            jax.ShapeDtypeStruct((rows, CH), bf16),
+            jax.ShapeDtypeStruct((1, 8, rows), f32),
         ],
         compiler_params=params(),
         cost_estimate=cost(16 * TH * rows * cells * CH // 2, 8 * cells * CH, 2 * TH * rows * cells),
@@ -1184,7 +1184,7 @@
     up, down, emb = send(up, "x"), send(down, "y"), send(emb, "c")
     first, second = send(first, "c"), send(second, "c")
 
-    log_rows = jnp.concatenate([cross_logs[0], cross_logs[1]], 1)
+    log_rows = cross_logs[0]
     gkv, query_g, future_grad = cross_backward(
         query, kv, gox, cross_mixed, log_rows, feats_b, gupd, to_query
     )

time: 415 us -> 414 us (level)
    unnamed x91 -> x81, local copies, waits for them, and re-layouts: 10.5 us -> 9.46 us
  transfers between devices with their start and end apart: 52 -> 52, of which waited for: 19 -> 20; matrix products, arithmetic and copies ran while one was open for 8% -> 8% of each run, Pallas kernels for 34% -> 33%
where the time goes in v10:
time: 414 us; the launch traced here: 407 us
  Pallas kernels  170 us (41%)
  waiting for transfers between devices  92.2 us (22%)
  starting transfers between devices  61.7 us (15%)
  other arithmetic  34.9 us (8%)
  local copies, waits for them, and re-layouts  27.3 us (7%)
  between operations  20.1 us (5%)
    ppermute x49, waiting for transfers between devices, xor_permute(): return lax.ppermute(values, axes, [(i, i ^ mask) for i in range(count)])  66 us
    ppermute x49, starting transfers between devices, xor_permute(): return lax.ppermute(values, axes, [(i, i ^ mask) for i in range(count)])  50.6 us
    pallas_call x1, Pallas kernels, mlp_block(): pl.pallas_call(functools.partial(mlp_kernel, sizes=slice_shape()), grid=(...  34.3 us
    pallas_call x1, Pallas kernels, cross_backward(): pl.pallas_call(cross_backward_kernel, grid=(cells // block,), in_specs=[p...  26.6 us
    pallas_call x1, Pallas kernels, embed_grad(): pl.pallas_call(functools.partial(embed_grad_kernel, sizes=slice_shape()),...  18.8 us
    all_to_all x1, waiting for transfers between devices, local(): lax.all_to_all(slices, AXES, split_axis=0, concat_axis=0, tiled=True)  15.8 us
    pallas_call x1, Pallas kernels, token_forward(): pl.pallas_call(token_forward_kernel, grid=(steps,), in_specs=[pl.BlockSpe...  15.3 us
    pallas_call x1, Pallas kernels, token_backward(): pl.pallas_call(functools.partial(token_backward_kernel, sizes=slice_shape...  14.4 us
  transfers between devices with their start and end apart: 52, of which 20 were waited for; matrix products, arithmetic and copies ran while one was open for 8% of the time, Pallas kernels for 33%

profile of v10, /device:TPU:0, one launch (start us, length us, event | category | flops | bytes accessed | tf_op | source)
XLA Modules:
  0.0 407.4 jit_solution(10253343936436756140)
XLA Ops:
  10.0 7.3 %all-to-all-start = ((bf16[32,8,8,256]{3,2,1,0:T(8,128)(2,1)}), bf16[32,8,8,256]{3,2,1,0:T(8,128)(2,1)S(1)}, u32[]{:S(2)}, u32[]{:S(2)}) async-start(bf16[32,8,8,256]{3,2,1,0:T(8,128)(2,1)} %copy.146), calls=%async_computation | async-start | bytes 2097152 | tf_op jit(solution)/shard_map/all_to_all | solution.py:1103
  27.9 15.8 %all-to-all-done = bf16[32,8,8,256]{3,2,1,0:T(8,128)(2,1)S(1)} async-done(((bf16[32,8,8,256]{3,2,1,0:T(8,128)(2,1)}), bf16[32,8,8,256]{3,2,1,0:T(8,128)(2,1)S(1)}, u32[]{:S(2)}, u32[]{:S(2)}) %all-to-all-start) | async-done | bytes 1048608 | tf_op jit(solution)/shard_map/all_to_all | solution.py:1103
  52.9 3.0 collective-permute-done.4
  61.2 4.1 %shard_map.186.x_ref = bf16[4224,768]{1,0:T(8,128)(2,1)} custom-call(s32[1]{0:T(128)} %bitcast.1.row_ref, bf16[1024,256]{1,0:T(8,128)(2,1)S(1)} %bitcast.300, bf16[1024,256]{1,0:T(8,128)(2,1)S(1)} %bitcast.307, bf16[1024,256]{1,0:T(8,128)(2,1)S(1)} %bitcast.308, bf16[1024,256]{1,0:T(8,128)(2,1)S(1)} %bitcast.309), custom_call_target="tpu_custom_call" | custom-call | bytes 8388608 | tf_op jit(solution)/shard_map/pallas_call | solution.py:233
  65.4 5.0 %collective-permute-done.7 = bf16[13,8,768]{2,1,0:T(8,128)(2,1)S(1)} collective-permute-done((bf16[13,8,768]{2,1,0:T(8,128)(2,1)S(1)}, bf16[13,8,768]{2,1,0:T(8,128)(2,1)S(1)}, u32[]{:S(2)}, u32[]{:S(2)}) %collective-permute-start.7) | collective-permute-done | bytes 159776 | tf_op jit(solution)/shard_map/ppermute | solution.py:63
  74.4 5.5 %collective-permute-done.9 = bf16[6,4,8,768]{3,2,1,0:T(8,128)(2,1)S(1)} collective-permute-done((bf16[6,4,8,768]{3,2,1,0:T(8,128)(2,1)S(1)}, bf16[6,4,8,768]{3,2,1,0:T(8,128)(2,1)S(1)}, u32[]{:S(2)}, u32[]{:S(2)}) %collective-permute-start.9) | collective-permute-done | bytes 294944 | tf_op jit(solution)/shard_map/ppermute | solution.py:63
  83.5 2.8 collective-permute-done.11
  100.4 15.3 %shard_map.187 = (bf16[4096,256]{1,0:T(8,128)(2,1)}, bf16[4096,256]{1,0:T(8,128)(2,1)}, bf16[4096,512]{1,0:T(8,128)(2,1)S(1)}, bf16[256,256]{1,0:T(8,128)(2,1)S(1)}) custom-call(bf16[4224,768]{1,0:T(8,128)(2,1)} %shard_map.186.x_ref, bf16[3,768,256]{2,1,0:T(8,128)(2,1)S(1)} %bitcast.303, bf16[256,512]{1,0:T(8,128)(2,1)S(1)} %pad_maximum_fusion.11.kv_w_ref), custom_call_target="tpu_custom_call" | custom-call | flops 5905580032 | bytes 14680064 | tf_op jit(solution)/shard_map/pallas_call | solution.py:932
  120.1 12.0 %shard_map.188 = (bf16[480,256]{1,0:T(8,128)(2,1)S(1)}, f32[1,8,480]{2,1,0:T(8,128)S(1)}) custom-call(bf16[480,256]{1,0:T(8,128)(2,1)S(1)} %fusion.2.q_ref, bf16[4096,512]{1,0:T(8,128)(2,1)S(1)} %get-tuple-element.247.k_ref.v_ref, bf16[4096,512]{1,0:T(8,128)(2,1)S(1)} %get-tuple-element.247.k_ref.v_ref), custom_call_target="tpu_custom_call" | custom-call | flops 16106127360 | bytes 8388608 | tf_op jit(solution)/shard_map/pallas_call | solution.py:325
  136.4 7.7 %shard_map.190 = (bf16[736,256]{1,0:T(8,128)(2,1)}, f32[736,768]{1,0:T(8,128)}, bf16[736,768]{1,0:T(8,128)(2,1)}, bf16[3,736,768]{2,1,0:T(8,128)(2,1)}) custom-call(bf16[256,256]{1,0:T(8,128)(2,1)S(1)} %get-tuple-element.238.pool_ref, bf16[480,256]{1,0:T(8,128)(2,1)S(1)} %bitcast.304, bf16[480,256]{1,0:T(8,128)(2,1)S(1)} %get-tuple-element.251.mixed_ref.o_ref, ...), custom_call_target="tpu_custom_call" | custom-call | flops 2894069760 | bytes 6782976 | tf_op jit(solution)/shard_map/pallas_call | solution.py:652
  146.1 12.0 %shard_map.191 = (bf16[736,768]{1,0:T(8,128)(2,1)}, f32[3,8,736]{2,1,0:T(8,128)S(1)}) custom-call(s32[1]{0:T(128)} %add.398.len_ref, bf16[3,736,768]{2,1,0:T(8,128)(2,1)S(1)} %copy-done.14, bf16[3,736,768]{2,1,0:T(8,128)(2,1)S(1)} %copy-done.14, bf16[3,736,768]{2,1,0:T(8,128)(2,1)S(1)} %copy-done.14), custom_call_target="tpu_custom_call" | custom-call | flops 6656360448 | bytes 4521984 | tf_op jit(solution)/shard_map/pallas_call | solution.py:468
  158.7 9.7 %all-gather.2.cloned.1.call-done.up_ref.down_ref = bf16[24,256,768]{2,1,0:T(8,128)(2,1)} async-done(((bf16[24,8,768]{2,1,0:T(8,128)(2,1)}), bf16[24,256,768]{2,1,0:T(8,128)(2,1)}) %all-gather.2.cloned.1.call-update) | async-done | bytes 9437200 | tf_op jit(solution)/shard_map/all_gather | solution.py:1136
  168.4 34.3 %shard_map.192 = (f32[736,768]{1,0:T(8,128)}, f32[736,768]{1,0:T(8,128)}, bf16[736,768]{1,0:T(8,128)(2,1)}, bf16[2,2,48,8,768]{4,3,2,1,0:T(8,128)(2,1)S(1)}, bf1...) custom-call(s32[1]{0:T(128)} %bitcast.core_ref, ...), custom_call_target="tpu_custom_call" | custom-call | flops 23441965056 | bytes 33914880 | tf_op jit(solution)/shard_map/pallas_call | solution.py:735
  205.7 13.0 %shard_map.193.g_ref = bf16[3,736,512]{2,1,0:T(8,128)(2,1)S(1)} custom-call(s32[1]{0:T(128)} %add.398.len_ref, bf16[3,736,768]{2,1,0:T(8,128)(2,1)} %get-tuple-element.256.q_ref.k_ref.v_ref, bf16[3,736,768]{2,1,0:T(8,128)(2,1)} %get-tuple-element.256.q_ref.k_ref.v_ref, bf16[3,736,768]{2,1,0:T(8,128)(2,1)} %get-tuple-element.256.q_ref.k_ref.v_ref, ...), custom_call_target="tpu_custom_call" | custom-call | flops 8875147264 | bytes 9043968 | tf_op jit(solution)/shard_map/pallas_call | solution.py:530
  226.7 18.8 %shard_map.194 = (bf16[2,2,24,8,768]{4,3,2,1,0:T(8,128)(2,1)S(1)}, bf16[2,2,24,8,768]{4,3,2,1,0:T(8,128)(2,1)S(1)}, bf16[2,2,12,8,768]{4,3,2,1,0:T(8,128)(2,1)S(...) custom-call(s32[1]{0:T(128)} %bitcast.core_ref, ...), custom_call_target="tpu_custom_call" | custom-call | flops 10225713152 | bytes 28262400 | tf_op jit(solution)/shard_map/pallas_call | solution.py:840
  245.5 6.4 %collective-permute-done.22 = bf16[2,48,8,768]{3,2,1,0:T(8,128)(2,1)S(1)} collective-permute-done((bf16[2,48,8,768]{3,2,1,0:T(8,128)(2,1)S(1)}, bf16[2,48,8,768]{3,2,1,0:T(8,128)(2,1)S(1)}, u32[]{:S(2)}, u32[]{:S(2)}) %collective-permute-start.22) | collective-permute-done | bytes 1179680 | tf_op jit(solution)/shard_map/ppermute | solution.py:63
  256.6 26.6 %shard_map.195 = (bf16[4096,512]{1,0:T(8,128)(2,1)S(1)}, bf16[256,256]{1,0:T(8,128)(2,1)S(1)}, f32[480,256]{1,0:T(8,128)}) custom-call(bf16[480,256]{1,0:T(8,128)(2,1)S(1)} %copy-done.10, bf16[4096,512]{1,0:T(8,128)(2,1)S(1)} %copy-done.19, bf16[4096,512]{1,0:T(8,128)(2,1)S(1)} %copy-done.19, bf16[480,256]{1,0:T(8,128)(2,1)S(1)} %get-tuple-element.310.do_ref, ...), custom_call_target="tpu_custom_call" | custom-call | flops 20132659200 | bytes 8388608 | tf_op jit(solution)/shard_map/pallas_call | solution.py:404
  289.0 14.4 %shard_map.196 = (f32[4096,256]{1,0:T(8,128)S(1)}, bf16[4096,256]{1,0:T(8,128)(2,1)S(1)}, bf16[2,2,52,8,256]{4,3,2,1,0:T(8,128)(2,1)S(1)}, bf16[2,2,52,8,256]{4,3,2,1,0:T(8,128)(2,1)S(1)}) custom-call(s32[1]{0:T(128)} %bitcast.core_ref, bf16[4096,512]{1,0:T(8,128)(2,1)S(1)} %get-tuple-element.337.dkv_ref, bf16[4096,256]{1,0:T(8,128)(2,1)} %get-tuple-element.338.slope_ref, ...), custom_call_target="tpu_custom_call" | custom-call | flops 6979321856 | bytes 20971520 | tf_op jit(solution)/shard_map/pallas_call | solution.py:994
  310.2 4.4 %collective-permute-done.35 = bf16[24,8,768]{2,1,0:T(8,128)(2,1)S(1)} collective-permute-done((bf16[24,8,768]{2,1,0:T(8,128)(2,1)S(1)}, bf16[24,8,768]{2,1,0:T(8,128)(2,1)S(1)}, u32[]{:S(2)}, u32[]{:S(2)}) %collective-permute-start.35) | collective-permute-done | bytes 294944 | tf_op jit(solution)/shard_map/ppermute | solution.py:63
  322.9 8.0 %shard_map.197 = bf16[4096,256]{1,0:T(8,128)(2,1)S(1)} custom-call(bf16[4096,256]{1,0:T(8,128)(2,1)S(1)} %get-tuple-element.381.gz_ref, f32[4096,256]{1,0:T(8,128)S(1)} %get-tuple-element.382.d_hidden_ref, bf16[9,256,256]{2,1,0:T(8,128)(2,1)S(1)} %get-tuple-element.444.conv_ref), custom_call_target="tpu_custom_call" | custom-call | flops 4831838208 | bytes 8388608 | tf_op jit(solution)/shard_map/pallas_call | solution.py:1060
  343.4 5.4 %collective-permute-done.45 = bf16[19,8,256]{2,1,0:T(8,128)(2,1)} collective-permute-done((bf16[19,8,256]{2,1,0:T(8,128)(2,1)}, bf16[19,8,256]{2,1,0:T(8,128)(2,1)}, u32[]{:S(2)}, u32[]{:S(2)}) %collective-permute-start.45) | collective-permute-done | bytes 77856 | tf_op jit(solution)/shard_map/ppermute | solution.py:63
  356.6 3.7 all-to-all-start.1
  363.6 22.6 %collective-permute-done.42 = bf16[16,64,256]{2,1,0:T(8,128)(2,1)S(1)} collective-permute-done((bf16[16,64,256]{2,1,0:T(8,128)(2,1)S(1)}, bf16[16,64,256]{2,1,0:T(8,128)(2,1)S(1)}, u32[]{:S(2)}, u32[]{:S(2)}) %collective-permute-start.42) | collective-permute-done | bytes 524320 | tf_op jit(solution)/shard_map/ppermute | solution.py:63
  392.5 6.5 %subtract_select_fusion = (f32[8,256,256]{2,1,0:T(8,128)}, f32[8,256,256]{2,1,0:T(8,128)}, f32[8,256,256]{2,1,0:T(8,128)}) fusion(f32[8,256,256]{2,1,0:T(8,128)S(1)} %copy-done.23, pred[8]{0:T(512)(128)(4,1)S(1)} %broadcast_compare_fusion, f32[8,256,256]{2,1,0:T(8,128)} %param.21, f32[8,256,256]{2,1,0:T(8,128)} %param.22, ...), kind=kLoop, calls=%fused_computation.14 | loop fusion | flops 10485760 | bytes 13631500 | tf_op jit(solution)/shard_map/jit(_where)/select_n | solution.py:1275
  (282 shorter events, 123.0 us)
Async XLA Ops:
  10.0 33.7 %all-to-all-start = ((bf16[32,8,8,256]{3,2,1,0:T(8,128)(2,1)}), bf16[32,8,8,256]{3,2,1,0:T(8,128)(2,1)S(1)}, u32[]{:S(2)}, u32[]{:S(2)}) async-start(bf16[32,8,8,256]{3,2,1,0:T(8,128)(2,1)} %copy.146), calls=%async_computation | async-start | bytes 2097152 | tf_op jit(solution)/shard_map/all_to_all | solution.py:1103
  17.3 151.1 %all-gather.2.cloned.1.call-start = ((), (), s32[]{:S(2)}) async-start(), calls=%async_computation.2 | async-start | bytes 9732096 | tf_op jit(solution)/shard_map/all_gather | solution.py:1136
  20.1 39.4 %collective-permute-start = (bf16[16,64,256]{2,1,0:T(8,128)(2,1)}, bf16[16,64,256]{2,1,0:T(8,128)(2,1)S(1)}, u32[]{:S(2)}, u32[]{:S(2)}) collective-permute-start(bf16[16,64,256]{2,1,0:T(8,128)(2,1)} %get-tuple-element.433), channel_id=1, source_target_pairs={{0,1},{1,0},{2,3},{3,2},{4,5},{5,4},{6,7},{7,6},{8,9},{9,8},{10,11... | collective-permute-start | bytes 1572872 | tf_op jit(solution)/shard_map/ppermute | solution.py:63
  21.9 39.3 %collective-permute-start.1 = (bf16[16,64,256]{2,1,0:T(8,128)(2,1)}, bf16[16,64,256]{2,1,0:T(8,128)(2,1)S(1)}, u32[]{:S(2)}, u32[]{:S(2)}) collective-permute-start(bf16[16,64,256]{2,1,0:T(8,128)(2,1)} %get-tuple-element.435), channel_id=1, source_target_pairs={{0,2},{1,3},{2,0},{3,1},{4,6},{5,7},{6,4},{7,5},{8,10},{9,11},{10,... | collective-permute-start | bytes 1572872 | tf_op jit(solution)/shard_map/ppermute | solution.py:63
  23.3 37.8 %collective-permute-start.2 = (bf16[16,64,256]{2,1,0:T(8,128)(2,1)}, bf16[16,64,256]{2,1,0:T(8,128)(2,1)S(1)}, u32[]{:S(2)}, u32[]{:S(2)}) collective-permute-start(bf16[16,64,256]{2,1,0:T(8,128)(2,1)} %get-tuple-element.432), channel_id=1, source_target_pairs={{0,3},{1,2},{2,1},{3,0},{4,7},{5,6},{6,5},{7,4},{8,11},{9,10},{10,... | collective-permute-start | bytes 1572872 | tf_op jit(solution)/shard_map/ppermute | solution.py:63
  91.7 24.1 %collective-permute-start.16 = (bf16[7,2,4,8,768]{4,3,2,1,0:T(8,128)(2,1)}, bf16[7,2,4,8,768]{4,3,2,1,0:T(8,128)(2,1)}, u32[]{:S(2)}, u32[]{:S(2)}) collective-permute-start(bf16[7,2,4,8,768]{4,3,2,1,0:T(8,128)(2,1)} %pad_maximum_fusion.4), channel_id=1, source_target_pairs={{0,1},{1,0},{2,3},{3,2},{4,5},{5,4},{6,7},{7,6},{8,9},{9,8},{10,11... | collective-permute-start | bytes 2064392 | tf_op jit(solution)/shard_map/ppermute | solution.py:63
  92.4 23.3 %collective-permute-start.15 = (bf16[6,2,4,8,768]{4,3,2,0,1:T(8,128)(2,1)}, bf16[6,2,4,8,768]{4,3,2,0,1:T(8,128)(2,1)}, u32[]{:S(2)}, u32[]{:S(2)}) collective-permute-start(bf16[6,2,4,8,768]{4,3,2,0,1:T(8,128)(2,1)} %pad_maximum_fusion.5), channel_id=1, source_target_pairs={{0,2},{2,0},{1,3},{3,1},{4,6},{6,4},{5,7},{7,5},{8,10},{10,8},{9,1... | collective-permute-start | bytes 1769480 | tf_op jit(solution)/shard_map/ppermute | solution.py:63
  204.1 14.7 %collective-permute-start.19 = (bf16[2,2,48,8,768]{4,3,2,1,0:T(8,128)(2,1)}, bf16[2,2,48,8,768]{4,3,2,1,0:T(8,128)(2,1)}, u32[]{:S(2)}, u32[]{:S(2)}) collective-permute-start(bf16[2,2,48,8,768]{4,3,2,1,0:T(8,128)(2,1)} %get-tuple-element.272), channel_id=1, source_target_pairs={{0,4},{4,0},{1,5},{5,1},{2,6},{6,2},{3,7},{7,3},{8,12},{12,8},{9,1... | collective-permute-start | bytes 7077896 | tf_op jit(solution)/shard_map/ppermute | solution.py:63
  223.7 28.2 %collective-permute-start.22 = (bf16[2,48,8,768]{3,2,1,0:T(8,128)(2,1)S(1)}, bf16[2,48,8,768]{3,2,1,0:T(8,128)(2,1)S(1)}, u32[]{:S(2)}, u32[]{:S(2)}) collective-permute-start(bf16[2,48,8,768]{3,2,1,0:T(8,128)(2,1)S(1)} %get-tuple-element.296), channel_id=1, source_target_pairs={{0,2},{2,0},{1,3},{3,1},{4,6},{6,4},{5,7},{7,5},{8,10},{10,8},{9,1... | collective-permute-start | bytes 3538952 | tf_op jit(solution)/shard_map/ppermute | solution.py:63
  225.3 27.8 %collective-permute-start.23 = (bf16[2,48,8,768]{3,2,1,0:T(8,128)(2,1)S(1)}, bf16[2,48,8,768]{3,2,1,0:T(8,128)(2,1)S(1)}, u32[]{:S(2)}, u32[]{:S(2)}) collective-permute-start(bf16[2,48,8,768]{3,2,1,0:T(8,128)(2,1)S(1)} %get-tuple-element.298), channel_id=1, source_target_pairs={{0,1},{1,0},{2,3},{3,2},{4,5},{5,4},{6,7},{7,6},{8,9},{9,8},{10,11... | collective-permute-start | bytes 3538952 | tf_op jit(solution)/shard_map/ppermute | solution.py:63
  253.9 29.3 %collective-permute-start.26 = (bf16[2,2,24,8,768]{4,3,2,1,0:T(8,128)(2,1)S(1)}, bf16[2,2,24,8,768]{4,3,2,1,0:T(8,128)(2,1)S(1)}, u32[]{:S(2)}, u32[]{:S(2)}) collective-permute-start(bf16[2,2,24,8,768]{4,3,2,1,0:T(8,128)(2,1)S(1)} %get-tuple-element.319), channel_id=1, source_target_pairs={{0,4},{4,0},{1,5},{5,1},{2,6},{6,2},{3,7},{7,3},{8,12},{12,8},{9,1... | collective-permute-start | bytes 3538952 | tf_op jit(solution)/shard_map/ppermute | solution.py:63
  254.0 29.2 %collective-permute-start.24 = (bf16[48,8,768]{2,1,0:T(8,128)(2,1)S(1)}, bf16[48,8,768]{2,1,0:T(8,128)(2,1)S(1)}, u32[]{:S(2)}, u32[]{:S(2)}) collective-permute-start(bf16[48,8,768]{2,1,0:T(8,128)(2,1)S(1)} %get-tuple-element.315), channel_id=1, source_target_pairs={{0,1},{1,0},{2,3},{3,2},{4,5},{5,4},{6,7},{7,6},{8,9},{9,8},{10,11... | collective-permute-start | bytes 1769480 | tf_op jit(solution)/shard_map/ppermute | solution.py:63
  255.4 27.7 %collective-permute-start.25 = (bf16[48,8,768]{2,1,0:T(8,128)(2,1)S(1)}, bf16[48,8,768]{2,1,0:T(8,128)(2,1)S(1)}, u32[]{:S(2)}, u32[]{:S(2)}) collective-permute-start(bf16[48,8,768]{2,1,0:T(8,128)(2,1)S(1)} %get-tuple-element.317), channel_id=1, source_target_pairs={{0,2},{2,0},{1,3},{3,1},{4,6},{6,4},{5,7},{7,5},{8,10},{10,8},{9,1... | collective-permute-start | bytes 1769480 | tf_op jit(solution)/shard_map/ppermute | solution.py:63
  256.1 27.1 %collective-permute-start.27 = (bf16[2,2,12,8,768]{4,3,2,1,0:T(8,128)(2,1)S(1)}, bf16[2,2,12,8,768]{4,3,2,1,0:T(8,128)(2,1)S(1)}, u32[]{:S(2)}, u32[]{:S(2)}) collective-permute-start(bf16[2,2,12,8,768]{4,3,2,1,0:T(8,128)(2,1)S(1)} %get-tuple-element.321), channel_id=1, source_target_pairs={{0,4},{4,0},{1,5},{5,1},{2,6},{6,2},{3,7},{7,3},{8,12},{12,8},{9,1... | collective-permute-start | bytes 1769480 | tf_op jit(solution)/shard_map/ppermute | solution.py:63
  256.1 27.1 %collective-permute-start.28 = (bf16[2,2,8,8,768]{4,3,2,1,0:T(8,128)(2,1)S(1)}, bf16[2,2,8,8,768]{4,3,2,1,0:T(8,128)(2,1)S(1)}, u32[]{:S(2)}, u32[]{:S(2)}) collective-permute-start(bf16[2,2,8,8,768]{4,3,2,1,0:T(8,128)(2,1)S(1)} %get-tuple-element.323), channel_id=1, source_target_pairs={{0,4},{4,0},{1,5},{5,1},{2,6},{6,2},{3,7},{7,3},{8,12},{12,8},{9,1... | collective-permute-start | bytes 1179656 | tf_op jit(solution)/shard_map/ppermute | solution.py:63
  285.5 19.6 %collective-permute-start.29 = (bf16[24,2,8,768]{3,2,0,1:T(8,128)(2,1)S(1)}, bf16[24,2,8,768]{3,2,0,1:T(8,128)(2,1)S(1)}, u32[]{:S(2)}, u32[]{:S(2)}) collective-permute-start(bf16[24,2,8,768]{3,2,0,1:T(8,128)(2,1)S(1)} %get-tuple-element.348), channel_id=1, source_target_pairs={{0,8},{8,0},{16,24},{24,16},{1,9},{9,1},{17,25},{25,17},{2,10},{10... | collective-permute-start | bytes 1769480 | tf_op jit(solution)/shard_map/ppermute | solution.py:63
  285.5 19.5 %collective-permute-start.30 = (bf16[2,24,8,768]{3,2,1,0:T(8,128)(2,1)S(1)}, bf16[2,24,8,768]{3,2,1,0:T(8,128)(2,1)S(1)}, u32[]{:S(2)}, u32[]{:S(2)}) collective-permute-start(bf16[2,24,8,768]{3,2,1,0:T(8,128)(2,1)S(1)} %get-tuple-element.350), channel_id=1, source_target_pairs={{0,1},{1,0},{2,3},{3,2},{4,5},{5,4},{6,7},{7,6},{8,9},{9,8},{10,11... | collective-permute-start | bytes 1769480 | tf_op jit(solution)/shard_map/ppermute | solution.py:63
  286.3 18.8 %collective-permute-start.31 = (bf16[2,24,8,768]{3,2,1,0:T(8,128)(2,1)S(1)}, bf16[2,24,8,768]{3,2,1,0:T(8,128)(2,1)S(1)}, u32[]{:S(2)}, u32[]{:S(2)}) collective-permute-start(bf16[2,24,8,768]{3,2,1,0:T(8,128)(2,1)S(1)} %get-tuple-element.352), channel_id=1, source_target_pairs={{0,2},{2,0},{1,3},{3,1},{4,6},{6,4},{5,7},{7,5},{8,10},{10,8},{9,1... | collective-permute-start | bytes 1769480 | tf_op jit(solution)/shard_map/ppermute | solution.py:63
  287.7 17.4 %collective-permute-start.32 = (bf16[2,8,8,768]{3,2,1,0:T(8,128)(2,1)S(1)}, bf16[2,8,8,768]{3,2,1,0:T(8,128)(2,1)S(1)}, u32[]{:S(2)}, u32[]{:S(2)}) collective-permute-start(bf16[2,8,8,768]{3,2,1,0:T(8,128)(2,1)S(1)} %get-tuple-element.354), channel_id=1, source_target_pairs={{0,1},{1,0},{2,3},{3,2},{4,5},{5,4},{6,7},{7,6},{8,9},{9,8},{10,11... | collective-permute-start | bytes 589832 | tf_op jit(solution)/shard_map/ppermute | solution.py:63
  308.5 22.4 %collective-permute-start.41 = (bf16[24,8,768]{2,1,0:T(8,128)(2,1)S(1)}, bf16[24,8,768]{2,1,0:T(8,128)(2,1)S(1)}, u32[]{:S(2)}, u32[]{:S(2)}) collective-permute-start(bf16[24,8,768]{2,1,0:T(8,128)(2,1)S(1)} %get-tuple-element.465), channel_id=1, source_target_pairs={{0,16},{8,24},{16,0},{24,8},{1,17},{9,25},{17,1},{25,9},{2,18},{10... | collective-permute-start | bytes 884744 | tf_op jit(solution)/shard_map/ppermute | solution.py:63
  334.0 16.4 %collective-permute-start.47 = (bf16[12,8,768]{2,1,0:T(8,128)(2,1)}, bf16[12,8,768]{2,1,0:T(8,128)(2,1)}, u32[]{:S(2)}, u32[]{:S(2)}) collective-permute-start(bf16[12,8,768]{2,1,0:T(8,128)(2,1)} %get-tuple-element.406), channel_id=1, source_target_pairs={{0,16},{8,24},{16,0},{24,8},{1,17},{9,25},{17,1},{25,9},{2,18},{10... | collective-permute-start | bytes 442376 | tf_op jit(solution)/shard_map/ppermute | solution.py:63
  356.6 32.8 %all-to-all-start.1 = ((bf16[32,9,8,256]{3,2,1,0:T(8,128)(2,1)}), bf16[32,9,8,256]{3,2,1,0:T(8,128)(2,1)}, u32[]{:S(2)}, u32[]{:S(2)}) async-start(bf16[32,9,8,256]{3,2,1,0:T(8,128)(2,1)} %bitcast.151), calls=%async_computation.1 | async-start | bytes 2359296 | tf_op jit(solution)/shard_map/all_to_all | solution.py:1254
  360.4 25.9 %collective-permute-start.42 = (bf16[16,64,256]{2,1,0:T(8,128)(2,1)S(1)}, bf16[16,64,256]{2,1,0:T(8,128)(2,1)S(1)}, u32[]{:S(2)}, u32[]{:S(2)}) collective-permute-start(bf16[16,64,256]{2,1,0:T(8,128)(2,1)S(1)} %copy-done.30), channel_id=1, source_target_pairs={{0,1},{1,0},{2,3},{3,2},{4,5},{5,4},{6,7},{7,6},{8,9},{9,8},{10,11... | collective-permute-start | bytes 1572872 | tf_op jit(solution)/shard_map/ppermute | solution.py:63
  362.1 24.1 %collective-permute-start.43 = (bf16[16,64,256]{2,1,0:T(8,128)(2,1)S(1)}, bf16[16,64,256]{2,1,0:T(8,128)(2,1)S(1)}, u32[]{:S(2)}, u32[]{:S(2)}) collective-permute-start(bf16[16,64,256]{2,1,0:T(8,128)(2,1)S(1)} %copy-done.29), channel_id=1, source_target_pairs={{0,2},{1,3},{2,0},{3,1},{4,6},{5,7},{6,4},{7,5},{8,10},{9,11},{10,... | collective-permute-start | bytes 1572872 | tf_op jit(solution)/shard_map/ppermute | solution.py:63
  (65 other events, 496.6 us)
Sparse Core Ops, SparseCore 0:
  80.0 88.2 all-gather.1

commit v11 on v10

--- a/solution.py
+++ b/solution.py
@@ -357,8 +357,35 @@
     )
 
 
+def cross_probs_kernel(q_ref, k_ref, l_ref, p_ref):
+    q = q_ref[...].astype(f32) * 0.125
+    for head in range(TH):
+        q_head = jnp.where(head_mask(q.shape, head), q, 0.0).astype(bf16)
+        scores = dot_nt(k_ref[...], q_head)
+        p_ref[head] = jnp.exp(scores - l_ref[head : head + 1, :]).astype(bf16)
+
+
+def cross_probs(query, kv, log_rows):
+    rows = query.shape[0]
+    cells = kv.shape[0]
+    block = 512
+    return pl.pallas_call(
+        cross_probs_kernel,
+        grid=(cells // block,),
+        in_specs=[
+            pl.BlockSpec((rows, CH), lambda i: (0, 0)),
+            pl.BlockSpec((block, CH), lambda i: (i, 0)),
+            pl.BlockSpec((8, rows), lambda i: (0, 0)),
+        ],
+        out_specs=pl.BlockSpec((TH, block, rows), lambda i: (0, i, 0)),
+        out_shape=lasting((TH, cells, rows), bf16),
+        compiler_params=params(),
+        cost_estimate=cost(2 * TH * rows * cells * CH, 2 * TH * rows * cells, TH * rows * cells),
+    )(query, stay(kv), log_rows)
+
+
 def cross_backward_kernel(
-    q_ref, k_ref, v_ref, do_ref, o_ref, l_ref, feats_ref, gupd_ref, query_w_ref,
+    q_ref, k_ref, v_ref, do_ref, o_ref, p_ref, feats_ref, gupd_ref, query_w_ref,
     dkv_ref, query_g_ref, future_ref, q_s, do_s, delta_s, dq_s,
 ):
     step = pl.program_id(0)
@@ -376,27 +403,26 @@
     cells = k_ref.shape[0]
     dk = jnp.zeros((cells, CH), f32)
     dv = jnp.zeros((cells, CH), f32)
-    dq = dq_s[...]
-    k = k_ref[...]
+    k_turned = k_ref[...].T
     for head in range(TH):
-        probs = jnp.exp(dot_nt(k, q_s[head]) - l_ref[head : head + 1, :])
+        probs = p_ref[head]
         d_probs = dot_nt(v_ref[...], do_s[head])
-        d_scores = (probs * (d_probs - delta_s[head : head + 1, :])).astype(bf16)
-        dv = dv + dot_nn(probs.astype(bf16), do_s[head])
+        d_scores = (probs.astype(f32) * (d_probs - delta_s[head : head + 1, :])).astype(bf16)
+        dv = dv + dot_nn(probs, do_s[head])
         dk = dk + dot_nn(d_scores, q_s[head])
-        dq = dq + jnp.where(head_mask((rows, CH), head), dot_tn(d_scores, k), 0.0)
-    dq_s[...] = dq
+        here = slice(head * HD, (head + 1) * HD)
+        dq_s[here, :] += dot_nn(k_turned[here, :], d_scores)
     dkv_ref[:, :CH] = dk.astype(bf16)
     dkv_ref[:, CH:] = dv.astype(bf16)
 
     @pl.when(step == pl.num_programs(0) - 1)
     def _():
-        gq = (dq_s[...] * 0.125).astype(bf16)
+        gq = (dq_s[...].T * 0.125).astype(bf16)
         query_g_ref[...] = dot_tn(feats_ref[...], gq).astype(bf16)
         future_ref[...] = gupd_ref[...] + dot_nt(gq, query_w_ref[...])
 
 
-def cross_backward(query, kv, d_out, out, log_rows, feats, gupd, to_query):
+def cross_backward(query, kv, d_out, out, probs, feats, gupd, to_query):
     rows = query.shape[0]
     cells = kv.shape[0]
     block = 1024
@@ -410,7 +436,7 @@
             pl.BlockSpec((block, CH), lambda i: (i, 1)),
             pl.BlockSpec((rows, CH), whole),
             pl.BlockSpec((rows, CH), whole),
-            pl.BlockSpec((8, rows), whole),
+            pl.BlockSpec((TH, block, rows), lambda i: (0, i, 0)),
             pl.BlockSpec((rows, CH), whole),
             pl.BlockSpec((rows, CH), whole),
             pl.BlockSpec((CH, CH), whole),
@@ -429,11 +455,11 @@
             pltpu.VMEM((TH, rows, CH), bf16),
             pltpu.VMEM((TH, rows, CH), bf16),
             pltpu.VMEM((8, rows), f32),
-            pltpu.VMEM((rows, CH), f32),
-        ],
-        compiler_params=params(),
+            pltpu.VMEM((CH, rows), f32),
+        ],
+        compiler_params=pltpu.CompilerParams(vmem_limit_bytes=MLP_BYTES),
         cost_estimate=cost(10 * TH * rows * cells * CH, 8 * cells * CH, TH * rows * cells),
-    )(query, kv, kv, d_out, out, log_rows, feats, gupd, to_query)
+    )(query, kv, kv, d_out, out, stay(probs), feats, gupd, to_query)
 
 
 def self_forward_kernel(len_ref, q_ref, k_ref, v_ref, o_ref, l_ref):
@@ -492,6 +518,7 @@
     dk_s[...] = jnp.zeros_like(dk_s)
     dv_s[...] = jnp.zeros_like(dv_s)
     delta = delta_rows(do_ref[...], o_ref[...])
+    k_turned = k_ref[0].T
     for start, count in ROW_BLOCKS:
         stop = start + count
         q = q_ref[0, start:stop, :].astype(f32) * 0.125
@@ -499,7 +526,7 @@
         row = lax.broadcasted_iota(jnp.int32, (1, count), 1) + start
         bound = jnp.minimum(row, length - 1)
         allowed = lax.broadcasted_iota(jnp.int32, (stop, count), 0) <= bound
-        dq = jnp.zeros((count, CH), f32)
+        dq = []
         k = k_ref[0, :stop, :]
         v = v_ref[0, :stop, :]
         dk = dk_s[:stop, :]
@@ -515,10 +542,10 @@
             d_scores = (probs * (d_probs - delta[head : head + 1, start:stop])).astype(bf16)
             dv = dv + dot_nn(probs.astype(bf16), d_head)
             dk = dk + dot_nn(d_scores, q_head)
-            dq = dq + jnp.where(mask, dot_tn(d_scores, k), 0.0)
+            dq.append(dot_nn(k_turned[head * HD : (head + 1) * HD, :stop], d_scores))
         dk_s[:stop, :] = dk
         dv_s[:stop, :] = dv
-        out_ref[0, start:stop, :] = (dq * 0.125).astype(bf16)
+        out_ref[0, start:stop, :] = (jnp.concatenate(dq, 0).T * 0.125).astype(bf16)
     out_ref[1] = dk_s[...].astype(bf16)
     out_ref[2] = dv_s[...].astype(bf16)
 
@@ -1155,6 +1182,9 @@
         pooled, feats_b, cross_mixed, to_out, weights, gain_one
     )
     mixed, logs = self_forward(qkv, length)
+    mixed, log_rows = tie((mixed, cross_logs[0]))
+    probs = cross_probs(query, kv, log_rows)
+    mixed, probs = tie((mixed, probs))
     (
         block_out, d_stream, gog, up_keep, up_give, down_keep, down_give, att_keep, att_give,
         gain_g_two,
@@ -1184,9 +1214,8 @@
     up, down, emb = send(up, "x"), send(down, "y"), send(emb, "c")
     first, second = send(first, "c"), send(second, "c")
 
-    log_rows = cross_logs[0]
     gkv, query_g, future_grad = cross_backward(
-        query, kv, gox, cross_mixed, log_rows, feats_b, gupd, to_query
+        query, kv, gox, cross_mixed, probs, feats_b, gupd, to_query
     )
     gkv, up, down, first, second, emb = hold((gkv,), up, down, first, second, emb)
     mlp = advance_near([split_z(jnp.concatenate(part, 0)) for part in zip(up, down)])

time: 414 us -> 411 us (level)
  waiting for transfers between devices: 92.2 us -> 83.9 us
    pallas_call x0 -> x1, Pallas kernels: none -> 10.4 us  [cross_probs(): pl.pallas_call(cross_probs_kernel, grid=(cells // block,), in_specs=[pl.B...]
    all_gather x1, waiting for transfers between devices: 9.65 us -> 0.63 us  [local(): mlp = lax.all_gather(mlp, AXES, axis=1, tiled=True)]
    pallas_call x1, Pallas kernels: 26.6 us -> 21.7 us  [cross_backward(): pl.pallas_call(cross_backward_kernel, grid=(cells // block,), in_specs=[p...]
    unnamed x81 -> x75, local copies, waits for them, and re-layouts: 9.46 us -> 9.51 us
  transfers between devices with their start and end apart: 52 -> 52, of which waited for: 20 -> 19; matrix products, arithmetic and copies ran while one was open for 8% -> 8% of each run, Pallas kernels for 33% -> 35%
where the time goes in v11:
time: 411 us; the launch traced here: 404 us
  Pallas kernels  174 us (42%)
  waiting for transfers between devices  83.9 us (20%)
  starting transfers between devices  64.5 us (16%)
  other arithmetic  33.5 us (8%)
  local copies, waits for them, and re-layouts  27.7 us (7%)
  between operations  20.1 us (5%)
    ppermute x49, waiting for transfers between devices, xor_permute(): return lax.ppermute(values, axes, [(i, i ^ mask) for i in range(count)])  66.9 us
    ppermute x49, starting transfers between devices, xor_permute(): return lax.ppermute(values, axes, [(i, i ^ mask) for i in range(count)])  52.9 us
    pallas_call x1, Pallas kernels, mlp_block(): pl.pallas_call(functools.partial(mlp_kernel, sizes=slice_shape()), grid=(...  34.3 us
    pallas_call x1, Pallas kernels, cross_backward(): pl.pallas_call(cross_backward_kernel, grid=(cells // block,), in_specs=[p...  21.7 us
    pallas_call x1, Pallas kernels, embed_grad(): pl.pallas_call(functools.partial(embed_grad_kernel, sizes=slice_shape()),...  18.4 us
    all_to_all x1, waiting for transfers between devices, local(): lax.all_to_all(slices, AXES, split_axis=0, concat_axis=0, tiled=True)  15.8 us
    pallas_call x1, Pallas kernels, token_forward(): pl.pallas_call(token_forward_kernel, grid=(steps,), in_specs=[pl.BlockSpe...  15.3 us
    pallas_call x1, Pallas kernels, token_backward(): pl.pallas_call(functools.partial(token_backward_kernel, sizes=slice_shape...  14.4 us
  transfers between devices with their start and end apart: 52, of which 19 were waited for; matrix products, arithmetic and copies ran while one was open for 8% of the time, Pallas kernels for 35%

profile of v11, /device:TPU:0, one launch (start us, length us, event | category | flops | bytes accessed | tf_op | source)
XLA Modules:
  0.0 404.4 jit_solution(12384640787492179734)
XLA Ops:
  10.0 7.3 %all-to-all-start = ((bf16[32,8,8,256]{3,2,1,0:T(8,128)(2,1)}), bf16[32,8,8,256]{3,2,1,0:T(8,128)(2,1)S(1)}, u32[]{:S(2)}, u32[]{:S(2)}) async-start(bf16[32,8,8,256]{3,2,1,0:T(8,128)(2,1)} %copy.146), calls=%async_computation | async-start | bytes 2097152 | tf_op jit(solution)/shard_map/all_to_all | solution.py:1130
  28.0 15.8 %all-to-all-done = bf16[32,8,8,256]{3,2,1,0:T(8,128)(2,1)S(1)} async-done(((bf16[32,8,8,256]{3,2,1,0:T(8,128)(2,1)}), bf16[32,8,8,256]{3,2,1,0:T(8,128)(2,1)S(1)}, u32[]{:S(2)}, u32[]{:S(2)}) %all-to-all-start) | async-done | bytes 1048608 | tf_op jit(solution)/shard_map/all_to_all | solution.py:1130
  61.2 4.1 %shard_map.186.x_ref = bf16[4224,768]{1,0:T(8,128)(2,1)} custom-call(s32[1]{0:T(128)} %bitcast.1.row_ref, bf16[1024,256]{1,0:T(8,128)(2,1)S(1)} %bitcast.300, bf16[1024,256]{1,0:T(8,128)(2,1)S(1)} %bitcast.307, bf16[1024,256]{1,0:T(8,128)(2,1)S(1)} %bitcast.308, bf16[1024,256]{1,0:T(8,128)(2,1)S(1)} %bitcast.309), custom_call_target="tpu_custom_call" | custom-call | bytes 8388608 | tf_op jit(solution)/shard_map/pallas_call | solution.py:233
  65.4 5.0 %collective-permute-done.7 = bf16[13,8,768]{2,1,0:T(8,128)(2,1)S(1)} collective-permute-done((bf16[13,8,768]{2,1,0:T(8,128)(2,1)S(1)}, bf16[13,8,768]{2,1,0:T(8,128)(2,1)S(1)}, u32[]{:S(2)}, u32[]{:S(2)}) %collective-permute-start.7) | collective-permute-done | bytes 159776 | tf_op jit(solution)/shard_map/ppermute | solution.py:63
  74.4 5.5 %collective-permute-done.9 = bf16[6,4,8,768]{3,2,1,0:T(8,128)(2,1)S(1)} collective-permute-done((bf16[6,4,8,768]{3,2,1,0:T(8,128)(2,1)S(1)}, bf16[6,4,8,768]{3,2,1,0:T(8,128)(2,1)S(1)}, u32[]{:S(2)}, u32[]{:S(2)}) %collective-permute-start.9) | collective-permute-done | bytes 294944 | tf_op jit(solution)/shard_map/ppermute | solution.py:63
  98.2 15.3 %shard_map.187 = (bf16[4096,256]{1,0:T(8,128)(2,1)}, bf16[4096,256]{1,0:T(8,128)(2,1)}, bf16[4096,512]{1,0:T(8,128)(2,1)S(1)}, bf16[256,256]{1,0:T(8,128)(2,1)S(1)}) custom-call(bf16[4224,768]{1,0:T(8,128)(2,1)} %shard_map.186.x_ref, bf16[3,768,256]{2,1,0:T(8,128)(2,1)S(1)} %bitcast.303, bf16[256,512]{1,0:T(8,128)(2,1)S(1)} %pad_maximum_fusion.11.kv_w_ref), custom_call_target="tpu_custom_call" | custom-call | flops 5905580032 | bytes 14680064 | tf_op jit(solution)/shard_map/pallas_call | solution.py:959
  117.2 12.0 %shard_map.188 = (bf16[480,256]{1,0:T(8,128)(2,1)S(1)}, f32[1,8,480]{2,1,0:T(8,128)S(1)}) custom-call(bf16[480,256]{1,0:T(8,128)(2,1)S(1)} %fusion.2.q_ref, bf16[4096,512]{1,0:T(8,128)(2,1)S(1)} %get-tuple-element.251.k_ref.v_ref, bf16[4096,512]{1,0:T(8,128)(2,1)S(1)} %get-tuple-element.251.k_ref.v_ref), custom_call_target="tpu_custom_call" | custom-call | flops 16106127360 | bytes 8388608 | tf_op jit(solution)/shard_map/pallas_call | solution.py:325
  134.1 7.7 %shard_map.190 = (bf16[736,256]{1,0:T(8,128)(2,1)}, f32[736,768]{1,0:T(8,128)}, bf16[736,768]{1,0:T(8,128)(2,1)}, bf16[3,736,768]{2,1,0:T(8,128)(2,1)}) custom-call(bf16[256,256]{1,0:T(8,128)(2,1)S(1)} %get-tuple-element.242.pool_ref, bf16[480,256]{1,0:T(8,128)(2,1)S(1)} %bitcast.304, bf16[480,256]{1,0:T(8,128)(2,1)S(1)} %get-tuple-element.255.mixed_ref.o_ref, ...), custom_call_target="tpu_custom_call" | custom-call | flops 2894069760 | bytes 6782976 | tf_op jit(solution)/shard_map/pallas_call | solution.py:679
  143.7 12.0 %shard_map.191 = (bf16[736,768]{1,0:T(8,128)(2,1)}, f32[3,8,736]{2,1,0:T(8,128)S(1)}) custom-call(s32[1]{0:T(128)} %add.398.len_ref, bf16[3,736,768]{2,1,0:T(8,128)(2,1)S(1)} %copy-done.16, bf16[3,736,768]{2,1,0:T(8,128)(2,1)S(1)} %copy-done.16, bf16[3,736,768]{2,1,0:T(8,128)(2,1)S(1)} %copy-done.16), custom_call_target="tpu_custom_call" | custom-call | flops 6656360448 | bytes 4521984 | tf_op jit(solution)/shard_map/pallas_call | solution.py:494
  156.3 10.4 %shard_map.192.p_ref = bf16[4,4096,480]{2,1,0:T(8,128)(2,1)} custom-call(bf16[480,256]{1,0:T(8,128)(2,1)S(1)} %fusion.2.q_ref, bf16[4096,512]{1,0:T(8,128)(2,1)} %copy-done.1, f32[8,480]{1,0:T(8,128)S(1)} %bitcast.313), custom_call_target="tpu_custom_call" | custom-call | flops 4026531840 | bytes 15728640 | tf_op jit(solution)/shard_map/pallas_call | solution.py:372
  167.3 34.3 %shard_map.193 = (f32[736,768]{1,0:T(8,128)}, f32[736,768]{1,0:T(8,128)}, bf16[736,768]{1,0:T(8,128)(2,1)}, bf16[2,2,48,8,768]{4,3,2,1,0:T(8,128)(2,1)S(1)}, bf1...) custom-call(s32[1]{0:T(128)} %bitcast.core_ref, ...), custom_call_target="tpu_custom_call" | custom-call | flops 23441965056 | bytes 33914880 | tf_op jit(solution)/shard_map/pallas_call | solution.py:762
  204.7 12.3 %shard_map.194.g_ref = bf16[3,736,512]{2,1,0:T(8,128)(2,1)S(1)} custom-call(s32[1]{0:T(128)} %add.398.len_ref, bf16[3,736,768]{2,1,0:T(8,128)(2,1)} %get-tuple-element.260.q_ref.k_ref.v_ref, bf16[3,736,768]{2,1,0:T(8,128)(2,1)} %get-tuple-element.260.q_ref.k_ref.v_ref, bf16[3,736,768]{2,1,0:T(8,128)(2,1)} %get-tuple-element.260.q_ref.k_ref.v_ref, ...), custom_call_target="tpu_custom_call" | custom-call | flops 8875147264 | bytes 9043968 | tf_op jit(solution)/shard_map/pallas_call | solution.py:557
  224.8 18.4 %shard_map.195 = (bf16[2,2,24,8,768]{4,3,2,1,0:T(8,128)(2,1)S(1)}, bf16[2,2,24,8,768]{4,3,2,1,0:T(8,128)(2,1)S(1)}, bf16[2,2,12,8,768]{4,3,2,1,0:T(8,128)(2,1)S(...) custom-call(s32[1]{0:T(128)} %bitcast.core_ref, ...), custom_call_target="tpu_custom_call" | custom-call | flops 10225713152 | bytes 28262400 | tf_op jit(solution)/shard_map/pallas_call | solution.py:867
  243.2 6.8 %collective-permute-done.22 = bf16[2,48,8,768]{3,2,1,0:T(8,128)(2,1)S(1)} collective-permute-done((bf16[2,48,8,768]{3,2,1,0:T(8,128)(2,1)S(1)}, bf16[2,48,8,768]{3,2,1,0:T(8,128)(2,1)S(1)}, u32[]{:S(2)}, u32[]{:S(2)}) %collective-permute-start.22) | collective-permute-done | bytes 1179680 | tf_op jit(solution)/shard_map/ppermute | solution.py:63
  254.7 21.7 %shard_map.196 = (bf16[4096,512]{1,0:T(8,128)(2,1)S(1)}, bf16[256,256]{1,0:T(8,128)(2,1)S(1)}, f32[480,256]{1,0:T(8,128)}) custom-call(bf16[480,256]{1,0:T(8,128)(2,1)S(1)} %copy-done.8, bf16[4096,512]{1,0:T(8,128)(2,1)S(1)} %copy-done.2, bf16[4096,512]{1,0:T(8,128)(2,1)S(1)} %copy-done.2, bf16[480,256]{1,0:T(8,128)(2,1)S(1)} %get-tuple-element.318.do_ref, ...), custom_call_target="tpu_custom_call" | custom-call | flops 20132659200 | bytes 8388608 | tf_op jit(solution)/shard_map/pallas_call | solution.py:430
  278.7 3.0 collective-permute-start.29
  284.6 14.4 %shard_map.197 = (f32[4096,256]{1,0:T(8,128)S(1)}, bf16[4096,256]{1,0:T(8,128)(2,1)S(1)}, bf16[2,2,52,8,256]{4,3,2,1,0:T(8,128)(2,1)S(1)}, bf16[2,2,52,8,256]{4,3,2,1,0:T(8,128)(2,1)S(1)}) custom-call(s32[1]{0:T(128)} %bitcast.core_ref, bf16[4096,512]{1,0:T(8,128)(2,1)S(1)} %get-tuple-element.345.dkv_ref, bf16[4096,256]{1,0:T(8,128)(2,1)} %get-tuple-element.346.slope_ref, ...), custom_call_target="tpu_custom_call" | custom-call | flops 6979321856 | bytes 20971520 | tf_op jit(solution)/shard_map/pallas_call | solution.py:1021
  306.6 3.1 collective-permute-done.35
  309.7 3.9 collective-permute-done.34
  318.0 8.0 %shard_map.198 = bf16[4096,256]{1,0:T(8,128)(2,1)S(1)} custom-call(bf16[4096,256]{1,0:T(8,128)(2,1)S(1)} %get-tuple-element.389.gz_ref, f32[4096,256]{1,0:T(8,128)S(1)} %get-tuple-element.390.d_hidden_ref, bf16[9,256,256]{2,1,0:T(8,128)(2,1)S(1)} %get-tuple-element.452.conv_ref), custom_call_target="tpu_custom_call" | custom-call | flops 4831838208 | bytes 8388608 | tf_op jit(solution)/shard_map/pallas_call | solution.py:1087
  340.3 4.9 %collective-permute-done.45 = bf16[19,8,256]{2,1,0:T(8,128)(2,1)} collective-permute-done((bf16[19,8,256]{2,1,0:T(8,128)(2,1)}, bf16[19,8,256]{2,1,0:T(8,128)(2,1)}, u32[]{:S(2)}, u32[]{:S(2)}) %collective-permute-start.45) | collective-permute-done | bytes 77856 | tf_op jit(solution)/shard_map/ppermute | solution.py:63
  353.0 4.3 %all-to-all-start.1 = ((bf16[32,9,8,256]{3,2,1,0:T(8,128)(2,1)}), bf16[32,9,8,256]{3,2,1,0:T(8,128)(2,1)}, u32[]{:S(2)}, u32[]{:S(2)}) async-start(bf16[32,9,8,256]{3,2,1,0:T(8,128)(2,1)} %bitcast.151), calls=%async_computation.1 | async-start | bytes 2359296 | tf_op jit(solution)/shard_map/all_to_all | solution.py:1283
  360.6 22.6 %collective-permute-done.42 = bf16[16,64,256]{2,1,0:T(8,128)(2,1)S(1)} collective-permute-done((bf16[16,64,256]{2,1,0:T(8,128)(2,1)S(1)}, bf16[16,64,256]{2,1,0:T(8,128)(2,1)S(1)}, u32[]{:S(2)}, u32[]{:S(2)}) %collective-permute-start.42) | collective-permute-done | bytes 524320 | tf_op jit(solution)/shard_map/ppermute | solution.py:63
  389.4 6.5 %subtract_select_fusion = (f32[8,256,256]{2,1,0:T(8,128)}, f32[8,256,256]{2,1,0:T(8,128)}, f32[8,256,256]{2,1,0:T(8,128)}) fusion(f32[8,256,256]{2,1,0:T(8,128)S(1)} %copy-done.21, pred[8]{0:T(512)(128)(4,1)S(1)} %broadcast_compare_fusion, f32[8,256,256]{2,1,0:T(8,128)} %param.21, f32[8,256,256]{2,1,0:T(8,128)} %param.22, ...), kind=kLoop, calls=%fused_computation.14 | loop fusion | flops 10485760 | bytes 13631500 | tf_op jit(solution)/shard_map/jit(_where)/select_n | solution.py:1304
  (277 shorter events, 125.0 us)
Async XLA Ops:
  10.0 33.7 %all-to-all-start = ((bf16[32,8,8,256]{3,2,1,0:T(8,128)(2,1)}), bf16[32,8,8,256]{3,2,1,0:T(8,128)(2,1)S(1)}, u32[]{:S(2)}, u32[]{:S(2)}) async-start(bf16[32,8,8,256]{3,2,1,0:T(8,128)(2,1)} %copy.146), calls=%async_computation | async-start | bytes 2097152 | tf_op jit(solution)/shard_map/all_to_all | solution.py:1130
  17.3 150.0 %all-gather.2.cloned.1.call-start = ((), (), s32[]{:S(2)}) async-start(), calls=%async_computation.2 | async-start | bytes 9732096 | tf_op jit(solution)/shard_map/all_gather | solution.py:1163
  20.1 39.4 %collective-permute-start = (bf16[16,64,256]{2,1,0:T(8,128)(2,1)}, bf16[16,64,256]{2,1,0:T(8,128)(2,1)S(1)}, u32[]{:S(2)}, u32[]{:S(2)}) collective-permute-start(bf16[16,64,256]{2,1,0:T(8,128)(2,1)} %get-tuple-element.441), channel_id=1, source_target_pairs={{0,1},{1,0},{2,3},{3,2},{4,5},{5,4},{6,7},{7,6},{8,9},{9,8},{10,11... | collective-permute-start | bytes 1572872 | tf_op jit(solution)/shard_map/ppermute | solution.py:63
  21.9 39.3 %collective-permute-start.1 = (bf16[16,64,256]{2,1,0:T(8,128)(2,1)}, bf16[16,64,256]{2,1,0:T(8,128)(2,1)S(1)}, u32[]{:S(2)}, u32[]{:S(2)}) collective-permute-start(bf16[16,64,256]{2,1,0:T(8,128)(2,1)} %get-tuple-element.443), channel_id=1, source_target_pairs={{0,2},{1,3},{2,0},{3,1},{4,6},{5,7},{6,4},{7,5},{8,10},{9,11},{10,... | collective-permute-start | bytes 1572872 | tf_op jit(solution)/shard_map/ppermute | solution.py:63
  23.3 37.8 %collective-permute-start.2 = (bf16[16,64,256]{2,1,0:T(8,128)(2,1)}, bf16[16,64,256]{2,1,0:T(8,128)(2,1)S(1)}, u32[]{:S(2)}, u32[]{:S(2)}) collective-permute-start(bf16[16,64,256]{2,1,0:T(8,128)(2,1)} %get-tuple-element.440), channel_id=1, source_target_pairs={{0,3},{1,2},{2,1},{3,0},{4,7},{5,6},{6,5},{7,4},{8,11},{9,10},{10,... | collective-permute-start | bytes 1572872 | tf_op jit(solution)/shard_map/ppermute | solution.py:63
  90.9 22.6 %collective-permute-start.16 = (bf16[7,2,4,8,768]{4,3,2,1,0:T(8,128)(2,1)}, bf16[7,2,4,8,768]{4,3,2,1,0:T(8,128)(2,1)}, u32[]{:S(2)}, u32[]{:S(2)}) collective-permute-start(bf16[7,2,4,8,768]{4,3,2,1,0:T(8,128)(2,1)} %pad_maximum_fusion.4), channel_id=1, source_target_pairs={{0,1},{1,0},{2,3},{3,2},{4,5},{5,4},{6,7},{7,6},{8,9},{9,8},{10,11... | collective-permute-start | bytes 2064392 | tf_op jit(solution)/shard_map/ppermute | solution.py:63
  91.6 21.9 %collective-permute-start.15 = (bf16[6,2,4,8,768]{4,3,2,0,1:T(8,128)(2,1)S(1)}, bf16[6,2,4,8,768]{4,3,2,0,1:T(8,128)(2,1)}, u32[]{:S(2)}, u32[]{:S(2)}) collective-permute-start(bf16[6,2,4,8,768]{4,3,2,0,1:T(8,128)(2,1)S(1)} %pad_maximum_fusion.5), channel_id=1, source_target_pairs={{0,2},{2,0},{1,3},{3,1},{4,6},{6,4},{5,7},{7,5},{8,10},{10,8},{9,1... | collective-permute-start | bytes 1769480 | tf_op jit(solution)/shard_map/ppermute | solution.py:63
  221.9 28.2 %collective-permute-start.22 = (bf16[2,48,8,768]{3,2,1,0:T(8,128)(2,1)S(1)}, bf16[2,48,8,768]{3,2,1,0:T(8,128)(2,1)S(1)}, u32[]{:S(2)}, u32[]{:S(2)}) collective-permute-start(bf16[2,48,8,768]{3,2,1,0:T(8,128)(2,1)S(1)} %get-tuple-element.304), channel_id=1, source_target_pairs={{0,2},{2,0},{1,3},{3,1},{4,6},{6,4},{5,7},{7,5},{8,10},{10,8},{9,1... | collective-permute-start | bytes 3538952 | tf_op jit(solution)/shard_map/ppermute | solution.py:63
  223.4 27.8 %collective-permute-start.23 = (bf16[2,48,8,768]{3,2,1,0:T(8,128)(2,1)S(1)}, bf16[2,48,8,768]{3,2,1,0:T(8,128)(2,1)S(1)}, u32[]{:S(2)}, u32[]{:S(2)}) collective-permute-start(bf16[2,48,8,768]{3,2,1,0:T(8,128)(2,1)S(1)} %get-tuple-element.306), channel_id=1, source_target_pairs={{0,1},{1,0},{2,3},{3,2},{4,5},{5,4},{6,7},{7,6},{8,9},{9,8},{10,11... | collective-permute-start | bytes 3538952 | tf_op jit(solution)/shard_map/ppermute | solution.py:63
  252.0 24.4 %collective-permute-start.26 = (bf16[2,2,24,8,768]{4,3,2,1,0:T(8,128)(2,1)S(1)}, bf16[2,2,24,8,768]{4,3,2,1,0:T(8,128)(2,1)S(1)}, u32[]{:S(2)}, u32[]{:S(2)}) collective-permute-start(bf16[2,2,24,8,768]{4,3,2,1,0:T(8,128)(2,1)S(1)} %get-tuple-element.327), channel_id=1, source_target_pairs={{0,4},{4,0},{1,5},{5,1},{2,6},{6,2},{3,7},{7,3},{8,12},{12,8},{9,1... | collective-permute-start | bytes 3538952 | tf_op jit(solution)/shard_map/ppermute | solution.py:63
  252.1 24.3 %collective-permute-start.24 = (bf16[48,8,768]{2,1,0:T(8,128)(2,1)S(1)}, bf16[48,8,768]{2,1,0:T(8,128)(2,1)S(1)}, u32[]{:S(2)}, u32[]{:S(2)}) collective-permute-start(bf16[48,8,768]{2,1,0:T(8,128)(2,1)S(1)} %get-tuple-element.323), channel_id=1, source_target_pairs={{0,1},{1,0},{2,3},{3,2},{4,5},{5,4},{6,7},{7,6},{8,9},{9,8},{10,11... | collective-permute-start | bytes 1769480 | tf_op jit(solution)/shard_map/ppermute | solution.py:63
  253.5 22.9 %collective-permute-start.25 = (bf16[48,8,768]{2,1,0:T(8,128)(2,1)S(1)}, bf16[48,8,768]{2,1,0:T(8,128)(2,1)S(1)}, u32[]{:S(2)}, u32[]{:S(2)}) collective-permute-start(bf16[48,8,768]{2,1,0:T(8,128)(2,1)S(1)} %get-tuple-element.325), channel_id=1, source_target_pairs={{0,2},{2,0},{1,3},{3,1},{4,6},{6,4},{5,7},{7,5},{8,10},{10,8},{9,1... | collective-permute-start | bytes 1769480 | tf_op jit(solution)/shard_map/ppermute | solution.py:63
  254.2 22.3 %collective-permute-start.27 = (bf16[2,2,12,8,768]{4,3,2,1,0:T(8,128)(2,1)S(1)}, bf16[2,2,12,8,768]{4,3,2,1,0:T(8,128)(2,1)S(1)}, u32[]{:S(2)}, u32[]{:S(2)}) collective-permute-start(bf16[2,2,12,8,768]{4,3,2,1,0:T(8,128)(2,1)S(1)} %get-tuple-element.329), channel_id=1, source_target_pairs={{0,4},{4,0},{1,5},{5,1},{2,6},{6,2},{3,7},{7,3},{8,12},{12,8},{9,1... | collective-permute-start | bytes 1769480 | tf_op jit(solution)/shard_map/ppermute | solution.py:63
  254.2 22.3 %collective-permute-start.28 = (bf16[2,2,8,8,768]{4,3,2,1,0:T(8,128)(2,1)S(1)}, bf16[2,2,8,8,768]{4,3,2,1,0:T(8,128)(2,1)S(1)}, u32[]{:S(2)}, u32[]{:S(2)}) collective-permute-start(bf16[2,2,8,8,768]{4,3,2,1,0:T(8,128)(2,1)S(1)} %get-tuple-element.331), channel_id=1, source_target_pairs={{0,4},{4,0},{1,5},{5,1},{2,6},{6,2},{3,7},{7,3},{8,12},{12,8},{9,1... | collective-permute-start | bytes 1179656 | tf_op jit(solution)/shard_map/ppermute | solution.py:63
  278.7 22.2 %collective-permute-start.29 = (bf16[24,2,8,768]{3,2,0,1:T(8,128)(2,1)S(1)}, bf16[24,2,8,768]{3,2,0,1:T(8,128)(2,1)S(1)}, u32[]{:S(2)}, u32[]{:S(2)}) collective-permute-start(bf16[24,2,8,768]{3,2,0,1:T(8,128)(2,1)S(1)} %get-tuple-element.356), channel_id=1, source_target_pairs={{0,8},{8,0},{16,24},{24,16},{1,9},{9,1},{17,25},{25,17},{2,10},{10... | collective-permute-start | bytes 1769480 | tf_op jit(solution)/shard_map/ppermute | solution.py:63
  281.8 19.2 %collective-permute-start.30 = (bf16[2,24,8,768]{3,2,1,0:T(8,128)(2,1)S(1)}, bf16[2,24,8,768]{3,2,1,0:T(8,128)(2,1)S(1)}, u32[]{:S(2)}, u32[]{:S(2)}) collective-permute-start(bf16[2,24,8,768]{3,2,1,0:T(8,128)(2,1)S(1)} %get-tuple-element.358), channel_id=1, source_target_pairs={{0,1},{1,0},{2,3},{3,2},{4,5},{5,4},{6,7},{7,6},{8,9},{9,8},{10,11... | collective-permute-start | bytes 1769480 | tf_op jit(solution)/shard_map/ppermute | solution.py:63
  283.1 17.9 %collective-permute-start.31 = (bf16[2,24,8,768]{3,2,1,0:T(8,128)(2,1)S(1)}, bf16[2,24,8,768]{3,2,1,0:T(8,128)(2,1)S(1)}, u32[]{:S(2)}, u32[]{:S(2)}) collective-permute-start(bf16[2,24,8,768]{3,2,1,0:T(8,128)(2,1)S(1)} %get-tuple-element.360), channel_id=1, source_target_pairs={{0,2},{2,0},{1,3},{3,1},{4,6},{6,4},{5,7},{7,5},{8,10},{10,8},{9,1... | collective-permute-start | bytes 1769480 | tf_op jit(solution)/shard_map/ppermute | solution.py:63
  284.3 16.6 %collective-permute-start.32 = (bf16[2,8,8,768]{3,2,1,0:T(8,128)(2,1)S(1)}, bf16[2,8,8,768]{3,2,1,0:T(8,128)(2,1)S(1)}, u32[]{:S(2)}, u32[]{:S(2)}) collective-permute-start(bf16[2,8,8,768]{3,2,1,0:T(8,128)(2,1)S(1)} %get-tuple-element.362), channel_id=1, source_target_pairs={{0,1},{1,0},{2,3},{3,2},{4,5},{5,4},{6,7},{7,6},{8,9},{9,8},{10,11... | collective-permute-start | bytes 589832 | tf_op jit(solution)/shard_map/ppermute | solution.py:63
  305.2 20.9 %collective-permute-start.41 = (bf16[24,8,768]{2,1,0:T(8,128)(2,1)S(1)}, bf16[24,8,768]{2,1,0:T(8,128)(2,1)S(1)}, u32[]{:S(2)}, u32[]{:S(2)}) collective-permute-start(bf16[24,8,768]{2,1,0:T(8,128)(2,1)S(1)} %get-tuple-element.473), channel_id=1, source_target_pairs={{0,16},{8,24},{16,0},{24,8},{1,17},{9,25},{17,1},{25,9},{2,18},{10... | collective-permute-start | bytes 884744 | tf_op jit(solution)/shard_map/ppermute | solution.py:63
  330.1 16.7 %collective-permute-start.47 = (bf16[12,8,768]{2,1,0:T(8,128)(2,1)}, bf16[12,8,768]{2,1,0:T(8,128)(2,1)}, u32[]{:S(2)}, u32[]{:S(2)}) collective-permute-start(bf16[12,8,768]{2,1,0:T(8,128)(2,1)} %get-tuple-element.414), channel_id=1, source_target_pairs={{0,16},{8,24},{16,0},{24,8},{1,17},{9,25},{17,1},{25,9},{2,18},{10... | collective-permute-start | bytes 442376 | tf_op jit(solution)/shard_map/ppermute | solution.py:63
  339.0 14.1 %collective-permute-start.48 = (bf16[16,64,256]{2,1,0:T(8,128)(2,1)}, bf16[16,64,256]{2,1,0:T(8,128)(2,1)S(1)}, u32[]{:S(2)}, u32[]{:S(2)}) collective-permute-start(bf16[16,64,256]{2,1,0:T(8,128)(2,1)} %get-tuple-element.436), channel_id=1, source_target_pairs={{0,3},{1,2},{2,1},{3,0},{4,7},{5,6},{6,5},{7,4},{8,11},{9,10},{10,... | collective-permute-start | bytes 1572872 | tf_op jit(solution)/shard_map/ppermute | solution.py:63
  353.0 33.4 %all-to-all-start.1 = ((bf16[32,9,8,256]{3,2,1,0:T(8,128)(2,1)}), bf16[32,9,8,256]{3,2,1,0:T(8,128)(2,1)}, u32[]{:S(2)}, u32[]{:S(2)}) async-start(bf16[32,9,8,256]{3,2,1,0:T(8,128)(2,1)} %bitcast.151), calls=%async_computation.1 | async-start | bytes 2359296 | tf_op jit(solution)/shard_map/all_to_all | solution.py:1283
  357.3 25.9 %collective-permute-start.42 = (bf16[16,64,256]{2,1,0:T(8,128)(2,1)S(1)}, bf16[16,64,256]{2,1,0:T(8,128)(2,1)S(1)}, u32[]{:S(2)}, u32[]{:S(2)}) collective-permute-start(bf16[16,64,256]{2,1,0:T(8,128)(2,1)S(1)} %copy-done.27), channel_id=1, source_target_pairs={{0,1},{1,0},{2,3},{3,2},{4,5},{5,4},{6,7},{7,6},{8,9},{9,8},{10,11... | collective-permute-start | bytes 1572872 | tf_op jit(solution)/shard_map/ppermute | solution.py:63
  359.1 24.1 %collective-permute-start.43 = (bf16[16,64,256]{2,1,0:T(8,128)(2,1)S(1)}, bf16[16,64,256]{2,1,0:T(8,128)(2,1)S(1)}, u32[]{:S(2)}, u32[]{:S(2)}) collective-permute-start(bf16[16,64,256]{2,1,0:T(8,128)(2,1)S(1)} %copy-done.26), channel_id=1, source_target_pairs={{0,2},{1,3},{2,0},{3,1},{4,6},{5,7},{6,4},{7,5},{8,10},{9,11},{10,... | collective-permute-start | bytes 1572872 | tf_op jit(solution)/shard_map/ppermute | solution.py:63
  (62 other events, 528.6 us)
Sparse Core Ops, SparseCore 0:
  80.0 87.2 all-gather.1

commit v12 on v11

--- a/solution.py
+++ b/solution.py
@@ -313,7 +313,7 @@
         shifted = jnp.exp(scores - peak)
         total = jnp.sum(shifted, -1, keepdims=True)
         part = dot_nn(shifted.astype(bf16), v_ref[...])
-        mixed = jnp.where(mask, part / total, mixed)
+        mixed = jnp.where(mask, part * (1.0 / total), mixed)
         stat = jnp.where(lane == head, peak + jnp.log(total), stat)
     o_ref[...] = mixed.astype(bf16)
     l_ref[0] = stat.T[:8]
@@ -482,7 +482,7 @@
             shifted = jnp.exp(scores - peak)
             total = jnp.sum(shifted, -1, keepdims=True)
             part = dot_nn(shifted.astype(bf16), v_ref[0, :stop, :])
-            mixed = jnp.where(mask, part / total, mixed)
+            mixed = jnp.where(mask, part * (1.0 / total), mixed)
             stat = jnp.where(lane == head, peak + jnp.log(total), stat)
         o_ref[start:stop, :] = mixed.astype(bf16)
         l_ref[0, :, start:stop] = stat.T[:8]

time: 411 us -> 411 us (level)
  no operation moved by 1% of the time
where the time goes in v12:
time: 411 us; the launch traced here: 404 us
  Pallas kernels  174 us (42%)
  waiting for transfers between devices  83.9 us (20%)
  starting transfers between devices  64.5 us (16%)
  other arithmetic  33.5 us (8%)
  local copies, waits for them, and re-layouts  27.7 us (7%)
  between operations  20.1 us (5%)
    ppermute x49, waiting for transfers between devices, xor_permute(): return lax.ppermute(values, axes, [(i, i ^ mask) for i in range(count)])  66.9 us
    ppermute x49, starting transfers between devices, xor_permute(): return lax.ppermute(values, axes, [(i, i ^ mask) for i in range(count)])  52.9 us
    pallas_call x1, Pallas kernels, mlp_block(): pl.pallas_call(functools.partial(mlp_kernel, sizes=slice_shape()), grid=(...  34.3 us
    pallas_call x1, Pallas kernels, cross_backward(): pl.pallas_call(cross_backward_kernel, grid=(cells // block,), in_specs=[p...  21.7 us
    pallas_call x1, Pallas kernels, embed_grad(): pl.pallas_call(functools.partial(embed_grad_kernel, sizes=slice_shape()),...  18.4 us
    all_to_all x1, waiting for transfers between devices, local(): lax.all_to_all(slices, AXES, split_axis=0, concat_axis=0, tiled=True)  15.8 us
    pallas_call x1, Pallas kernels, token_forward(): pl.pallas_call(token_forward_kernel, grid=(steps,), in_specs=[pl.BlockSpe...  15.3 us
    pallas_call x1, Pallas kernels, token_backward(): pl.pallas_call(functools.partial(token_backward_kernel, sizes=slice_shape...  14.4 us
  transfers between devices with their start and end apart: 52, of which 19 were waited for; matrix products, arithmetic and copies ran while one was open for 8% of the time, Pallas kernels for 35%

profile of v12, /device:TPU:0, one launch (start us, length us, event | category | flops | bytes accessed | tf_op | source)
XLA Modules:
  0.0 404.4 jit_solution(12384640787492179734)
XLA Ops:
  10.0 7.3 %all-to-all-start = ((bf16[32,8,8,256]{3,2,1,0:T(8,128)(2,1)}), bf16[32,8,8,256]{3,2,1,0:T(8,128)(2,1)S(1)}, u32[]{:S(2)}, u32[]{:S(2)}) async-start(bf16[32,8,8,256]{3,2,1,0:T(8,128)(2,1)} %copy.146), calls=%async_computation | async-start | bytes 2097152 | tf_op jit(solution)/shard_map/all_to_all | solution.py:1130
  28.0 15.8 %all-to-all-done = bf16[32,8,8,256]{3,2,1,0:T(8,128)(2,1)S(1)} async-done(((bf16[32,8,8,256]{3,2,1,0:T(8,128)(2,1)}), bf16[32,8,8,256]{3,2,1,0:T(8,128)(2,1)S(1)}, u32[]{:S(2)}, u32[]{:S(2)}) %all-to-all-start) | async-done | bytes 1048608 | tf_op jit(solution)/shard_map/all_to_all | solution.py:1130
  61.2 4.1 %shard_map.186.x_ref = bf16[4224,768]{1,0:T(8,128)(2,1)} custom-call(s32[1]{0:T(128)} %bitcast.1.row_ref, bf16[1024,256]{1,0:T(8,128)(2,1)S(1)} %bitcast.300, bf16[1024,256]{1,0:T(8,128)(2,1)S(1)} %bitcast.307, bf16[1024,256]{1,0:T(8,128)(2,1)S(1)} %bitcast.308, bf16[1024,256]{1,0:T(8,128)(2,1)S(1)} %bitcast.309), custom_call_target="tpu_custom_call" | custom-call | bytes 8388608 | tf_op jit(solution)/shard_map/pallas_call | solution.py:233
  65.4 5.0 %collective-permute-done.7 = bf16[13,8,768]{2,1,0:T(8,128)(2,1)S(1)} collective-permute-done((bf16[13,8,768]{2,1,0:T(8,128)(2,1)S(1)}, bf16[13,8,768]{2,1,0:T(8,128)(2,1)S(1)}, u32[]{:S(2)}, u32[]{:S(2)}) %collective-permute-start.7) | collective-permute-done | bytes 159776 | tf_op jit(solution)/shard_map/ppermute | solution.py:63
  74.4 5.5 %collective-permute-done.9 = bf16[6,4,8,768]{3,2,1,0:T(8,128)(2,1)S(1)} collective-permute-done((bf16[6,4,8,768]{3,2,1,0:T(8,128)(2,1)S(1)}, bf16[6,4,8,768]{3,2,1,0:T(8,128)(2,1)S(1)}, u32[]{:S(2)}, u32[]{:S(2)}) %collective-permute-start.9) | collective-permute-done | bytes 294944 | tf_op jit(solution)/shard_map/ppermute | solution.py:63
  98.2 15.3 %shard_map.187 = (bf16[4096,256]{1,0:T(8,128)(2,1)}, bf16[4096,256]{1,0:T(8,128)(2,1)}, bf16[4096,512]{1,0:T(8,128)(2,1)S(1)}, bf16[256,256]{1,0:T(8,128)(2,1)S(1)}) custom-call(bf16[4224,768]{1,0:T(8,128)(2,1)} %shard_map.186.x_ref, bf16[3,768,256]{2,1,0:T(8,128)(2,1)S(1)} %bitcast.303, bf16[256,512]{1,0:T(8,128)(2,1)S(1)} %pad_maximum_fusion.11.kv_w_ref), custom_call_target="tpu_custom_call" | custom-call | flops 5905580032 | bytes 14680064 | tf_op jit(solution)/shard_map/pallas_call | solution.py:959
  117.2 12.0 %shard_map.188 = (bf16[480,256]{1,0:T(8,128)(2,1)S(1)}, f32[1,8,480]{2,1,0:T(8,128)S(1)}) custom-call(bf16[480,256]{1,0:T(8,128)(2,1)S(1)} %fusion.2.q_ref, bf16[4096,512]{1,0:T(8,128)(2,1)S(1)} %get-tuple-element.251.k_ref.v_ref, bf16[4096,512]{1,0:T(8,128)(2,1)S(1)} %get-tuple-element.251.k_ref.v_ref), custom_call_target="tpu_custom_call" | custom-call | flops 16106127360 | bytes 8388608 | tf_op jit(solution)/shard_map/pallas_call | solution.py:325
  134.1 7.7 %shard_map.190 = (bf16[736,256]{1,0:T(8,128)(2,1)}, f32[736,768]{1,0:T(8,128)}, bf16[736,768]{1,0:T(8,128)(2,1)}, bf16[3,736,768]{2,1,0:T(8,128)(2,1)}) custom-call(bf16[256,256]{1,0:T(8,128)(2,1)S(1)} %get-tuple-element.242.pool_ref, bf16[480,256]{1,0:T(8,128)(2,1)S(1)} %bitcast.304, bf16[480,256]{1,0:T(8,128)(2,1)S(1)} %get-tuple-element.255.mixed_ref.o_ref, ...), custom_call_target="tpu_custom_call" | custom-call | flops 2894069760 | bytes 6782976 | tf_op jit(solution)/shard_map/pallas_call | solution.py:679
  143.7 12.0 %shard_map.191 = (bf16[736,768]{1,0:T(8,128)(2,1)}, f32[3,8,736]{2,1,0:T(8,128)S(1)}) custom-call(s32[1]{0:T(128)} %add.398.len_ref, bf16[3,736,768]{2,1,0:T(8,128)(2,1)S(1)} %copy-done.16, bf16[3,736,768]{2,1,0:T(8,128)(2,1)S(1)} %copy-done.16, bf16[3,736,768]{2,1,0:T(8,128)(2,1)S(1)} %copy-done.16), custom_call_target="tpu_custom_call" | custom-call | flops 6656360448 | bytes 4521984 | tf_op jit(solution)/shard_map/pallas_call | solution.py:494
  156.3 10.4 %shard_map.192.p_ref = bf16[4,4096,480]{2,1,0:T(8,128)(2,1)} custom-call(bf16[480,256]{1,0:T(8,128)(2,1)S(1)} %fusion.2.q_ref, bf16[4096,512]{1,0:T(8,128)(2,1)} %copy-done.1, f32[8,480]{1,0:T(8,128)S(1)} %bitcast.313), custom_call_target="tpu_custom_call" | custom-call | flops 4026531840 | bytes 15728640 | tf_op jit(solution)/shard_map/pallas_call | solution.py:372
  167.3 34.3 %shard_map.193 = (f32[736,768]{1,0:T(8,128)}, f32[736,768]{1,0:T(8,128)}, bf16[736,768]{1,0:T(8,128)(2,1)}, bf16[2,2,48,8,768]{4,3,2,1,0:T(8,128)(2,1)S(1)}, bf1...) custom-call(s32[1]{0:T(128)} %bitcast.core_ref, ...), custom_call_target="tpu_custom_call" | custom-call | flops 23441965056 | bytes 33914880 | tf_op jit(solution)/shard_map/pallas_call | solution.py:762
  204.7 12.3 %shard_map.194.g_ref = bf16[3,736,512]{2,1,0:T(8,128)(2,1)S(1)} custom-call(s32[1]{0:T(128)} %add.398.len_ref, bf16[3,736,768]{2,1,0:T(8,128)(2,1)} %get-tuple-element.260.q_ref.k_ref.v_ref, bf16[3,736,768]{2,1,0:T(8,128)(2,1)} %get-tuple-element.260.q_ref.k_ref.v_ref, bf16[3,736,768]{2,1,0:T(8,128)(2,1)} %get-tuple-element.260.q_ref.k_ref.v_ref, ...), custom_call_target="tpu_custom_call" | custom-call | flops 8875147264 | bytes 9043968 | tf_op jit(solution)/shard_map/pallas_call | solution.py:557
  224.8 18.4 %shard_map.195 = (bf16[2,2,24,8,768]{4,3,2,1,0:T(8,128)(2,1)S(1)}, bf16[2,2,24,8,768]{4,3,2,1,0:T(8,128)(2,1)S(1)}, bf16[2,2,12,8,768]{4,3,2,1,0:T(8,128)(2,1)S(...) custom-call(s32[1]{0:T(128)} %bitcast.core_ref, ...), custom_call_target="tpu_custom_call" | custom-call | flops 10225713152 | bytes 28262400 | tf_op jit(solution)/shard_map/pallas_call | solution.py:867
  243.2 6.8 %collective-permute-done.22 = bf16[2,48,8,768]{3,2,1,0:T(8,128)(2,1)S(1)} collective-permute-done((bf16[2,48,8,768]{3,2,1,0:T(8,128)(2,1)S(1)}, bf16[2,48,8,768]{3,2,1,0:T(8,128)(2,1)S(1)}, u32[]{:S(2)}, u32[]{:S(2)}) %collective-permute-start.22) | collective-permute-done | bytes 1179680 | tf_op jit(solution)/shard_map/ppermute | solution.py:63
  254.7 21.7 %shard_map.196 = (bf16[4096,512]{1,0:T(8,128)(2,1)S(1)}, bf16[256,256]{1,0:T(8,128)(2,1)S(1)}, f32[480,256]{1,0:T(8,128)}) custom-call(bf16[480,256]{1,0:T(8,128)(2,1)S(1)} %copy-done.8, bf16[4096,512]{1,0:T(8,128)(2,1)S(1)} %copy-done.2, bf16[4096,512]{1,0:T(8,128)(2,1)S(1)} %copy-done.2, bf16[480,256]{1,0:T(8,128)(2,1)S(1)} %get-tuple-element.318.do_ref, ...), custom_call_target="tpu_custom_call" | custom-call | flops 20132659200 | bytes 8388608 | tf_op jit(solution)/shard_map/pallas_call | solution.py:430
  278.7 3.0 collective-permute-start.29
  284.6 14.4 %shard_map.197 = (f32[4096,256]{1,0:T(8,128)S(1)}, bf16[4096,256]{1,0:T(8,128)(2,1)S(1)}, bf16[2,2,52,8,256]{4,3,2,1,0:T(8,128)(2,1)S(1)}, bf16[2,2,52,8,256]{4,3,2,1,0:T(8,128)(2,1)S(1)}) custom-call(s32[1]{0:T(128)} %bitcast.core_ref, bf16[4096,512]{1,0:T(8,128)(2,1)S(1)} %get-tuple-element.345.dkv_ref, bf16[4096,256]{1,0:T(8,128)(2,1)} %get-tuple-element.346.slope_ref, ...), custom_call_target="tpu_custom_call" | custom-call | flops 6979321856 | bytes 20971520 | tf_op jit(solution)/shard_map/pallas_call | solution.py:1021
  306.6 3.1 collective-permute-done.35
  309.7 3.9 collective-permute-done.34
  318.0 8.0 %shard_map.198 = bf16[4096,256]{1,0:T(8,128)(2,1)S(1)} custom-call(bf16[4096,256]{1,0:T(8,128)(2,1)S(1)} %get-tuple-element.389.gz_ref, f32[4096,256]{1,0:T(8,128)S(1)} %get-tuple-element.390.d_hidden_ref, bf16[9,256,256]{2,1,0:T(8,128)(2,1)S(1)} %get-tuple-element.452.conv_ref), custom_call_target="tpu_custom_call" | custom-call | flops 4831838208 | bytes 8388608 | tf_op jit(solution)/shard_map/pallas_call | solution.py:1087
  340.3 4.9 %collective-permute-done.45 = bf16[19,8,256]{2,1,0:T(8,128)(2,1)} collective-permute-done((bf16[19,8,256]{2,1,0:T(8,128)(2,1)}, bf16[19,8,256]{2,1,0:T(8,128)(2,1)}, u32[]{:S(2)}, u32[]{:S(2)}) %collective-permute-start.45) | collective-permute-done | bytes 77856 | tf_op jit(solution)/shard_map/ppermute | solution.py:63
  353.0 4.3 %all-to-all-start.1 = ((bf16[32,9,8,256]{3,2,1,0:T(8,128)(2,1)}), bf16[32,9,8,256]{3,2,1,0:T(8,128)(2,1)}, u32[]{:S(2)}, u32[]{:S(2)}) async-start(bf16[32,9,8,256]{3,2,1,0:T(8,128)(2,1)} %bitcast.151), calls=%async_computation.1 | async-start | bytes 2359296 | tf_op jit(solution)/shard_map/all_to_all | solution.py:1283
  360.6 22.6 %collective-permute-done.42 = bf16[16,64,256]{2,1,0:T(8,128)(2,1)S(1)} collective-permute-done((bf16[16,64,256]{2,1,0:T(8,128)(2,1)S(1)}, bf16[16,64,256]{2,1,0:T(8,128)(2,1)S(1)}, u32[]{:S(2)}, u32[]{:S(2)}) %collective-permute-start.42) | collective-permute-done | bytes 524320 | tf_op jit(solution)/shard_map/ppermute | solution.py:63
  389.4 6.5 %subtract_select_fusion = (f32[8,256,256]{2,1,0:T(8,128)}, f32[8,256,256]{2,1,0:T(8,128)}, f32[8,256,256]{2,1,0:T(8,128)}) fusion(f32[8,256,256]{2,1,0:T(8,128)S(1)} %copy-done.21, pred[8]{0:T(512)(128)(4,1)S(1)} %broadcast_compare_fusion, f32[8,256,256]{2,1,0:T(8,128)} %param.21, f32[8,256,256]{2,1,0:T(8,128)} %param.22, ...), kind=kLoop, calls=%fused_computation.14 | loop fusion | flops 10485760 | bytes 13631500 | tf_op jit(solution)/shard_map/jit(_where)/select_n | solution.py:1304
  (277 shorter events, 125.0 us)
Async XLA Ops:
  10.0 33.7 %all-to-all-start = ((bf16[32,8,8,256]{3,2,1,0:T(8,128)(2,1)}), bf16[32,8,8,256]{3,2,1,0:T(8,128)(2,1)S(1)}, u32[]{:S(2)}, u32[]{:S(2)}) async-start(bf16[32,8,8,256]{3,2,1,0:T(8,128)(2,1)} %copy.146), calls=%async_computation | async-start | bytes 2097152 | tf_op jit(solution)/shard_map/all_to_all | solution.py:1130
  17.3 150.0 %all-gather.2.cloned.1.call-start = ((), (), s32[]{:S(2)}) async-start(), calls=%async_computation.2 | async-start | bytes 9732096 | tf_op jit(solution)/shard_map/all_gather | solution.py:1163
  20.1 39.4 %collective-permute-start = (bf16[16,64,256]{2,1,0:T(8,128)(2,1)}, bf16[16,64,256]{2,1,0:T(8,128)(2,1)S(1)}, u32[]{:S(2)}, u32[]{:S(2)}) collective-permute-start(bf16[16,64,256]{2,1,0:T(8,128)(2,1)} %get-tuple-element.441), channel_id=1, source_target_pairs={{0,1},{1,0},{2,3},{3,2},{4,5},{5,4},{6,7},{7,6},{8,9},{9,8},{10,11... | collective-permute-start | bytes 1572872 | tf_op jit(solution)/shard_map/ppermute | solution.py:63
  21.9 39.3 %collective-permute-start.1 = (bf16[16,64,256]{2,1,0:T(8,128)(2,1)}, bf16[16,64,256]{2,1,0:T(8,128)(2,1)S(1)}, u32[]{:S(2)}, u32[]{:S(2)}) collective-permute-start(bf16[16,64,256]{2,1,0:T(8,128)(2,1)} %get-tuple-element.443), channel_id=1, source_target_pairs={{0,2},{1,3},{2,0},{3,1},{4,6},{5,7},{6,4},{7,5},{8,10},{9,11},{10,... | collective-permute-start | bytes 1572872 | tf_op jit(solution)/shard_map/ppermute | solution.py:63
  23.3 37.8 %collective-permute-start.2 = (bf16[16,64,256]{2,1,0:T(8,128)(2,1)}, bf16[16,64,256]{2,1,0:T(8,128)(2,1)S(1)}, u32[]{:S(2)}, u32[]{:S(2)}) collective-permute-start(bf16[16,64,256]{2,1,0:T(8,128)(2,1)} %get-tuple-element.440), channel_id=1, source_target_pairs={{0,3},{1,2},{2,1},{3,0},{4,7},{5,6},{6,5},{7,4},{8,11},{9,10},{10,... | collective-permute-start | bytes 1572872 | tf_op jit(solution)/shard_map/ppermute | solution.py:63
  90.9 22.6 %collective-permute-start.16 = (bf16[7,2,4,8,768]{4,3,2,1,0:T(8,128)(2,1)}, bf16[7,2,4,8,768]{4,3,2,1,0:T(8,128)(2,1)}, u32[]{:S(2)}, u32[]{:S(2)}) collective-permute-start(bf16[7,2,4,8,768]{4,3,2,1,0:T(8,128)(2,1)} %pad_maximum_fusion.4), channel_id=1, source_target_pairs={{0,1},{1,0},{2,3},{3,2},{4,5},{5,4},{6,7},{7,6},{8,9},{9,8},{10,11... | collective-permute-start | bytes 2064392 | tf_op jit(solution)/shard_map/ppermute | solution.py:63
  91.6 21.9 %collective-permute-start.15 = (bf16[6,2,4,8,768]{4,3,2,0,1:T(8,128)(2,1)S(1)}, bf16[6,2,4,8,768]{4,3,2,0,1:T(8,128)(2,1)}, u32[]{:S(2)}, u32[]{:S(2)}) collective-permute-start(bf16[6,2,4,8,768]{4,3,2,0,1:T(8,128)(2,1)S(1)} %pad_maximum_fusion.5), channel_id=1, source_target_pairs={{0,2},{2,0},{1,3},{3,1},{4,6},{6,4},{5,7},{7,5},{8,10},{10,8},{9,1... | collective-permute-start | bytes 1769480 | tf_op jit(solution)/shard_map/ppermute | solution.py:63
  221.9 28.2 %collective-permute-start.22 = (bf16[2,48,8,768]{3,2,1,0:T(8,128)(2,1)S(1)}, bf16[2,48,8,768]{3,2,1,0:T(8,128)(2,1)S(1)}, u32[]{:S(2)}, u32[]{:S(2)}) collective-permute-start(bf16[2,48,8,768]{3,2,1,0:T(8,128)(2,1)S(1)} %get-tuple-element.304), channel_id=1, source_target_pairs={{0,2},{2,0},{1,3},{3,1},{4,6},{6,4},{5,7},{7,5},{8,10},{10,8},{9,1... | collective-permute-start | bytes 3538952 | tf_op jit(solution)/shard_map/ppermute | solution.py:63
  223.4 27.8 %collective-permute-start.23 = (bf16[2,48,8,768]{3,2,1,0:T(8,128)(2,1)S(1)}, bf16[2,48,8,768]{3,2,1,0:T(8,128)(2,1)S(1)}, u32[]{:S(2)}, u32[]{:S(2)}) collective-permute-start(bf16[2,48,8,768]{3,2,1,0:T(8,128)(2,1)S(1)} %get-tuple-element.306), channel_id=1, source_target_pairs={{0,1},{1,0},{2,3},{3,2},{4,5},{5,4},{6,7},{7,6},{8,9},{9,8},{10,11... | collective-permute-start | bytes 3538952 | tf_op jit(solution)/shard_map/ppermute | solution.py:63
  252.0 24.4 %collective-permute-start.26 = (bf16[2,2,24,8,768]{4,3,2,1,0:T(8,128)(2,1)S(1)}, bf16[2,2,24,8,768]{4,3,2,1,0:T(8,128)(2,1)S(1)}, u32[]{:S(2)}, u32[]{:S(2)}) collective-permute-start(bf16[2,2,24,8,768]{4,3,2,1,0:T(8,128)(2,1)S(1)} %get-tuple-element.327), channel_id=1, source_target_pairs={{0,4},{4,0},{1,5},{5,1},{2,6},{6,2},{3,7},{7,3},{8,12},{12,8},{9,1... | collective-permute-start | bytes 3538952 | tf_op jit(solution)/shard_map/ppermute | solution.py:63
  252.1 24.3 %collective-permute-start.24 = (bf16[48,8,768]{2,1,0:T(8,128)(2,1)S(1)}, bf16[48,8,768]{2,1,0:T(8,128)(2,1)S(1)}, u32[]{:S(2)}, u32[]{:S(2)}) collective-permute-start(bf16[48,8,768]{2,1,0:T(8,128)(2,1)S(1)} %get-tuple-element.323), channel_id=1, source_target_pairs={{0,1},{1,0},{2,3},{3,2},{4,5},{5,4},{6,7},{7,6},{8,9},{9,8},{10,11... | collective-permute-start | bytes 1769480 | tf_op jit(solution)/shard_map/ppermute | solution.py:63
  253.5 22.9 %collective-permute-start.25 = (bf16[48,8,768]{2,1,0:T(8,128)(2,1)S(1)}, bf16[48,8,768]{2,1,0:T(8,128)(2,1)S(1)}, u32[]{:S(2)}, u32[]{:S(2)}) collective-permute-start(bf16[48,8,768]{2,1,0:T(8,128)(2,1)S(1)} %get-tuple-element.325), channel_id=1, source_target_pairs={{0,2},{2,0},{1,3},{3,1},{4,6},{6,4},{5,7},{7,5},{8,10},{10,8},{9,1... | collective-permute-start | bytes 1769480 | tf_op jit(solution)/shard_map/ppermute | solution.py:63
  254.2 22.3 %collective-permute-start.27 = (bf16[2,2,12,8,768]{4,3,2,1,0:T(8,128)(2,1)S(1)}, bf16[2,2,12,8,768]{4,3,2,1,0:T(8,128)(2,1)S(1)}, u32[]{:S(2)}, u32[]{:S(2)}) collective-permute-start(bf16[2,2,12,8,768]{4,3,2,1,0:T(8,128)(2,1)S(1)} %get-tuple-element.329), channel_id=1, source_target_pairs={{0,4},{4,0},{1,5},{5,1},{2,6},{6,2},{3,7},{7,3},{8,12},{12,8},{9,1... | collective-permute-start | bytes 1769480 | tf_op jit(solution)/shard_map/ppermute | solution.py:63
  254.2 22.3 %collective-permute-start.28 = (bf16[2,2,8,8,768]{4,3,2,1,0:T(8,128)(2,1)S(1)}, bf16[2,2,8,8,768]{4,3,2,1,0:T(8,128)(2,1)S(1)}, u32[]{:S(2)}, u32[]{:S(2)}) collective-permute-start(bf16[2,2,8,8,768]{4,3,2,1,0:T(8,128)(2,1)S(1)} %get-tuple-element.331), channel_id=1, source_target_pairs={{0,4},{4,0},{1,5},{5,1},{2,6},{6,2},{3,7},{7,3},{8,12},{12,8},{9,1... | collective-permute-start | bytes 1179656 | tf_op jit(solution)/shard_map/ppermute | solution.py:63
  278.7 22.2 %collective-permute-start.29 = (bf16[24,2,8,768]{3,2,0,1:T(8,128)(2,1)S(1)}, bf16[24,2,8,768]{3,2,0,1:T(8,128)(2,1)S(1)}, u32[]{:S(2)}, u32[]{:S(2)}) collective-permute-start(bf16[24,2,8,768]{3,2,0,1:T(8,128)(2,1)S(1)} %get-tuple-element.356), channel_id=1, source_target_pairs={{0,8},{8,0},{16,24},{24,16},{1,9},{9,1},{17,25},{25,17},{2,10},{10... | collective-permute-start | bytes 1769480 | tf_op jit(solution)/shard_map/ppermute | solution.py:63
  281.8 19.2 %collective-permute-start.30 = (bf16[2,24,8,768]{3,2,1,0:T(8,128)(2,1)S(1)}, bf16[2,24,8,768]{3,2,1,0:T(8,128)(2,1)S(1)}, u32[]{:S(2)}, u32[]{:S(2)}) collective-permute-start(bf16[2,24,8,768]{3,2,1,0:T(8,128)(2,1)S(1)} %get-tuple-element.358), channel_id=1, source_target_pairs={{0,1},{1,0},{2,3},{3,2},{4,5},{5,4},{6,7},{7,6},{8,9},{9,8},{10,11... | collective-permute-start | bytes 1769480 | tf_op jit(solution)/shard_map/ppermute | solution.py:63
  283.1 17.9 %collective-permute-start.31 = (bf16[2,24,8,768]{3,2,1,0:T(8,128)(2,1)S(1)}, bf16[2,24,8,768]{3,2,1,0:T(8,128)(2,1)S(1)}, u32[]{:S(2)}, u32[]{:S(2)}) collective-permute-start(bf16[2,24,8,768]{3,2,1,0:T(8,128)(2,1)S(1)} %get-tuple-element.360), channel_id=1, source_target_pairs={{0,2},{2,0},{1,3},{3,1},{4,6},{6,4},{5,7},{7,5},{8,10},{10,8},{9,1... | collective-permute-start | bytes 1769480 | tf_op jit(solution)/shard_map/ppermute | solution.py:63
  284.3 16.6 %collective-permute-start.32 = (bf16[2,8,8,768]{3,2,1,0:T(8,128)(2,1)S(1)}, bf16[2,8,8,768]{3,2,1,0:T(8,128)(2,1)S(1)}, u32[]{:S(2)}, u32[]{:S(2)}) collective-permute-start(bf16[2,8,8,768]{3,2,1,0:T(8,128)(2,1)S(1)} %get-tuple-element.362), channel_id=1, source_target_pairs={{0,1},{1,0},{2,3},{3,2},{4,5},{5,4},{6,7},{7,6},{8,9},{9,8},{10,11... | collective-permute-start | bytes 589832 | tf_op jit(solution)/shard_map/ppermute | solution.py:63
  305.2 20.9 %collective-permute-start.41 = (bf16[24,8,768]{2,1,0:T(8,128)(2,1)S(1)}, bf16[24,8,768]{2,1,0:T(8,128)(2,1)S(1)}, u32[]{:S(2)}, u32[]{:S(2)}) collective-permute-start(bf16[24,8,768]{2,1,0:T(8,128)(2,1)S(1)} %get-tuple-element.473), channel_id=1, source_target_pairs={{0,16},{8,24},{16,0},{24,8},{1,17},{9,25},{17,1},{25,9},{2,18},{10... | collective-permute-start | bytes 884744 | tf_op jit(solution)/shard_map/ppermute | solution.py:63
  330.1 16.7 %collective-permute-start.47 = (bf16[12,8,768]{2,1,0:T(8,128)(2,1)}, bf16[12,8,768]{2,1,0:T(8,128)(2,1)}, u32[]{:S(2)}, u32[]{:S(2)}) collective-permute-start(bf16[12,8,768]{2,1,0:T(8,128)(2,1)} %get-tuple-element.414), channel_id=1, source_target_pairs={{0,16},{8,24},{16,0},{24,8},{1,17},{9,25},{17,1},{25,9},{2,18},{10... | collective-permute-start | bytes 442376 | tf_op jit(solution)/shard_map/ppermute | solution.py:63
  339.0 14.1 %collective-permute-start.48 = (bf16[16,64,256]{2,1,0:T(8,128)(2,1)}, bf16[16,64,256]{2,1,0:T(8,128)(2,1)S(1)}, u32[]{:S(2)}, u32[]{:S(2)}) collective-permute-start(bf16[16,64,256]{2,1,0:T(8,128)(2,1)} %get-tuple-element.436), channel_id=1, source_target_pairs={{0,3},{1,2},{2,1},{3,0},{4,7},{5,6},{6,5},{7,4},{8,11},{9,10},{10,... | collective-permute-start | bytes 1572872 | tf_op jit(solution)/shard_map/ppermute | solution.py:63
  353.0 33.4 %all-to-all-start.1 = ((bf16[32,9,8,256]{3,2,1,0:T(8,128)(2,1)}), bf16[32,9,8,256]{3,2,1,0:T(8,128)(2,1)}, u32[]{:S(2)}, u32[]{:S(2)}) async-start(bf16[32,9,8,256]{3,2,1,0:T(8,128)(2,1)} %bitcast.151), calls=%async_computation.1 | async-start | bytes 2359296 | tf_op jit(solution)/shard_map/all_to_all | solution.py:1283
  357.3 25.9 %collective-permute-start.42 = (bf16[16,64,256]{2,1,0:T(8,128)(2,1)S(1)}, bf16[16,64,256]{2,1,0:T(8,128)(2,1)S(1)}, u32[]{:S(2)}, u32[]{:S(2)}) collective-permute-start(bf16[16,64,256]{2,1,0:T(8,128)(2,1)S(1)} %copy-done.27), channel_id=1, source_target_pairs={{0,1},{1,0},{2,3},{3,2},{4,5},{5,4},{6,7},{7,6},{8,9},{9,8},{10,11... | collective-permute-start | bytes 1572872 | tf_op jit(solution)/shard_map/ppermute | solution.py:63
  359.1 24.1 %collective-permute-start.43 = (bf16[16,64,256]{2,1,0:T(8,128)(2,1)S(1)}, bf16[16,64,256]{2,1,0:T(8,128)(2,1)S(1)}, u32[]{:S(2)}, u32[]{:S(2)}) collective-permute-start(bf16[16,64,256]{2,1,0:T(8,128)(2,1)S(1)} %copy-done.26), channel_id=1, source_target_pairs={{0,2},{1,3},{2,0},{3,1},{4,6},{5,7},{6,4},{7,5},{8,10},{9,11},{10,... | collective-permute-start | bytes 1572872 | tf_op jit(solution)/shard_map/ppermute | solution.py:63
  (62 other events, 528.6 us)
Sparse Core Ops, SparseCore 0:
  80.0 87.2 all-gather.1
